TPU v7x, 32 devices: a whole 2x2x4 slice. The times are simulated.
32 devices in a mesh: fsdp: 16 (over z, y, x), tp: 2 (over core).
Axes of the slice: x: 2, y: 2, z: 4, core: 2. Of those that a mesh axis runs over, the one named last changes fastest.
Arguments:
- hidden_in: bfloat16 [8192, 2048], P(('fsdp', 'tp')), may hold values from -6 to 6
- out_grad: bfloat16 [8192, 2048], P(('fsdp', 'tp')), may hold values from -6 to 6
- segments: int32 [8192], P('fsdp'), may hold values from 0 to 16, as said below
- positions: int32 [8192], P('fsdp'), may hold values from 0 to 2047, as said below
- w_query: bfloat16 [2048, 2048], P('fsdp', 'tp'), may hold values from -0.125 to 0.125
- key_weight: bfloat16 [2048, 1024], P('fsdp', 'tp'), may hold values from -0.125 to 0.125
- value_weight: bfloat16 [2048, 1024], P('fsdp', 'tp'), may hold values from -0.125 to 0.125
- w_output: bfloat16 [2048, 2048], P('tp', 'fsdp'), may hold values from -1 to 1
- w_gate: bfloat16 [2048, 6144], P('fsdp', 'tp'), may hold values from -0.125 to 0.125
- w_up: bfloat16 [2048, 6144], P('fsdp', 'tp'), may hold values from -0.125 to 0.125
- w_down: bfloat16 [6144, 2048], P('tp', 'fsdp'), may hold values from -0.078125 to 0.078125
- attn_gain: bfloat16 [2048], P('fsdp'), may hold values from 0.5 to 1.5
- mlp_gain: bfloat16 [2048], P('fsdp'), may hold values from 0.5 to 1.5
- query_gain: bfloat16 [128], P('fsdp'), may hold values from 0.5 to 1.5
- key_gain: bfloat16 [128], P('fsdp'), may hold values from 0.5 to 1.5
Outputs:
- hidden_out: bfloat16 [8192, 2048], P(('fsdp', 'tp'))
- grad_in: float32 [8192, 2048], P(('fsdp', 'tp'))
- grad_query: float32 [2048, 2048], P('fsdp', 'tp')
- grad_key: float32 [2048, 1024], P('fsdp', 'tp')
- grad_value: float32 [2048, 1024], P('fsdp', 'tp')
- grad_output: float32 [2048, 2048], P('tp', 'fsdp')
- grad_gate: float32 [2048, 6144], P('fsdp', 'tp')
- grad_up: float32 [2048, 6144], P('fsdp', 'tp')
- grad_down: float32 [6144, 2048], P('tp', 'fsdp')
- grad_attn_gain: float32 [2048], P('fsdp')
- grad_mlp_gain: float32 [2048], P('fsdp')
- grad_query_gain: float32 [128], P('fsdp')
- grad_key_gain: float32 [128], P('fsdp')
Inputs may be any that keep to these rules, and one draw needn't show every extreme that they name: `segments`: numbers start at 0 in each sequence of 512 tokens and never fall along it; every sequence reaches the largest number; one document of each sequence covers all of its middle half. `positions`: each token's place within its document, the first document of a sequence counting from an offset below 2048.
All inputs are finite; a program needn't handle non-finite values.
Results may differ from a plain program's by a relative error of at most 0.013.
Values may be sent and summed in bfloat16 or wider, within the bound.
No kernel may reach another device: no remote copies, remote signals or barrier semaphores. Data moves between devices by JAX's collectives and lax.ppermute only.
A program may use at most 320 MiB of HBM per device.

v0:
```python
import jax
import jax.numpy as jnp
from jax import lax
from jax.sharding import PartitionSpec as P

epsilon = 1e-06
rope_base = 1000000.0


def normalize(operand, norm_gain):
    return (
        operand
        * lax.rsqrt(jnp.mean(operand * operand, axis=-1, keepdims=True) + epsilon)
        * norm_gain
    )


def norm_back(operand, norm_gain, upstream):
    factor = lax.rsqrt(jnp.mean(operand * operand, axis=-1, keepdims=True) + epsilon)
    weighted = upstream * norm_gain
    inner = jnp.mean(weighted * operand, axis=-1, keepdims=True)
    operand_grad = factor * weighted - operand * factor * factor * factor * inner
    gain_grad = jnp.sum((upstream * operand * factor).reshape(-1, operand.shape[-1]), axis=0)
    return (operand_grad, gain_grad)


def rotate(operand, cosine_table, sine_table):
    half_size = operand.shape[-1] // 2
    lead_half = operand[..., :half_size]
    tail_half = operand[..., half_size:]
    return jnp.concatenate(
        [
            lead_half * cosine_table - tail_half * sine_table,
            tail_half * cosine_table + lead_half * sine_table,
        ],
        axis=-1,
    )


def tables(positions, head_size):
    indices = jnp.arange(head_size // 2).astype(jnp.float32)
    frequency = rope_base ** (-2.0 * indices / head_size)
    angles = positions.astype(jnp.float32)[..., None] * frequency
    return (jnp.cos(angles), jnp.sin(angles))


def widen(local_rows):
    return lax.all_gather(local_rows, "tp", axis=0, tiled=True)


def narrow(partial_terms):
    return lax.psum_scatter(partial_terms, "tp", scatter_dimension=0, tiled=True)


def mask_scores(query_blk, key_matrix, seg_blk, seg_all, first_row, scale):
    scores = (
        jnp.einsum("sgrd,tgd->grst", query_blk, key_matrix, preferred_element_type=jnp.float32)
        * scale
    )
    query_place = first_row + jnp.arange(query_blk.shape[0])
    key_place = jnp.arange(key_matrix.shape[0])
    allowed = (seg_blk[:, None] == seg_all[None, :]) & (key_place[None, :] <= query_place[:, None])
    return jnp.where(allowed, scores, -1e30)


def fetch_attention(w_query, key_weight, value_weight, w_output, attn_gain, query_gain, key_gain):
    return (
        lax.all_gather(w_query, "fsdp", axis=0, tiled=True),
        lax.all_gather(key_weight, "fsdp", axis=0, tiled=True),
        lax.all_gather(value_weight, "fsdp", axis=0, tiled=True),
        lax.all_gather(w_output, "fsdp", axis=1, tiled=True),
        lax.all_gather(attn_gain, "fsdp", axis=0, tiled=True),
        lax.all_gather(query_gain, "fsdp", axis=0, tiled=True),
        lax.all_gather(key_gain, "fsdp", axis=0, tiled=True),
    )


def fetch_mlp(w_gate, w_up, w_down, mlp_gain):
    return (
        lax.all_gather(w_gate, "fsdp", axis=0, tiled=True),
        lax.all_gather(w_up, "fsdp", axis=0, tiled=True),
        lax.all_gather(w_down, "fsdp", axis=1, tiled=True),
        lax.all_gather(mlp_gain, "fsdp", axis=0, tiled=True),
    )


def on_device(
    hidden_in,
    out_grad,
    segments,
    positions,
    w_query,
    key_weight,
    value_weight,
    w_output,
    w_gate,
    w_up,
    w_down,
    attn_gain,
    mlp_gain,
    query_gain,
    key_gain,
):
    attn_set = fetch_attention(
        w_query, key_weight, value_weight, w_output, attn_gain, query_gain, key_gain
    )
    full_query, full_key, full_value, full_output = (
        attn_set[0],
        attn_set[1],
        attn_set[2],
        attn_set[3],
    )
    gain_in = attn_set[4].astype(jnp.float32)
    gain_query = attn_set[5].astype(jnp.float32)
    gain_key = attn_set[6].astype(jnp.float32)
    head_size = gain_query.shape[0]
    scale = head_size ** (-0.5)
    residual_in = hidden_in.astype(jnp.float32)
    input_normalized = normalize(residual_in, gain_in).astype(jnp.bfloat16)
    gathered_in = widen(input_normalized)
    seq_len = gathered_in.shape[0]
    q_heads = full_query.shape[1] // head_size
    kv_heads = full_key.shape[1] // head_size
    repeat = q_heads // kv_heads
    cosine_table, sine_table = tables(positions, head_size)
    cosine_table = cosine_table[:, None, :]
    sine_table = sine_table[:, None, :]
    query_raw = jnp.dot(gathered_in, full_query, preferred_element_type=jnp.float32).reshape(
        seq_len, q_heads, head_size
    )
    key_unrotated = jnp.dot(gathered_in, full_key, preferred_element_type=jnp.float32).reshape(
        seq_len, kv_heads, head_size
    )
    query_rows = (
        rotate(normalize(query_raw, gain_query), cosine_table, sine_table)
        .astype(jnp.bfloat16)
        .reshape(seq_len, kv_heads, repeat, head_size)
    )
    key_matrix = rotate(normalize(key_unrotated, gain_key), cosine_table, sine_table).astype(
        jnp.bfloat16
    )
    value_matrix = (
        jnp.dot(gathered_in, full_value, preferred_element_type=jnp.float32)
        .astype(jnp.bfloat16)
        .reshape(seq_len, kv_heads, head_size)
    )
    block_rows = min(512, seq_len)
    block_count = seq_len // block_rows
    query_blocks = query_rows.reshape(block_count, block_rows, kv_heads, repeat, head_size)
    seg_blocks = segments.reshape(block_count, block_rows)
    block_starts = jnp.arange(block_count) * block_rows

    def forward_block(block_item):
        query_blk, seg_blk, first_row = block_item
        scores = mask_scores(query_blk, key_matrix, seg_blk, segments, first_row, scale)
        row_top = jnp.max(scores, axis=-1, keepdims=True)
        exp_terms = jnp.exp(scores - row_top)
        row_total = jnp.sum(exp_terms, axis=-1, keepdims=True)
        prob_low = (exp_terms / row_total).astype(jnp.bfloat16)
        attended_blk = jnp.einsum(
            "grst,tgd->sgrd", prob_low, value_matrix, preferred_element_type=jnp.float32
        )
        return (attended_blk.astype(jnp.bfloat16), (row_top + jnp.log(row_total))[..., 0])

    attended_blocks, lse_blocks = lax.map(forward_block, (query_blocks, seg_blocks, block_starts))
    attention_output = attended_blocks.reshape(seq_len, q_heads * head_size)
    middle = residual_in + narrow(
        jnp.dot(attention_output, full_output, preferred_element_type=jnp.float32)
    )
    mlp_set = fetch_mlp(w_gate, w_up, w_down, mlp_gain)
    full_gate, full_up, full_down = (mlp_set[0], mlp_set[1], mlp_set[2])
    gain_mid = mlp_set[3].astype(jnp.float32)
    normed_mid = normalize(middle, gain_mid).astype(jnp.bfloat16)
    gathered_mid = widen(normed_mid)
    gate_proj = jnp.dot(gathered_mid, full_gate, preferred_element_type=jnp.float32)
    up_proj = jnp.dot(gathered_mid, full_up, preferred_element_type=jnp.float32)
    sigma = jax.nn.sigmoid(gate_proj)
    activated = (gate_proj * sigma * up_proj).astype(jnp.bfloat16)
    hidden_out = (
        middle + narrow(jnp.dot(activated, full_down, preferred_element_type=jnp.float32))
    ).astype(jnp.bfloat16)
    back_mlp = (
        lax.all_gather(w_gate, "fsdp", axis=0, tiled=True),
        lax.all_gather(w_up, "fsdp", axis=0, tiled=True),
        lax.all_gather(w_down, "fsdp", axis=1, tiled=True),
        lax.all_gather(mlp_gain, "fsdp", axis=0, tiled=True),
    )
    back_gate, back_up, back_down = (back_mlp[0], back_mlp[1], back_mlp[2])
    upstream = out_grad.astype(jnp.float32)
    gathered_grad = widen(out_grad)
    down_grad_w = jnp.dot(activated.T, gathered_grad, preferred_element_type=jnp.float32)
    act_grad = jnp.dot(gathered_grad, back_down.T, preferred_element_type=jnp.float32)
    gate_grad = (act_grad * up_proj * sigma * (1.0 + gate_proj * (1.0 - sigma))).astype(
        jnp.bfloat16
    )
    up_grad = (act_grad * gate_proj * sigma).astype(jnp.bfloat16)
    gate_grad_w = jnp.dot(gathered_mid.T, gate_grad, preferred_element_type=jnp.float32)
    up_grad_w = jnp.dot(gathered_mid.T, up_grad, preferred_element_type=jnp.float32)
    mid_normed_grad = jnp.dot(gate_grad, back_gate.T, preferred_element_type=jnp.float32) + jnp.dot(
        up_grad, back_up.T, preferred_element_type=jnp.float32
    )
    mid_norm_part, mlp_gain_grad = norm_back(middle, gain_mid, narrow(mid_normed_grad))
    middle_grad = upstream + mid_norm_part
    shard_gate, shard_up, shard_down, shard_mlp_gain = (
        lax.psum_scatter(gate_grad_w, "fsdp", scatter_dimension=0, tiled=True),
        lax.psum_scatter(up_grad_w, "fsdp", scatter_dimension=0, tiled=True),
        lax.psum_scatter(down_grad_w, "fsdp", scatter_dimension=1, tiled=True),
        lax.psum_scatter(mlp_gain_grad, "fsdp", scatter_dimension=0, tiled=True),
    )
    back_attn = (
        lax.all_gather(w_query, "fsdp", axis=0, tiled=True),
        lax.all_gather(key_weight, "fsdp", axis=0, tiled=True),
        lax.all_gather(value_weight, "fsdp", axis=0, tiled=True),
        lax.all_gather(w_output, "fsdp", axis=1, tiled=True),
        lax.all_gather(attn_gain, "fsdp", axis=0, tiled=True),
        lax.all_gather(query_gain, "fsdp", axis=0, tiled=True),
        lax.all_gather(key_gain, "fsdp", axis=0, tiled=True),
    )
    back_query, back_key, back_value, back_output = (
        back_attn[0],
        back_attn[1],
        back_attn[2],
        back_attn[3],
    )
    gathered_branch = widen(middle_grad.astype(jnp.bfloat16))
    output_grad_w = jnp.dot(attention_output.T, gathered_branch, preferred_element_type=jnp.float32)
    attended_grad = jnp.dot(
        gathered_branch, back_output.T, preferred_element_type=jnp.float32
    ).astype(jnp.bfloat16)
    grad_blocks = attended_grad.reshape(block_count, block_rows, kv_heads, repeat, head_size)

    def backward_block(totals, block_item):
        key_total, value_total = totals
        query_blk, grad_blk, seg_blk, first_row, lse_blk = block_item
        scores = mask_scores(query_blk, key_matrix, seg_blk, segments, first_row, scale)
        prob_rows = jnp.exp(scores - lse_blk[..., None])
        prob_low = prob_rows.astype(jnp.bfloat16)
        prob_grad = jnp.einsum(
            "sgrd,tgd->grst", grad_blk, value_matrix, preferred_element_type=jnp.float32
        )
        row_delta = jnp.sum(prob_rows * prob_grad, axis=-1, keepdims=True)
        score_grad = (prob_rows * (prob_grad - row_delta)).astype(jnp.bfloat16)
        query_part = (
            jnp.einsum("grst,tgd->sgrd", score_grad, key_matrix, preferred_element_type=jnp.float32)
            * scale
        )
        key_total = (
            key_total
            + jnp.einsum(
                "grst,sgrd->tgd", score_grad, query_blk, preferred_element_type=jnp.float32
            )
            * scale
        )
        value_total = value_total + jnp.einsum(
            "grst,sgrd->tgd", prob_low, grad_blk, preferred_element_type=jnp.float32
        )
        return ((key_total, value_total), query_part)

    starting = jnp.zeros((seq_len, kv_heads, head_size), jnp.float32)
    (key_grad, value_grad), query_parts = lax.scan(
        backward_block,
        (starting, starting),
        (query_blocks, grad_blocks, seg_blocks, block_starts, lse_blocks),
    )
    query_grad = query_parts.reshape(seq_len, q_heads, head_size)
    query_back, query_gain_grad = norm_back(
        query_raw, gain_query, rotate(query_grad, cosine_table, -sine_table)
    )
    key_back, key_gain_grad = norm_back(
        key_unrotated, gain_key, rotate(key_grad, cosine_table, -sine_table)
    )
    query_back = query_back.astype(jnp.bfloat16).reshape(seq_len, q_heads * head_size)
    key_back = key_back.astype(jnp.bfloat16).reshape(seq_len, kv_heads * head_size)
    value_back = value_grad.astype(jnp.bfloat16).reshape(seq_len, kv_heads * head_size)
    query_grad_w = jnp.dot(gathered_in.T, query_back, preferred_element_type=jnp.float32)
    key_grad_w = jnp.dot(gathered_in.T, key_back, preferred_element_type=jnp.float32)
    value_grad_w = jnp.dot(gathered_in.T, value_back, preferred_element_type=jnp.float32)
    in_normed_grad = jnp.dot(query_back, back_query.T, preferred_element_type=jnp.float32)
    in_normed_grad = in_normed_grad + jnp.dot(
        key_back, back_key.T, preferred_element_type=jnp.float32
    )
    in_normed_grad = in_normed_grad + jnp.dot(
        value_back, back_value.T, preferred_element_type=jnp.float32
    )
    in_norm_part, attn_gain_grad = norm_back(residual_in, gain_in, narrow(in_normed_grad))
    grad_in = middle_grad + in_norm_part
    (
        shard_query,
        shard_key,
        shard_value,
        shard_output,
        shard_attn_gain,
        shard_query_gain,
        shard_key_gain,
    ) = (
        lax.psum_scatter(query_grad_w, "fsdp", scatter_dimension=0, tiled=True),
        lax.psum_scatter(key_grad_w, "fsdp", scatter_dimension=0, tiled=True),
        lax.psum_scatter(value_grad_w, "fsdp", scatter_dimension=0, tiled=True),
        lax.psum_scatter(output_grad_w, "fsdp", scatter_dimension=1, tiled=True),
        lax.psum_scatter(attn_gain_grad, "fsdp", scatter_dimension=0, tiled=True),
        lax.psum_scatter(query_gain_grad, "fsdp", scatter_dimension=0, tiled=True),
        lax.psum_scatter(key_gain_grad, "fsdp", scatter_dimension=0, tiled=True),
    )
    sum_attn_gain, sum_mlp_gain, sum_query_gain, sum_key_gain = lax.psum(
        (shard_attn_gain, shard_mlp_gain, shard_query_gain, shard_key_gain), "tp"
    )
    return (
        hidden_out,
        grad_in,
        shard_query,
        shard_key,
        shard_value,
        shard_output,
        shard_gate,
        shard_up,
        shard_down,
        sum_attn_gain,
        sum_mlp_gain,
        sum_query_gain,
        sum_key_gain,
    )


def solution(mesh):
    in_specs = (
        P(("fsdp", "tp"), None),
        P(("fsdp", "tp"), None),
        P("fsdp"),
        P("fsdp"),
        P("fsdp", "tp"),
        P("fsdp", "tp"),
        P("fsdp", "tp"),
        P("tp", "fsdp"),
        P("fsdp", "tp"),
        P("fsdp", "tp"),
        P("tp", "fsdp"),
        P("fsdp"),
        P("fsdp"),
        P("fsdp"),
        P("fsdp"),
    )
    out_specs = (
        P(("fsdp", "tp"), None),
        P(("fsdp", "tp"), None),
        P("fsdp", "tp"),
        P("fsdp", "tp"),
        P("fsdp", "tp"),
        P("tp", "fsdp"),
        P("fsdp", "tp"),
        P("fsdp", "tp"),
        P("tp", "fsdp"),
        P("fsdp"),
        P("fsdp"),
        P("fsdp"),
        P("fsdp"),
    )
    return jax.shard_map(
        on_device, mesh=mesh, in_specs=in_specs, out_specs=out_specs, check_vma=False
    )
```

profile of v0, /device:TPU:0, one launch (start us, length us, event | category | flops | bytes accessed | tf_op | source)
XLA Modules:
  0.0 2752.4 jit_solution(15646757769257953416)
XLA Ops:
  7.2 42.4 %all-gather = bf16[16,1,128]{2,1,0:T(2,128)(2,1)S(1)} all-gather(bf16[1,1,128]{2,1,0:T(2,128)(2,1)} %bitcast.199), channel_id=1, replica_groups=mesh['fsdp'=16,'tp'=2] {'fsdp'}, dimensions={0}, use_global_device_ids=true | all-gather | bytes 4352 | tf_op jit(solution)/shard_map/all_gather | solution.py:72
  51.7 2.5 fusion.11
  58.7 36.7 %all-reduce.8 = (bf16[128]{0:T(256)(128)(2,1)S(1)}, bf16[128]{0:T(256)(128)(2,1)S(1)}) all-reduce(bf16[128]{0:T(256)(128)(2,1)S(1)} %dynamic-update-slice.1, bf16[128]{0:T(256)(128)(2,1)S(1)} %dynamic-update-slice), channel_id=1, replica_groups=mesh['fsdp'=16,'tp'=2] {'fsdp'}, use_global_device_ids=true, to_apply=%add.1 | all-reduce | flops 256 | bytes 1024
  96.4 1.8 fusion.41
  98.2 27.4 all-gather.18.cloned.1.call-done
  125.6 3.5 multiply_reduce_fusion.6
  131.5 56.2 %all-gather.16.cloned.1.call-done = bf16[2048,512]{1,0:T(8,128)(2,1)} async-done(((bf16[128,512]{1,0:T(8,128)(2,1)}), bf16[2048,512]{1,0:T(8,128)(2,1)}) %all-gather.16.cloned.1.call-update) | async-done | bytes 2097168 | tf_op jit(solution)/shard_map/all_gather | solution.py:70
  187.7 3.7 convolution_convert_fusion.1
  191.4 73.7 %all-gather.20.cloned.1.call-done = bf16[2048,1024]{1,0:T(8,128)(2,1)} async-done(((bf16[128,1024]{1,0:T(8,128)(2,1)}), bf16[2048,1024]{1,0:T(8,128)(2,1)}) %all-gather.20.cloned.1.call-update) | async-done | bytes 4194320 | tf_op jit(solution)/shard_map/all_gather | solution.py:68
  265.1 4.5 fusion.49
  276.1 2.5 fusion.48
  279.8 2.1 copy-done
  281.9 1.7 fusion.26
  283.7 71.9 %all-gather.22.cloned.1.call-done = bf16[1024,2048]{1,0:T(8,128)(2,1)} async-done(((bf16[1024,128]{1,0:T(8,128)(2,1)}), bf16[1024,2048]{1,0:T(8,128)(2,1)}) %all-gather.22.cloned.1.call-update) | async-done | bytes 4194320 | tf_op jit(solution)/shard_map/all_gather | solution.py:71
  355.5 6.5 fusion.50
  362.7 37.6 %all-gather.1 = bf16[16,1,128]{2,1,0:T(2,128)(2,1)S(1)} all-gather(bf16[1,1,128]{2,1,0:T(2,128)(2,1)S(1)} %bitcast.200), channel_id=1, replica_groups=mesh['fsdp'=16,'tp'=2] {'fsdp'}, dimensions={0}, use_global_device_ids=true | all-gather | bytes 4352 | tf_op jit(solution)/shard_map/all_gather | solution.py:83
  400.3 1.9 multiply_reduce_fusion.3
  406.6 3.7 all-gather.24.cloned.1.call-done
  410.3 156.4 %all-gather.26.cloned.1.call-done = bf16[2048,3072]{1,0:T(8,128)(2,1)} async-done(((bf16[128,3072]{1,0:T(8,128)(2,1)}), bf16[2048,3072]{1,0:T(8,128)(2,1)}) %all-gather.26.cloned.1.call-update) | async-done | bytes 12582928 | tf_op jit(solution)/shard_map/all_gather | solution.py:80
  566.7 12.1 fusion.51
  578.8 141.3 %all-gather.28.cloned.1.call-done = bf16[2048,3072]{1,0:T(8,128)(2,1)} async-done(((bf16[128,3072]{1,0:T(8,128)(2,1)}), bf16[2048,3072]{1,0:T(8,128)(2,1)}) %all-gather.28.cloned.1.call-update) | async-done | bytes 12582928 | tf_op jit(solution)/shard_map/all_gather | solution.py:81
  720.1 12.0 fusion.52
  732.1 198.5 %all-gather.30.cloned.1.call-done = bf16[3072,2048]{1,0:T(8,128)(2,1)} async-done(((bf16[3072,128]{1,0:T(8,128)(2,1)}), bf16[3072,2048]{1,0:T(8,128)(2,1)}) %all-gather.30.cloned.1.call-update) | async-done | bytes 12582928 | tf_op jit(solution)/shard_map/all_gather | solution.py:82
  930.6 17.5 multiply_convert_fusion
  948.1 12.1 fusion.54
  960.1 11.9 convolution_add_fusion
  972.1 10.3 reduce-scatter.16.cloned.1.call-done
  982.4 2.9 multiply_reduce_fusion
  985.3 1.8 fusion.45
  987.2 11.9 all-gather.34.cloned.1.call-done
  999.2 5.2 convolution_convert_fusion
  1005.4 5.5 fusion
  1011.0 2.9 fusion.2
  1016.8 2.4 fusion.32
  1019.3 2.0 copy.108
  1021.3 1.9 copy.107
  1023.2 2.8 multiply_subtract_fusion
  1026.2 2.4 multiply_reduce_fusion.1
  1032.1 2.6 copy.83
  1034.8 1.5 fusion.36
  1038.8 2.0 fusion.18
  1041.7 2.5 fusion.55
  1046.1 3.3 add_add_fusion
  1049.5 11.9 fusion.53
  1061.4 5.3 fusion.58
  1066.7 4.9 fusion.59
  1071.7 7.9 fusion.57
  1079.9 7.6 fusion.60
  1087.6 14.3 fusion.61
  1101.9 14.0 fusion.62
  1116.3 14.0 fusion.63
  1133.0 2.3 reshape.252
  1135.5 2.7 reshape.251
  1138.4 2.0 copy.88
  1144.3 2.3 fusion.22
  1146.6 77.8 %all-reduce.6 = (f32[2048]{0:T(1024)S(1)}, f32[2048]{0:T(1024)S(1)}, f32[128]{0:T(128)S(1)}, f32[128]{0:T(128)S(1)}) all-reduce(f32[2048]{0:T(1024)S(1)} %get-tuple-element.61, f32[2048]{0:T(1024)S(1)} %copy-done.55, f32[128]{0:T(128)S(1)} %fusion.25, f32[128]{0:T(128)S(1)} %fusion.39), channel_id=13, replica_groups=mesh['fsdp'=16,'tp'=2] {'fsdp'}, use_global_device_ids=true, to_apply=%region_23.24.clone | all-reduce | flops 4352 | bytes 34816
  1224.6 3.0 all-reduce.7
  1227.6 6.3 fusion.15
  1233.9 43.2 %reduce-scatter.24.cloned.1.call-done = f32[128,512]{1,0:T(8,128)} async-done(((f32[2048,512]{1,0:T(8,128)}), f32[128,512]{1,0:T(8,128)}) %reduce-scatter.24.cloned.1.call-update) | async-done | bytes 262160 | tf_op jit(solution)/shard_map/reduce_scatter | solution.py:298
  1277.1 180.1 %reduce-scatter.20.cloned.1.call-done = f32[128,1024]{1,0:T(8,128)} async-done(((f32[2048,1024]{1,0:T(8,128)}), f32[128,1024]{1,0:T(8,128)}) %reduce-scatter.20.cloned.1.call-update) | async-done | bytes 524304 | tf_op jit(solution)/shard_map/reduce_scatter | solution.py:296
  1457.2 183.1 %reduce-scatter.26.cloned.1.call-done = f32[1024,128]{1,0:T(8,128)} async-done(((f32[1024,2048]{1,0:T(8,128)}), f32[1024,128]{1,0:T(8,128)}) %reduce-scatter.26.cloned.1.call-update) | async-done | bytes 524304 | tf_op jit(solution)/shard_map/reduce_scatter | solution.py:299
  1640.4 370.3 %reduce-scatter.28.cloned.1.call-done = f32[128,3072]{1,0:T(8,128)} async-done(((f32[2048,3072]{1,0:T(8,128)}), f32[128,3072]{1,0:T(8,128)}) %reduce-scatter.28.cloned.1.call-update) | async-done | bytes 1572880 | tf_op jit(solution)/shard_map/reduce_scatter | solution.py:205
  2010.7 367.1 %reduce-scatter.30.cloned.1.call-done = f32[128,3072]{1,0:T(8,128)} async-done(((f32[2048,3072]{1,0:T(8,128)}), f32[128,3072]{1,0:T(8,128)}) %reduce-scatter.30.cloned.1.call-update) | async-done | bytes 1572880 | tf_op jit(solution)/shard_map/reduce_scatter | solution.py:206
  2377.8 367.3 %reduce-scatter.32.cloned.1.call-done = f32[3072,128]{1,0:T(8,128)} async-done(((f32[3072,2048]{1,0:T(8,128)}), f32[3072,128]{1,0:T(8,128)}) %reduce-scatter.32.cloned.1.call-update) | async-done | bytes 1572880 | tf_op jit(solution)/shard_map/reduce_scatter | solution.py:207
  (249 shorter events, 41.3 us)
Async XLA Ops:
  7.2 91.0 %all-gather.14.cloned.1.call-start = ((), (), s32[]{:S(2)}) async-start(), calls=%async_computation.11 | async-start | bytes 3145728 | tf_op jit(solution)/shard_map/all_gather | solution.py:48
  51.1 5.8 copy-start.63
  51.1 7.1 copy-start.67
  51.1 7.3 copy-start.68
  51.1 44.3 %copy-start.64 = (s32[512]{0:T(512)S(1)}, s32[512]{0:T(512)}, u32[]{:S(2)}) copy-start(s32[512]{0:T(512)} %param.18) | copy-start | bytes 6148
  51.2 44.3 %copy-start.62 = (s32[512]{0:T(512)S(1)}, s32[512]{0:T(512)}, u32[]{:S(2)}) copy-start(s32[512]{0:T(512)} %param.17) | copy-start | bytes 6148
  54.3 71.3 %all-gather.18.cloned.1.call-start = ((), (), s32[]{:S(2)}) async-start(), calls=%async_computation.13 | async-start | bytes 2228224 | tf_op jit(solution)/shard_map/all_gather | solution.py:69
  55.0 132.7 %all-gather.16.cloned.1.call-start = ((), (), s32[]{:S(2)}) async-start(), calls=%async_computation.12 | async-start | bytes 2228224 | tf_op jit(solution)/shard_map/all_gather | solution.py:70
  55.7 209.4 %all-gather.20.cloned.1.call-start = ((), (), s32[]{:S(2)}) async-start(), calls=%async_computation.14 | async-start | bytes 4456448 | tf_op jit(solution)/shard_map/all_gather | solution.py:68
  56.3 299.2 %all-gather.22.cloned.1.call-start = ((), (), s32[]{:S(2)}) async-start(), calls=%async_computation.15 | async-start | bytes 4456448 | tf_op jit(solution)/shard_map/all_gather | solution.py:71
  56.9 343.4 %reduce-scatter.12.cloned.1.call-start = ((), (), s32[]{:S(2)}) async-start(), calls=%async_computation.16 | async-start | bytes 6291456 | tf_op jit(solution)/shard_map/reduce_scatter | solution.py:52
  98.2 176.1 %copy-start.27 = (f32[512,64]{1,0:T(8,128)}, f32[512,64]{1,0:T(8,128)S(1)}, u32[]{:S(2)}) copy-start(f32[512,64]{1,0:T(8,128)S(1)} %get-tuple-element.107) | copy-start | bytes 393220
  130.8 57.0 %copy-start.12 = (bf16[512,2048]{1,0:T(8,128)(2,1)S(1)}, bf16[512,2048]{1,0:T(8,128)(2,1)}, u32[]{:S(2)}) copy-start(bf16[512,2048]{1,0:T(8,128)(2,1)} %all-gather.14.cloned.1.call-done) | copy-start | bytes 6291460
  131.5 144.0 %copy-start.31 = (bf16[512,4,64]{2,0,1:T(8,128)(2,1)}, bf16[512,4,64]{2,0,1:T(8,128)(2,1)S(1)}, u32[]{:S(2)}) copy-start(bf16[512,4,64]{2,0,1:T(8,128)(2,1)S(1)} %get-tuple-element.103) | copy-start | bytes 786436
  131.5 144.0 %copy-start.33 = (bf16[512,4,64]{2,0,1:T(8,128)(2,1)}, bf16[512,4,64]{2,0,1:T(8,128)(2,1)S(1)}, u32[]{:S(2)}) copy-start(bf16[512,4,64]{2,0,1:T(8,128)(2,1)S(1)} %get-tuple-element.104) | copy-start | bytes 786436
  275.3 3.3 copy-start.13
  275.5 3.1 copy-start.15
  278.6 3.3 copy-start
  278.6 3.3 copy-start.47
  283.6 78.4 %copy-start.42 = (bf16[4,128,2,512]{3,1,2,0:T(8,128)(2,1)}, bf16[4,128,2,512]{3,1,2,0:T(8,128)(2,1)S(1)}, u32[]{:S(2)}) copy-start(bf16[4,128,2,512]{3,1,2,0:T(8,128)(2,1)S(1)} %fusion.26) | copy-start | bytes 3145732
  362.0 38.3 %copy-start.5 = (bf16[256,2048]{1,0:T(8,128)(2,1)S(1)}, bf16[256,2048]{1,0:T(8,128)(2,1)}, u32[]{:S(2)}) copy-start(bf16[256,2048]{1,0:T(8,128)(2,1)} %param.15) | copy-start | bytes 3145732
  362.0 48.3 %all-gather.24.cloned.1.call-start = ((), (), s32[]{:S(2)}) async-start(), calls=%async_computation.17 | async-start | bytes 3145728 | tf_op jit(solution)/shard_map/all_gather | solution.py:48
  400.3 585.0 %copy-start.49 = (f32[16,1,128]{2,1,0:T(1,128)}, f32[16,1,128]{2,1,0:T(1,128)S(1)}, u32[]{:S(2)}) copy-start(f32[16,1,128]{2,1,0:T(1,128)S(1)} %convert_element_type.118) | copy-start | bytes 24580
  402.3 583.0 %copy-start.1 = (f32[256,2048]{1,0:T(8,128)}, f32[256,2048]{1,0:T(8,128)S(1)}, u32[]{:S(2)}) copy-start(f32[256,2048]{1,0:T(8,128)S(1)} %get-tuple-element.89) | copy-start | bytes 6291460
  402.3 583.0 %copy-start.56 = (f32[256]{0:T(256)}, f32[256]{0:T(256)S(1)}, u32[]{:S(2)}) copy-start(f32[256]{0:T(256)S(1)} %add_rsqrt_fusion.2) | copy-start | bytes 3076
  403.7 163.0 %all-gather.26.cloned.1.call-start = ((), (), s32[]{:S(2)}) async-start(), calls=%async_computation.18 | async-start | bytes 13369344 | tf_op jit(solution)/shard_map/all_gather | solution.py:80
  404.5 315.6 %all-gather.28.cloned.1.call-start = ((), (), s32[]{:S(2)}) async-start(), calls=%async_computation.19 | async-start | bytes 13369344 | tf_op jit(solution)/shard_map/all_gather | solution.py:81
  405.2 326.9 %all-gather.32.cloned.1.call-start = ((), (), s32[]{:S(2)}) async-start(), calls=%async_computation.22 | async-start | bytes 3145728 | tf_op jit(solution)/shard_map/all_gather | solution.py:48
  405.8 524.8 %all-gather.30.cloned.1.call-start = ((), (), s32[]{:S(2)}) async-start(), calls=%async_computation.20 | async-start | bytes 13369344 | tf_op jit(solution)/shard_map/all_gather | solution.py:82
  406.5 575.9 %reduce-scatter.16.cloned.1.call-start = ((), (), s32[]{:S(2)}) async-start(), calls=%async_computation.23 | async-start | bytes 6291456 | tf_op jit(solution)/shard_map/reduce_scatter | solution.py:52
  948.1 12.1 copy-start.69
  972.0 13.3 copy-start.19
  972.0 27.1 all-gather.34.cloned.1.call-start
  982.4 2.9 copy-start.9
  987.1 157.1 %reduce-scatter.18.cloned.1.call-start = ((), (), s32[]{:S(2)}) async-start(), calls=%async_computation.25 | async-start | bytes 6291456 | tf_op jit(solution)/shard_map/reduce_scatter | solution.py:52
  1004.9 6.0 slice-start
  1005.4 5.5 slice-start.1
  1011.0 2.9 copy-start.32
  1011.0 2.9 copy-start.34
  1023.2 2.9 copy-start.4
  1026.1 2.5 copy-start.7
  1026.2 3.1 copy-start.39
  1029.8 2.3 copy-start.22
  1029.8 2.3 copy-start.24
  1032.1 2.6 copy-start.21
  1032.1 2.6 copy-start.54
  1036.3 7.9 copy-start.29
  1036.3 2.4 copy-start.26
  1038.7 3.0 copy-start.66
  1041.7 2.6 copy-start.43
  1049.4 178.2 %reduce-scatter.14.cloned.1.call-start = ((), (), s32[]{:S(2)}) async-start(), calls=%async_computation.21 | async-start | bytes 6291456 | tf_op jit(solution)/shard_map/reduce_scatter | solution.py:52
  1061.3 172.6 %reduce-scatter.22.cloned.1.call-start = ((), (), s32[]{:S(2)}) async-start(), calls=%async_computation.27 | async-start | bytes 4456448 | tf_op jit(solution)/shard_map/reduce_scatter | solution.py:297
  1066.7 210.4 %reduce-scatter.24.cloned.1.call-start = ((), (), s32[]{:S(2)}) async-start(), calls=%async_computation.28 | async-start | bytes 4456448 | tf_op jit(solution)/shard_map/reduce_scatter | solution.py:298
  1071.7 385.6 %reduce-scatter.20.cloned.1.call-start = ((), (), s32[]{:S(2)}) async-start(), calls=%async_computation.26 | async-start | bytes 8912896 | tf_op jit(solution)/shard_map/reduce_scatter | solution.py:296
  1079.7 560.7 %reduce-scatter.26.cloned.1.call-start = ((), (), s32[]{:S(2)}) async-start(), calls=%async_computation.29 | async-start | bytes 8912896 | tf_op jit(solution)/shard_map/reduce_scatter | solution.py:299
  1087.6 923.1 %reduce-scatter.28.cloned.1.call-start = ((), (), s32[]{:S(2)}) async-start(), calls=%async_computation.30 | async-start | bytes 26738688 | tf_op jit(solution)/shard_map/reduce_scatter | solution.py:205
  1101.9 1275.9 %reduce-scatter.30.cloned.1.call-start = ((), (), s32[]{:S(2)}) async-start(), calls=%async_computation.31 | async-start | bytes 26738688 | tf_op jit(solution)/shard_map/reduce_scatter | solution.py:206
  1116.0 1629.1 %reduce-scatter.32.cloned.1.call-start = ((), (), s32[]{:S(2)}) async-start(), calls=%async_computation.32 | async-start | bytes 26738688 | tf_op jit(solution)/shard_map/reduce_scatter | solution.py:207
  1138.4 2.8 copy-start.37
  1144.2 2.4 copy-start.55
  1144.2 83.4 %copy-start.2 = (f32[256,2048]{1,0:T(8,128)S(1)}, f32[256,2048]{1,0:T(8,128)}, u32[]{:S(2)}) copy-start(f32[256,2048]{1,0:T(8,128)} %copy-done.1) | copy-start | bytes 6291460
  1144.2 83.4 %copy-start.50 = (f32[16,1,128]{2,1,0:T(1,128)S(1)}, f32[16,1,128]{2,1,0:T(1,128)}, u32[]{:S(2)}) copy-start(f32[16,1,128]{2,1,0:T(1,128)} %copy-done.49) | copy-start | bytes 24580
  1144.2 83.4 %copy-start.57 = (f32[256]{0:T(256)S(1)}, f32[256]{0:T(256)}, u32[]{:S(2)}) copy-start(f32[256]{0:T(256)} %copy-done.56) | copy-start | bytes 3076
  1144.2 83.4 %copy-start.61 = (f32[256]{0:T(256)S(1)}, f32[256]{0:T(256)}, u32[]{:S(2)}) copy-start(f32[256]{0:T(256)} %copy-done.60) | copy-start | bytes 3076
  (30 other events, 40.7 us)
Sparse Core Ops, SparseCore 0:
  54.4 6.4 all-gather.13
  63.6 61.8 all-gather.17
  128.3 59.3 all-gather.15
  190.4 74.7 all-gather.19
  267.7 87.7 all-gather.21
  362.2 10.2 reduce-scatter.11
  403.8 6.4 all-gather.23
  413.5 153.1 all-gather.25
  569.9 150.1 all-gather.27
  721.6 8.7 all-gather.31
  733.4 197.1 all-gather.29
  972.1 10.2 reduce-scatter.15
  987.3 11.8 all-gather.33
  1049.5 13.2 reduce-scatter.17
  1065.0 13.3 reduce-scatter.13
  1081.1 97.3 reduce-scatter.21
  1181.3 95.8 reduce-scatter.23
  1279.8 177.3 reduce-scatter.19
  1460.1 180.2 reduce-scatter.25
  1646.5 364.0 reduce-scatter.27
  2017.0 360.7 reduce-scatter.29
  2384.1 360.9 reduce-scatter.31
where the time goes:
time: 2760 us; the launch traced here: 2750 us
  waiting for transfers between devices  2270 us (82%)
  blocking collectives  197 us (7%)
  matrix products  190 us (7%)
  other arithmetic  44.4 us (2%)
  local copies, waits for them, and re-layouts  33.4 us (1%)
    reduce_scatter x1, waiting for transfers between devices, on_device(): lax.psum_scatter(gate_grad_w, 'fsdp', scatter_dimension=0, tiled=True)  370 us
    reduce_scatter x1, waiting for transfers between devices, on_device(): lax.psum_scatter(down_grad_w, 'fsdp', scatter_dimension=1, tiled=True)  367 us
    reduce_scatter x1, waiting for transfers between devices, on_device(): lax.psum_scatter(up_grad_w, 'fsdp', scatter_dimension=0, tiled=True)  367 us
    all_gather x1, waiting for transfers between devices, fetch_mlp(): lax.all_gather(w_down, 'fsdp', axis=1, tiled=True)  199 us
    reduce_scatter x1, waiting for transfers between devices, on_device(): lax.psum_scatter(output_grad_w, 'fsdp', scatter_dimension=1, tiled=True)  183 us
    reduce_scatter x1, waiting for transfers between devices, on_device(): lax.psum_scatter(query_grad_w, 'fsdp', scatter_dimension=0, tiled=True)  180 us
    all_gather x1, waiting for transfers between devices, fetch_mlp(): lax.all_gather(w_gate, 'fsdp', axis=0, tiled=True)  156 us
    all_gather x1, waiting for transfers between devices, fetch_mlp(): lax.all_gather(w_up, 'fsdp', axis=0, tiled=True)  141 us
  transfers between devices with their start and end apart: 22, of which 16 were waited for; matrix products, arithmetic and copies ran while one was open for 5% of the time, Pallas kernels for 0%

commit v1 on v0

v1 whole, which is shorter than its diff:
```python
import functools

import jax
import jax.numpy as jnp
from jax import lax
from jax.experimental import pallas as pl
from jax.experimental.pallas import tpu as pltpu
from jax.sharding import Mesh, PartitionSpec as P

epsilon = 1e-06
rope_base = 1000000.0
bf16 = jnp.bfloat16
f32 = jnp.float32
BESIDE = pl.CostEstimate(flops=1 << 20, bytes_accessed=1 << 16, transcendentals=0)


def dot(left, right):
    return jnp.dot(left, right, preferred_element_type=f32)


def dot_right_t(left, right):
    return lax.dot_general(left, right, (((1,), (1,)), ((), ())), preferred_element_type=f32)


def dot_left_t(left, right):
    return lax.dot_general(left, right, (((0,), (0,)), ((), ())), preferred_element_type=f32)


def normalize(operand, norm_gain):
    return (
        operand
        * lax.rsqrt(jnp.mean(operand * operand, axis=-1, keepdims=True) + epsilon)
        * norm_gain
    )


def norm_back(operand, norm_gain, upstream):
    factor = lax.rsqrt(jnp.mean(operand * operand, axis=-1, keepdims=True) + epsilon)
    weighted = upstream * norm_gain
    inner = jnp.mean(weighted * operand, axis=-1, keepdims=True)
    return factor * weighted - operand * factor * factor * factor * inner


def tables(positions, head_size):
    indices = jnp.arange(head_size // 2).astype(f32)
    frequency = rope_base ** (-2.0 * indices / head_size)
    angles = positions.astype(f32)[..., None] * frequency
    cosine, sine = jnp.cos(angles), jnp.sin(angles)
    return (jnp.concatenate([cosine, cosine], -1), jnp.concatenate([-sine, sine], -1))


def half_turn(operand):
    return pltpu.roll(operand, operand.shape[-1] // 2, 1)


def lay_in_order(scratch, refs, core):
    half = refs[0].shape[1]
    for j, ref in enumerate(refs):
        scratch[pl.ds(pl.multiple_of((core ^ j) * half, half), half)] = ref[0]


def head_rows(raw, heads, repeat, gains, cosine, sine):
    size = gains.shape[1]

    def turned(column, gain):
        rows = normalize(raw[:, column * size : (column + 1) * size], gain)
        return (rows * cosine + half_turn(rows) * sine).astype(bf16)

    queries = [turned(h, gains[0:1]) for h in range(heads * repeat)]
    keys = [turned(heads * repeat + g, gains[1:2]) for g in range(heads)]
    first = heads * repeat + heads
    values = [
        raw[:, (first + g) * size : (first + g + 1) * size].astype(bf16) for g in range(heads)
    ]
    return queries, keys, values


def masked_probs(key, query, allowed):
    scores = dot_right_t(key, query) * query.shape[1] ** (-0.5)
    scores = jnp.where(allowed, scores, -1e30)
    exp_terms = jnp.exp(scores - jnp.max(scores, axis=0, keepdims=True))
    return exp_terms * (1.0 / jnp.sum(exp_terms, axis=0, keepdims=True))


def query_strips(rows, column_ref, row_ref):
    step = min(128, rows)
    for first in range(0, rows, step):
        seen = first + step
        keys = lax.broadcasted_iota(jnp.int32, (seen, step), 0)
        queries = lax.broadcasted_iota(jnp.int32, (seen, step), 1) + first
        same = column_ref[0, :seen, 0:1] == row_ref[0, 0:1, first:seen]
        yield slice(first, seen), seen, same & (keys <= queries)


def attend_kernel(cores, heads, repeat, core_ref, *refs):
    raws, refs = refs[:cores], refs[cores:]
    cos_ref, sin_ref, column_ref, row_ref, gain_ref = refs[:5]
    outs, raw, rows_out = refs[5:-2], refs[-2], refs[-1]
    core = core_ref[0]
    half = raws[0].shape[1]
    lay_in_order(raw, raws, core)
    queries, keys, values = head_rows(
        raw, heads, repeat, gain_ref[...], cos_ref[0], sin_ref[0]
    )
    size = gain_ref.shape[1]
    turned = [value.astype(f32).T.astype(bf16) for value in values]
    for at, seen, allowed in query_strips(raw.shape[0], column_ref, row_ref):
        for h, query in enumerate(queries):
            g = h // repeat
            probs = masked_probs(keys[g][:seen], query[at], allowed).astype(bf16)
            rows = dot(turned[g][:, :seen], probs).T
            rows_out[at, h * size : (h + 1) * size] = rows.astype(bf16)
    for j, out in enumerate(outs):
        out[0] = rows_out[pl.ds(pl.multiple_of((core ^ j) * half, half), half)]


def attend_back_kernel(cores, heads, repeat, core_ref, *refs):
    raws, grads, refs = refs[:cores], refs[cores : 2 * cores], refs[2 * cores :]
    cos_ref, sin_ref, column_ref, row_ref, gain_ref = refs[:5]
    outs, gain_out = refs[5 : 5 + cores], refs[5 + cores]
    raw, grad, totals, rows_out = refs[6 + cores :]
    core = core_ref[0]
    half = raws[0].shape[1]
    cosine, sine, gains = cos_ref[0], sin_ref[0], gain_ref[...]
    lay_in_order(raw, raws, core)
    lay_in_order(grad, grads, core)
    queries, keys, values = head_rows(raw, heads, repeat, gains, cosine, sine)
    size = gains.shape[1]
    scale = size ** (-0.5)
    count = heads * repeat

    @pl.when(pl.program_id(0) == 0)
    def _():
        gain_out[...] = jnp.zeros_like(gain_out)

    def columns(i):
        return slice(i * size, (i + 1) * size)

    turned_keys = [key.astype(f32).T.astype(bf16) for key in keys]
    totals[:, count * size :] = jnp.zeros_like(totals[:, count * size :])
    for at, seen, allowed in query_strips(raw.shape[0], column_ref, row_ref):
        for g in range(heads):
            key_grad = value_grad = None
            for h in range(g * repeat, (g + 1) * repeat):
                probs = masked_probs(keys[g][:seen], queries[h][at], allowed)
                out_grad = grad[at, columns(h)]
                prob_grad = dot_right_t(values[g][:seen], out_grad)
                delta = jnp.sum(probs * prob_grad, axis=0, keepdims=True)
                score_grad = (probs * (prob_grad - delta)).astype(bf16)
                totals[at, columns(h)] = dot(turned_keys[g][:, :seen], score_grad).T * scale
                key_part = dot(score_grad, queries[h][at])
                value_part = dot(probs.astype(bf16), out_grad)
                key_grad = key_part if key_grad is None else key_grad + key_part
                value_grad = value_part if value_grad is None else value_grad + value_part
            totals[:seen, columns(count + g)] += key_grad * scale
            totals[:seen, columns(count + heads + g)] += value_grad
    for i in range(count + heads):
        row = 0 if i < count else 1
        upstream = totals[:, columns(i)]
        turned = upstream * cosine - half_turn(upstream) * sine
        rows = raw[:, columns(i)]
        factor = lax.rsqrt(jnp.mean(rows * rows, axis=-1, keepdims=True) + epsilon)
        gain_out[row : row + 1] += jnp.sum(turned * rows * factor, axis=0, keepdims=True)
        back = norm_back(rows, gains[row : row + 1], turned)
        rows_out[:, columns(i)] = back.astype(bf16)
    rows_out[:, (count + heads) * size :] = totals[:, (count + heads) * size :].astype(bf16)
    for j, out in enumerate(outs):
        out[0] = rows_out[pl.ds(pl.multiple_of((core ^ j) * half, half), half)]


def attention_call(kernel, name, core, halves, shared, gains, outs, extra_out, scratch):
    def per_sequence(array):
        return pl.BlockSpec((1,) + array.shape[1:], lambda i: (i, 0, 0))

    whole = pl.BlockSpec(gains.shape, lambda i: (0, 0))
    out_specs = [per_sequence(shape) for shape in outs] + [
        pl.BlockSpec(shape.shape, lambda i: (0, 0)) for shape in extra_out
    ]
    return pl.pallas_call(
        kernel,
        grid=(halves[0].shape[0],),
        in_specs=[pl.BlockSpec(memory_space=pltpu.SMEM)]
        + [per_sequence(array) for array in halves + shared]
        + [whole],
        out_specs=out_specs,
        out_shape=outs + extra_out,
        scratch_shapes=[pltpu.VMEM(shape, dtype) for shape, dtype in scratch],
        compiler_params=pltpu.CompilerParams(vmem_limit_bytes=48 << 20),
        cost_estimate=BESIDE,
        name=name,
    )(core.reshape(1), *halves, *shared, gains)


def resident(shape):
    zeros = (0,) * len(shape)
    return pl.BlockSpec(shape, lambda i: zeros, pipeline_mode=pl.Buffered(1))


def project_kernel(count, *refs):
    lefts, rights, outs = refs[:count], refs[count : 2 * count], refs[2 * count :]
    total = dot_right_t(lefts[0][...], rights[0][0])
    for left, right in zip(lefts[1:], rights[1:]):
        total = total + dot_right_t(left[...], right[0])
    first = 0
    for out in outs:
        out[...] = total[first : first + out.shape[0]].astype(out.dtype)
        first += out.shape[0]


def project(lefts, rights, places, first, sizes, step, name):
    parts = rights[0].shape[0]
    rows = sum(sizes)

    def left_spec(left):
        return pl.BlockSpec(
            (rows, left.shape[1]), lambda i: (first // rows, 0), pipeline_mode=pl.Buffered(1)
        )

    def right_spec(left, place):
        return pl.BlockSpec((1, step, left.shape[1]), lambda i: (i, 0, place))

    return list(
        pl.pallas_call(
            functools.partial(project_kernel, len(lefts)),
            grid=(parts,),
            in_specs=[left_spec(left) for left in lefts]
            + [right_spec(left, place) for left, place in zip(lefts, places)],
            out_specs=[pl.BlockSpec((size, step), lambda i: (0, i)) for size in sizes],
            out_shape=[
                jax.ShapeDtypeStruct((size, parts * step), bf16 if first or k else f32)
                for k, size in enumerate(sizes)
            ],
            compiler_params=pltpu.CompilerParams(vmem_limit_bytes=56 << 20),
            cost_estimate=BESIDE,
            name=name,
        )(*lefts, *rights)
    )


def project_and_send(lefts, rights, places, rows, step, name):
    if lax.axis_size("model") == 1:
        return project(lefts, rights, places, 0, [rows], step, name)[0], [], []
    half = rows // 2
    far = project(lefts, rights, places, 3 * rows, [half] * 2, step, name + "_far")
    got = [trade(far[0], "model", 1), trade(far[1], "model", 2)]
    own, *near = project(lefts, rights, places, 0, [rows] + [half] * 4, step, name)
    return own, got, send_near(near, got)


def put_rows(whole, pieces, change):
    first = 0
    for piece in pieces:
        whole[first : first + piece.shape[0]] = change(piece[...])
        first += piece.shape[0]


def rows_kernel(kind, count, *refs):
    (own, base), got, refs = refs[:2], refs[2 : 2 + count], list(refs[2 + count :])
    total = own[...]
    if count == 4:
        upper = got[0][...].astype(f32) + got[1][...].astype(f32)
        lower = got[2][...].astype(f32) + got[3][...].astype(f32)
        total += jnp.where(pl.program_id(0) < pl.num_programs(0) // 2, upper, lower)
    else:
        for piece in got:
            total += piece[...].astype(f32)
    rows = base[...].astype(f32)
    if kind == "sum":
        refs[0][...] = (rows + total).astype(bf16)
    elif kind == "norm":
        gain, whole, low = refs
        whole[...] = rows + total
        low[...] = normalize(rows + total, gain[...]).astype(bf16)
    else:
        gain, more, whole = refs[:3]
        total = more[...].astype(f32) + norm_back(rows, gain[...], total)
        whole[...] = total
        for low in refs[3:]:
            low[...] = total.astype(bf16)


def rows_call(kind, own, base, got, gain, more, dtypes, name):
    rows, width = own.shape
    step = rows // 4
    strip = pl.BlockSpec((step, width), lambda i: (i, 0))
    upper = pl.BlockSpec((step, width), lambda i: (jnp.minimum(i, 1), 0))
    lower = pl.BlockSpec((step, width), lambda i: (jnp.maximum(i - 2, 0), 0))
    operands = [own, base] + list(got)
    in_specs = [strip, strip]
    in_specs += [upper, upper, lower, lower] if len(got) == 4 else [strip] * len(got)
    if gain is not None:
        operands.append(gain.reshape(1, width))
        in_specs.append(resident((1, width)))
    if more is not None:
        operands.append(more)
        in_specs.append(strip)
    return list(
        pl.pallas_call(
            functools.partial(rows_kernel, kind, len(got)),
            grid=(4,),
            in_specs=in_specs,
            out_specs=[strip] * len(dtypes),
            out_shape=[jax.ShapeDtypeStruct((rows, width), dtype) for dtype in dtypes],
            compiler_params=pltpu.CompilerParams(vmem_limit_bytes=32 << 20),
            cost_estimate=BESIDE,
            name=name,
        )(*operands)
    )


def rows_product_kernel(count, normed, *refs):
    pieces, refs = refs[:count], list(refs[count:])
    gain = refs.pop(0)[...] if normed else None
    weight, out = refs[0], refs[-1]
    whole = pieces[0]
    if count > 1 or normed:
        whole = refs[1]

        def change(rows):
            return normalize(rows.astype(f32), gain).astype(bf16) if normed else rows

        put_rows(whole, pieces, change)
    columns = weight.shape[2]
    out[...] = dot(whole[...], weight[...].reshape(-1, columns)).astype(out.dtype)


def rows_product(pieces, gain, weight, block, place, step, dtype, name):
    rows = sum(piece.shape[0] for piece in pieces)
    parts, width = weight.shape[0], pieces[0].shape[1]
    joined = len(pieces) > 1 or gain is not None
    shapes = [jax.ShapeDtypeStruct((rows, width), bf16)] if joined else []
    shapes += [jax.ShapeDtypeStruct((rows, block), dtype)]
    gains = [] if gain is None else [gain.reshape(1, -1)]
    got = pl.pallas_call(
        functools.partial(rows_product_kernel, len(pieces), gain is not None),
        grid=(1,),
        in_specs=[resident(piece.shape) for piece in list(pieces) + gains]
        + [
            pl.BlockSpec(
                (parts, step, block), lambda i: (0, 0, place), pipeline_mode=pl.Buffered(1)
            )
        ],
        out_specs=[resident(shape.shape) for shape in shapes],
        out_shape=shapes,
        compiler_params=pltpu.CompilerParams(vmem_limit_bytes=56 << 20),
        cost_estimate=BESIDE,
        name=name,
    )(*pieces, *gains, weight)
    return (got[0], got[1]) if joined else (pieces[0], got[0])


def weight_grad_kernel(counts, number, *refs):
    count = sum(counts)
    lefts, rights, refs = refs[:count], refs[count : 2 * count], refs[2 * count :]
    received, below, out = refs[:number], refs[number:-1], refs[-1]
    rows = lefts[0].shape[1]
    first = pair = 0
    for size in counts:
        total = dot_left_t(lefts[pair][...], rights[pair][...])
        for i in range(pair + 1, pair + size):
            total = total + dot_left_t(lefts[i][...], rights[i][...])
        pair += size
        at = slice(first, first + total.shape[1])
        for block in received:
            total = total + block[0, :, at].astype(f32)
        out[0, :rows, at] = total.astype(bf16)
        first += total.shape[1]
    for block in below:
        out[0, rows:] = block[...]


def weight_grad(groups, received, below, step, name):
    pairs = [pair for group in groups for pair in group]
    rows, width = pairs[0][0].shape
    columns = sum(group[0][1].shape[1] for group in groups)
    deep = step + sum(block.shape[0] for block in below)
    return pl.pallas_call(
        functools.partial(
            weight_grad_kernel, [len(group) for group in groups], len(received)
        ),
        grid=(width // step,),
        in_specs=[pl.BlockSpec((rows, step), lambda i: (0, i))] * len(pairs)
        + [resident(right.shape) for _, right in pairs]
        + [pl.BlockSpec((1, step, columns), lambda i: (i, 0, 0))] * len(received)
        + [resident(block.shape) for block in below],
        out_specs=pl.BlockSpec((1, deep, columns), lambda i: (i, 0, 0)),
        out_shape=jax.ShapeDtypeStruct((width // step, deep, columns), bf16),
        compiler_params=pltpu.CompilerParams(vmem_limit_bytes=56 << 20),
        cost_estimate=BESIDE,
        name=name,
    )(*[left for left, _ in pairs], *[right for _, right in pairs], *received, *below)


def near_kernel(size, widths, me_ref, *refs):
    pieces, outs = refs[:size], refs[size:]
    rows = pieces[0].shape[0]
    for k, piece in enumerate(pieces):
        at = pl.ds(pl.multiple_of((me_ref[0] ^ k) * rows, rows), rows)
        first = 0
        for out, width in zip(outs, widths):
            out[at] = piece[:, first : first + width]
            first += width


def near_call(me, pieces, widths, name):
    rows = len(pieces) * pieces[0].shape[0]
    shapes = [jax.ShapeDtypeStruct((rows, width), bf16) for width in widths]
    return list(
        pl.pallas_call(
            functools.partial(near_kernel, len(pieces), widths),
            grid=(1,),
            in_specs=[pl.BlockSpec(memory_space=pltpu.SMEM)]
            + [resident(piece.shape) for piece in pieces],
            out_specs=[resident(shape.shape) for shape in shapes],
            out_shape=shapes,
            compiler_params=pltpu.CompilerParams(vmem_limit_bytes=32 << 20),
            cost_estimate=BESIDE,
            name=name,
        )(me.reshape(1), *pieces)
    )


def owned_kernel(size, layout, weighted, me_ref, *refs):
    count = size * len(layout)
    pieces, refs = refs[:count], refs[count:]
    weights, gain, refs = refs[:weighted], refs[weighted], refs[weighted + 1 :]
    outs, sums, below = refs[:-2], refs[-2], refs[-1]
    rows = gain.shape[0]
    total = jnp.zeros((rows, 1), f32)
    under = None
    for c, ranges in enumerate(layout):
        for k in range(size):
            piece = pieces[c * size + k]
            owner = me_ref[0] ^ k
            first = 0
            for number, place, wide, count, turned in ranges:
                block = piece[:rows, first : first + count].astype(f32)
                first += count
                at = pl.ds(pl.multiple_of(owner * wide + place, 128), count)
                if turned:
                    outs[number][at] = block.T
                    continue
                outs[number][:, at] = block
                if number < weighted:
                    product = weights[number][:, at].astype(f32) * block
                    total = total + jnp.sum(product, axis=1, keepdims=True)
            if piece.shape[0] > rows:
                more = piece[rows : rows + 8].astype(f32)
                under = more if under is None else under + more
    sums[...] = jnp.broadcast_to(total / gain[:, 0:1], sums.shape)
    below[...] = jnp.zeros_like(below) if under is None else under


def owned_call(me, chunks, layout, weights, gain, shapes, name):
    size = len(chunks[0])
    pieces = [piece for chunk in chunks for piece in chunk]
    rows = gain.shape[0]
    outs = [jax.ShapeDtypeStruct(shape, f32) for shape in shapes]
    outs += [jax.ShapeDtypeStruct((rows, 128), f32)]
    outs += [jax.ShapeDtypeStruct((8, pieces[0].shape[1]), f32)]
    column = jnp.broadcast_to(gain.astype(f32)[:, None], (rows, 128))
    operands = pieces + list(weights) + [column]
    return pl.pallas_call(
        functools.partial(owned_kernel, size, layout, len(weights)),
        grid=(1,),
        in_specs=[pl.BlockSpec(memory_space=pltpu.SMEM)]
        + [resident(array.shape) for array in operands],
        out_specs=[resident(shape.shape) for shape in outs],
        out_shape=outs,
        compiler_params=pltpu.CompilerParams(vmem_limit_bytes=48 << 20),
        cost_estimate=BESIDE,
        name=name,
    )(me.reshape(1), *operands)


def hidden_kernel(first, cores, x_count, g_count, tiles, *refs):
    refs = list(refs)

    def pop(number):
        taken, refs[:number] = refs[:number], []
        return taken

    x_pieces, g_pieces = (pop(x_count), pop(g_count)) if first else ([], [])
    x_all, g_all = (None, None) if first else pop(2)
    weights = [pop(3) for _ in range(cores)]
    if first:
        x_all, g_all = pop(2)
    grads_out, acts_out = pop(cores), pop(cores)
    step = pl.program_id(0)

    if first:

        @pl.when(step == 0)
        def _():
            put_rows(x_all, x_pieces, lambda rows: rows)
            put_rows(g_all, g_pieces, lambda rows: rows)

    def one_core(j):
        w_gate, w_up, w_down = (ref[...].reshape(-1, ref.shape[2]) for ref in weights[j])
        tile = w_gate.shape[1]
        place = step - j * tiles
        gate_place = pl.ds(pl.multiple_of(place * tile, tile), tile)
        up_place = pl.ds(pl.multiple_of((tiles + place) * tile, tile), tile)
        rows = x_all.shape[0] // 2
        for at in (slice(0, rows), slice(rows, None)):
            gate = dot(x_all[at], w_gate)
            up = dot(x_all[at], w_up)
            act_grad = dot(g_all[at], w_down)
            sigma = 1.0 / (1.0 + jnp.exp(-gate))
            silu = gate * sigma
            gate_grad = act_grad * up * sigma * (1.0 + gate * (1.0 - sigma))
            acts_out[j][at, gate_place] = (silu * up).astype(bf16)
            grads_out[j][at, gate_place] = gate_grad.astype(bf16)
            grads_out[j][at, up_place] = (act_grad * silu).astype(bf16)

    for j in range(cores):
        pl.when((step >= j * tiles) & (step < (j + 1) * tiles))(functools.partial(one_core, j))


def hidden_call(x_pieces, g_pieces, weights, name):
    cores, first = len(weights), len(x_pieces) > 1
    data, near, columns = weights[0].shape
    width = data * near
    units = columns // 3
    tile = min(256, units)
    tiles = units // tile
    rows = sum(piece.shape[0] for piece in x_pieces)

    def weight_specs(j):
        return [
            pl.BlockSpec(
                (data, near, tile),
                lambda i, k=k: (0, 0, k * tiles + jnp.clip(i - j * tiles, 0, tiles - 1)),
            )
            for k in range(3)
        ]

    operands = list(x_pieces) + list(g_pieces)
    in_specs = [resident(array.shape) for array in operands]
    for j, weight in enumerate(weights):
        in_specs += weight_specs(j)
        operands += [weight] * 3
    shapes = [jax.ShapeDtypeStruct((rows, width), bf16)] * 2 if first else []
    shapes += [jax.ShapeDtypeStruct((rows, 2 * units), bf16)] * cores
    shapes += [jax.ShapeDtypeStruct((rows, units), bf16)] * cores
    got = pl.pallas_call(
        functools.partial(
            hidden_kernel, first, cores, len(x_pieces), len(g_pieces), tiles
        ),
        grid=(cores * tiles,),
        in_specs=in_specs,
        out_specs=[resident(shape.shape) for shape in shapes],
        out_shape=shapes,
        compiler_params=pltpu.CompilerParams(vmem_limit_bytes=60 << 20),
        cost_estimate=BESIDE,
        name=name,
    )(*operands)
    got = list(got)
    kept, got = (got[:2], got[2:]) if first else ([x_pieces[0], g_pieces[0]], got)
    return kept, got[:cores], got[cores:]


def phase(always, body):
    def never():
        return jax.tree.map(lambda leaf: jnp.zeros(leaf.shape, leaf.dtype), jax.eval_shape(body))

    return lax.cond(always, body, never)


def trade(block, axis, step):
    return lax.ppermute(block, axis, [(i, i ^ step) for i in range(lax.axis_size(axis))])


def spread(block, *first):
    if lax.axis_size("model") == 1:
        return [block]
    near = [block, trade(block, "model", 1), trade(block, "model", 2)]
    return near + far_halves(near, *first)


def far_halves(near, *first):
    half = near[0].shape[0] // 2
    _, by_x, by_y = after(near, *first) if first else near
    return [trade(by_x[:half], "model", 2), trade(by_y[half:], "model", 1)]


def send_near(near, far):
    x_upper, x_lower, y_upper, y_lower = near
    x_upper, y_lower = after((x_upper, y_lower), *far)
    y_upper = (y_upper.astype(f32) + far[0].astype(f32)).astype(bf16)
    x_lower = (x_lower.astype(f32) + far[1].astype(f32)).astype(bf16)
    return [
        trade(x_upper, "model", 1),
        trade(y_upper, "model", 2),
        trade(x_lower, "model", 1),
        trade(y_lower, "model", 2),
    ]


def swap(piece_of):
    me = lax.axis_index("model")
    others = range(1, lax.axis_size("model"))
    return [piece_of(me)] + [trade(piece_of(me ^ k), "model", k) for k in others]


def take(array, index, count):
    size = array.shape[1] // count
    return lax.dynamic_slice_in_dim(array, index * size, size, 1)


def rows_at(array):
    return lambda i: lax.dynamic_index_in_dim(array, i, 0, keepdims=False)


def in_order(pieces):
    me = lax.axis_index("model")
    size = len(pieces)
    return jnp.stack(
        [lax.select_n(me, *[pieces[j ^ i] for j in range(size)]) for i in range(size)]
    )


def after(value, *first):
    return lax.optimization_barrier((value,) + first)[0]


def on_device(
    hidden_in,
    out_grad,
    segments,
    positions,
    w_query,
    key_weight,
    value_weight,
    w_output,
    w_gate,
    w_up,
    w_down,
    attn_gain,
    mlp_gain,
    query_gain,
    key_gain,
):
    data = lax.axis_size("data")
    model = lax.axis_size("model")
    cores = lax.axis_size("tp")
    core = lax.axis_index("tp")
    seq_len = positions.shape[0]
    half = seq_len // cores
    shard = w_query.shape[0]
    width = hidden_in.shape[1]
    head_size = query_gain.shape[0] * data * model
    q_heads = w_query.shape[1] // model // head_size
    kv_heads = key_weight.shape[1] // model // head_size
    repeat = q_heads // kv_heads
    q_cols = q_heads * head_size
    kv_cols = kv_heads * head_size
    cols = q_cols + 2 * kv_cols
    wide = cols + q_cols
    ff = w_gate.shape[1] // model
    always = (segments[0] * segments[0] + segments[0]) % 2 == 0

    small = jnp.concatenate([attn_gain, mlp_gain, query_gain, key_gain])
    small_rows = -(-small.shape[0] // wide)
    place_rows = -(-seq_len // wide)

    def as_rows(vector, rows):
        return jnp.pad(vector, (0, rows * wide - vector.shape[0])).reshape(rows, wide)

    extra = jnp.concatenate(
        [
            as_rows(small, small_rows),
            as_rows(segments.astype(bf16), place_rows),
            as_rows((positions // 8).astype(bf16), place_rows),
            as_rows((positions % 8).astype(bf16), place_rows),
        ]
    )
    extra = jnp.pad(extra, ((0, -extra.shape[0] % 16), (0, 0)))
    turned_output = w_output.T

    def attn_piece(i):
        parts = [
            take(w_query, i, model),
            take(key_weight, i, model),
            take(value_weight, i, model),
            take(turned_output, i, model),
        ]
        return jnp.concatenate([jnp.concatenate(parts, axis=1), extra])

    turned_down = w_down.T
    chunks = [ff - ff // 3, ff // 3] if ff % 768 == 0 else [ff]
    starts = [sum(chunks[:c]) for c in range(len(chunks))]

    def over_data(pieces):
        return lax.all_gather(pieces, "data", axis=0, tiled=False)

    attn_got = swap(attn_piece)
    x_sent, attn_got = lax.optimization_barrier((hidden_in, attn_got))
    x_near = [x_sent, trade(x_sent, "model", 1), trade(x_sent, "model", 2)]
    tied = lax.optimization_barrier((w_gate, w_up, turned_down, x_near))
    w_gate_sent, w_up_sent, turned_down, x_near = tied
    x_blocks = x_near + far_halves(x_near)
    mlp_got = swap(
        lambda i: jnp.concatenate(
            [
                take(weight, i, model)[:, first : first + count]
                for first, count in zip(starts, chunks)
                for weight in (w_gate_sent, w_up_sent, turned_down)
            ],
            axis=1,
        )
    )

    def places_of(first):
        rows = [
            got[shard + first : shard + first + place_rows].reshape(-1)[:seq_len]
            for got in attn_got
        ]
        return jnp.stack(rows).astype(f32)

    seg_all = places_of(small_rows)
    pos_all = 8.0 * places_of(small_rows + place_rows) + places_of(small_rows + 2 * place_rows)
    cosine, sine = tables(pos_all, head_size)

    attn_near = in_order(attn_got)
    gain_rows = attn_near[:, shard : shard + small_rows].reshape(-1, wide)
    gain_rows = jnp.pad(gain_rows, ((0, -gain_rows.shape[0] % 16), (0, 0)))
    near = jnp.concatenate([attn_near[:, :shard].reshape(-1, wide), gain_rows])
    me = lax.axis_index("model")
    mlp_near = near_call(me, mlp_got, [3 * count for count in chunks], "hidden_exchange")
    attn_full = over_data(near)
    tied = lax.optimization_barrier((attn_full, mlp_near, x_blocks, cosine, sine))
    attn_full, mlp_near, x_blocks, cosine, sine = tied
    mlp_full = [over_data(piece) for piece in mlp_near]

    gains = attn_full[:, model * shard : model * shard + model * small_rows]
    gains = gains.reshape(data * model, -1).astype(f32)
    part = query_gain.shape[0]
    gain_in = gains[:, :shard].reshape(-1)
    gain_mid = gains[:, shard : 2 * shard].reshape(-1)
    gain_query = gains[:, 2 * shard : 2 * shard + part].reshape(-1)
    gain_key = gains[:, 2 * shard + part : 2 * shard + 2 * part].reshape(-1)
    def with_cores(weight):
        return [weight] + [trade(weight, "tp", j) for j in range(1, cores)]

    near_rows = model * shard
    grad_sent, mlp_near = lax.optimization_barrier((out_grad, mlp_near))
    grad_blocks = [out_grad] + [trade(grad_sent, "model", k) for k in range(1, model)]

    seg_rows = jnp.pad(seg_all[:, None], ((0, 0), (0, 7), (0, 0)))
    seg_columns = seg_all[:, :, None]
    head_gains = jnp.pad(jnp.stack([gain_query, gain_key]), ((0, 6), (0, 0)))
    shared = [cosine, sine, seg_columns, seg_rows]
    o_place = [cols // q_cols] * cores

    def attention_phase():
        w_attn = with_cores(attn_full)
        normed_in, first_raw = rows_product(
            x_blocks, gain_in, w_attn[0], cols, 0, near_rows, f32, "query_key_value"
        )
        raw = [first_raw.reshape(model, half, cols)]
        for j in range(1, cores):
            mine = rows_product(
                [normed_in], None, w_attn[j], cols, 0, near_rows, f32, "query_key_value_other"
            )[1]
            raw.append(trade(mine, "tp", j).reshape(model, half, cols))
        attended = attention_call(
            functools.partial(attend_kernel, cores, kv_heads, repeat),
            "attend",
            core,
            raw,
            shared,
            head_gains,
            [jax.ShapeDtypeStruct((model, half, q_cols), bf16)] * cores,
            [],
            [((seq_len, cols), f32), ((seq_len, q_cols), bf16)],
        )
        att_pieces = [attended[0]] + [trade(attended[j], "tp", j) for j in range(1, cores)]
        att_flat = [piece.reshape(-1, q_cols) for piece in att_pieces]
        all_rows = with_cores(normed_in)
        return w_attn[1:], all_rows, raw, att_flat, list(attended)

    w_others, normed_in, raw, att_flat, attended = phase(always, attention_phase)
    w_attn = [attn_full] + w_others
    att_flat, grad_blocks = lax.optimization_barrier((att_flat, grad_blocks))

    def data_sum(total):
        return lax.psum_scatter(total, "data", scatter_dimension=0, tiled=False)

    def out_phase():
        own, _, got = project_and_send(
            att_flat, w_attn, o_place, half, near_rows, "attention_out"
        )
        middle, low = rows_call(
            "norm", own, hidden_in, got, gain_mid, None, [f32, bf16], "middle"
        )
        return middle, spread(low)

    middle, mid_blocks = phase(always, out_phase)

    def hidden_others(kept, rows, name):
        return [
            weight_grad([[(kept[k], rows[k][j])] for k in range(2)], [], (), near_rows, name)
            for j in range(1, cores)
        ]

    def hidden_own(kept, rows, received, name):
        pairs = [[(kept[k], rows[k][0])] for k in range(2)]
        return weight_grad(pairs, received, (), near_rows, name)

    def first_phase():
        weights = with_cores(mlp_full[0])
        rows, *by_core = hidden_call(mid_blocks, grad_blocks, weights[:1], "hidden_units_a")
        by_core = [by_core]
        for weight in weights[1:]:
            got = hidden_call(*[[whole] for whole in rows], [weight], "hidden_units_a_other")
            by_core.append(got[1:])
        first_rows = [[got[k][0] for got in by_core] for k in range(2)]
        others = hidden_others(rows, first_rows, "hidden_weights_a_other")
        received = [trade(other, "tp", j + 1) for j, other in enumerate(others)]
        return weights[1:], rows, first_rows, received

    other_weights, kept, first_rows, received = phase(always, first_phase)
    w_mlp = [[mlp_full[0]] + other_weights]
    mlp_sums = []
    if len(chunks) > 1:
        w_mlp.append(with_cores(after(mlp_full[1], *received)))
        mlp_sums.append(data_sum(hidden_own(kept, first_rows, received, "hidden_weights_a")))
    count = cores * len(chunks)
    both_cores = [w for pair in w_mlp for w in pair]

    def hidden_phase():
        rows = [first_rows]
        if len(chunks) > 1:
            wholes = [[whole] for whole in kept]
            rows.append(hidden_call(*wholes, w_mlp[1], "hidden_units_b")[1:])
        own, _, got = project_and_send(
            [grads for pair in rows for grads in pair[0]],
            both_cores,
            [0] * count,
            half,
            near_rows,
            "normed_mid_grad",
        )
        others = hidden_others(kept, after(rows[-1], own), "hidden_weights_b_other")
        return own, got, rows[-1], others, [acts for pair in rows for acts in pair[1]]

    mid_part, mid_got, last_rows, others, act_rows = phase(always, hidden_phase)

    def branch_phase():
        middle_grad, branch_own = rows_call(
            "back", mid_part, middle, mid_got, gain_mid, out_grad, [f32, bf16], "middle_grad"
        )
        down_parts = project(
            act_rows, both_cores, [2] * count, 0, [half] * model, near_rows, "hidden_out"
        )
        branch_blocks = spread(branch_own, *down_parts)
        received = [trade(other, "tp", j + 1) for j, other in enumerate(others)]
        last = after(last_rows, branch_own, *down_parts)
        total = hidden_own(kept, last, received, "hidden_weights_b")
        return middle_grad, branch_blocks, total, down_parts

    middle_grad, branch_blocks, total, down_parts = phase(always, branch_phase)
    mlp_sums.append(data_sum(total))
    down_got = [trade(down_parts[k], "model", k) for k in range(1, model)]

    def attend_back_phase():
        att_grads, rows = [], branch_blocks
        for j in reversed(range(cores)):
            branch, piece = rows_product(
                rows, None, w_attn[j], q_cols, o_place[j], near_rows, bf16, "attended_grad"
            )
            rows = [branch]
            piece = piece.reshape(model, half, q_cols)
            att_grads.insert(0, trade(piece, "tp", j) if j else piece)
        *qkv_back, head_grads = attention_call(
            functools.partial(attend_back_kernel, cores, kv_heads, repeat),
            "attend_back",
            core,
            raw + att_grads,
            shared,
            head_gains,
            [jax.ShapeDtypeStruct((model, half, cols), bf16)] * cores,
            [jax.ShapeDtypeStruct(head_gains.shape, f32)],
            [
                ((seq_len, cols), f32),
                ((seq_len, q_cols), bf16),
                ((seq_len, cols), f32),
                ((seq_len, cols), bf16),
            ],
        )
        return with_cores(branch), list(qkv_back), head_grads

    branch, qkv_back, head_grads = phase(always, attend_back_phase)
    tied = lax.optimization_barrier((qkv_back, mlp_sums[:-1], down_got))
    qkv_back, first_sums, down_got = tied
    first_got = [swap(rows_at(total.reshape(model, shard, -1))) for total in first_sums]

    def attention_weights_phase():
        back_pieces = [qkv_back[0]] + [trade(qkv_back[j], "tp", j) for j in range(1, cores)]
        ride = head_grads[:2].reshape(-1)
        ride = jnp.pad(ride, (0, ride_rows * wide - ride.shape[0])).astype(bf16)
        ride = jnp.pad(ride.reshape(ride_rows, wide), ((0, -ride_rows % 16), (0, 0)))
        groups = [
            [(normed_in[j], qkv_back[j].reshape(-1, cols)) for j in range(cores)],
            [(branch[j], attended[j].reshape(-1, q_cols)) for j in range(cores)],
        ]
        attn_total = weight_grad(groups, [], [ride], near_rows, "attention_weights")
        return attn_total, [piece.reshape(-1, cols) for piece in back_pieces]

    ride_rows = -(-2 * head_size // wide)
    attn_total, back_flat = phase(always, attention_weights_phase)
    attn_total, first_got = lax.optimization_barrier((attn_total, first_got))
    attn_sum = data_sum(attn_total)
    back_flat, last_sum = lax.optimization_barrier((back_flat, mlp_sums[-1]))

    def last_phase():
        own, in_far, in_got = project_and_send(
            back_flat, w_attn, [0] * cores, half, near_rows, "normed_in_grad"
        )
        hidden_out = rows_call(
            "sum", down_parts[0], middle, down_got, None, None, [bf16], "hidden_out_sum"
        )[0]
        last_got = swap(rows_at(after(last_sum.reshape(model, shard, -1), *in_far)))
        grad_in = rows_call(
            "back", own, hidden_in, in_got, gain_in, middle_grad, [f32], "grad_in"
        )[0]

        layout = [
            [(0, first, ff, size, False), (1, first, ff, size, False), (2, first, ff, size, True)]
            for first, size in zip(starts, chunks)
        ]
        shapes = [w_gate.shape, w_up.shape, w_down.shape]
        owned = owned_call(
            me, first_got + [last_got], layout, [w_gate, w_up], mlp_gain, shapes, "hidden_owned"
        )
        return hidden_out, grad_in, owned[:3], owned[3][:, 0]

    got = phase(always, last_phase)
    hidden_out, grad_in, (grad_gate, grad_up, grad_down), mlp_part = got
    attn_sum = after(attn_sum, grad_in)
    weight_rows = attn_sum[:near_rows].reshape(model, shard, wide)
    gain_row = attn_sum[near_rows:]
    gain_row = jnp.broadcast_to(gain_row, (model,) + gain_row.shape)
    attn_rows = jnp.concatenate([weight_rows, gain_row], axis=1)
    attn_got = swap(rows_at(attn_rows))
    layout = [
        [
            (0, 0, q_cols, q_cols, False),
            (1, 0, kv_cols, kv_cols, False),
            (2, 0, kv_cols, kv_cols, False),
            (3, 0, q_cols, q_cols, True),
        ]
    ]
    weights = [w_query, key_weight, value_weight]
    shapes = [weight.shape for weight in weights] + [w_output.shape]
    owned = owned_call(me, [attn_got], layout, weights, attn_gain, shapes, "attention_owned")
    grad_query, grad_key, grad_value, grad_output, attn_part, gain_sums = owned
    gain_sums = gain_sums[:ride_rows].reshape(-1)[: 2 * head_size]
    sums = lax.psum(jnp.concatenate([attn_part[:, 0], mlp_part, gain_sums]), "tp")
    where = lax.axis_index("data") * model + lax.axis_index("model")
    first = 2 * shard + where * part
    return (
        hidden_out,
        grad_in,
        grad_query,
        grad_key,
        grad_value,
        grad_output,
        grad_gate,
        grad_up,
        grad_down,
        sums[:shard],
        sums[shard : 2 * shard],
        lax.dynamic_slice_in_dim(sums, first, part),
        lax.dynamic_slice_in_dim(sums, first + head_size, part),
    )


def solution(mesh):
    fsdp, tp = mesh.shape["fsdp"], mesh.shape["tp"]
    model = 4 if fsdp % 4 == 0 else 1
    split = Mesh(mesh.devices.reshape(fsdp // model, model, tp), ("data", "model", "tp"))
    batch = ("data", "model")
    rows = P(("data", "model", "tp"), None)
    into = P(batch, "tp")
    back = P("tp", batch)
    in_specs = (rows, rows, P(batch), P(batch), into, into, into, back, into, into, back)
    in_specs = in_specs + (P(batch),) * 4
    out_specs = (rows, rows, into, into, into, back, into, into, back) + (P(batch),) * 4
    return jax.shard_map(
        on_device, mesh=split, in_specs=in_specs, out_specs=out_specs, check_vma=False
    )
```

time: 2760 us -> 584 us (0.21)
  waiting for transfers between devices: 2270 us -> 212 us
  Pallas kernels: 0 us -> 234 us
  blocking collectives: 197 us -> 2.47 us
  matrix products: 190 us -> 0 us
  starting transfers between devices: 1.35 us -> 57.7 us
  other arithmetic: 44.4 us -> 16.1 us
    reduce_scatter x11 -> x3, waiting for transfers between devices: 1520 us -> 0.04 us  [data_sum(): return lax.psum_scatter(total, 'data', scatter_dimension=0, tiled=False)]
    all_gather x11 -> x3, waiting for transfers between devices: 741 us -> 2.49 us  [over_data(): return lax.all_gather(pieces, 'data', axis=0, tiled=False)]
    pallas_call x0 -> x28, Pallas kernels: none -> 234 us  [the longest x7 55 us: project(): pl.pallas_call(functools.partial(project_kernel, len(lefts)), grid=(parts...]
    ppermute x0 -> x62, waiting for transfers between devices: none -> 209 us  [trade(): lax.ppermute(block, axis, [(i, i ^ step) for i in range(lax.axis_size(axi...]
    dot_general x27 -> x0, matrix products: 190 us -> none  [the longest x1 17.5 us: on_device(): jnp.dot(gathered_grad, back_down.T, preferred_element_type=jnp.float32)]
    unnamed x2 -> x0, blocking collectives: 114 us -> none
    all_gather x2 -> x0, blocking collectives: 79.9 us -> none  [the longest x1 42.4 us: fetch_attention(): lax.all_gather(attn_gain, 'fsdp', axis=0, tiled=True)]
    ppermute x0 -> x62, starting transfers between devices: none -> 57.5 us  [trade(): lax.ppermute(block, axis, [(i, i ^ step) for i in range(lax.axis_size(axi...]
  transfers between devices with their start and end apart: 22 -> 68, of which waited for: 16 -> 39; matrix products, arithmetic and copies ran while one was open for 5% -> 6% of each run, Pallas kernels for 0% -> 41%
where the time goes in v1:
time: 584 us; the launch traced here: 575 us
  Pallas kernels  234 us (40%)
  waiting for transfers between devices  212 us (36%)
  starting transfers between devices  57.7 us (10%)
  local copies, waits for them, and re-layouts  33.7 us (6%)
  between operations  17.1 us (3%)
  other arithmetic  16.1 us (3%)
    ppermute x62, waiting for transfers between devices, trade(): lax.ppermute(block, axis, [(i, i ^ step) for i in range(lax.axis_size(axi...  209 us
    ppermute x62, starting transfers between devices, trade(): lax.ppermute(block, axis, [(i, i ^ step) for i in range(lax.axis_size(axi...  57.5 us
    pallas_call x7, Pallas kernels, project(): pl.pallas_call(functools.partial(project_kernel, len(lefts)), grid=(parts...  55 us
    pallas_call x5, Pallas kernels, weight_grad(): pl.pallas_call(functools.partial(weight_grad_kernel, [len(group) for grou...  54 us
    pallas_call x3, Pallas kernels, hidden_call(): pl.pallas_call(functools.partial(hidden_kernel, first, cores, len(x_piece...  43.9 us
    pallas_call x2, Pallas kernels, attention_call(): pl.pallas_call(kernel, grid=(halves[0].shape[0],), in_specs=[pl.BlockSpec...  29.8 us
    pallas_call x4, Pallas kernels, rows_product(): pl.pallas_call(functools.partial(rows_product_kernel, len(pieces), gain i...  25.7 us
    pallas_call x4, Pallas kernels, rows_call(): pl.pallas_call(functools.partial(rows_kernel, kind, len(got)), grid=(4,),...  18.9 us
  transfers between devices with their start and end apart: 68, of which 39 were waited for; matrix products, arithmetic and copies ran while one was open for 6% of the time, Pallas kernels for 41%

profile of v1, /device:TPU:0, one launch (start us, length us, event | category | flops | bytes accessed | tf_op | source)
XLA Modules:
  0.0 575.0 jit_solution(6848105967302158669)
XLA Ops:
  12.8 3.0 collective-permute-start.39
  17.5 4.6 collective-permute-done.39
  22.0 5.4 collective-permute-done.40
  36.5 17.0 %collective-permute-done.42 = bf16[256,2048]{1,0:T(8,128)(2,1)} collective-permute-done((bf16[256,2048]{1,0:T(8,128)(2,1)S(1)}, bf16[256,2048]{1,0:T(8,128)(2,1)}, u32[]{:S(2)}, u32[]{:S(2)}) %collective-permute-start.42) | collective-permute-done | bytes 1048608 | tf_op jit(solution)/shard_map/ppermute | solution.py:571
  56.3 2.3 collective-permute-start.46
  62.1 3.7 fusion.2
  66.5 4.8 collective-permute-done.44.refs_1_
  71.4 13.2 %collective-permute-done.45.refs_2_ = bf16[128,2304]{1,0:T(8,128)(2,1)S(1)} collective-permute-done((bf16[128,2304]{1,0:T(8,128)(2,1)S(1)}, bf16[128,2304]{1,0:T(8,128)(2,1)S(1)}, u32[]{:S(2)}, u32[]{:S(2)}) %collective-permute-start.45) | collective-permute-done | bytes 589856 | tf_op jit(solution)/shard_map/ppermute | solution.py:571
  86.2 6.2 %collective-permute-done.47 = bf16[128,2048]{1,0:T(8,128)(2,1)} collective-permute-done((bf16[128,2048]{1,0:T(8,128)(2,1)S(1)}, bf16[128,2048]{1,0:T(8,128)(2,1)}, u32[]{:S(2)}, u32[]{:S(2)}) %collective-permute-start.47) | collective-permute-done | bytes 524320 | tf_op jit(solution)/shard_map/ppermute | solution.py:571
  92.4 2.5 all-gather.7.cloned.1.call-done
  103.6 33.8 %conditional.8 = (bf16[4,528,768]{2,1,0:T(8,128)(2,1)S(1)}, bf16[1024,2048]{1,0:T(8,128)(2,1)}, bf16[1024,2048]{1,0:T(8,128)(2,1)}, f32[4,256,512]{2,1,0:T(8,128...) conditional(s32[]{:T(128)} %convert_element_type.141, () %tuple.98, ...), branch_computations={%region_0.1_spmd, %region_1.2_spmd} | conditional | flops 3145728 | bytes 67453216 | solution.py:567
  103.9 7.6 %query_key_value.1 = (bf16[1024,2048]{1,0:T(8,128)(2,1)}, f32[1024,512]{1,0:T(8,128)}) custom-call(bf16[256,2048]{1,0:T(8,128)(2,1)S(1)} %get-tuple-element.188.refs_0_, bf16[256,2048]{1,0:T(8,128)(2,1)} %get-tuple-element.214.refs_1_, bf16[256,2048]{1,0:T(8,128)(2,1)} %get-tuple-element.215.refs_2_, bf16[128,2048]{1,0:T(8,128)(2,1)} %get-tuple-element.216.refs_3_, ...), custom_call_target="tpu_custom_call" | custom-call | flops 1048576 | bytes 65536 | tf_op jit(solution)/shard_map/cond/branch_1_fun/query_key_value/pallas_call | solution.py:334
  112.0 7.0 %query_key_value_other.1 = f32[1024,512]{1,0:T(8,128)} custom-call(bf16[1024,2048]{1,0:T(8,128)(2,1)} %get-tuple-element.749.refs_0_, bf16[4,528,768]{2,1,0:T(8,128)(2,1)S(1)} %collective-permute-done.refs_1_), custom_call_target="tpu_custom_call" | custom-call | flops 1048576 | bytes 65536 | tf_op jit(solution)/shard_map/cond/branch_1_fun/query_key_value_other/pallas_call | solution.py:334
  119.4 4.1 collective-permute-done.2
  123.5 11.6 %attend.1 = (bf16[4,256,256]{2,1,0:T(8,128)(2,1)}, bf16[4,256,256]{2,1,0:T(8,128)(2,1)}) custom-call(s32[1]{0:T(128)} %bitcast.3.core_ref, f32[4,256,512]{2,1,0:T(8,128)} %bitcast.1.refs_0_, f32[4,256,512]{2,1,0:T(8,128)} %bitcast.2.refs_1_, f32[4,512,128]{2,1,0:T(8,128)S(1)} %get-tuple-element.222.refs_2_, f32[4,512,128]{2,1,0:T(8,128)S(1)} %get-tuple-element.223.refs_3_, ...), custom_call_target="tpu_custom_call" | custom-call | flops 1048576 | bytes 65536 | tf_op jit(solution)/shard_map/cond/branch_1_fun/attend/pallas_call | solution.py:179
  137.4 7.2 %collective-permute-done.50 = bf16[256,2048]{1,0:T(8,128)(2,1)} collective-permute-done((bf16[256,2048]{1,0:T(8,128)(2,1)}, bf16[256,2048]{1,0:T(8,128)(2,1)}, u32[]{:S(2)}, u32[]{:S(2)}) %collective-permute-start.50) | collective-permute-done | bytes 1048608 | tf_op jit(solution)/shard_map/ppermute | solution.py:571
  144.6 79.3 %conditional.9 = (f32[256,2048]{1,0:T(8,128)}, bf16[256,2048]{1,0:T(8,128)(2,1)}, bf16[256,2048]{1,0:T(8,128)(2,1)}, bf16[256,2048]{1,0:T(8,128)(2,1)}, bf16[128...) conditional(s32[]{:T(128)} %convert_element_type.141, () %tuple.97, (bf16[1024,256]{1,0:T(8,128)(2,1)}, ...), branch_computations={%region_2.3_spmd, %region_3.4_spmd} | conditional | flops 5242880 | bytes 56164884 | solution.py:567
  144.6 4.3 attention_out_far.1
  150.9 4.8 attention_out.1
  155.7 5.9 %collective-permute-done.13 = bf16[128,2048]{1,0:T(8,128)(2,1)S(1)} collective-permute-done((bf16[128,2048]{1,0:T(8,128)(2,1)}, bf16[128,2048]{1,0:T(8,128)(2,1)S(1)}, u32[]{:S(2)}, u32[]{:S(2)}) %collective-permute-start.13) | collective-permute-done | bytes 524320 | tf_op jit(solution)/shard_map/cond/branch_1_fun/ppermute | solution.py:571
  169.2 8.5 %collective-permute-done.15.refs_2_ = bf16[128,2048]{1,0:T(8,128)(2,1)S(1)} collective-permute-done((bf16[128,2048]{1,0:T(8,128)(2,1)}, bf16[128,2048]{1,0:T(8,128)(2,1)S(1)}, u32[]{:S(2)}, u32[]{:S(2)}) %collective-permute-start.15) | collective-permute-done | bytes 524320 | tf_op jit(solution)/shard_map/cond/branch_1_fun/ppermute | solution.py:571
  178.4 7.7 %collective-permute-done.16.refs_3_ = bf16[128,2048]{1,0:T(8,128)(2,1)S(1)} collective-permute-done((bf16[128,2048]{1,0:T(8,128)(2,1)S(1)}, bf16[128,2048]{1,0:T(8,128)(2,1)S(1)}, u32[]{:S(2)}, u32[]{:S(2)}) %collective-permute-start.16) | collective-permute-done | bytes 524320 | tf_op jit(solution)/shard_map/cond/branch_1_fun/ppermute | solution.py:571
  186.1 2.6 middle.1
  190.4 20.3 %collective-permute-done.19 = bf16[256,2048]{1,0:T(8,128)(2,1)} collective-permute-done((bf16[256,2048]{1,0:T(8,128)(2,1)}, bf16[256,2048]{1,0:T(8,128)(2,1)}, u32[]{:S(2)}, u32[]{:S(2)}) %collective-permute-start.19) | collective-permute-done | bytes 1048608 | tf_op jit(solution)/shard_map/cond/branch_1_fun/ppermute | solution.py:571
  214.6 8.6 %collective-permute-done.21 = bf16[128,2048]{1,0:T(8,128)(2,1)} collective-permute-done((bf16[128,2048]{1,0:T(8,128)(2,1)S(1)}, bf16[128,2048]{1,0:T(8,128)(2,1)}, u32[]{:S(2)}, u32[]{:S(2)}) %collective-permute-start.21) | collective-permute-done | bytes 524320 | tf_op jit(solution)/shard_map/cond/branch_1_fun/ppermute | solution.py:571
  223.9 52.2 %conditional.10 = (bf16[4,512,1536]{2,1,0:T(8,128)(2,1)}, bf16[1024,2048]{1,0:T(8,128)(2,1)}, bf16[1024,2048]{1,0:T(8,128)(2,1)}, bf16[1024,1024]{1,0:T(8,128)(2...) conditional(s32[]{:T(128)} %convert_element_type.141, () %tuple.96, ...), branch_computations={%region_4.5_spmd, %region_5.6_spmd} | conditional | flops 3145728 | bytes 50528400 | solution.py:567
  224.3 16.0 %hidden_units_a.1 = (bf16[1024,2048]{1,0:T(8,128)(2,1)}, bf16[1024,2048]{1,0:T(8,128)(2,1)}, bf16[1024,1024]{1,0:T(8,128)(2,1)S(1)}, bf16[1024,512]{1,0:T(8,128)(2,1)S(1)}) custom-call(bf16[256,2048]{1,0:T(8,128)(2,1)} %get-tuple-element.247.refs_0_, bf16[256,2048]{1,0:T(8,128)(2,1)} %get-tuple-element.248.refs_1_, ...), custom_call_target="tpu_custom_call" | custom-call | flops 1048576 | bytes 65536 | tf_op jit(solution)/shard_map/cond/branch_1_fun/hidden_units_a/pallas_call | solution.py:546
  240.3 13.8 %hidden_units_a_other.1 = (bf16[1024,1024]{1,0:T(8,128)(2,1)}, bf16[1024,512]{1,0:T(8,128)(2,1)}) custom-call(bf16[1024,2048]{1,0:T(8,128)(2,1)} %get-tuple-element.778.refs_0_, bf16[1024,2048]{1,0:T(8,128)(2,1)} %get-tuple-element.779.refs_1_, bf16[4,512,1536]{2,1,0:T(8,128)(2,1)} %collective-permute-done.4.refs_2_.refs_3_.refs_4_, ...), custom_call_target="tpu_custom_call" | custom-call | flops 1048576 | bytes 65536 | tf_op jit(solution)/shard_map/cond/branch_1_fun/hidden_units_a_other/pallas_call | solution.py:546
  254.1 11.4 %hidden_weights_a_other.1 = bf16[4,512,1536]{2,1,0:T(8,128)(2,1)} custom-call(bf16[1024,2048]{1,0:T(8,128)(2,1)} %get-tuple-element.778.refs_0_, bf16[1024,2048]{1,0:T(8,128)(2,1)} %get-tuple-element.779.refs_1_, bf16[1024,1024]{1,0:T(8,128)(2,1)} %get-tuple-element.781.refs_2_, bf16[1024,512]{1,0:T(8,128)(2,1)} %get-tuple-element.783.refs_3_), custom_call_target="tpu_custom_call" | custom-call | flops 1048576 | bytes 65536 | tf_op jit(solution)/shard_map/cond/branch_1_fun/hidden_weights_a_other/pallas_call | solution.py:377
  265.9 10.1 %collective-permute-done.5 = bf16[4,512,1536]{2,1,0:T(8,128)(2,1)} collective-permute-done((bf16[4,512,1536]{2,1,0:T(8,128)(2,1)}, bf16[4,512,1536]{2,1,0:T(8,128)(2,1)}, u32[]{:S(2)}, u32[]{:S(2)}) %collective-permute-start.5) | collective-permute-done | bytes 6291488 | tf_op jit(solution)/shard_map/cond/branch_1_fun/ppermute | solution.py:571
  276.0 12.7 %hidden_weights_a.1 = bf16[4,512,1536]{2,1,0:T(8,128)(2,1)} custom-call(bf16[1024,2048]{1,0:T(8,128)(2,1)} %get-tuple-element.545.refs_0_, bf16[1024,2048]{1,0:T(8,128)(2,1)} %get-tuple-element.546.refs_1_, bf16[1024,1024]{1,0:T(8,128)(2,1)S(1)} %get-tuple-element.549.refs_2_, bf16[1024,512]{1,0:T(8,128)(2,1)S(1)} %get-tuple-element.552.refs_3_, ...), custom_call_target="tpu_custom_call" | custom-call | flops 1048576 | bytes 65536 | tf_op jit(solution)/shard_map/hidden_weights_a/pallas_call | solution.py:377
  289.2 5.5 collective-permute-done.52
  296.4 68.6 %conditional.11 = (f32[256,2048]{1,0:T(8,128)}, bf16[128,2048]{1,0:T(8,128)(2,1)}, bf16[128,2048]{1,0:T(8,128)(2,1)}, bf16[128,2048]{1,0:T(8,128)(2,1)}, bf16[12...) conditional(s32[]{:T(128)} %convert_element_type.141, () %tuple.95, ...), branch_computations={%region_6.7_spmd, %region_7.8_spmd} | conditional | flops 6291456 | bytes 57934364 | solution.py:567
  296.5 14.2 %hidden_units_b.1 = (bf16[1024,512]{1,0:T(8,128)(2,1)}, bf16[1024,512]{1,0:T(8,128)(2,1)}, bf16[1024,256]{1,0:T(8,128)(2,1)S(1)}, bf16[1024,256]{1,0:T(8,128)(2,1)}) custom-call(bf16[1024,2048]{1,0:T(8,128)(2,1)} %get-tuple-element.264.refs_0_, bf16[1024,2048]{1,0:T(8,128)(2,1)} %get-tuple-element.265.refs_1_, ...), custom_call_target="tpu_custom_call" | custom-call | flops 1048576 | bytes 65536 | tf_op jit(solution)/shard_map/cond/branch_1_fun/hidden_units_b/pallas_call | solution.py:546
  310.8 9.3 %normed_mid_grad_far.1 = (bf16[128,2048]{1,0:T(8,128)(2,1)}, bf16[128,2048]{1,0:T(8,128)(2,1)}) custom-call(bf16[1024,1024]{1,0:T(8,128)(2,1)} %get-tuple-element.262.refs_0_, bf16[1024,1024]{1,0:T(8,128)(2,1)} %get-tuple-element.263.refs_1_, bf16[1024,512]{1,0:T(8,128)(2,1)} %get-tuple-element.804.refs_2_, ...), custom_call_target="tpu_custom_call" | custom-call | flops 1048576 | bytes 65536 | tf_op jit(solution)/shard_map/cond/branch_1_fun/normed_mid_grad_far/pallas_call | solution.py:223
  322.4 14.8 %normed_mid_grad.1 = (f32[256,2048]{1,0:T(8,128)}, bf16[128,2048]{1,0:T(8,128)(2,1)}, bf16[128,2048]{1,0:T(8,128)(2,1)}, bf16[128,2048]{1,0:T(8,128)(2,1)}, bf16[128,2048]{1,0:T(8,128)(2,1)}) custom-call(bf16[1024,1024]{1,0:T(8,128)(2,1)} %get-tuple-element.262.refs_0_, bf16[1024,1024]{1,0:T(8,128)(2,1)} %get-tuple-element.263.refs_1_, ...), custom_call_target="tpu_custom_call" | custom-call | flops 1048576 | bytes 65536 | tf_op jit(solution)/shard_map/cond/branch_1_fun/normed_mid_grad/pallas_call | solution.py:223
  344.7 1.9 copy.154
  346.6 8.1 %hidden_weights_b_other.1 = bf16[4,512,768]{2,1,0:T(8,128)(2,1)} custom-call(bf16[1024,2048]{1,0:T(8,128)(2,1)} %get-tuple-element.264.refs_0_, bf16[1024,2048]{1,0:T(8,128)(2,1)} %get-tuple-element.265.refs_1_, bf16[1024,512]{1,0:T(8,128)(2,1)} %get-tuple-element.283.refs_3_.refs_2_, bf16[1024,256]{1,0:T(8,128)(2,1)} %get-tuple-element.284.refs_3_), custom_call_target="tpu_custom_call" | custom-call | flops 1048576 | bytes 65536 | tf_op jit(solution)/shard_map/cond/branch_1_fun/hidden_weights_b_other/pallas_call | solution.py:377
  355.4 8.1 %collective-permute-done.25 = bf16[128,2048]{1,0:T(8,128)(2,1)} collective-permute-done((bf16[128,2048]{1,0:T(8,128)(2,1)S(1)}, bf16[128,2048]{1,0:T(8,128)(2,1)}, u32[]{:S(2)}, u32[]{:S(2)}) %collective-permute-start.25) | collective-permute-done | bytes 524320 | tf_op jit(solution)/shard_map/cond/branch_1_fun/ppermute | solution.py:571
  365.0 49.9 %conditional.12 = (f32[256,2048]{1,0:T(8,128)}, bf16[256,2048]{1,0:T(8,128)(2,1)}, bf16[256,2048]{1,0:T(8,128)(2,1)}, bf16[256,2048]{1,0:T(8,128)(2,1)}, bf16[12...) conditional(s32[]{:T(128)} %convert_element_type.141, () %tuple.91, ...), branch_computations={%region_8.9_spmd, %region_9.10_spmd} | conditional | flops 3145728 | bytes 56820056 | solution.py:567
  365.3 6.8 %middle_grad.1 = (f32[256,2048]{1,0:T(8,128)}, bf16[256,2048]{1,0:T(8,128)(2,1)}) custom-call(f32[256,2048]{1,0:T(8,128)} %get-tuple-element.287.refs_0_, f32[256,2048]{1,0:T(8,128)} %get-tuple-element.288.refs_1_, bf16[128,2048]{1,0:T(8,128)(2,1)} %get-tuple-element.289.refs_2_, bf16[128,2048]{1,0:T(8,128)(2,1)} %get-tuple-element.290.refs_3_, ...), custom_call_target="tpu_custom_call" | custom-call | flops 1048576 | bytes 65536 | tf_op jit(solution)/shard_map/cond/branch_1_fun/middle_grad/pallas_call | solution.py:298
  374.1 10.4 %hidden_out.1 = (f32[256,2048]{1,0:T(8,128)}, bf16[256,2048]{1,0:T(8,128)(2,1)}, bf16[256,2048]{1,0:T(8,128)(2,1)}, bf16[256,2048]{1,0:T(8,128)(2,1)}) custom-call(bf16[1024,512]{1,0:T(8,128)(2,1)S(1)} %copy-done.23, bf16[1024,512]{1,0:T(8,128)(2,1)} %get-tuple-element.298.refs_1_, bf16[1024,256]{1,0:T(8,128)(2,1)} %get-tuple-element.299.refs_2_, ...), custom_call_target="tpu_custom_call" | custom-call | flops 1048576 | bytes 65536 | tf_op jit(solution)/shard_map/cond/branch_1_fun/hidden_out/pallas_call | solution.py:223
  384.4 13.6 %collective-permute-done.6 = bf16[256,2048]{1,0:T(8,128)(2,1)} collective-permute-done((bf16[256,2048]{1,0:T(8,128)(2,1)}, bf16[256,2048]{1,0:T(8,128)(2,1)}, u32[]{:S(2)}, u32[]{:S(2)}) %collective-permute-start.6) | collective-permute-done | bytes 1048608 | tf_op jit(solution)/shard_map/cond/branch_1_fun/ppermute | solution.py:571
  403.3 9.2 %hidden_weights_b.1 = bf16[4,512,768]{2,1,0:T(8,128)(2,1)} custom-call(bf16[1024,2048]{1,0:T(8,128)(2,1)} %get-tuple-element.311.refs_0_, bf16[1024,2048]{1,0:T(8,128)(2,1)} %get-tuple-element.312.refs_1_, bf16[1024,512]{1,0:T(8,128)(2,1)} %get-tuple-element.315.refs_2_, bf16[1024,256]{1,0:T(8,128)(2,1)S(1)} %get-tuple-element.316.refs_3_, ...), custom_call_target="tpu_custom_call" | custom-call | flops 1048576 | bytes 65536 | tf_op jit(solution)/shard_map/cond/branch_1_fun/hidden_weights_b/pallas_call | solution.py:377
  418.6 33.1 %conditional.13 = (bf16[1024,2048]{1,0:T(8,128)(2,1)}, bf16[1024,2048]{1,0:T(8,128)(2,1)}, bf16[4,256,512]{2,1,0:T(8,128)(2,1)}, bf16[4,256,512]{2,1,0:T(8,128)(2,1)}, f32[8,128]{1,0:T(8,128)S(1)}) conditional(s32[]{:T(128)} %convert_element_type.141, () %tuple.107, (bf16[256,2048]{1,0:T(8,128)(2,1)}, bf16[256,2048]{1,0:T(8,128)(2,1)}, ...), branch_computations={%region_10.11_spmd, %region_11.12_spmd} | conditional | flops 3145728 | bytes 25378992 | solution.py:567
  418.6 6.4 %attended_grad.2 = (bf16[1024,2048]{1,0:T(8,128)(2,1)}, bf16[1024,256]{1,0:T(8,128)(2,1)}) custom-call(bf16[256,2048]{1,0:T(8,128)(2,1)} %get-tuple-element.318.refs_0_, bf16[256,2048]{1,0:T(8,128)(2,1)} %get-tuple-element.319.refs_1_, bf16[256,2048]{1,0:T(8,128)(2,1)} %get-tuple-element.320.refs_2_, bf16[128,2048]{1,0:T(8,128)(2,1)} %get-tuple-element.321.refs_3_, ...), custom_call_target="tpu_custom_call" | custom-call | flops 1048576 | bytes 65536 | tf_op jit(solution)/shard_map/cond/branch_1_fun/attended_grad/pallas_call | solution.py:334
  425.8 4.7 attended_grad.3
  430.5 2.0 collective-permute-done.12.refs_3_
  433.6 18.1 %attend_back.1 = (bf16[4,256,512]{2,1,0:T(8,128)(2,1)}, bf16[4,256,512]{2,1,0:T(8,128)(2,1)}, f32[8,128]{1,0:T(8,128)S(1)}) custom-call(s32[1]{0:T(128)} %bitcast.8.core_ref, f32[4,256,512]{2,1,0:T(8,128)} %get-tuple-element.326.refs_0_, f32[4,256,512]{2,1,0:T(8,128)} %get-tuple-element.327.refs_1_, bf16[4,256,256]{2,1,0:T(8,128)(2,1)S(1)} %bitcast.89, ...), custom_call_target="tpu_custom_call" | custom-call | flops 1048576 | bytes 65536 | tf_op jit(solution)/shard_map/cond/branch_1_fun/attend_back/pallas_call | solution.py:179
  451.7 8.9 %collective-permute-done.54 = bf16[256,2048]{1,0:T(8,128)(2,1)} collective-permute-done((bf16[256,2048]{1,0:T(8,128)(2,1)}, bf16[256,2048]{1,0:T(8,128)(2,1)}, u32[]{:S(2)}, u32[]{:S(2)}) %collective-permute-start.54) | collective-permute-done | bytes 1048608 | tf_op jit(solution)/shard_map/ppermute | solution.py:571
  462.1 2.6 dynamic-slice_bitcast_fusion.4
  468.2 13.6 %conditional.14 = (bf16[4,528,768]{2,1,0:T(8,128)(2,1)}, bf16[1024,512]{1,0:T(8,128)(2,1)}, bf16[1024,512]{1,0:T(8,128)(2,1)}) conditional(s32[]{:T(128)} %convert_element_type.141, () %tuple.110, (bf16[4,256,512]{2,1,0:T(8,128)(2,1)}, bf16[4,256,512]{2,1,0:T(8,128)(2,1)}, bf16[4,256,256]{2,1,0:T(8,128)(2,1)}, bf16[4,256,256]{2,1,0:T(8,128)(2,1)}, ...), branch_computations={%region_13.14_spmd, %region_14.15_spmd} | conditional | flops 1049600 | bytes 5341214 | solution.py:567
  469.2 12.7 %attention_weights.1 = bf16[4,528,768]{2,1,0:T(8,128)(2,1)} custom-call(bf16[1024,2048]{1,0:T(8,128)(2,1)} %get-tuple-element.338.refs_0_, bf16[1024,2048]{1,0:T(8,128)(2,1)} %get-tuple-element.339.refs_1_, bf16[1024,2048]{1,0:T(8,128)(2,1)} %get-tuple-element.340.refs_2_, bf16[1024,2048]{1,0:T(8,128)(2,1)} %get-tuple-element.341.refs_3_, ...), custom_call_target="tpu_custom_call" | custom-call | flops 1048576 | bytes 65536 | tf_op jit(solution)/shard_map/cond/branch_1_fun/attention_weights/pallas_call | solution.py:377
  483.8 65.8 %conditional.15 = (bf16[256,2048]{1,0:T(8,128)(2,1)}, f32[256,2048]{1,0:T(8,128)}, f32[128,3072]{1,0:T(8,128)}, f32[128,3072]{1,0:T(8,128)}, f32[3072,128]{1,0:T(8,128)}, /*index=5*/f32[128]{0:T(128)S(1)}) conditional(s32[]{:T(128)} %convert_element_type.141, () %tuple.90, (f32[256,2048]{1,0:T(8,128)}, f32[256,2048]{1,0:T(8,128)}, ...), branch_computations={%region_16.17_spmd, %region_17.18_spmd} | conditional | flops 7340050 | bytes 45746224 | solution.py:567
  483.8 4.5 normed_in_grad_far.1
  490.6 6.9 %normed_in_grad.1 = (f32[256,2048]{1,0:T(8,128)}, bf16[128,2048]{1,0:T(8,128)(2,1)}, bf16[128,2048]{1,0:T(8,128)(2,1)}, bf16[128,2048]{1,0:T(8,128)(2,1)}, bf16[128,2048]{1,0:T(8,128)(2,1)}) custom-call(bf16[1024,512]{1,0:T(8,128)(2,1)} %get-tuple-element.352.refs_0_, bf16[1024,512]{1,0:T(8,128)(2,1)} %get-tuple-element.353.refs_1_, ...), custom_call_target="tpu_custom_call" | custom-call | flops 1048576 | bytes 65536 | tf_op jit(solution)/shard_map/cond/branch_1_fun/normed_in_grad/pallas_call | solution.py:223
  497.5 5.3 collective-permute-done.30
  512.9 20.9 %collective-permute-done.37.refs_6_ = bf16[128,768]{1,0:T(8,128)(2,1)S(1)} collective-permute-done((bf16[128,768]{1,0:T(8,128)(2,1)S(1)}, bf16[128,768]{1,0:T(8,128)(2,1)S(1)}, u32[]{:S(2)}, u32[]{:S(2)}) %collective-permute-start.37) | collective-permute-done | bytes 196640 | tf_op jit(solution)/shard_map/cond/branch_1_fun/ppermute | solution.py:571
  535.5 4.9 hidden_out_sum.1
  540.5 4.2 hidden_owned.1
  544.9 4.7 grad_in.1
  555.2 3.9 collective-permute-done.59.refs_1_
  559.1 3.4 collective-permute-done.60.refs_2_
  564.1 2.5 psum.7
  (290 shorter events, 111.2 us)
Async XLA Ops:
  7.2 87.7 %all-gather.7.cloned.1.call-start = ((), (), s32[]{:S(2)}) async-start(), calls=%async_computation.6 | async-start | bytes 4055040 | tf_op jit(solution)/shard_map/all_gather | solution.py:695
  12.8 9.3 %collective-permute-start.39 = (bf16[144,768]{1,0:T(8,128)(2,1)S(1)}, bf16[144,768]{1,0:T(8,128)(2,1)S(1)}, u32[]{:S(2)}, u32[]{:S(2)}) collective-permute-start(bf16[144,768]{1,0:T(8,128)(2,1)S(1)} %get-tuple-element.724), channel_id=1, source_target_pairs={{0,2},{2,0},{4,6},{6,4},{1,3},{3,1},{5,7},{7,5},{8,10},{10,8},{12,... | collective-permute-start | bytes 663560 | tf_op jit(solution)/shard_map/ppermute | solution.py:571
  15.8 11.6 %collective-permute-start.40 = (bf16[144,768]{1,0:T(8,128)(2,1)S(1)}, bf16[144,768]{1,0:T(8,128)(2,1)S(1)}, u32[]{:S(2)}, u32[]{:S(2)}) collective-permute-start(bf16[144,768]{1,0:T(8,128)(2,1)S(1)} %get-tuple-element.725), channel_id=1, source_target_pairs={{0,4},{2,6},{4,0},{6,2},{1,5},{3,7},{5,1},{7,3},{8,12},{10,14},{12... | collective-permute-start | bytes 663560 | tf_op jit(solution)/shard_map/ppermute | solution.py:571
  17.3 10.1 %collective-permute-start.41 = (bf16[144,768]{1,0:T(8,128)(2,1)S(1)}, bf16[144,768]{1,0:T(8,128)(2,1)S(1)}, u32[]{:S(2)}, u32[]{:S(2)}) collective-permute-start(bf16[144,768]{1,0:T(8,128)(2,1)S(1)} %get-tuple-element.723), channel_id=1, source_target_pairs={{0,6},{2,4},{4,2},{6,0},{1,7},{3,5},{5,3},{7,1},{8,14},{10,12},{12... | collective-permute-start | bytes 663560 | tf_op jit(solution)/shard_map/ppermute | solution.py:571
  29.3 194.6 %all-gather.9.cloned.1.call-start = ((), (), s32[]{:S(2)}) async-start(), calls=%async_computation.7 | async-start | bytes 7864320 | tf_op jit(solution)/shard_map/all_gather | solution.py:695
  29.7 23.9 %collective-permute-start.42 = (bf16[256,2048]{1,0:T(8,128)(2,1)S(1)}, bf16[256,2048]{1,0:T(8,128)(2,1)}, u32[]{:S(2)}, u32[]{:S(2)}) collective-permute-start(bf16[256,2048]{1,0:T(8,128)(2,1)S(1)} %copy-done.19), channel_id=1, source_target_pairs={{0,2},{2,0},{4,6},{6,4},{1,3},{3,1},{5,7},{7,5},{8,10},{10,8},{12,... | collective-permute-start | bytes 3145736 | tf_op jit(solution)/shard_map/ppermute | solution.py:571
  30.9 23.9 %collective-permute-start.43 = (bf16[256,2048]{1,0:T(8,128)(2,1)S(1)}, bf16[256,2048]{1,0:T(8,128)(2,1)}, u32[]{:S(2)}, u32[]{:S(2)}) collective-permute-start(bf16[256,2048]{1,0:T(8,128)(2,1)S(1)} %copy-done.19), channel_id=1, source_target_pairs={{0,4},{2,6},{4,0},{6,2},{1,5},{3,7},{5,1},{7,3},{8,12},{10,14},{12... | collective-permute-start | bytes 3145736 | tf_op jit(solution)/shard_map/ppermute | solution.py:571
  55.1 16.3 %collective-permute-start.44 = (bf16[128,2304]{1,0:T(8,128)(2,1)S(1)}, bf16[128,2304]{1,0:T(8,128)(2,1)S(1)}, u32[]{:S(2)}, u32[]{:S(2)}) collective-permute-start(bf16[128,2304]{1,0:T(8,128)(2,1)S(1)} %get-tuple-element.665), channel_id=1, source_target_pairs={{0,2},{2,0},{4,6},{6,4},{1,3},{3,1},{5,7},{7,5},{8,10},{10,8},{12,... | collective-permute-start | bytes 1769480 | tf_op jit(solution)/shard_map/ppermute | solution.py:571
  55.7 28.9 %collective-permute-start.45 = (bf16[128,2304]{1,0:T(8,128)(2,1)S(1)}, bf16[128,2304]{1,0:T(8,128)(2,1)S(1)}, u32[]{:S(2)}, u32[]{:S(2)}) collective-permute-start(bf16[128,2304]{1,0:T(8,128)(2,1)S(1)} %get-tuple-element.664), channel_id=1, source_target_pairs={{0,4},{2,6},{4,0},{6,2},{1,5},{3,7},{5,1},{7,3},{8,12},{10,14},{12... | collective-permute-start | bytes 1769480 | tf_op jit(solution)/shard_map/ppermute | solution.py:571
  56.3 28.3 %collective-permute-start.46 = (bf16[128,2304]{1,0:T(8,128)(2,1)S(1)}, bf16[128,2304]{1,0:T(8,128)(2,1)S(1)}, u32[]{:S(2)}, u32[]{:S(2)}) collective-permute-start(bf16[128,2304]{1,0:T(8,128)(2,1)S(1)} %get-tuple-element.663), channel_id=1, source_target_pairs={{0,6},{2,4},{4,2},{6,0},{1,7},{3,5},{5,3},{7,1},{8,14},{10,12},{12... | collective-permute-start | bytes 1769480 | tf_op jit(solution)/shard_map/ppermute | solution.py:571
  59.7 32.7 %collective-permute-start.47 = (bf16[128,2048]{1,0:T(8,128)(2,1)S(1)}, bf16[128,2048]{1,0:T(8,128)(2,1)}, u32[]{:S(2)}, u32[]{:S(2)}) collective-permute-start(bf16[128,2048]{1,0:T(8,128)(2,1)S(1)} %slice.245), channel_id=1, source_target_pairs={{0,4},{2,6},{4,0},{6,2},{1,5},{3,7},{5,1},{7,3},{8,12},{10,14},{12... | collective-permute-start | bytes 1572872 | tf_op jit(solution)/shard_map/ppermute | solution.py:571
  61.5 30.9 %collective-permute-start.48 = (bf16[128,2048]{1,0:T(8,128)(2,1)S(1)}, bf16[128,2048]{1,0:T(8,128)(2,1)}, u32[]{:S(2)}, u32[]{:S(2)}) collective-permute-start(bf16[128,2048]{1,0:T(8,128)(2,1)S(1)} %slice.246), channel_id=1, source_target_pairs={{0,2},{2,0},{4,6},{6,4},{1,3},{3,1},{5,7},{7,5},{8,10},{10,8},{12,... | collective-permute-start | bytes 1572872 | tf_op jit(solution)/shard_map/ppermute | solution.py:571
  94.9 193.9 %all-gather.11.cloned.1.call-start = ((), (), s32[]{:S(2)}) async-start(), calls=%async_computation.8 | async-start | bytes 3932160 | tf_op jit(solution)/shard_map/all_gather | solution.py:695
  95.6 366.5 %reduce-scatter.4.cloned.1.call-start = ((), (), s32[]{:S(2)}) async-start(), calls=%async_computation.3 | async-start | bytes 7864320 | tf_op jit(solution)/shard_map/reduce_scatter | solution.py:788
  95.7 41.7 %collective-permute-start.49 = (bf16[256,2048]{1,0:T(8,128)(2,1)}, bf16[256,2048]{1,0:T(8,128)(2,1)}, u32[]{:S(2)}, u32[]{:S(2)}) collective-permute-start(bf16[256,2048]{1,0:T(8,128)(2,1)} %param.32), channel_id=1, source_target_pairs={{0,2},{2,0},{4,6},{6,4},{1,3},{3,1},{5,7},{7,5},{8,10},{10,8},{12,... | collective-permute-start | bytes 3145736 | tf_op jit(solution)/shard_map/ppermute | solution.py:571
  97.2 47.4 %collective-permute-start.50 = (bf16[256,2048]{1,0:T(8,128)(2,1)}, bf16[256,2048]{1,0:T(8,128)(2,1)}, u32[]{:S(2)}, u32[]{:S(2)}) collective-permute-start(bf16[256,2048]{1,0:T(8,128)(2,1)} %param.32), channel_id=1, source_target_pairs={{0,4},{2,6},{4,0},{6,2},{1,5},{3,7},{5,1},{7,3},{8,12},{10,14},{12... | collective-permute-start | bytes 3145736 | tf_op jit(solution)/shard_map/ppermute | solution.py:571
  98.7 45.9 %collective-permute-start.51 = (bf16[256,2048]{1,0:T(8,128)(2,1)}, bf16[256,2048]{1,0:T(8,128)(2,1)}, u32[]{:S(2)}, u32[]{:S(2)}) collective-permute-start(bf16[256,2048]{1,0:T(8,128)(2,1)} %param.32), channel_id=1, source_target_pairs={{0,6},{2,4},{4,2},{6,0},{1,7},{3,5},{5,3},{7,1},{8,14},{10,12},{12... | collective-permute-start | bytes 3145736 | tf_op jit(solution)/shard_map/ppermute | solution.py:571
  103.8 8.2 %collective-permute-start = (bf16[4,528,768]{2,1,0:T(8,128)(2,1)}, bf16[4,528,768]{2,1,0:T(8,128)(2,1)S(1)}, u32[]{:S(2)}, u32[]{:S(2)}) collective-permute-start(bf16[4,528,768]{2,1,0:T(8,128)(2,1)} %get-tuple-element.187.refs_6_), channel_id=1, source_target_pairs={{0,1},{1,0},{2,3},{3,2},{4,5},{5,4},{6,7},{7,6},{8,9},{9,8},{10,11... | collective-permute-start | bytes 9732104 | tf_op jit(solution)/shard_map/cond/branch_1_fun/ppermute | solution.py:571
  111.5 25.6 %collective-permute-start.1 = (bf16[1024,2048]{1,0:T(8,128)(2,1)}, bf16[1024,2048]{1,0:T(8,128)(2,1)}, u32[]{:S(2)}, u32[]{:S(2)}) collective-permute-start(bf16[1024,2048]{1,0:T(8,128)(2,1)} %get-tuple-element.749.refs_0_), channel_id=1, source_target_pairs={{0,1},{1,0},{2,3},{3,2},{4,5},{5,4},{6,7},{7,6},{8,9},{9,8},{10,11... | collective-permute-start | bytes 12582920 | tf_op jit(solution)/shard_map/cond/branch_1_fun/ppermute | solution.py:571
  148.8 12.7 %collective-permute-start.13 = (bf16[128,2048]{1,0:T(8,128)(2,1)}, bf16[128,2048]{1,0:T(8,128)(2,1)S(1)}, u32[]{:S(2)}, u32[]{:S(2)}) collective-permute-start(bf16[128,2048]{1,0:T(8,128)(2,1)} %get-tuple-element.237), channel_id=1, source_target_pairs={{0,2},{2,0},{4,6},{6,4},{1,3},{3,1},{5,7},{7,5},{8,10},{10,8},{12,... | collective-permute-start | bytes 1572872 | tf_op jit(solution)/shard_map/cond/branch_1_fun/ppermute | solution.py:571
  150.0 12.7 %collective-permute-start.14 = (bf16[128,2048]{1,0:T(8,128)(2,1)}, bf16[128,2048]{1,0:T(8,128)(2,1)S(1)}, u32[]{:S(2)}, u32[]{:S(2)}) collective-permute-start(bf16[128,2048]{1,0:T(8,128)(2,1)} %get-tuple-element.238), channel_id=1, source_target_pairs={{0,4},{2,6},{4,0},{6,2},{1,5},{3,7},{5,1},{7,3},{8,12},{10,14},{12... | collective-permute-start | bytes 1572872 | tf_op jit(solution)/shard_map/cond/branch_1_fun/ppermute | solution.py:571
  162.7 15.1 %collective-permute-start.15 = (bf16[128,2048]{1,0:T(8,128)(2,1)}, bf16[128,2048]{1,0:T(8,128)(2,1)S(1)}, u32[]{:S(2)}, u32[]{:S(2)}) collective-permute-start(bf16[128,2048]{1,0:T(8,128)(2,1)} %get-tuple-element.239), channel_id=1, source_target_pairs={{0,2},{2,0},{4,6},{6,4},{1,3},{3,1},{5,7},{7,5},{8,10},{10,8},{12,... | collective-permute-start | bytes 1572872 | tf_op jit(solution)/shard_map/cond/branch_1_fun/ppermute | solution.py:571
  163.3 15.1 %collective-permute-start.18 = (bf16[128,2048]{1,0:T(8,128)(2,1)}, bf16[128,2048]{1,0:T(8,128)(2,1)S(1)}, u32[]{:S(2)}, u32[]{:S(2)}) collective-permute-start(bf16[128,2048]{1,0:T(8,128)(2,1)} %get-tuple-element.242), channel_id=1, source_target_pairs={{0,4},{2,6},{4,0},{6,2},{1,5},{3,7},{5,1},{7,3},{8,12},{10,14},{12... | collective-permute-start | bytes 1572872 | tf_op jit(solution)/shard_map/cond/branch_1_fun/ppermute | solution.py:571
  165.0 21.0 %collective-permute-start.16 = (bf16[128,2048]{1,0:T(8,128)(2,1)S(1)}, bf16[128,2048]{1,0:T(8,128)(2,1)S(1)}, u32[]{:S(2)}, u32[]{:S(2)}) collective-permute-start(bf16[128,2048]{1,0:T(8,128)(2,1)S(1)} %add_convert_fusion.1), channel_id=1, source_target_pairs={{0,4},{2,6},{4,0},{6,2},{1,5},{3,7},{5,1},{7,3},{8,12},{10,14},{12... | collective-permute-start | bytes 1572872 | tf_op jit(solution)/shard_map/cond/branch_1_fun/ppermute | solution.py:571
  167.7 18.3 %collective-permute-start.17 = (bf16[128,2048]{1,0:T(8,128)(2,1)S(1)}, bf16[128,2048]{1,0:T(8,128)(2,1)S(1)}, u32[]{:S(2)}, u32[]{:S(2)}) collective-permute-start(bf16[128,2048]{1,0:T(8,128)(2,1)S(1)} %add_convert_fusion), channel_id=1, source_target_pairs={{0,2},{2,0},{4,6},{6,4},{1,3},{3,1},{5,7},{7,5},{8,10},{10,8},{12,... | collective-permute-start | bytes 1572872 | tf_op jit(solution)/shard_map/cond/branch_1_fun/ppermute | solution.py:571
  188.6 22.1 %collective-permute-start.19 = (bf16[256,2048]{1,0:T(8,128)(2,1)}, bf16[256,2048]{1,0:T(8,128)(2,1)}, u32[]{:S(2)}, u32[]{:S(2)}) collective-permute-start(bf16[256,2048]{1,0:T(8,128)(2,1)} %get-tuple-element.764), channel_id=1, source_target_pairs={{0,2},{2,0},{4,6},{6,4},{1,3},{3,1},{5,7},{7,5},{8,10},{10,8},{12,... | collective-permute-start | bytes 3145736 | tf_op jit(solution)/shard_map/cond/branch_1_fun/ppermute | solution.py:571
  190.1 23.3 %collective-permute-start.20 = (bf16[256,2048]{1,0:T(8,128)(2,1)}, bf16[256,2048]{1,0:T(8,128)(2,1)}, u32[]{:S(2)}, u32[]{:S(2)}) collective-permute-start(bf16[256,2048]{1,0:T(8,128)(2,1)} %get-tuple-element.764), channel_id=1, source_target_pairs={{0,4},{2,6},{4,0},{6,2},{1,5},{3,7},{5,1},{7,3},{8,12},{10,14},{12... | collective-permute-start | bytes 3145736 | tf_op jit(solution)/shard_map/cond/branch_1_fun/ppermute | solution.py:571
  211.8 11.4 %collective-permute-start.21 = (bf16[128,2048]{1,0:T(8,128)(2,1)S(1)}, bf16[128,2048]{1,0:T(8,128)(2,1)}, u32[]{:S(2)}, u32[]{:S(2)}) collective-permute-start(bf16[128,2048]{1,0:T(8,128)(2,1)S(1)} %slice.271), channel_id=1, source_target_pairs={{0,4},{2,6},{4,0},{6,2},{1,5},{3,7},{5,1},{7,3},{8,12},{10,14},{12... | collective-permute-start | bytes 1572872 | tf_op jit(solution)/shard_map/cond/branch_1_fun/ppermute | solution.py:571
  214.5 9.4 %collective-permute-start.22 = (bf16[128,2048]{1,0:T(8,128)(2,1)S(1)}, bf16[128,2048]{1,0:T(8,128)(2,1)}, u32[]{:S(2)}, u32[]{:S(2)}) collective-permute-start(bf16[128,2048]{1,0:T(8,128)(2,1)S(1)} %slice.272), channel_id=1, source_target_pairs={{0,2},{2,0},{4,6},{6,4},{1,3},{3,1},{5,7},{7,5},{8,10},{10,8},{12,... | collective-permute-start | bytes 1572872 | tf_op jit(solution)/shard_map/cond/branch_1_fun/ppermute | solution.py:571
  224.3 16.0 %collective-permute-start.4 = (bf16[4,512,1536]{2,1,0:T(8,128)(2,1)}, bf16[4,512,1536]{2,1,0:T(8,128)(2,1)}, u32[]{:S(2)}, u32[]{:S(2)}) collective-permute-start(bf16[4,512,1536]{2,1,0:T(8,128)(2,1)} %get-tuple-element.246.refs_9_.refs_10_.refs_11_), channel_id=1, source_target_pairs={{0,1},{1,0},{2,3},{3,2},{4,5},{5,4},{6,7},{7,6},{8,9},{9,8},{10,11... | collective-permute-start | bytes 18874376 | tf_op jit(solution)/shard_map/cond/branch_1_fun/ppermute | solution.py:571
  265.5 10.5 %collective-permute-start.5 = (bf16[4,512,1536]{2,1,0:T(8,128)(2,1)}, bf16[4,512,1536]{2,1,0:T(8,128)(2,1)}, u32[]{:S(2)}, u32[]{:S(2)}) collective-permute-start(bf16[4,512,1536]{2,1,0:T(8,128)(2,1)} %hidden_weights_a_other.1), channel_id=1, source_target_pairs={{0,1},{1,0},{2,3},{3,2},{4,5},{5,4},{6,7},{7,6},{8,9},{9,8},{10,11... | collective-permute-start | bytes 18874376 | tf_op jit(solution)/shard_map/cond/branch_1_fun/ppermute | solution.py:571
  288.7 193.4 %reduce-scatter.6.cloned.1.call-start = ((), (), s32[]{:S(2)}) async-start(), calls=%async_computation.4 | async-start | bytes 3932160 | tf_op jit(solution)/shard_map/reduce_scatter | solution.py:788
  320.0 17.2 %collective-permute-start.24 = (bf16[128,2048]{1,0:T(8,128)(2,1)}, bf16[128,2048]{1,0:T(8,128)(2,1)S(1)}, u32[]{:S(2)}, u32[]{:S(2)}) collective-permute-start(bf16[128,2048]{1,0:T(8,128)(2,1)} %get-tuple-element.276), channel_id=1, source_target_pairs={{0,4},{2,6},{4,0},{6,2},{1,5},{3,7},{5,1},{7,3},{8,12},{10,14},{12... | collective-permute-start | bytes 1572872 | tf_op jit(solution)/shard_map/cond/branch_1_fun/ppermute | solution.py:571
  320.9 18.3 %collective-permute-start.23 = (bf16[128,2048]{1,0:T(8,128)(2,1)}, bf16[128,2048]{1,0:T(8,128)(2,1)S(1)}, u32[]{:S(2)}, u32[]{:S(2)}) collective-permute-start(bf16[128,2048]{1,0:T(8,128)(2,1)} %get-tuple-element.275), channel_id=1, source_target_pairs={{0,2},{2,0},{4,6},{6,4},{1,3},{3,1},{5,7},{7,5},{8,10},{10,8},{12,... | collective-permute-start | bytes 1572872 | tf_op jit(solution)/shard_map/cond/branch_1_fun/ppermute | solution.py:571
  338.5 16.2 %collective-permute-start.27 = (bf16[128,2048]{1,0:T(8,128)(2,1)S(1)}, bf16[128,2048]{1,0:T(8,128)(2,1)}, u32[]{:S(2)}, u32[]{:S(2)}) collective-permute-start(bf16[128,2048]{1,0:T(8,128)(2,1)S(1)} %add_convert_fusion.2), channel_id=1, source_target_pairs={{0,2},{2,0},{4,6},{6,4},{1,3},{3,1},{5,7},{7,5},{8,10},{10,8},{12,... | collective-permute-start | bytes 1572872 | tf_op jit(solution)/shard_map/cond/branch_1_fun/ppermute | solution.py:571
  340.3 15.0 %collective-permute-start.26 = (bf16[128,2048]{1,0:T(8,128)(2,1)S(1)}, bf16[128,2048]{1,0:T(8,128)(2,1)}, u32[]{:S(2)}, u32[]{:S(2)}) collective-permute-start(bf16[128,2048]{1,0:T(8,128)(2,1)S(1)} %add_convert_fusion.3), channel_id=1, source_target_pairs={{0,4},{2,6},{4,0},{6,2},{1,5},{3,7},{5,1},{7,3},{8,12},{10,14},{12... | collective-permute-start | bytes 1572872 | tf_op jit(solution)/shard_map/cond/branch_1_fun/ppermute | solution.py:571
  341.6 21.9 %collective-permute-start.25 = (bf16[128,2048]{1,0:T(8,128)(2,1)S(1)}, bf16[128,2048]{1,0:T(8,128)(2,1)}, u32[]{:S(2)}, u32[]{:S(2)}) collective-permute-start(bf16[128,2048]{1,0:T(8,128)(2,1)S(1)} %copy-done.40), channel_id=1, source_target_pairs={{0,2},{2,0},{4,6},{6,4},{1,3},{3,1},{5,7},{7,5},{8,10},{10,8},{12,... | collective-permute-start | bytes 1572872 | tf_op jit(solution)/shard_map/cond/branch_1_fun/ppermute | solution.py:571
  342.3 22.7 %collective-permute-start.28 = (bf16[128,2048]{1,0:T(8,128)(2,1)S(1)}, bf16[128,2048]{1,0:T(8,128)(2,1)}, u32[]{:S(2)}, u32[]{:S(2)}) collective-permute-start(bf16[128,2048]{1,0:T(8,128)(2,1)S(1)} %copy-done.39), channel_id=1, source_target_pairs={{0,4},{2,6},{4,0},{6,2},{1,5},{3,7},{5,1},{7,3},{8,12},{10,14},{12... | collective-permute-start | bytes 1572872 | tf_op jit(solution)/shard_map/cond/branch_1_fun/ppermute | solution.py:571
  365.2 38.1 %collective-permute-start.10 = (bf16[4,512,768]{2,1,0:T(8,128)(2,1)}, bf16[4,512,768]{2,1,0:T(8,128)(2,1)}, u32[]{:S(2)}, u32[]{:S(2)}) collective-permute-start(bf16[4,512,768]{2,1,0:T(8,128)(2,1)} %get-tuple-element.317), channel_id=1, source_target_pairs={{0,1},{1,0},{2,3},{3,2},{4,5},{5,4},{6,7},{7,6},{8,9},{9,8},{10,11... | collective-permute-start | bytes 9437192 | tf_op jit(solution)/shard_map/cond/branch_1_fun/ppermute | solution.py:571
  372.1 25.8 %collective-permute-start.6 = (bf16[256,2048]{1,0:T(8,128)(2,1)}, bf16[256,2048]{1,0:T(8,128)(2,1)}, u32[]{:S(2)}, u32[]{:S(2)}) collective-permute-start(bf16[256,2048]{1,0:T(8,128)(2,1)} %get-tuple-element.825), channel_id=1, source_target_pairs={{0,2},{2,0},{4,6},{6,4},{1,3},{3,1},{5,7},{7,5},{8,10},{10,8},{12,... | collective-permute-start | bytes 3145736 | tf_op jit(solution)/shard_map/cond/branch_1_fun/ppermute | solution.py:571
  373.6 25.6 %collective-permute-start.7 = (bf16[256,2048]{1,0:T(8,128)(2,1)}, bf16[256,2048]{1,0:T(8,128)(2,1)}, u32[]{:S(2)}, u32[]{:S(2)}) collective-permute-start(bf16[256,2048]{1,0:T(8,128)(2,1)} %get-tuple-element.825), channel_id=1, source_target_pairs={{0,4},{2,6},{4,0},{6,2},{1,5},{3,7},{5,1},{7,3},{8,12},{10,14},{12... | collective-permute-start | bytes 3145736 | tf_op jit(solution)/shard_map/cond/branch_1_fun/ppermute | solution.py:571
  400.2 13.4 %collective-permute-start.8 = (bf16[128,2048]{1,0:T(8,128)(2,1)S(1)}, bf16[128,2048]{1,0:T(8,128)(2,1)}, u32[]{:S(2)}, u32[]{:S(2)}) collective-permute-start(bf16[128,2048]{1,0:T(8,128)(2,1)S(1)} %slice.161), channel_id=1, source_target_pairs={{0,4},{2,6},{4,0},{6,2},{1,5},{3,7},{5,1},{7,3},{8,12},{10,14},{12... | collective-permute-start | bytes 1572872 | tf_op jit(solution)/shard_map/cond/branch_1_fun/ppermute | solution.py:571
  401.9 13.1 %collective-permute-start.9 = (bf16[128,2048]{1,0:T(8,128)(2,1)S(1)}, bf16[128,2048]{1,0:T(8,128)(2,1)}, u32[]{:S(2)}, u32[]{:S(2)}) collective-permute-start(bf16[128,2048]{1,0:T(8,128)(2,1)S(1)} %slice.162), channel_id=1, source_target_pairs={{0,2},{2,0},{4,6},{6,4},{1,3},{3,1},{5,7},{7,5},{8,10},{10,8},{12,... | collective-permute-start | bytes 1572872 | tf_op jit(solution)/shard_map/cond/branch_1_fun/ppermute | solution.py:571
  415.0 134.6 %reduce-scatter.8.cloned.1.call-start = ((), (), s32[]{:S(2)}) async-start(), calls=%async_computation.5 | async-start | bytes 4055040 | tf_op jit(solution)/shard_map/reduce_scatter | solution.py:788
  415.0 36.7 %collective-permute-start.53 = (bf16[256,2048]{1,0:T(8,128)(2,1)}, bf16[256,2048]{1,0:T(8,128)(2,1)}, u32[]{:S(2)}, u32[]{:S(2)}) collective-permute-start(bf16[256,2048]{1,0:T(8,128)(2,1)} %get-tuple-element.577), channel_id=1, source_target_pairs={{0,2},{2,0},{4,6},{6,4},{1,3},{3,1},{5,7},{7,5},{8,10},{10,8},{12,... | collective-permute-start | bytes 3145736 | tf_op jit(solution)/shard_map/ppermute | solution.py:571
  416.4 44.1 %collective-permute-start.54 = (bf16[256,2048]{1,0:T(8,128)(2,1)}, bf16[256,2048]{1,0:T(8,128)(2,1)}, u32[]{:S(2)}, u32[]{:S(2)}) collective-permute-start(bf16[256,2048]{1,0:T(8,128)(2,1)} %get-tuple-element.578), channel_id=1, source_target_pairs={{0,4},{2,6},{4,0},{6,2},{1,5},{3,7},{5,1},{7,3},{8,12},{10,14},{12... | collective-permute-start | bytes 3145736 | tf_op jit(solution)/shard_map/ppermute | solution.py:571
  417.3 44.8 %collective-permute-start.55 = (bf16[256,2048]{1,0:T(8,128)(2,1)}, bf16[256,2048]{1,0:T(8,128)(2,1)}, u32[]{:S(2)}, u32[]{:S(2)}) collective-permute-start(bf16[256,2048]{1,0:T(8,128)(2,1)} %get-tuple-element.579), channel_id=1, source_target_pairs={{0,6},{2,4},{4,2},{6,0},{1,7},{3,5},{5,3},{7,1},{8,14},{10,12},{12... | collective-permute-start | bytes 3145736 | tf_op jit(solution)/shard_map/ppermute | solution.py:571
  424.9 26.8 %collective-permute-start.11 = (bf16[1024,2048]{1,0:T(8,128)(2,1)}, bf16[1024,2048]{1,0:T(8,128)(2,1)}, u32[]{:S(2)}, u32[]{:S(2)}) collective-permute-start(bf16[1024,2048]{1,0:T(8,128)(2,1)} %get-tuple-element.840.refs_0_), channel_id=1, source_target_pairs={{0,1},{1,0},{2,3},{3,2},{4,5},{5,4},{6,7},{7,6},{8,9},{9,8},{10,11... | collective-permute-start | bytes 12582920 | tf_op jit(solution)/shard_map/cond/branch_1_fun/ppermute | solution.py:571
  425.0 7.6 %collective-permute-start.12 = (bf16[4,256,256]{2,1,0:T(8,128)(2,1)}, bf16[4,256,256]{2,1,0:T(8,128)(2,1)S(1)}, u32[]{:S(2)}, u32[]{:S(2)}) collective-permute-start(bf16[4,256,256]{2,1,0:T(8,128)(2,1)} %bitcast.122), channel_id=1, source_target_pairs={{0,1},{1,0},{2,3},{3,2},{4,5},{5,4},{6,7},{7,6},{8,9},{9,8},{10,11... | collective-permute-start | bytes 1572872 | tf_op jit(solution)/shard_map/cond/branch_1_fun/ppermute | solution.py:571
  464.7 17.2 %collective-permute-start.56 = (bf16[128,1536]{1,0:T(8,128)(2,1)}, bf16[128,1536]{1,0:T(8,128)(2,1)}, u32[]{:S(2)}, u32[]{:S(2)}) collective-permute-start(bf16[128,1536]{1,0:T(8,128)(2,1)} %get-tuple-element.653), channel_id=1, source_target_pairs={{0,2},{2,0},{4,6},{6,4},{1,3},{3,1},{5,7},{7,5},{8,10},{10,8},{12,... | collective-permute-start | bytes 1179656 | tf_op jit(solution)/shard_map/ppermute | solution.py:571
  465.4 16.7 %collective-permute-start.57 = (bf16[128,1536]{1,0:T(8,128)(2,1)}, bf16[128,1536]{1,0:T(8,128)(2,1)}, u32[]{:S(2)}, u32[]{:S(2)}) collective-permute-start(bf16[128,1536]{1,0:T(8,128)(2,1)} %get-tuple-element.652), channel_id=1, source_target_pairs={{0,4},{2,6},{4,0},{6,2},{1,5},{3,7},{5,1},{7,3},{8,12},{10,14},{12... | collective-permute-start | bytes 1179656 | tf_op jit(solution)/shard_map/ppermute | solution.py:571
  467.0 15.1 %collective-permute-start.58 = (bf16[128,1536]{1,0:T(8,128)(2,1)}, bf16[128,1536]{1,0:T(8,128)(2,1)}, u32[]{:S(2)}, u32[]{:S(2)}) collective-permute-start(bf16[128,1536]{1,0:T(8,128)(2,1)} %get-tuple-element.651), channel_id=1, source_target_pairs={{0,6},{2,4},{4,2},{6,0},{1,7},{3,5},{5,3},{7,1},{8,14},{10,12},{12... | collective-permute-start | bytes 1179656 | tf_op jit(solution)/shard_map/ppermute | solution.py:571
  468.4 13.4 %collective-permute-start.29 = (bf16[4,256,512]{2,1,0:T(8,128)(2,1)}, bf16[4,256,512]{2,1,0:T(8,128)(2,1)}, u32[]{:S(2)}, u32[]{:S(2)}) collective-permute-start(bf16[4,256,512]{2,1,0:T(8,128)(2,1)} %get-tuple-element.343), channel_id=1, source_target_pairs={{0,1},{1,0},{2,3},{3,2},{4,5},{5,4},{6,7},{7,6},{8,9},{9,8},{10,11... | collective-permute-start | bytes 3145736 | tf_op jit(solution)/shard_map/cond/branch_1_fun/ppermute | solution.py:571
  488.3 14.6 %collective-permute-start.30 = (bf16[128,2048]{1,0:T(8,128)(2,1)}, bf16[128,2048]{1,0:T(8,128)(2,1)}, u32[]{:S(2)}, u32[]{:S(2)}) collective-permute-start(bf16[128,2048]{1,0:T(8,128)(2,1)} %get-tuple-element.360), channel_id=1, source_target_pairs={{0,2},{2,0},{4,6},{6,4},{1,3},{3,1},{5,7},{7,5},{8,10},{10,8},{12,... | collective-permute-start | bytes 1572872 | tf_op jit(solution)/shard_map/cond/branch_1_fun/ppermute | solution.py:571
  489.0 14.3 %collective-permute-start.31 = (bf16[128,2048]{1,0:T(8,128)(2,1)}, bf16[128,2048]{1,0:T(8,128)(2,1)}, u32[]{:S(2)}, u32[]{:S(2)}) collective-permute-start(bf16[128,2048]{1,0:T(8,128)(2,1)} %get-tuple-element.361), channel_id=1, source_target_pairs={{0,4},{2,6},{4,0},{6,2},{1,5},{3,7},{5,1},{7,3},{8,12},{10,14},{12... | collective-permute-start | bytes 1572872 | tf_op jit(solution)/shard_map/cond/branch_1_fun/ppermute | solution.py:571
  503.4 8.0 %collective-permute-start.36 = (bf16[128,768]{1,0:T(8,128)(2,1)S(1)}, bf16[128,768]{1,0:T(8,128)(2,1)S(1)}, u32[]{:S(2)}, u32[]{:S(2)}) collective-permute-start(bf16[128,768]{1,0:T(8,128)(2,1)S(1)} %get-tuple-element.649), channel_id=1, source_target_pairs={{0,2},{2,0},{4,6},{6,4},{1,3},{3,1},{5,7},{7,5},{8,10},{10,8},{12,... | collective-permute-start | bytes 589832 | tf_op jit(solution)/shard_map/cond/branch_1_fun/ppermute | solution.py:571
  504.7 40.0 %collective-permute-start.32 = (bf16[128,2048]{1,0:T(8,128)(2,1)}, bf16[128,2048]{1,0:T(8,128)(2,1)S(1)}, u32[]{:S(2)}, u32[]{:S(2)}) collective-permute-start(bf16[128,2048]{1,0:T(8,128)(2,1)} %get-tuple-element.362), channel_id=1, source_target_pairs={{0,2},{2,0},{4,6},{6,4},{1,3},{3,1},{5,7},{7,5},{8,10},{10,8},{12,... | collective-permute-start | bytes 1572872 | tf_op jit(solution)/shard_map/cond/branch_1_fun/ppermute | solution.py:571
  505.5 39.3 %collective-permute-start.35 = (bf16[128,2048]{1,0:T(8,128)(2,1)}, bf16[128,2048]{1,0:T(8,128)(2,1)S(1)}, u32[]{:S(2)}, u32[]{:S(2)}) collective-permute-start(bf16[128,2048]{1,0:T(8,128)(2,1)} %get-tuple-element.365), channel_id=1, source_target_pairs={{0,4},{2,6},{4,0},{6,2},{1,5},{3,7},{5,1},{7,3},{8,12},{10,14},{12... | collective-permute-start | bytes 1572872 | tf_op jit(solution)/shard_map/cond/branch_1_fun/ppermute | solution.py:571
  508.4 36.4 %collective-permute-start.33 = (bf16[128,2048]{1,0:T(8,128)(2,1)S(1)}, bf16[128,2048]{1,0:T(8,128)(2,1)S(1)}, u32[]{:S(2)}, u32[]{:S(2)}) collective-permute-start(bf16[128,2048]{1,0:T(8,128)(2,1)S(1)} %add_convert_fusion.5), channel_id=1, source_target_pairs={{0,4},{2,6},{4,0},{6,2},{1,5},{3,7},{5,1},{7,3},{8,12},{10,14},{12... | collective-permute-start | bytes 1572872 | tf_op jit(solution)/shard_map/cond/branch_1_fun/ppermute | solution.py:571
  510.1 34.7 %collective-permute-start.34 = (bf16[128,2048]{1,0:T(8,128)(2,1)S(1)}, bf16[128,2048]{1,0:T(8,128)(2,1)S(1)}, u32[]{:S(2)}, u32[]{:S(2)}) collective-permute-start(bf16[128,2048]{1,0:T(8,128)(2,1)S(1)} %add_convert_fusion.4), channel_id=1, source_target_pairs={{0,2},{2,0},{4,6},{6,4},{1,3},{3,1},{5,7},{7,5},{8,10},{10,8},{12,... | collective-permute-start | bytes 1572872 | tf_op jit(solution)/shard_map/cond/branch_1_fun/ppermute | solution.py:571
  511.4 22.4 %collective-permute-start.37 = (bf16[128,768]{1,0:T(8,128)(2,1)S(1)}, bf16[128,768]{1,0:T(8,128)(2,1)S(1)}, u32[]{:S(2)}, u32[]{:S(2)}) collective-permute-start(bf16[128,768]{1,0:T(8,128)(2,1)S(1)} %get-tuple-element.648), channel_id=1, source_target_pairs={{0,4},{2,6},{4,0},{6,2},{1,5},{3,7},{5,1},{7,3},{8,12},{10,14},{12... | collective-permute-start | bytes 589832 | tf_op jit(solution)/shard_map/cond/branch_1_fun/ppermute | solution.py:571
  551.6 7.5 %collective-permute-start.59 = (bf16[144,768]{1,0:T(8,128)(2,1)S(1)}, bf16[144,768]{1,0:T(8,128)(2,1)S(1)}, u32[]{:S(2)}, u32[]{:S(2)}) collective-permute-start(bf16[144,768]{1,0:T(8,128)(2,1)S(1)} %get-tuple-element.657), channel_id=1, source_target_pairs={{0,2},{2,0},{4,6},{6,4},{1,3},{3,1},{5,7},{7,5},{8,10},{10,8},{12,... | collective-permute-start | bytes 663560 | tf_op jit(solution)/shard_map/ppermute | solution.py:571
  553.0 9.5 %collective-permute-start.60 = (bf16[144,768]{1,0:T(8,128)(2,1)S(1)}, bf16[144,768]{1,0:T(8,128)(2,1)S(1)}, u32[]{:S(2)}, u32[]{:S(2)}) collective-permute-start(bf16[144,768]{1,0:T(8,128)(2,1)S(1)} %get-tuple-element.658), channel_id=1, source_target_pairs={{0,4},{2,6},{4,0},{6,2},{1,5},{3,7},{5,1},{7,3},{8,12},{10,14},{12... | collective-permute-start | bytes 663560 | tf_op jit(solution)/shard_map/ppermute | solution.py:571
  554.0 8.5 %collective-permute-start.61 = (bf16[144,768]{1,0:T(8,128)(2,1)S(1)}, bf16[144,768]{1,0:T(8,128)(2,1)S(1)}, u32[]{:S(2)}, u32[]{:S(2)}) collective-permute-start(bf16[144,768]{1,0:T(8,128)(2,1)S(1)} %get-tuple-element.655), channel_id=1, source_target_pairs={{0,6},{2,4},{4,2},{6,0},{1,7},{3,5},{5,3},{7,1},{8,14},{10,12},{12... | collective-permute-start | bytes 663560 | tf_op jit(solution)/shard_map/ppermute | solution.py:571
  (47 other events, 518.4 us)
Sparse Core Ops, SparseCore 0:
  29.4 65.4 all-gather.6
  97.0 113.9 all-gather.8
  213.2 61.7 all-gather.10
  288.8 109.9 reduce-scatter.3
  415.1 59.4 reduce-scatter.5
  482.2 61.1 reduce-scatter.7

commit v2 on v1

--- a/solution.py
+++ b/solution.py
@@ -260,48 +260,56 @@
     if count == 4:
         upper = got[0][...].astype(f32) + got[1][...].astype(f32)
         lower = got[2][...].astype(f32) + got[3][...].astype(f32)
-        total += jnp.where(pl.program_id(0) < pl.num_programs(0) // 2, upper, lower)
+        total += jnp.where(pl.program_id(0) == 0, upper, lower)
     else:
         for piece in got:
             total += piece[...].astype(f32)
     rows = base[...].astype(f32)
     if kind == "sum":
         refs[0][...] = (rows + total).astype(bf16)
-    elif kind == "norm":
-        gain, whole, low = refs
-        whole[...] = rows + total
-        low[...] = normalize(rows + total, gain[...]).astype(bf16)
+        return
+    gain = refs[0][...]
+    if kind == "norm":
+        whole, *low = refs[1:]
+        total = rows + total
+        sent = normalize(total, gain)
     else:
-        gain, more, whole = refs[:3]
-        total = more[...].astype(f32) + norm_back(rows, gain[...], total)
-        whole[...] = total
-        for low in refs[3:]:
-            low[...] = total.astype(bf16)
-
-
-def rows_call(kind, own, base, got, gain, more, dtypes, name):
+        more, whole, *low = refs[1:]
+        total = more[...].astype(f32) + norm_back(rows, gain, total)
+        sent = total
+    whole[...] = total
+    for place, half in enumerate(low):
+
+        @pl.when(pl.program_id(0) == place)
+        def _():
+            half[...] = sent.astype(bf16)
+
+
+def rows_call(kind, own, base, got, gain, more, sent, name):
     rows, width = own.shape
-    step = rows // 4
+    step = rows // 2
     strip = pl.BlockSpec((step, width), lambda i: (i, 0))
-    upper = pl.BlockSpec((step, width), lambda i: (jnp.minimum(i, 1), 0))
-    lower = pl.BlockSpec((step, width), lambda i: (jnp.maximum(i - 2, 0), 0))
+    half = resident((step, width))
     operands = [own, base] + list(got)
-    in_specs = [strip, strip]
-    in_specs += [upper, upper, lower, lower] if len(got) == 4 else [strip] * len(got)
+    in_specs = [strip, strip] + [half if len(got) == 4 else strip] * len(got)
     if gain is not None:
         operands.append(gain.reshape(1, width))
         in_specs.append(resident((1, width)))
     if more is not None:
         operands.append(more)
         in_specs.append(strip)
+    out_specs, shapes = [strip], [jax.ShapeDtypeStruct((rows, width), bf16 if gain is None else f32)]
+    if sent:
+        out_specs += [half] * 2
+        shapes += [jax.ShapeDtypeStruct((step, width), bf16)] * 2
     return list(
         pl.pallas_call(
             functools.partial(rows_kernel, kind, len(got)),
-            grid=(4,),
+            grid=(2,),
             in_specs=in_specs,
-            out_specs=[strip] * len(dtypes),
-            out_shape=[jax.ShapeDtypeStruct((rows, width), dtype) for dtype in dtypes],
-            compiler_params=pltpu.CompilerParams(vmem_limit_bytes=32 << 20),
+            out_specs=out_specs,
+            out_shape=shapes,
+            compiler_params=pltpu.CompilerParams(vmem_limit_bytes=48 << 20),
             cost_estimate=BESIDE,
             name=name,
         )(*operands)
@@ -571,17 +579,24 @@
     return lax.ppermute(block, axis, [(i, i ^ step) for i in range(lax.axis_size(axis))])
 
 
-def spread(block, *first):
+def halves(rows):
+    middle = rows.shape[0] // 2
+    return [rows[:middle], rows[middle:]]
+
+
+def spread_near(own):
     if lax.axis_size("model") == 1:
-        return [block]
-    near = [block, trade(block, "model", 1), trade(block, "model", 2)]
-    return near + far_halves(near, *first)
-
-
-def far_halves(near, *first):
-    half = near[0].shape[0] // 2
-    _, by_x, by_y = after(near, *first) if first else near
-    return [trade(by_x[:half], "model", 2), trade(by_y[half:], "model", 1)]
+        return list(own)
+    return list(own) + [trade(half, "model", k) for k in (1, 2) for half in own]
+
+
+def spread_far(near, *first):
+    if len(near) == 2:
+        return []
+    upper, lower = near[2], near[5]
+    if first:
+        upper, lower = after((upper, lower), *first)
+    return [trade(upper, "model", 2), trade(lower, "model", 1)]
 
 
 def send_near(near, far):
@@ -695,11 +710,10 @@
         return lax.all_gather(pieces, "data", axis=0, tiled=False)
 
     attn_got = swap(attn_piece)
-    x_sent, attn_got = lax.optimization_barrier((hidden_in, attn_got))
-    x_near = [x_sent, trade(x_sent, "model", 1), trade(x_sent, "model", 2)]
+    x_near = spread_near(lax.optimization_barrier((halves(hidden_in), attn_got))[0])
     tied = lax.optimization_barrier((w_gate, w_up, turned_down, x_near))
     w_gate_sent, w_up_sent, turned_down, x_near = tied
-    x_blocks = x_near + far_halves(x_near)
+    x_blocks = x_near + spread_far(x_near)
     mlp_got = swap(
         lambda i: jnp.concatenate(
             [
@@ -744,8 +758,7 @@
         return [weight] + [trade(weight, "tp", j) for j in range(1, cores)]
 
     near_rows = model * shard
-    grad_sent, mlp_near = lax.optimization_barrier((out_grad, mlp_near))
-    grad_blocks = [out_grad] + [trade(grad_sent, "model", k) for k in range(1, model)]
+    grad_near = spread_near(after(halves(out_grad), *x_blocks, *mlp_near))
 
     seg_rows = jnp.pad(seg_all[:, None], ((0, 0), (0, 7), (0, 0)))
     seg_columns = seg_all[:, :, None]
@@ -753,7 +766,7 @@
     shared = [cosine, sine, seg_columns, seg_rows]
     o_place = [cols // q_cols] * cores
 
-    def attention_phase():
+    def product_phase():
         w_attn = with_cores(attn_full)
         normed_in, first_raw = rows_product(
             x_blocks, gain_in, w_attn[0], cols, 0, near_rows, f32, "query_key_value"
@@ -764,6 +777,14 @@
                 [normed_in], None, w_attn[j], cols, 0, near_rows, f32, "query_key_value_other"
             )[1]
             raw.append(trade(mine, "tp", j).reshape(model, half, cols))
+        return w_attn[1:], normed_in, raw
+
+    w_others, own_normed, raw = phase(always, product_phase)
+    w_attn = [attn_full] + w_others
+    raw, grad_near = lax.optimization_barrier((raw, grad_near))
+
+    def attention_phase():
+        far = spread_far(grad_near)
         attended = attention_call(
             functools.partial(attend_kernel, cores, kv_heads, repeat),
             "attend",
@@ -775,14 +796,14 @@
             [],
             [((seq_len, cols), f32), ((seq_len, q_cols), bf16)],
         )
+        attended, far = lax.optimization_barrier((list(attended), far))
         att_pieces = [attended[0]] + [trade(attended[j], "tp", j) for j in range(1, cores)]
         att_flat = [piece.reshape(-1, q_cols) for piece in att_pieces]
-        all_rows = with_cores(normed_in)
-        return w_attn[1:], all_rows, raw, att_flat, list(attended)
-
-    w_others, normed_in, raw, att_flat, attended = phase(always, attention_phase)
-    w_attn = [attn_full] + w_others
-    att_flat, grad_blocks = lax.optimization_barrier((att_flat, grad_blocks))
+        return with_cores(own_normed)[1:], att_flat, attended, far
+
+    normed_others, att_flat, attended, grad_far = phase(always, attention_phase)
+    normed_in = [own_normed] + normed_others
+    grad_blocks = grad_near + grad_far
 
     def data_sum(total):
         return lax.psum_scatter(total, "data", scatter_dimension=0, tiled=False)
@@ -791,49 +812,50 @@
         own, _, got = project_and_send(
             att_flat, w_attn, o_place, half, near_rows, "attention_out"
         )
-        middle, low = rows_call(
-            "norm", own, hidden_in, got, gain_mid, None, [f32, bf16], "middle"
-        )
-        return middle, spread(low)
+        middle, *low = rows_call("norm", own, hidden_in, got, gain_mid, None, True, "middle")
+        near = spread_near(low)
+        return middle, near + spread_far(near)
 
     middle, mid_blocks = phase(always, out_phase)
 
-    def hidden_others(kept, rows, name):
+    def for_own_core(rows):
         return [
-            weight_grad([[(kept[k], rows[k][j])] for k in range(2)], [], (), near_rows, name)
-            for j in range(1, cores)
+            [rows[k][0]] + [trade(rows[k][j], "tp", j) for j in range(1, cores)] for k in range(2)
         ]
 
-    def hidden_own(kept, rows, received, name):
-        pairs = [[(kept[k], rows[k][0])] for k in range(2)]
-        return weight_grad(pairs, received, (), near_rows, name)
+    def hidden_weights(kept, rows, name):
+        groups = [[(kept[k][j], rows[k][j]) for j in range(cores)] for k in range(2)]
+        return weight_grad(groups, [], (), near_rows, name)
 
     def first_phase():
         weights = with_cores(mlp_full[0])
         rows, *by_core = hidden_call(mid_blocks, grad_blocks, weights[:1], "hidden_units_a")
+        kept = [with_cores(whole) for whole in rows]
         by_core = [by_core]
         for weight in weights[1:]:
             got = hidden_call(*[[whole] for whole in rows], [weight], "hidden_units_a_other")
             by_core.append(got[1:])
         first_rows = [[got[k][0] for got in by_core] for k in range(2)]
-        others = hidden_others(rows, first_rows, "hidden_weights_a_other")
-        received = [trade(other, "tp", j + 1) for j, other in enumerate(others)]
-        return weights[1:], rows, first_rows, received
-
-    other_weights, kept, first_rows, received = phase(always, first_phase)
+        total = hidden_weights(kept, for_own_core(first_rows), "hidden_weights_a")
+        return weights[1:], kept, first_rows, total
+
+    other_weights, kept, first_rows, total = phase(always, first_phase)
     w_mlp = [[mlp_full[0]] + other_weights]
+    wholes = [[kept[k][0]] for k in range(2)]
     mlp_sums = []
     if len(chunks) > 1:
-        w_mlp.append(with_cores(after(mlp_full[1], *received)))
-        mlp_sums.append(data_sum(hidden_own(kept, first_rows, received, "hidden_weights_a")))
+        mlp_sums.append(data_sum(total))
     count = cores * len(chunks)
-    both_cores = [w for pair in w_mlp for w in pair]
 
     def hidden_phase():
-        rows = [first_rows]
+        rows, weights = [first_rows], list(w_mlp)
         if len(chunks) > 1:
-            wholes = [[whole] for whole in kept]
-            rows.append(hidden_call(*wholes, w_mlp[1], "hidden_units_b")[1:])
+            weights.append(with_cores(mlp_full[1]))
+            by_core = [
+                hidden_call(*wholes, [weight], "hidden_units_b")[1:] for weight in weights[1]
+            ]
+            rows.append([[got[k][0] for got in by_core] for k in range(2)])
+        both_cores = [w for pair in weights for w in pair]
         own, _, got = project_and_send(
             [grads for pair in rows for grads in pair[0]],
             both_cores,
@@ -842,26 +864,29 @@
             near_rows,
             "normed_mid_grad",
         )
-        others = hidden_others(kept, after(rows[-1], own), "hidden_weights_b_other")
-        return own, got, rows[-1], others, [acts for pair in rows for acts in pair[1]]
-
-    mid_part, mid_got, last_rows, others, act_rows = phase(always, hidden_phase)
+        last_rows = after(for_own_core(rows[-1]), own)
+        total = hidden_weights(kept, last_rows, "hidden_weights_b")
+        acts = [acts for pair in rows for acts in pair[1]]
+        return own, got, total, acts, [w for pair in weights[1:] for w in pair[1:]]
+
+    mid_part, mid_got, total, act_rows, other_weights = phase(always, hidden_phase)
+    if len(chunks) > 1:
+        mlp_sums.append(data_sum(total))
+        w_mlp.append([mlp_full[1]] + other_weights)
+    both_cores = [w for pair in w_mlp for w in pair]
 
     def branch_phase():
-        middle_grad, branch_own = rows_call(
-            "back", mid_part, middle, mid_got, gain_mid, out_grad, [f32, bf16], "middle_grad"
+        middle_grad, *low = rows_call(
+            "back", mid_part, middle, mid_got, gain_mid, out_grad, True, "middle_grad"
         )
         down_parts = project(
             act_rows, both_cores, [2] * count, 0, [half] * model, near_rows, "hidden_out"
         )
-        branch_blocks = spread(branch_own, *down_parts)
-        received = [trade(other, "tp", j + 1) for j, other in enumerate(others)]
-        last = after(last_rows, branch_own, *down_parts)
-        total = hidden_own(kept, last, received, "hidden_weights_b")
-        return middle_grad, branch_blocks, total, down_parts
-
-    middle_grad, branch_blocks, total, down_parts = phase(always, branch_phase)
-    mlp_sums.append(data_sum(total))
+        near = spread_near(low)
+        branch_blocks = near + spread_far(near, *down_parts)
+        return middle_grad, branch_blocks, down_parts
+
+    middle_grad, branch_blocks, down_parts = phase(always, branch_phase)
     down_got = [trade(down_parts[k], "model", k) for k in range(1, model)]
 
     def attend_back_phase():
@@ -892,9 +917,6 @@
         return with_cores(branch), list(qkv_back), head_grads
 
     branch, qkv_back, head_grads = phase(always, attend_back_phase)
-    tied = lax.optimization_barrier((qkv_back, mlp_sums[:-1], down_got))
-    qkv_back, first_sums, down_got = tied
-    first_got = [swap(rows_at(total.reshape(model, shard, -1))) for total in first_sums]
 
     def attention_weights_phase():
         back_pieces = [qkv_back[0]] + [trade(qkv_back[j], "tp", j) for j in range(1, cores)]
@@ -910,24 +932,32 @@
 
     ride_rows = -(-2 * head_size // wide)
     attn_total, back_flat = phase(always, attention_weights_phase)
-    attn_total, first_got = lax.optimization_barrier((attn_total, first_got))
+    attn_total, down_got = lax.optimization_barrier((attn_total, down_got))
     attn_sum = data_sum(attn_total)
-    back_flat, last_sum = lax.optimization_barrier((back_flat, mlp_sums[-1]))
-
-    def last_phase():
-        own, in_far, in_got = project_and_send(
+    back_flat, first_sums = lax.optimization_barrier((back_flat, mlp_sums[:-1]))
+
+    def exchanged(total):
+        return swap(rows_at(total.reshape(model, shard, -1)))
+
+    def in_grad_phase():
+        own, _, got = project_and_send(
             back_flat, w_attn, [0] * cores, half, near_rows, "normed_in_grad"
         )
+        return own, got, [exchanged(total) for total in first_sums]
+
+    in_part, in_got, first_got = phase(always, in_grad_phase)
+    in_got, last_sum = lax.optimization_barrier((in_got, mlp_sums[-1]))
+
+    def last_phase():
+        last_got = exchanged(last_sum)
         hidden_out = rows_call(
-            "sum", down_parts[0], middle, down_got, None, None, [bf16], "hidden_out_sum"
+            "sum", down_parts[0], middle, down_got, None, None, False, "hidden_out_sum"
         )[0]
-        last_got = swap(rows_at(after(last_sum.reshape(model, shard, -1), *in_far)))
         grad_in = rows_call(
-            "back", own, hidden_in, in_got, gain_in, middle_grad, [f32], "grad_in"
+            "back", in_part, hidden_in, in_got, gain_in, middle_grad, False, "grad_in"
         )[0]
-
         layout = [
-            [(0, first, ff, size, False), (1, first, ff, size, False), (2, first, ff, size, True)]
+            [(kind, first, ff, size, kind == 2) for kind in range(3)]
             for first, size in zip(starts, chunks)
         ]
         shapes = [w_gate.shape, w_up.shape, w_down.shape]

time: 584 us -> 570 us (0.976)
  waiting for transfers between devices: 212 us -> 194 us
  starting transfers between devices: 57.7 us -> 68.1 us
    ppermute x62 -> x75, waiting for transfers between devices: 209 us -> 193 us  [trade(): lax.ppermute(block, axis, [(i, i ^ step) for i in range(lax.axis_size(axi...]
    ppermute x62 -> x75, starting transfers between devices: 57.5 us -> 67.9 us  [trade(): lax.ppermute(block, axis, [(i, i ^ step) for i in range(lax.axis_size(axi...]
    pallas_call x5 -> x3, Pallas kernels: 54 us -> 44.6 us  [weight_grad(): pl.pallas_call(functools.partial(weight_grad_kernel, [len(group) for grou...]
    pallas_call x3 -> x4, Pallas kernels: 43.9 us -> 49.5 us  [hidden_call(): pl.pallas_call(functools.partial(hidden_kernel, first, cores, len(x_piece...]
  transfers between devices with their start and end apart: 68 -> 81, of which waited for: 39 -> 38; matrix products, arithmetic and copies ran while one was open for 6% -> 6% of each run, Pallas kernels for 41% -> 41%
where the time goes in v2:
time: 570 us; the launch traced here: 561 us
  Pallas kernels  230 us (40%)
  waiting for transfers between devices  194 us (34%)
  starting transfers between devices  68.1 us (12%)
  local copies, waits for them, and re-layouts  29.9 us (5%)
  other arithmetic  17.9 us (3%)
  between operations  17.2 us (3%)
    ppermute x75, waiting for transfers between devices, trade(): lax.ppermute(block, axis, [(i, i ^ step) for i in range(lax.axis_size(axi...  193 us
    ppermute x75, starting transfers between devices, trade(): lax.ppermute(block, axis, [(i, i ^ step) for i in range(lax.axis_size(axi...  67.9 us
    pallas_call x7, Pallas kernels, project(): pl.pallas_call(functools.partial(project_kernel, len(lefts)), grid=(parts...  56.1 us
    pallas_call x4, Pallas kernels, hidden_call(): pl.pallas_call(functools.partial(hidden_kernel, first, cores, len(x_piece...  49.5 us
    pallas_call x3, Pallas kernels, weight_grad(): pl.pallas_call(functools.partial(weight_grad_kernel, [len(group) for grou...  44.6 us
    pallas_call x2, Pallas kernels, attention_call(): pl.pallas_call(kernel, grid=(halves[0].shape[0],), in_specs=[pl.BlockSpec...  29.8 us
    pallas_call x4, Pallas kernels, rows_product(): pl.pallas_call(functools.partial(rows_product_kernel, len(pieces), gain i...  24.1 us
    pallas_call x4, Pallas kernels, rows_call(): pl.pallas_call(functools.partial(rows_kernel, kind, len(got)), grid=(2,),...  18.5 us
  transfers between devices with their start and end apart: 81, of which 38 were waited for; matrix products, arithmetic and copies ran while one was open for 6% of the time, Pallas kernels for 41%

profile of v2, /device:TPU:0, one launch (start us, length us, event | category | flops | bytes accessed | tf_op | source)
XLA Modules:
  0.0 561.2 jit_solution(18346165741929481519)
XLA Ops:
  12.8 3.0 collective-permute-start.53
  17.5 4.6 collective-permute-done.53
  22.1 5.4 collective-permute-done.54
  37.7 8.3 %collective-permute-done.56 = bf16[128,2048]{1,0:T(8,128)(2,1)S(1)} collective-permute-done((bf16[128,2048]{1,0:T(8,128)(2,1)S(1)}, bf16[128,2048]{1,0:T(8,128)(2,1)S(1)}, u32[]{:S(2)}, u32[]{:S(2)}) %collective-permute-start.56) | collective-permute-done | bytes 524320 | tf_op jit(solution)/shard_map/ppermute | solution.py:579
  46.0 8.9 %collective-permute-done.57 = bf16[128,2048]{1,0:T(8,128)(2,1)S(1)} collective-permute-done((bf16[128,2048]{1,0:T(8,128)(2,1)S(1)}, bf16[128,2048]{1,0:T(8,128)(2,1)S(1)}, u32[]{:S(2)}, u32[]{:S(2)}) %collective-permute-start.57) | collective-permute-done | bytes 524320 | tf_op jit(solution)/shard_map/ppermute | solution.py:579
  61.9 3.7 fusion.2
  68.3 4.5 collective-permute-done.60.refs_1_
  72.8 13.9 %collective-permute-done.61.refs_2_ = bf16[128,2304]{1,0:T(8,128)(2,1)S(1)} collective-permute-done((bf16[128,2304]{1,0:T(8,128)(2,1)S(1)}, bf16[128,2304]{1,0:T(8,128)(2,1)S(1)}, u32[]{:S(2)}, u32[]{:S(2)}) %collective-permute-start.61) | collective-permute-done | bytes 589856 | tf_op jit(solution)/shard_map/ppermute | solution.py:579
  88.2 6.5 %collective-permute-done.63 = bf16[128,2048]{1,0:T(8,128)(2,1)S(1)} collective-permute-done((bf16[128,2048]{1,0:T(8,128)(2,1)S(1)}, bf16[128,2048]{1,0:T(8,128)(2,1)S(1)}, u32[]{:S(2)}, u32[]{:S(2)}) %collective-permute-start.63) | collective-permute-done | bytes 524320 | tf_op jit(solution)/shard_map/ppermute | solution.py:579
  99.7 2.3 fusion.36
  106.5 18.4 %conditional.10 = (bf16[4,528,768]{2,1,0:T(8,128)(2,1)}, bf16[1024,2048]{1,0:T(8,128)(2,1)}, f32[4,256,512]{2,1,0:T(8,128)}, f32[4,256,512]{2,1,0:T(8,128)}) conditional(s32[]{:T(128)} %convert_element_type.143, () %tuple.112, (bf16[4,528,768]{2,1,0:T(8,128)(2,1)S(1)}, f32[16,128]{1,0:T(8,128)S(1)}, bf16[128,2048]{1,0:T(8,128)(2,1)}, ...), branch_computations={%region_0.1_spmd, %region_1.2_spmd} | conditional | flops 2097152 | bytes 21495920 | solution.py:575
  106.8 7.0 %query_key_value.1 = (bf16[1024,2048]{1,0:T(8,128)(2,1)}, f32[1024,512]{1,0:T(8,128)}) custom-call(bf16[128,2048]{1,0:T(8,128)(2,1)} %get-tuple-element.251.refs_0_, bf16[128,2048]{1,0:T(8,128)(2,1)} %get-tuple-element.252.refs_1_, bf16[128,2048]{1,0:T(8,128)(2,1)} %get-tuple-element.253.refs_2_, bf16[128,2048]{1,0:T(8,128)(2,1)} %get-tuple-element.254.refs_3_, ...), custom_call_target="tpu_custom_call" | custom-call | flops 1048576 | bytes 65536 | tf_op jit(solution)/shard_map/cond/branch_1_fun/query_key_value/pallas_call | solution.py:342
  113.8 6.6 %query_key_value_other.1 = f32[1024,512]{1,0:T(8,128)} custom-call(bf16[1024,2048]{1,0:T(8,128)(2,1)} %get-tuple-element.850.refs_0_, bf16[4,528,768]{2,1,0:T(8,128)(2,1)} %collective-permute-done.refs_1_), custom_call_target="tpu_custom_call" | custom-call | flops 1048576 | bytes 65536 | tf_op jit(solution)/shard_map/cond/branch_1_fun/query_key_value_other/pallas_call | solution.py:342
  120.8 4.1 collective-permute-done.1
  127.8 18.1 %conditional.11 = (bf16[1024,2048]{1,0:T(8,128)(2,1)}, bf16[1024,256]{1,0:T(8,128)(2,1)}, bf16[1024,256]{1,0:T(8,128)(2,1)}, bf16[4,256,256]{2,1,0:T(8,128)(2,1)...) conditional(s32[]{:T(128)} %convert_element_type.143, () %tuple.111, ...), branch_computations={%region_2.3_spmd, %region_3.4_spmd} | conditional | flops 1048576 | bytes 24199384 | solution.py:575
  130.2 11.7 %attend.1 = (bf16[4,256,256]{2,1,0:T(8,128)(2,1)}, bf16[4,256,256]{2,1,0:T(8,128)(2,1)}) custom-call(s32[1]{0:T(128)} %bitcast.3.core_ref, f32[4,256,512]{2,1,0:T(8,128)} %get-tuple-element.264.refs_0_, f32[4,256,512]{2,1,0:T(8,128)} %get-tuple-element.265.refs_1_, f32[4,512,128]{2,1,0:T(8,128)} %get-tuple-element.266.refs_2_, ...), custom_call_target="tpu_custom_call" | custom-call | flops 1048576 | bytes 65536 | tf_op jit(solution)/shard_map/cond/branch_1_fun/attend/pallas_call | solution.py:179
  146.7 82.1 %conditional.12 = (f32[256,2048]{1,0:T(8,128)}, bf16[128,2048]{1,0:T(8,128)(2,1)}, bf16[128,2048]{1,0:T(8,128)(2,1)}, bf16[128,2048]{1,0:T(8,128)(2,1)}, bf16[12...) conditional(s32[]{:T(128)} %convert_element_type.143, ...), branch_computations={%region_4.5_spmd, %region_5.6_spmd} | conditional | flops 5242880 | bytes 49873504 | solution.py:575
  146.7 4.4 attention_out_far.1
  152.3 5.2 attention_out.1
  157.5 7.8 %collective-permute-done.19 = bf16[128,2048]{1,0:T(8,128)(2,1)S(1)} collective-permute-done((bf16[128,2048]{1,0:T(8,128)(2,1)}, bf16[128,2048]{1,0:T(8,128)(2,1)S(1)}, u32[]{:S(2)}, u32[]{:S(2)}) %collective-permute-start.19) | collective-permute-done | bytes 524320 | tf_op jit(solution)/shard_map/cond/branch_1_fun/ppermute | solution.py:579
  172.1 8.5 %collective-permute-done.21.refs_2_ = bf16[128,2048]{1,0:T(8,128)(2,1)S(1)} collective-permute-done((bf16[128,2048]{1,0:T(8,128)(2,1)}, bf16[128,2048]{1,0:T(8,128)(2,1)S(1)}, u32[]{:S(2)}, u32[]{:S(2)}) %collective-permute-start.21) | collective-permute-done | bytes 524320 | tf_op jit(solution)/shard_map/cond/branch_1_fun/ppermute | solution.py:579
  182.1 9.0 %collective-permute-done.22.refs_3_ = bf16[128,2048]{1,0:T(8,128)(2,1)S(1)} collective-permute-done((bf16[128,2048]{1,0:T(8,128)(2,1)S(1)}, bf16[128,2048]{1,0:T(8,128)(2,1)S(1)}, u32[]{:S(2)}, u32[]{:S(2)}) %collective-permute-start.22) | collective-permute-done | bytes 524320 | tf_op jit(solution)/shard_map/cond/branch_1_fun/ppermute | solution.py:579
  191.2 2.7 middle.1
  197.9 11.1 %collective-permute-done.25 = bf16[128,2048]{1,0:T(8,128)(2,1)} collective-permute-done((bf16[128,2048]{1,0:T(8,128)(2,1)}, bf16[128,2048]{1,0:T(8,128)(2,1)}, u32[]{:S(2)}, u32[]{:S(2)}) %collective-permute-start.25) | collective-permute-done | bytes 524320 | tf_op jit(solution)/shard_map/cond/branch_1_fun/ppermute | solution.py:579
  211.1 9.2 %collective-permute-done.26 = bf16[128,2048]{1,0:T(8,128)(2,1)} collective-permute-done((bf16[128,2048]{1,0:T(8,128)(2,1)}, bf16[128,2048]{1,0:T(8,128)(2,1)}, u32[]{:S(2)}, u32[]{:S(2)}) %collective-permute-start.26) | collective-permute-done | bytes 524320 | tf_op jit(solution)/shard_map/cond/branch_1_fun/ppermute | solution.py:579
  220.9 7.9 %collective-permute-done.29 = bf16[128,2048]{1,0:T(8,128)(2,1)} collective-permute-done((bf16[128,2048]{1,0:T(8,128)(2,1)}, bf16[128,2048]{1,0:T(8,128)(2,1)}, u32[]{:S(2)}, u32[]{:S(2)}) %collective-permute-start.29) | collective-permute-done | bytes 524320 | tf_op jit(solution)/shard_map/cond/branch_1_fun/ppermute | solution.py:579
  228.8 58.7 %conditional.13 = (bf16[4,512,1536]{2,1,0:T(8,128)(2,1)}, bf16[1024,2048]{1,0:T(8,128)(2,1)}, bf16[1024,2048]{1,0:T(8,128)(2,1)}, bf16[1024,2048]{1,0:T(8,128)(2...) conditional(s32[]{:T(128)} %convert_element_type.143, ...), branch_computations={%region_6.7_spmd, %region_7.8_spmd} | conditional | flops 3145728 | bytes 84083016 | solution.py:575
  229.3 16.8 %hidden_units_a.1 = (bf16[1024,2048]{1,0:T(8,128)(2,1)}, bf16[1024,2048]{1,0:T(8,128)(2,1)}, bf16[1024,1024]{1,0:T(8,128)(2,1)}, bf16[1024,512]{1,0:T(8,128)(2,1)}) custom-call(bf16[128,2048]{1,0:T(8,128)(2,1)} %get-tuple-element.298.refs_0_, bf16[128,2048]{1,0:T(8,128)(2,1)} %get-tuple-element.299.refs_1_, bf16[128,2048]{1,0:T(8,128)(2,1)} %get-tuple-element.300.refs_2_, ...), custom_call_target="tpu_custom_call" | custom-call | flops 1048576 | bytes 65536 | tf_op jit(solution)/shard_map/cond/branch_1_fun/hidden_units_a/pallas_call | solution.py:554
  246.8 13.7 %hidden_units_a_other.1 = (bf16[1024,1024]{1,0:T(8,128)(2,1)}, bf16[1024,512]{1,0:T(8,128)(2,1)}) custom-call(bf16[1024,2048]{1,0:T(8,128)(2,1)} %get-tuple-element.896.refs_0_, bf16[1024,2048]{1,0:T(8,128)(2,1)} %get-tuple-element.898.refs_1_.refs_2_, bf16[4,512,1536]{2,1,0:T(8,128)(2,1)} %collective-permute-done.6.refs_2_.refs_3_.refs_4_, ...), custom_call_target="tpu_custom_call" | custom-call | flops 1048576 | bytes 65536 | tf_op jit(solution)/shard_map/cond/branch_1_fun/hidden_units_a_other/pallas_call | solution.py:554
  261.0 5.4 collective-permute-done.10.refs_7_
  268.2 19.4 %hidden_weights_a.1 = bf16[4,512,1536]{2,1,0:T(8,128)(2,1)} custom-call(bf16[1024,2048]{1,0:T(8,128)(2,1)} %get-tuple-element.896.refs_0_, bf16[1024,2048]{1,0:T(8,128)(2,1)} %collective-permute-done.7.refs_1_, bf16[1024,2048]{1,0:T(8,128)(2,1)} %get-tuple-element.898.refs_1_.refs_2_, bf16[1024,2048]{1,0:T(8,128)(2,1)} %collective-permute-done.8.refs_3_, ...), custom_call_target="tpu_custom_call" | custom-call | flops 1048576 | bytes 65536 | tf_op jit(solution)/shard_map/cond/branch_1_fun/hidden_weights_a/pallas_call | solution.py:385
  287.6 74.8 %conditional.14 = (f32[256,2048]{1,0:T(8,128)}, bf16[128,2048]{1,0:T(8,128)(2,1)}, bf16[128,2048]{1,0:T(8,128)(2,1)}, bf16[128,2048]{1,0:T(8,128)(2,1)}, bf16[12...) conditional(s32[]{:T(128)} %convert_element_type.143, ...), branch_computations={%region_8.9_spmd, %region_9.10_spmd} | conditional | flops 7340032 | bytes 68485760 | solution.py:575
  288.3 10.1 %hidden_units_b.2 = (bf16[1024,512]{1,0:T(8,128)(2,1)}, bf16[1024,256]{1,0:T(8,128)(2,1)}) custom-call(bf16[1024,2048]{1,0:T(8,128)(2,1)} %get-tuple-element.322.refs_0_, bf16[1024,2048]{1,0:T(8,128)(2,1)} %get-tuple-element.323.refs_1_.refs_2_, bf16[4,512,768]{2,1,0:T(8,128)(2,1)} %get-tuple-element.324.refs_2_.refs_3_.refs_4_.refs_6_, ...), custom_call_target="tpu_custom_call" | custom-call | flops 1048576 | bytes 65536 | tf_op jit(solution)/shard_map/cond/branch_1_fun/hidden_units_b/pallas_call | solution.py:554
  298.4 8.9 %hidden_units_b.3 = (bf16[1024,512]{1,0:T(8,128)(2,1)}, bf16[1024,256]{1,0:T(8,128)(2,1)S(1)}) custom-call(bf16[1024,2048]{1,0:T(8,128)(2,1)} %get-tuple-element.322.refs_0_, bf16[1024,2048]{1,0:T(8,128)(2,1)} %get-tuple-element.323.refs_1_.refs_2_, bf16[4,512,768]{2,1,0:T(8,128)(2,1)} %collective-permute-done.31.refs_2_.refs_3_.refs_4_.refs_7_, ...), custom_call_target="tpu_custom_call" | custom-call | flops 1048576 | bytes 65536 | tf_op jit(solution)/shard_map/cond/branch_1_fun/hidden_units_b/pallas_call | solution.py:554
  307.3 9.6 %normed_mid_grad_far.1 = (bf16[128,2048]{1,0:T(8,128)(2,1)}, bf16[128,2048]{1,0:T(8,128)(2,1)}) custom-call(bf16[1024,1024]{1,0:T(8,128)(2,1)} %get-tuple-element.320.refs_0_, bf16[1024,1024]{1,0:T(8,128)(2,1)} %get-tuple-element.321.refs_1_, bf16[1024,512]{1,0:T(8,128)(2,1)} %get-tuple-element.342.refs_2_.refs_4_, ...), custom_call_target="tpu_custom_call" | custom-call | flops 1048576 | bytes 65536 | tf_op jit(solution)/shard_map/cond/branch_1_fun/normed_mid_grad_far/pallas_call | solution.py:223
  318.4 14.9 %normed_mid_grad.1 = (f32[256,2048]{1,0:T(8,128)}, bf16[128,2048]{1,0:T(8,128)(2,1)}, bf16[128,2048]{1,0:T(8,128)(2,1)}, bf16[128,2048]{1,0:T(8,128)(2,1)}, bf16[128,2048]{1,0:T(8,128)(2,1)}) custom-call(bf16[1024,1024]{1,0:T(8,128)(2,1)} %get-tuple-element.320.refs_0_, bf16[1024,1024]{1,0:T(8,128)(2,1)} %get-tuple-element.321.refs_1_, ...), custom_call_target="tpu_custom_call" | custom-call | flops 1048576 | bytes 65536 | tf_op jit(solution)/shard_map/cond/branch_1_fun/normed_mid_grad/pallas_call | solution.py:223
  337.1 2.1 collective-permute-start.35
  340.3 2.3 copy.159
  342.6 12.8 %hidden_weights_b.1 = bf16[4,512,768]{2,1,0:T(8,128)(2,1)} custom-call(bf16[1024,2048]{1,0:T(8,128)(2,1)} %get-tuple-element.322.refs_0_, bf16[1024,2048]{1,0:T(8,128)(2,1)} %get-tuple-element.338.refs_1_, bf16[1024,2048]{1,0:T(8,128)(2,1)} %get-tuple-element.323.refs_1_.refs_2_, bf16[1024,2048]{1,0:T(8,128)(2,1)} %get-tuple-element.339.refs_3_, ...), custom_call_target="tpu_custom_call" | custom-call | flops 1048576 | bytes 65536 | tf_op jit(solution)/shard_map/cond/branch_1_fun/hidden_weights_b/pallas_call | solution.py:385
  355.3 4.7 collective-permute-done.34
  360.1 2.4 collective-permute-done.37
  362.5 43.1 %conditional.15 = (f32[256,2048]{1,0:T(8,128)}, bf16[128,2048]{1,0:T(8,128)(2,1)}, bf16[128,2048]{1,0:T(8,128)(2,1)}, bf16[128,2048]{1,0:T(8,128)(2,1)}, bf16[12...) conditional(s32[]{:T(128)} %convert_element_type.143, ...), branch_computations={%region_10.11_spmd, %region_11.12_spmd} | conditional | flops 2097152 | bytes 37880180 | solution.py:575
  362.8 6.3 %middle_grad.1 = (f32[256,2048]{1,0:T(8,128)}, bf16[128,2048]{1,0:T(8,128)(2,1)}, bf16[128,2048]{1,0:T(8,128)(2,1)}) custom-call(f32[256,2048]{1,0:T(8,128)} %get-tuple-element.348.refs_0_, f32[256,2048]{1,0:T(8,128)} %get-tuple-element.349.refs_1_, bf16[128,2048]{1,0:T(8,128)(2,1)} %get-tuple-element.350.refs_2_, ...), custom_call_target="tpu_custom_call" | custom-call | flops 1048576 | bytes 65536 | tf_op jit(solution)/shard_map/cond/branch_1_fun/middle_grad/pallas_call | solution.py:306
  373.1 10.5 %hidden_out.1 = (f32[256,2048]{1,0:T(8,128)}, bf16[256,2048]{1,0:T(8,128)(2,1)}, bf16[256,2048]{1,0:T(8,128)(2,1)}, bf16[256,2048]{1,0:T(8,128)(2,1)}) custom-call(bf16[1024,512]{1,0:T(8,128)(2,1)} %get-tuple-element.359.refs_0_, bf16[1024,512]{1,0:T(8,128)(2,1)} %get-tuple-element.360.refs_1_, bf16[1024,256]{1,0:T(8,128)(2,1)} %get-tuple-element.361.refs_2_, ...), custom_call_target="tpu_custom_call" | custom-call | flops 1048576 | bytes 65536 | tf_op jit(solution)/shard_map/cond/branch_1_fun/hidden_out/pallas_call | solution.py:223
  388.0 7.5 %collective-permute-done.12 = bf16[128,2048]{1,0:T(8,128)(2,1)} collective-permute-done((bf16[128,2048]{1,0:T(8,128)(2,1)}, bf16[128,2048]{1,0:T(8,128)(2,1)}, u32[]{:S(2)}, u32[]{:S(2)}) %collective-permute-start.12) | collective-permute-done | bytes 524320 | tf_op jit(solution)/shard_map/cond/branch_1_fun/ppermute | solution.py:579
  396.5 9.1 %collective-permute-done.15 = bf16[128,2048]{1,0:T(8,128)(2,1)} collective-permute-done((bf16[128,2048]{1,0:T(8,128)(2,1)}, bf16[128,2048]{1,0:T(8,128)(2,1)}, u32[]{:S(2)}, u32[]{:S(2)}) %collective-permute-start.15) | collective-permute-done | bytes 524320 | tf_op jit(solution)/shard_map/cond/branch_1_fun/ppermute | solution.py:579
  409.1 32.6 %conditional.16 = (bf16[1024,2048]{1,0:T(8,128)(2,1)}, bf16[1024,2048]{1,0:T(8,128)(2,1)}, bf16[4,256,512]{2,1,0:T(8,128)(2,1)}, bf16[4,256,512]{2,1,0:T(8,128)(2,1)}, f32[8,128]{1,0:T(8,128)S(1)}) conditional(s32[]{:T(128)} %convert_element_type.143, () %tuple.122, (bf16[128,2048]{1,0:T(8,128)(2,1)}, bf16[128,2048]{1,0:T(8,128)(2,1)}, ...), branch_computations={%region_12.13_spmd, %region_13.14_spmd} | conditional | flops 3145728 | bytes 25378992 | solution.py:575
  409.1 5.8 %attended_grad.2 = (bf16[1024,2048]{1,0:T(8,128)(2,1)}, bf16[1024,256]{1,0:T(8,128)(2,1)}) custom-call(bf16[128,2048]{1,0:T(8,128)(2,1)} %get-tuple-element.373.refs_0_, bf16[128,2048]{1,0:T(8,128)(2,1)} %get-tuple-element.374.refs_1_, bf16[128,2048]{1,0:T(8,128)(2,1)} %get-tuple-element.375.refs_2_, bf16[128,2048]{1,0:T(8,128)(2,1)} %get-tuple-element.376.refs_3_, ...), custom_call_target="tpu_custom_call" | custom-call | flops 1048576 | bytes 65536 | tf_op jit(solution)/shard_map/cond/branch_1_fun/attended_grad/pallas_call | solution.py:342
  415.8 4.7 attended_grad.3
  423.6 18.1 %attend_back.1 = (bf16[4,256,512]{2,1,0:T(8,128)(2,1)}, bf16[4,256,512]{2,1,0:T(8,128)(2,1)}, f32[8,128]{1,0:T(8,128)S(1)}) custom-call(s32[1]{0:T(128)} %bitcast.8.core_ref, f32[4,256,512]{2,1,0:T(8,128)} %get-tuple-element.384.refs_0_, f32[4,256,512]{2,1,0:T(8,128)} %get-tuple-element.385.refs_1_, bf16[4,256,256]{2,1,0:T(8,128)(2,1)S(1)} %bitcast.89, ...), custom_call_target="tpu_custom_call" | custom-call | flops 1048576 | bytes 65536 | tf_op jit(solution)/shard_map/cond/branch_1_fun/attend_back/pallas_call | solution.py:179
  441.7 13.8 %conditional.17 = (bf16[4,528,768]{2,1,0:T(8,128)(2,1)}, bf16[1024,512]{1,0:T(8,128)(2,1)}, bf16[1024,512]{1,0:T(8,128)(2,1)}) conditional(s32[]{:T(128)} %convert_element_type.143, () %tuple.121, (bf16[4,256,512]{2,1,0:T(8,128)(2,1)}, bf16[4,256,512]{2,1,0:T(8,128)(2,1)}, bf16[4,256,256]{2,1,0:T(8,128)(2,1)S(1)}, bf16[4,256,256]{2,1,0:T(8,128)(2,1)}, ...), branch_computations={%region_14.15_spmd, %region_15.16_spmd} | conditional | flops 1049600 | bytes 5341214 | solution.py:575
  443.1 12.4 %attention_weights.1 = bf16[4,528,768]{2,1,0:T(8,128)(2,1)} custom-call(bf16[1024,2048]{1,0:T(8,128)(2,1)} %get-tuple-element.396.refs_0_, bf16[1024,2048]{1,0:T(8,128)(2,1)} %get-tuple-element.397.refs_1_, bf16[1024,2048]{1,0:T(8,128)(2,1)} %get-tuple-element.398.refs_2_, bf16[1024,2048]{1,0:T(8,128)(2,1)} %get-tuple-element.399.refs_3_, ...), custom_call_target="tpu_custom_call" | custom-call | flops 1048576 | bytes 65536 | tf_op jit(solution)/shard_map/cond/branch_1_fun/attention_weights/pallas_call | solution.py:385
  457.4 59.1 %conditional.18 = (f32[256,2048]{1,0:T(8,128)}, bf16[128,2048]{1,0:T(8,128)(2,1)}, bf16[128,2048]{1,0:T(8,128)(2,1)}, bf16[128,2048]{1,0:T(8,128)(2,1)}, bf16[12...) conditional(s32[]{:T(128)} %convert_element_type.143, ...), branch_computations={%region_17.18_spmd, %region_18.19_spmd} | conditional | flops 4194322 | bytes 23724684 | solution.py:575
  457.4 4.6 normed_in_grad_far.1
  464.6 2.2 dynamic-slice_bitcast_fusion
  468.3 6.9 %normed_in_grad.1 = (f32[256,2048]{1,0:T(8,128)}, bf16[128,2048]{1,0:T(8,128)(2,1)}, bf16[128,2048]{1,0:T(8,128)(2,1)}, bf16[128,2048]{1,0:T(8,128)(2,1)}, bf16[128,2048]{1,0:T(8,128)(2,1)}) custom-call(bf16[1024,512]{1,0:T(8,128)(2,1)} %get-tuple-element.405.refs_0_, bf16[1024,512]{1,0:T(8,128)(2,1)} %get-tuple-element.406.refs_1_, ...), custom_call_target="tpu_custom_call" | custom-call | flops 1048576 | bytes 65536 | tf_op jit(solution)/shard_map/cond/branch_1_fun/normed_in_grad/pallas_call | solution.py:223
  488.5 28.1 %collective-permute-done.49 = bf16[128,1536]{1,0:T(8,128)(2,1)} collective-permute-done((bf16[128,1536]{1,0:T(8,128)(2,1)S(1)}, bf16[128,1536]{1,0:T(8,128)(2,1)}, u32[]{:S(2)}, u32[]{:S(2)}) %collective-permute-start.49) | collective-permute-done | bytes 393248 | tf_op jit(solution)/shard_map/cond/branch_1_fun/ppermute | solution.py:579
  516.6 18.8 %conditional.19 = (bf16[256,2048]{1,0:T(8,128)(2,1)}, f32[256,2048]{1,0:T(8,128)}, f32[128,3072]{1,0:T(8,128)}, f32[128,3072]{1,0:T(8,128)}, f32[3072,128]{1,0:T(8,128)}, /*index=5*/f32[128]{0:T(128)S(1)}) conditional(s32[]{:T(128)} %convert_element_type.143, () %tuple.103, (f32[256,2048]{1,0:T(8,128)}, f32[256,2048]{1,0:T(8,128)}, ...), branch_computations={%region_20.21_spmd, %region_21.22_spmd} | conditional | flops 3145746 | bytes 14681816 | solution.py:575
  521.5 4.3 hidden_out_sum.1
  525.8 5.3 grad_in.1
  531.2 4.1 hidden_owned.1
  541.1 4.7 collective-permute-done.72.refs_1_
  545.8 3.0 collective-permute-done.73.refs_2_
  550.4 2.5 psum.7
  (316 shorter events, 122.8 us)
Async XLA Ops:
  7.2 88.4 %all-gather.7.cloned.1.call-start = ((), (), s32[]{:S(2)}) async-start(), calls=%async_computation.6 | async-start | bytes 4055040 | tf_op jit(solution)/shard_map/all_gather | solution.py:710
  29.3 199.6 %all-gather.9.cloned.1.call-start = ((), (), s32[]{:S(2)}) async-start(), calls=%async_computation.7 | async-start | bytes 7864320 | tf_op jit(solution)/shard_map/all_gather | solution.py:710
  31.1 14.9 %collective-permute-start.56 = (bf16[128,2048]{1,0:T(8,128)(2,1)S(1)}, bf16[128,2048]{1,0:T(8,128)(2,1)S(1)}, u32[]{:S(2)}, u32[]{:S(2)}) collective-permute-start(bf16[128,2048]{1,0:T(8,128)(2,1)S(1)} %get-tuple-element.605), channel_id=1, source_target_pairs={{0,2},{2,0},{4,6},{6,4},{1,3},{3,1},{5,7},{7,5},{8,10},{10,8},{12,... | collective-permute-start | bytes 1572872 | tf_op jit(solution)/shard_map/ppermute | solution.py:579
  32.3 22.6 %collective-permute-start.58 = (bf16[128,2048]{1,0:T(8,128)(2,1)S(1)}, bf16[128,2048]{1,0:T(8,128)(2,1)S(1)}, u32[]{:S(2)}, u32[]{:S(2)}) collective-permute-start(bf16[128,2048]{1,0:T(8,128)(2,1)S(1)} %get-tuple-element.605), channel_id=1, source_target_pairs={{0,4},{2,6},{4,0},{6,2},{1,5},{3,7},{5,1},{7,3},{8,12},{10,14},{12... | collective-permute-start | bytes 1572872 | tf_op jit(solution)/shard_map/ppermute | solution.py:579
  33.2 21.7 %collective-permute-start.57 = (bf16[128,2048]{1,0:T(8,128)(2,1)S(1)}, bf16[128,2048]{1,0:T(8,128)(2,1)S(1)}, u32[]{:S(2)}, u32[]{:S(2)}) collective-permute-start(bf16[128,2048]{1,0:T(8,128)(2,1)S(1)} %get-tuple-element.606), channel_id=1, source_target_pairs={{0,2},{2,0},{4,6},{6,4},{1,3},{3,1},{5,7},{7,5},{8,10},{10,8},{12,... | collective-permute-start | bytes 1572872 | tf_op jit(solution)/shard_map/ppermute | solution.py:579
  34.7 21.4 %collective-permute-start.59 = (bf16[128,2048]{1,0:T(8,128)(2,1)S(1)}, bf16[128,2048]{1,0:T(8,128)(2,1)S(1)}, u32[]{:S(2)}, u32[]{:S(2)}) collective-permute-start(bf16[128,2048]{1,0:T(8,128)(2,1)S(1)} %get-tuple-element.606), channel_id=1, source_target_pairs={{0,4},{2,6},{4,0},{6,2},{1,5},{3,7},{5,1},{7,3},{8,12},{10,14},{12... | collective-permute-start | bytes 1572872 | tf_op jit(solution)/shard_map/ppermute | solution.py:579
  56.4 16.3 %collective-permute-start.60 = (bf16[128,2304]{1,0:T(8,128)(2,1)S(1)}, bf16[128,2304]{1,0:T(8,128)(2,1)S(1)}, u32[]{:S(2)}, u32[]{:S(2)}) collective-permute-start(bf16[128,2304]{1,0:T(8,128)(2,1)S(1)} %get-tuple-element.773), channel_id=1, source_target_pairs={{0,2},{2,0},{4,6},{6,4},{1,3},{3,1},{5,7},{7,5},{8,10},{10,8},{12,... | collective-permute-start | bytes 1769480 | tf_op jit(solution)/shard_map/ppermute | solution.py:579
  57.8 28.9 %collective-permute-start.61 = (bf16[128,2304]{1,0:T(8,128)(2,1)S(1)}, bf16[128,2304]{1,0:T(8,128)(2,1)S(1)}, u32[]{:S(2)}, u32[]{:S(2)}) collective-permute-start(bf16[128,2304]{1,0:T(8,128)(2,1)S(1)} %get-tuple-element.772), channel_id=1, source_target_pairs={{0,4},{2,6},{4,0},{6,2},{1,5},{3,7},{5,1},{7,3},{8,12},{10,14},{12... | collective-permute-start | bytes 1769480 | tf_op jit(solution)/shard_map/ppermute | solution.py:579
  58.3 28.4 %collective-permute-start.62 = (bf16[128,2304]{1,0:T(8,128)(2,1)S(1)}, bf16[128,2304]{1,0:T(8,128)(2,1)S(1)}, u32[]{:S(2)}, u32[]{:S(2)}) collective-permute-start(bf16[128,2304]{1,0:T(8,128)(2,1)S(1)} %get-tuple-element.771), channel_id=1, source_target_pairs={{0,6},{2,4},{4,2},{6,0},{1,7},{3,5},{5,3},{7,1},{8,14},{10,12},{12... | collective-permute-start | bytes 1769480 | tf_op jit(solution)/shard_map/ppermute | solution.py:579
  60.0 34.7 %collective-permute-start.63 = (bf16[128,2048]{1,0:T(8,128)(2,1)S(1)}, bf16[128,2048]{1,0:T(8,128)(2,1)S(1)}, u32[]{:S(2)}, u32[]{:S(2)}) collective-permute-start(bf16[128,2048]{1,0:T(8,128)(2,1)S(1)} %collective-permute-done.56), channel_id=1, source_target_pairs={{0,4},{2,6},{4,0},{6,2},{1,5},{3,7},{5,1},{7,3},{8,12},{10,14},{12... | collective-permute-start | bytes 1572872 | tf_op jit(solution)/shard_map/ppermute | solution.py:579
  60.7 34.9 %collective-permute-start.64 = (bf16[128,2048]{1,0:T(8,128)(2,1)S(1)}, bf16[128,2048]{1,0:T(8,128)(2,1)}, u32[]{:S(2)}, u32[]{:S(2)}) collective-permute-start(bf16[128,2048]{1,0:T(8,128)(2,1)S(1)} %collective-permute-done.59), channel_id=1, source_target_pairs={{0,2},{2,0},{4,6},{6,4},{1,3},{3,1},{5,7},{7,5},{8,10},{10,8},{12,... | collective-permute-start | bytes 1572872 | tf_op jit(solution)/shard_map/ppermute | solution.py:579
  95.6 192.0 %all-gather.11.cloned.1.call-start = ((), (), s32[]{:S(2)}) async-start(), calls=%async_computation.8 | async-start | bytes 3932160 | tf_op jit(solution)/shard_map/all_gather | solution.py:710
  96.3 359.3 %reduce-scatter.4.cloned.1.call-start = ((), (), s32[]{:S(2)}) async-start(), calls=%async_computation.3 | async-start | bytes 7864320 | tf_op jit(solution)/shard_map/reduce_scatter | solution.py:809
  102.1 22.9 %collective-permute-start.65 = (bf16[128,2048]{1,0:T(8,128)(2,1)}, bf16[128,2048]{1,0:T(8,128)(2,1)}, u32[]{:S(2)}, u32[]{:S(2)}) collective-permute-start(bf16[128,2048]{1,0:T(8,128)(2,1)} %get-tuple-element.636), channel_id=1, source_target_pairs={{0,2},{2,0},{4,6},{6,4},{1,3},{3,1},{5,7},{7,5},{8,10},{10,8},{12,... | collective-permute-start | bytes 1572872 | tf_op jit(solution)/shard_map/ppermute | solution.py:579
  102.9 23.7 %collective-permute-start.67 = (bf16[128,2048]{1,0:T(8,128)(2,1)}, bf16[128,2048]{1,0:T(8,128)(2,1)}, u32[]{:S(2)}, u32[]{:S(2)}) collective-permute-start(bf16[128,2048]{1,0:T(8,128)(2,1)} %get-tuple-element.636), channel_id=1, source_target_pairs={{0,4},{2,6},{4,0},{6,2},{1,5},{3,7},{5,1},{7,3},{8,12},{10,14},{12... | collective-permute-start | bytes 1572872 | tf_op jit(solution)/shard_map/ppermute | solution.py:579
  104.4 22.2 %collective-permute-start.66 = (bf16[128,2048]{1,0:T(8,128)(2,1)}, bf16[128,2048]{1,0:T(8,128)(2,1)}, u32[]{:S(2)}, u32[]{:S(2)}) collective-permute-start(bf16[128,2048]{1,0:T(8,128)(2,1)} %get-tuple-element.637), channel_id=1, source_target_pairs={{0,2},{2,0},{4,6},{6,4},{1,3},{3,1},{5,7},{7,5},{8,10},{10,8},{12,... | collective-permute-start | bytes 1572872 | tf_op jit(solution)/shard_map/ppermute | solution.py:579
  105.0 22.9 %collective-permute-start.68 = (bf16[128,2048]{1,0:T(8,128)(2,1)}, bf16[128,2048]{1,0:T(8,128)(2,1)}, u32[]{:S(2)}, u32[]{:S(2)}) collective-permute-start(bf16[128,2048]{1,0:T(8,128)(2,1)} %get-tuple-element.637), channel_id=1, source_target_pairs={{0,4},{2,6},{4,0},{6,2},{1,5},{3,7},{5,1},{7,3},{8,12},{10,14},{12... | collective-permute-start | bytes 1572872 | tf_op jit(solution)/shard_map/ppermute | solution.py:579
  127.8 18.1 %collective-permute-start.2 = (bf16[1024,2048]{1,0:T(8,128)(2,1)}, bf16[1024,2048]{1,0:T(8,128)(2,1)}, u32[]{:S(2)}, u32[]{:S(2)}) collective-permute-start(bf16[1024,2048]{1,0:T(8,128)(2,1)} %get-tuple-element.262), channel_id=1, source_target_pairs={{0,1},{1,0},{2,3},{3,2},{4,5},{5,4},{6,7},{7,6},{8,9},{9,8},{10,11... | collective-permute-start | bytes 12582920 | tf_op jit(solution)/shard_map/cond/branch_1_fun/ppermute | solution.py:579
  127.8 14.7 %collective-permute-start.3 = (bf16[128,2048]{1,0:T(8,128)(2,1)}, bf16[128,2048]{1,0:T(8,128)(2,1)}, u32[]{:S(2)}, u32[]{:S(2)}) collective-permute-start(bf16[128,2048]{1,0:T(8,128)(2,1)} %get-tuple-element.273), channel_id=1, source_target_pairs={{0,4},{2,6},{4,0},{6,2},{1,5},{3,7},{5,1},{7,3},{8,12},{10,14},{12... | collective-permute-start | bytes 1572872 | tf_op jit(solution)/shard_map/cond/branch_1_fun/ppermute | solution.py:579
  129.3 14.4 %collective-permute-start.4 = (bf16[128,2048]{1,0:T(8,128)(2,1)}, bf16[128,2048]{1,0:T(8,128)(2,1)}, u32[]{:S(2)}, u32[]{:S(2)}) collective-permute-start(bf16[128,2048]{1,0:T(8,128)(2,1)} %get-tuple-element.274), channel_id=1, source_target_pairs={{0,2},{2,0},{4,6},{6,4},{1,3},{3,1},{5,7},{7,5},{8,10},{10,8},{12,... | collective-permute-start | bytes 1572872 | tf_op jit(solution)/shard_map/cond/branch_1_fun/ppermute | solution.py:579
  151.1 14.2 %collective-permute-start.19 = (bf16[128,2048]{1,0:T(8,128)(2,1)}, bf16[128,2048]{1,0:T(8,128)(2,1)S(1)}, u32[]{:S(2)}, u32[]{:S(2)}) collective-permute-start(bf16[128,2048]{1,0:T(8,128)(2,1)} %get-tuple-element.287), channel_id=1, source_target_pairs={{0,2},{2,0},{4,6},{6,4},{1,3},{3,1},{5,7},{7,5},{8,10},{10,8},{12,... | collective-permute-start | bytes 1572872 | tf_op jit(solution)/shard_map/cond/branch_1_fun/ppermute | solution.py:579
  151.7 13.9 %collective-permute-start.20 = (bf16[128,2048]{1,0:T(8,128)(2,1)}, bf16[128,2048]{1,0:T(8,128)(2,1)S(1)}, u32[]{:S(2)}, u32[]{:S(2)}) collective-permute-start(bf16[128,2048]{1,0:T(8,128)(2,1)} %get-tuple-element.288), channel_id=1, source_target_pairs={{0,4},{2,6},{4,0},{6,2},{1,5},{3,7},{5,1},{7,3},{8,12},{10,14},{12... | collective-permute-start | bytes 1572872 | tf_op jit(solution)/shard_map/cond/branch_1_fun/ppermute | solution.py:579
  165.6 15.1 %collective-permute-start.21 = (bf16[128,2048]{1,0:T(8,128)(2,1)}, bf16[128,2048]{1,0:T(8,128)(2,1)S(1)}, u32[]{:S(2)}, u32[]{:S(2)}) collective-permute-start(bf16[128,2048]{1,0:T(8,128)(2,1)} %get-tuple-element.289), channel_id=1, source_target_pairs={{0,2},{2,0},{4,6},{6,4},{1,3},{3,1},{5,7},{7,5},{8,10},{10,8},{12,... | collective-permute-start | bytes 1572872 | tf_op jit(solution)/shard_map/cond/branch_1_fun/ppermute | solution.py:579
  167.1 15.1 %collective-permute-start.24 = (bf16[128,2048]{1,0:T(8,128)(2,1)}, bf16[128,2048]{1,0:T(8,128)(2,1)S(1)}, u32[]{:S(2)}, u32[]{:S(2)}) collective-permute-start(bf16[128,2048]{1,0:T(8,128)(2,1)} %get-tuple-element.292), channel_id=1, source_target_pairs={{0,4},{2,6},{4,0},{6,2},{1,5},{3,7},{5,1},{7,3},{8,12},{10,14},{12... | collective-permute-start | bytes 1572872 | tf_op jit(solution)/shard_map/cond/branch_1_fun/ppermute | solution.py:579
  168.8 22.4 %collective-permute-start.22 = (bf16[128,2048]{1,0:T(8,128)(2,1)S(1)}, bf16[128,2048]{1,0:T(8,128)(2,1)S(1)}, u32[]{:S(2)}, u32[]{:S(2)}) collective-permute-start(bf16[128,2048]{1,0:T(8,128)(2,1)S(1)} %add_convert_fusion.1), channel_id=1, source_target_pairs={{0,4},{2,6},{4,0},{6,2},{1,5},{3,7},{5,1},{7,3},{8,12},{10,14},{12... | collective-permute-start | bytes 1572872 | tf_op jit(solution)/shard_map/cond/branch_1_fun/ppermute | solution.py:579
  171.5 19.6 %collective-permute-start.23 = (bf16[128,2048]{1,0:T(8,128)(2,1)S(1)}, bf16[128,2048]{1,0:T(8,128)(2,1)S(1)}, u32[]{:S(2)}, u32[]{:S(2)}) collective-permute-start(bf16[128,2048]{1,0:T(8,128)(2,1)S(1)} %add_convert_fusion), channel_id=1, source_target_pairs={{0,2},{2,0},{4,6},{6,4},{1,3},{3,1},{5,7},{7,5},{8,10},{10,8},{12,... | collective-permute-start | bytes 1572872 | tf_op jit(solution)/shard_map/cond/branch_1_fun/ppermute | solution.py:579
  193.9 15.2 %collective-permute-start.25 = (bf16[128,2048]{1,0:T(8,128)(2,1)}, bf16[128,2048]{1,0:T(8,128)(2,1)}, u32[]{:S(2)}, u32[]{:S(2)}) collective-permute-start(bf16[128,2048]{1,0:T(8,128)(2,1)} %get-tuple-element.877), channel_id=1, source_target_pairs={{0,2},{2,0},{4,6},{6,4},{1,3},{3,1},{5,7},{7,5},{8,10},{10,8},{12,... | collective-permute-start | bytes 1572872 | tf_op jit(solution)/shard_map/cond/branch_1_fun/ppermute | solution.py:579
  194.5 15.2 %collective-permute-start.28 = (bf16[128,2048]{1,0:T(8,128)(2,1)}, bf16[128,2048]{1,0:T(8,128)(2,1)}, u32[]{:S(2)}, u32[]{:S(2)}) collective-permute-start(bf16[128,2048]{1,0:T(8,128)(2,1)} %get-tuple-element.878), channel_id=1, source_target_pairs={{0,4},{2,6},{4,0},{6,2},{1,5},{3,7},{5,1},{7,3},{8,12},{10,14},{12... | collective-permute-start | bytes 1572872 | tf_op jit(solution)/shard_map/cond/branch_1_fun/ppermute | solution.py:579
  195.0 25.2 %collective-permute-start.26 = (bf16[128,2048]{1,0:T(8,128)(2,1)}, bf16[128,2048]{1,0:T(8,128)(2,1)}, u32[]{:S(2)}, u32[]{:S(2)}) collective-permute-start(bf16[128,2048]{1,0:T(8,128)(2,1)} %get-tuple-element.878), channel_id=1, source_target_pairs={{0,2},{2,0},{4,6},{6,4},{1,3},{3,1},{5,7},{7,5},{8,10},{10,8},{12,... | collective-permute-start | bytes 1572872 | tf_op jit(solution)/shard_map/cond/branch_1_fun/ppermute | solution.py:579
  196.5 24.4 %collective-permute-start.27 = (bf16[128,2048]{1,0:T(8,128)(2,1)}, bf16[128,2048]{1,0:T(8,128)(2,1)}, u32[]{:S(2)}, u32[]{:S(2)}) collective-permute-start(bf16[128,2048]{1,0:T(8,128)(2,1)} %get-tuple-element.877), channel_id=1, source_target_pairs={{0,4},{2,6},{4,0},{6,2},{1,5},{3,7},{5,1},{7,3},{8,12},{10,14},{12... | collective-permute-start | bytes 1572872 | tf_op jit(solution)/shard_map/cond/branch_1_fun/ppermute | solution.py:579
  209.0 19.8 %collective-permute-start.29 = (bf16[128,2048]{1,0:T(8,128)(2,1)}, bf16[128,2048]{1,0:T(8,128)(2,1)}, u32[]{:S(2)}, u32[]{:S(2)}) collective-permute-start(bf16[128,2048]{1,0:T(8,128)(2,1)} %collective-permute-done.25), channel_id=1, source_target_pairs={{0,4},{2,6},{4,0},{6,2},{1,5},{3,7},{5,1},{7,3},{8,12},{10,14},{12... | collective-permute-start | bytes 1572872 | tf_op jit(solution)/shard_map/cond/branch_1_fun/ppermute | solution.py:579
  209.6 19.2 %collective-permute-start.30 = (bf16[128,2048]{1,0:T(8,128)(2,1)}, bf16[128,2048]{1,0:T(8,128)(2,1)}, u32[]{:S(2)}, u32[]{:S(2)}) collective-permute-start(bf16[128,2048]{1,0:T(8,128)(2,1)} %collective-permute-done.28), channel_id=1, source_target_pairs={{0,2},{2,0},{4,6},{6,4},{1,3},{3,1},{5,7},{7,5},{8,10},{10,8},{12,... | collective-permute-start | bytes 1572872 | tf_op jit(solution)/shard_map/cond/branch_1_fun/ppermute | solution.py:579
  229.2 17.5 %collective-permute-start.6 = (bf16[4,512,1536]{2,1,0:T(8,128)(2,1)}, bf16[4,512,1536]{2,1,0:T(8,128)(2,1)}, u32[]{:S(2)}, u32[]{:S(2)}) collective-permute-start(bf16[4,512,1536]{2,1,0:T(8,128)(2,1)} %get-tuple-element.297.refs_16_.refs_17_.refs_18_), channel_id=1, source_target_pairs={{0,1},{1,0},{2,3},{3,2},{4,5},{5,4},{6,7},{7,6},{8,9},{9,8},{10,11... | collective-permute-start | bytes 18874376 | tf_op jit(solution)/shard_map/cond/branch_1_fun/ppermute | solution.py:579
  246.2 14.9 %collective-permute-start.7 = (bf16[1024,2048]{1,0:T(8,128)(2,1)}, bf16[1024,2048]{1,0:T(8,128)(2,1)}, u32[]{:S(2)}, u32[]{:S(2)}) collective-permute-start(bf16[1024,2048]{1,0:T(8,128)(2,1)} %get-tuple-element.896.refs_0_), channel_id=1, source_target_pairs={{0,1},{1,0},{2,3},{3,2},{4,5},{5,4},{6,7},{7,6},{8,9},{9,8},{10,11... | collective-permute-start | bytes 12582920 | tf_op jit(solution)/shard_map/cond/branch_1_fun/ppermute | solution.py:579
  246.7 14.3 %collective-permute-start.8 = (bf16[1024,2048]{1,0:T(8,128)(2,1)}, bf16[1024,2048]{1,0:T(8,128)(2,1)}, u32[]{:S(2)}, u32[]{:S(2)}) collective-permute-start(bf16[1024,2048]{1,0:T(8,128)(2,1)} %get-tuple-element.898.refs_1_.refs_2_), channel_id=1, source_target_pairs={{0,1},{1,0},{2,3},{3,2},{4,5},{5,4},{6,7},{7,6},{8,9},{9,8},{10,11... | collective-permute-start | bytes 12582920 | tf_op jit(solution)/shard_map/cond/branch_1_fun/ppermute | solution.py:579
  287.6 229.0 %reduce-scatter.6.cloned.1.call-start = ((), (), s32[]{:S(2)}) async-start(), calls=%async_computation.4 | async-start | bytes 3932160 | tf_op jit(solution)/shard_map/reduce_scatter | solution.py:809
  316.9 16.5 %collective-permute-start.33 = (bf16[128,2048]{1,0:T(8,128)(2,1)}, bf16[128,2048]{1,0:T(8,128)(2,1)}, u32[]{:S(2)}, u32[]{:S(2)}) collective-permute-start(bf16[128,2048]{1,0:T(8,128)(2,1)} %get-tuple-element.333), channel_id=1, source_target_pairs={{0,4},{2,6},{4,0},{6,2},{1,5},{3,7},{5,1},{7,3},{8,12},{10,14},{12... | collective-permute-start | bytes 1572872 | tf_op jit(solution)/shard_map/cond/branch_1_fun/ppermute | solution.py:579
  316.9 18.9 %collective-permute-start.32 = (bf16[128,2048]{1,0:T(8,128)(2,1)}, bf16[128,2048]{1,0:T(8,128)(2,1)}, u32[]{:S(2)}, u32[]{:S(2)}) collective-permute-start(bf16[128,2048]{1,0:T(8,128)(2,1)} %get-tuple-element.332), channel_id=1, source_target_pairs={{0,2},{2,0},{4,6},{6,4},{1,3},{3,1},{5,7},{7,5},{8,10},{10,8},{12,... | collective-permute-start | bytes 1572872 | tf_op jit(solution)/shard_map/cond/branch_1_fun/ppermute | solution.py:579
  317.9 24.7 %collective-permute-start.38 = (bf16[1024,512]{1,0:T(8,128)(2,1)S(1)}, bf16[1024,512]{1,0:T(8,128)(2,1)}, u32[]{:S(2)}, u32[]{:S(2)}) collective-permute-start(bf16[1024,512]{1,0:T(8,128)(2,1)S(1)} %copy-done.14), channel_id=1, source_target_pairs={{0,1},{1,0},{2,3},{3,2},{4,5},{5,4},{6,7},{7,6},{8,9},{9,8},{10,11... | collective-permute-start | bytes 3145736 | tf_op jit(solution)/shard_map/cond/branch_1_fun/ppermute | solution.py:579
  317.9 22.3 %collective-permute-start.39 = (bf16[1024,256]{1,0:T(8,128)(2,1)S(1)}, bf16[1024,256]{1,0:T(8,128)(2,1)}, u32[]{:S(2)}, u32[]{:S(2)}) collective-permute-start(bf16[1024,256]{1,0:T(8,128)(2,1)S(1)} %get-tuple-element.925), channel_id=1, source_target_pairs={{0,1},{1,0},{2,3},{3,2},{4,5},{5,4},{6,7},{7,6},{8,9},{9,8},{10,11... | collective-permute-start | bytes 1572872 | tf_op jit(solution)/shard_map/cond/branch_1_fun/ppermute | solution.py:579
  334.7 20.6 %collective-permute-start.36 = (bf16[128,2048]{1,0:T(8,128)(2,1)S(1)}, bf16[128,2048]{1,0:T(8,128)(2,1)}, u32[]{:S(2)}, u32[]{:S(2)}) collective-permute-start(bf16[128,2048]{1,0:T(8,128)(2,1)S(1)} %add_convert_fusion.2), channel_id=1, source_target_pairs={{0,2},{2,0},{4,6},{6,4},{1,3},{3,1},{5,7},{7,5},{8,10},{10,8},{12,... | collective-permute-start | bytes 1572872 | tf_op jit(solution)/shard_map/cond/branch_1_fun/ppermute | solution.py:579
  337.1 18.2 %collective-permute-start.35 = (bf16[128,2048]{1,0:T(8,128)(2,1)S(1)}, bf16[128,2048]{1,0:T(8,128)(2,1)}, u32[]{:S(2)}, u32[]{:S(2)}) collective-permute-start(bf16[128,2048]{1,0:T(8,128)(2,1)S(1)} %add_convert_fusion.3), channel_id=1, source_target_pairs={{0,4},{2,6},{4,0},{6,2},{1,5},{3,7},{5,1},{7,3},{8,12},{10,14},{12... | collective-permute-start | bytes 1572872 | tf_op jit(solution)/shard_map/cond/branch_1_fun/ppermute | solution.py:579
  339.2 20.8 %collective-permute-start.34 = (bf16[128,2048]{1,0:T(8,128)(2,1)S(1)}, bf16[128,2048]{1,0:T(8,128)(2,1)}, u32[]{:S(2)}, u32[]{:S(2)}) collective-permute-start(bf16[128,2048]{1,0:T(8,128)(2,1)S(1)} %copy-done.40), channel_id=1, source_target_pairs={{0,2},{2,0},{4,6},{6,4},{1,3},{3,1},{5,7},{7,5},{8,10},{10,8},{12,... | collective-permute-start | bytes 1572872 | tf_op jit(solution)/shard_map/cond/branch_1_fun/ppermute | solution.py:579
  340.2 22.2 %collective-permute-start.37 = (bf16[128,2048]{1,0:T(8,128)(2,1)S(1)}, bf16[128,2048]{1,0:T(8,128)(2,1)}, u32[]{:S(2)}, u32[]{:S(2)}) collective-permute-start(bf16[128,2048]{1,0:T(8,128)(2,1)S(1)} %copy-done.39), channel_id=1, source_target_pairs={{0,4},{2,6},{4,0},{6,2},{1,5},{3,7},{5,1},{7,3},{8,12},{10,14},{12... | collective-permute-start | bytes 1572872 | tf_op jit(solution)/shard_map/cond/branch_1_fun/ppermute | solution.py:579
  362.5 173.0 %reduce-scatter.8.cloned.1.call-start = ((), (), s32[]{:S(2)}) async-start(), calls=%async_computation.5 | async-start | bytes 4055040 | tf_op jit(solution)/shard_map/reduce_scatter | solution.py:809
  369.0 15.2 %collective-permute-start.11 = (bf16[128,2048]{1,0:T(8,128)(2,1)}, bf16[128,2048]{1,0:T(8,128)(2,1)}, u32[]{:S(2)}, u32[]{:S(2)}) collective-permute-start(bf16[128,2048]{1,0:T(8,128)(2,1)} %get-tuple-element.941), channel_id=1, source_target_pairs={{0,2},{2,0},{4,6},{6,4},{1,3},{3,1},{5,7},{7,5},{8,10},{10,8},{12,... | collective-permute-start | bytes 1572872 | tf_op jit(solution)/shard_map/cond/branch_1_fun/ppermute | solution.py:579
  370.1 15.2 %collective-permute-start.14 = (bf16[128,2048]{1,0:T(8,128)(2,1)}, bf16[128,2048]{1,0:T(8,128)(2,1)}, u32[]{:S(2)}, u32[]{:S(2)}) collective-permute-start(bf16[128,2048]{1,0:T(8,128)(2,1)} %get-tuple-element.942), channel_id=1, source_target_pairs={{0,4},{2,6},{4,0},{6,2},{1,5},{3,7},{5,1},{7,3},{8,12},{10,14},{12... | collective-permute-start | bytes 1572872 | tf_op jit(solution)/shard_map/cond/branch_1_fun/ppermute | solution.py:579
  371.8 23.7 %collective-permute-start.12 = (bf16[128,2048]{1,0:T(8,128)(2,1)}, bf16[128,2048]{1,0:T(8,128)(2,1)}, u32[]{:S(2)}, u32[]{:S(2)}) collective-permute-start(bf16[128,2048]{1,0:T(8,128)(2,1)} %get-tuple-element.942), channel_id=1, source_target_pairs={{0,2},{2,0},{4,6},{6,4},{1,3},{3,1},{5,7},{7,5},{8,10},{10,8},{12,... | collective-permute-start | bytes 1572872 | tf_op jit(solution)/shard_map/cond/branch_1_fun/ppermute | solution.py:579
  372.8 23.6 %collective-permute-start.13 = (bf16[128,2048]{1,0:T(8,128)(2,1)}, bf16[128,2048]{1,0:T(8,128)(2,1)}, u32[]{:S(2)}, u32[]{:S(2)}) collective-permute-start(bf16[128,2048]{1,0:T(8,128)(2,1)} %get-tuple-element.941), channel_id=1, source_target_pairs={{0,4},{2,6},{4,0},{6,2},{1,5},{3,7},{5,1},{7,3},{8,12},{10,14},{12... | collective-permute-start | bytes 1572872 | tf_op jit(solution)/shard_map/cond/branch_1_fun/ppermute | solution.py:579
  385.2 20.4 %collective-permute-start.15 = (bf16[128,2048]{1,0:T(8,128)(2,1)}, bf16[128,2048]{1,0:T(8,128)(2,1)}, u32[]{:S(2)}, u32[]{:S(2)}) collective-permute-start(bf16[128,2048]{1,0:T(8,128)(2,1)} %collective-permute-done.11), channel_id=1, source_target_pairs={{0,4},{2,6},{4,0},{6,2},{1,5},{3,7},{5,1},{7,3},{8,12},{10,14},{12... | collective-permute-start | bytes 1572872 | tf_op jit(solution)/shard_map/cond/branch_1_fun/ppermute | solution.py:579
  387.0 18.6 %collective-permute-start.16 = (bf16[128,2048]{1,0:T(8,128)(2,1)}, bf16[128,2048]{1,0:T(8,128)(2,1)}, u32[]{:S(2)}, u32[]{:S(2)}) collective-permute-start(bf16[128,2048]{1,0:T(8,128)(2,1)} %collective-permute-done.14), channel_id=1, source_target_pairs={{0,2},{2,0},{4,6},{6,4},{1,3},{3,1},{5,7},{7,5},{8,10},{10,8},{12,... | collective-permute-start | bytes 1572872 | tf_op jit(solution)/shard_map/cond/branch_1_fun/ppermute | solution.py:579
  405.6 49.9 %collective-permute-start.69 = (bf16[256,2048]{1,0:T(8,128)(2,1)}, bf16[256,2048]{1,0:T(8,128)(2,1)}, u32[]{:S(2)}, u32[]{:S(2)}) collective-permute-start(bf16[256,2048]{1,0:T(8,128)(2,1)} %get-tuple-element.680), channel_id=1, source_target_pairs={{0,2},{2,0},{4,6},{6,4},{1,3},{3,1},{5,7},{7,5},{8,10},{10,8},{12,... | collective-permute-start | bytes 3145736 | tf_op jit(solution)/shard_map/ppermute | solution.py:579
  406.7 48.9 %collective-permute-start.70 = (bf16[256,2048]{1,0:T(8,128)(2,1)}, bf16[256,2048]{1,0:T(8,128)(2,1)}, u32[]{:S(2)}, u32[]{:S(2)}) collective-permute-start(bf16[256,2048]{1,0:T(8,128)(2,1)} %get-tuple-element.681), channel_id=1, source_target_pairs={{0,4},{2,6},{4,0},{6,2},{1,5},{3,7},{5,1},{7,3},{8,12},{10,14},{12... | collective-permute-start | bytes 3145736 | tf_op jit(solution)/shard_map/ppermute | solution.py:579
  408.1 47.4 %collective-permute-start.71 = (bf16[256,2048]{1,0:T(8,128)(2,1)}, bf16[256,2048]{1,0:T(8,128)(2,1)}, u32[]{:S(2)}, u32[]{:S(2)}) collective-permute-start(bf16[256,2048]{1,0:T(8,128)(2,1)} %get-tuple-element.682), channel_id=1, source_target_pairs={{0,6},{2,4},{4,2},{6,0},{1,7},{3,5},{5,3},{7,1},{8,14},{10,12},{12... | collective-permute-start | bytes 3145736 | tf_op jit(solution)/shard_map/ppermute | solution.py:579
  414.9 26.8 %collective-permute-start.17 = (bf16[1024,2048]{1,0:T(8,128)(2,1)}, bf16[1024,2048]{1,0:T(8,128)(2,1)}, u32[]{:S(2)}, u32[]{:S(2)}) collective-permute-start(bf16[1024,2048]{1,0:T(8,128)(2,1)} %get-tuple-element.958.refs_0_), channel_id=1, source_target_pairs={{0,1},{1,0},{2,3},{3,2},{4,5},{5,4},{6,7},{7,6},{8,9},{9,8},{10,11... | collective-permute-start | bytes 12582920 | tf_op jit(solution)/shard_map/cond/branch_1_fun/ppermute | solution.py:579
  462.0 15.1 %collective-permute-start.41 = (bf16[128,2048]{1,0:T(8,128)(2,1)}, bf16[128,2048]{1,0:T(8,128)(2,1)}, u32[]{:S(2)}, u32[]{:S(2)}) collective-permute-start(bf16[128,2048]{1,0:T(8,128)(2,1)} %get-tuple-element.412), channel_id=1, source_target_pairs={{0,2},{2,0},{4,6},{6,4},{1,3},{3,1},{5,7},{7,5},{8,10},{10,8},{12,... | collective-permute-start | bytes 1572872 | tf_op jit(solution)/shard_map/cond/branch_1_fun/ppermute | solution.py:579
  463.1 15.1 %collective-permute-start.42 = (bf16[128,2048]{1,0:T(8,128)(2,1)}, bf16[128,2048]{1,0:T(8,128)(2,1)}, u32[]{:S(2)}, u32[]{:S(2)}) collective-permute-start(bf16[128,2048]{1,0:T(8,128)(2,1)} %get-tuple-element.413), channel_id=1, source_target_pairs={{0,4},{2,6},{4,0},{6,2},{1,5},{3,7},{5,1},{7,3},{8,12},{10,14},{12... | collective-permute-start | bytes 1572872 | tf_op jit(solution)/shard_map/cond/branch_1_fun/ppermute | solution.py:579
  466.8 18.8 %collective-permute-start.47 = (bf16[128,1536]{1,0:T(8,128)(2,1)S(1)}, bf16[128,1536]{1,0:T(8,128)(2,1)}, u32[]{:S(2)}, u32[]{:S(2)}) collective-permute-start(bf16[128,1536]{1,0:T(8,128)(2,1)S(1)} %get-tuple-element.753), channel_id=1, source_target_pairs={{0,2},{2,0},{4,6},{6,4},{1,3},{3,1},{5,7},{7,5},{8,10},{10,8},{12,... | collective-permute-start | bytes 1179656 | tf_op jit(solution)/shard_map/cond/branch_1_fun/ppermute | solution.py:579
  467.7 19.0 %collective-permute-start.48 = (bf16[128,1536]{1,0:T(8,128)(2,1)S(1)}, bf16[128,1536]{1,0:T(8,128)(2,1)}, u32[]{:S(2)}, u32[]{:S(2)}) collective-permute-start(bf16[128,1536]{1,0:T(8,128)(2,1)S(1)} %get-tuple-element.752), channel_id=1, source_target_pairs={{0,4},{2,6},{4,0},{6,2},{1,5},{3,7},{5,1},{7,3},{8,12},{10,14},{12... | collective-permute-start | bytes 1179656 | tf_op jit(solution)/shard_map/cond/branch_1_fun/ppermute | solution.py:579
  478.3 38.3 %collective-permute-start.43 = (bf16[128,2048]{1,0:T(8,128)(2,1)}, bf16[128,2048]{1,0:T(8,128)(2,1)}, u32[]{:S(2)}, u32[]{:S(2)}) collective-permute-start(bf16[128,2048]{1,0:T(8,128)(2,1)} %get-tuple-element.414), channel_id=1, source_target_pairs={{0,2},{2,0},{4,6},{6,4},{1,3},{3,1},{5,7},{7,5},{8,10},{10,8},{12,... | collective-permute-start | bytes 1572872 | tf_op jit(solution)/shard_map/cond/branch_1_fun/ppermute | solution.py:579
  479.2 37.4 %collective-permute-start.46 = (bf16[128,2048]{1,0:T(8,128)(2,1)}, bf16[128,2048]{1,0:T(8,128)(2,1)}, u32[]{:S(2)}, u32[]{:S(2)}) collective-permute-start(bf16[128,2048]{1,0:T(8,128)(2,1)} %get-tuple-element.417), channel_id=1, source_target_pairs={{0,4},{2,6},{4,0},{6,2},{1,5},{3,7},{5,1},{7,3},{8,12},{10,14},{12... | collective-permute-start | bytes 1572872 | tf_op jit(solution)/shard_map/cond/branch_1_fun/ppermute | solution.py:579
  482.0 34.6 %collective-permute-start.44 = (bf16[128,2048]{1,0:T(8,128)(2,1)S(1)}, bf16[128,2048]{1,0:T(8,128)(2,1)}, u32[]{:S(2)}, u32[]{:S(2)}) collective-permute-start(bf16[128,2048]{1,0:T(8,128)(2,1)S(1)} %add_convert_fusion.5), channel_id=1, source_target_pairs={{0,4},{2,6},{4,0},{6,2},{1,5},{3,7},{5,1},{7,3},{8,12},{10,14},{12... | collective-permute-start | bytes 1572872 | tf_op jit(solution)/shard_map/cond/branch_1_fun/ppermute | solution.py:579
  485.5 31.0 %collective-permute-start.45 = (bf16[128,2048]{1,0:T(8,128)(2,1)S(1)}, bf16[128,2048]{1,0:T(8,128)(2,1)}, u32[]{:S(2)}, u32[]{:S(2)}) collective-permute-start(bf16[128,2048]{1,0:T(8,128)(2,1)S(1)} %add_convert_fusion.4), channel_id=1, source_target_pairs={{0,2},{2,0},{4,6},{6,4},{1,3},{3,1},{5,7},{7,5},{8,10},{10,8},{12,... | collective-permute-start | bytes 1572872 | tf_op jit(solution)/shard_map/cond/branch_1_fun/ppermute | solution.py:579
  486.7 29.9 %collective-permute-start.49 = (bf16[128,1536]{1,0:T(8,128)(2,1)S(1)}, bf16[128,1536]{1,0:T(8,128)(2,1)}, u32[]{:S(2)}, u32[]{:S(2)}) collective-permute-start(bf16[128,1536]{1,0:T(8,128)(2,1)S(1)} %get-tuple-element.751), channel_id=1, source_target_pairs={{0,6},{2,4},{4,2},{6,0},{1,7},{3,5},{5,3},{7,1},{8,14},{10,12},{12... | collective-permute-start | bytes 1179656 | tf_op jit(solution)/shard_map/cond/branch_1_fun/ppermute | solution.py:579
  (62 other events, 707.9 us)
Sparse Core Ops, SparseCore 0:
  29.4 65.4 all-gather.6
  97.0 113.9 all-gather.8
  212.6 61.7 all-gather.10
  287.7 108.5 reduce-scatter.3
  398.4 60.7 reduce-scatter.5
  461.4 61.8 reduce-scatter.7

commit v3 on v2

--- a/solution.py
+++ b/solution.py
@@ -83,7 +83,7 @@
 
 
 def query_strips(rows, column_ref, row_ref):
-    step = min(128, rows)
+    step = min(256, rows)
     for first in range(0, rows, step):
         seen = first + step
         keys = lax.broadcasted_iota(jnp.int32, (seen, step), 0)
@@ -196,11 +196,16 @@
     return pl.BlockSpec(shape, lambda i: zeros, pipeline_mode=pl.Buffered(1))
 
 
-def project_kernel(count, *refs):
+def project_kernel(count, few, *refs):
     lefts, rights, outs = refs[:count], refs[count : 2 * count], refs[2 * count :]
-    total = dot_right_t(lefts[0][...], rights[0][0])
+
+    def product(left, right):
+        return dot_right_t(right[0], left[...]) if few else dot_right_t(left[...], right[0])
+
+    total = product(lefts[0], rights[0])
     for left, right in zip(lefts[1:], rights[1:]):
-        total = total + dot_right_t(left[...], right[0])
+        total = total + product(left, right)
+    total = total.T if few else total
     first = 0
     for out in outs:
         out[...] = total[first : first + out.shape[0]].astype(out.dtype)
@@ -221,7 +226,7 @@
 
     return list(
         pl.pallas_call(
-            functools.partial(project_kernel, len(lefts)),
+            functools.partial(project_kernel, len(lefts), bool(first)),
             grid=(parts,),
             in_specs=[left_spec(left) for left in lefts]
             + [right_spec(left, place) for left, place in zip(lefts, places)],
@@ -316,45 +321,47 @@
     )
 
 
-def rows_product_kernel(count, normed, *refs):
+def rows_product_kernel(count, normed, number, *refs):
     pieces, refs = refs[:count], list(refs[count:])
     gain = refs.pop(0)[...] if normed else None
-    weight, out = refs[0], refs[-1]
+    weights, refs = refs[:number], refs[number:]
     whole = pieces[0]
     if count > 1 or normed:
-        whole = refs[1]
+        whole = refs.pop(0)
 
         def change(rows):
             return normalize(rows.astype(f32), gain).astype(bf16) if normed else rows
 
         put_rows(whole, pieces, change)
-    columns = weight.shape[2]
-    out[...] = dot(whole[...], weight[...].reshape(-1, columns)).astype(out.dtype)
-
-
-def rows_product(pieces, gain, weight, block, place, step, dtype, name):
+    for weight, out in zip(weights, refs):
+        matrix = weight[...].reshape(-1, weight.shape[2])
+        out[...] = dot(whole[...], matrix).astype(out.dtype)
+
+
+def rows_product(pieces, gain, weights, block, place, step, dtype, name):
     rows = sum(piece.shape[0] for piece in pieces)
-    parts, width = weight.shape[0], pieces[0].shape[1]
+    parts, width = weights[0].shape[0], pieces[0].shape[1]
     joined = len(pieces) > 1 or gain is not None
     shapes = [jax.ShapeDtypeStruct((rows, width), bf16)] if joined else []
-    shapes += [jax.ShapeDtypeStruct((rows, block), dtype)]
+    shapes += [jax.ShapeDtypeStruct((rows, block), dtype)] * len(weights)
     gains = [] if gain is None else [gain.reshape(1, -1)]
     got = pl.pallas_call(
-        functools.partial(rows_product_kernel, len(pieces), gain is not None),
+        functools.partial(rows_product_kernel, len(pieces), gain is not None, len(weights)),
         grid=(1,),
         in_specs=[resident(piece.shape) for piece in list(pieces) + gains]
         + [
             pl.BlockSpec(
                 (parts, step, block), lambda i: (0, 0, place), pipeline_mode=pl.Buffered(1)
             )
-        ],
+        ]
+        * len(weights),
         out_specs=[resident(shape.shape) for shape in shapes],
         out_shape=shapes,
         compiler_params=pltpu.CompilerParams(vmem_limit_bytes=56 << 20),
         cost_estimate=BESIDE,
         name=name,
-    )(*pieces, *gains, weight)
-    return (got[0], got[1]) if joined else (pieces[0], got[0])
+    )(*pieces, *gains, *weights)
+    return (got[0], list(got[1:])) if joined else (pieces[0], list(got))
 
 
 def weight_grad_kernel(counts, number, *refs):
@@ -710,7 +717,9 @@
         return lax.all_gather(pieces, "data", axis=0, tiled=False)
 
     attn_got = swap(attn_piece)
-    x_near = spread_near(lax.optimization_barrier((halves(hidden_in), attn_got))[0])
+    tied = lax.optimization_barrier((halves(hidden_in), halves(out_grad), attn_got))
+    grad_halves = tied[1]
+    x_near = spread_near(tied[0])
     tied = lax.optimization_barrier((w_gate, w_up, turned_down, x_near))
     w_gate_sent, w_up_sent, turned_down, x_near = tied
     x_blocks = x_near + spread_far(x_near)
@@ -758,7 +767,7 @@
         return [weight] + [trade(weight, "tp", j) for j in range(1, cores)]
 
     near_rows = model * shard
-    grad_near = spread_near(after(halves(out_grad), *x_blocks, *mlp_near))
+    grad_near = spread_near(after(grad_halves, *x_blocks, *mlp_near))
 
     seg_rows = jnp.pad(seg_all[:, None], ((0, 0), (0, 7), (0, 0)))
     seg_columns = seg_all[:, :, None]
@@ -769,13 +778,13 @@
     def product_phase():
         w_attn = with_cores(attn_full)
         normed_in, first_raw = rows_product(
-            x_blocks, gain_in, w_attn[0], cols, 0, near_rows, f32, "query_key_value"
-        )
-        raw = [first_raw.reshape(model, half, cols)]
+            x_blocks, gain_in, w_attn[:1], cols, 0, near_rows, f32, "query_key_value"
+        )
+        raw = [first_raw[0].reshape(model, half, cols)]
         for j in range(1, cores):
             mine = rows_product(
-                [normed_in], None, w_attn[j], cols, 0, near_rows, f32, "query_key_value_other"
-            )[1]
+                [normed_in], None, [w_attn[j]], cols, 0, near_rows, f32, "query_key_value_other"
+            )[1][0]
             raw.append(trade(mine, "tp", j).reshape(model, half, cols))
         return w_attn[1:], normed_in, raw
 
@@ -890,14 +899,11 @@
     down_got = [trade(down_parts[k], "model", k) for k in range(1, model)]
 
     def attend_back_phase():
-        att_grads, rows = [], branch_blocks
-        for j in reversed(range(cores)):
-            branch, piece = rows_product(
-                rows, None, w_attn[j], q_cols, o_place[j], near_rows, bf16, "attended_grad"
-            )
-            rows = [branch]
-            piece = piece.reshape(model, half, q_cols)
-            att_grads.insert(0, trade(piece, "tp", j) if j else piece)
+        branch, products = rows_product(
+            branch_blocks, None, w_attn, q_cols, o_place[0], near_rows, bf16, "attended_grad"
+        )
+        products = [piece.reshape(model, half, q_cols) for piece in products]
+        att_grads = [trade(piece, "tp", j) if j else piece for j, piece in enumerate(products)]
         *qkv_back, head_grads = attention_call(
             functools.partial(attend_back_kernel, cores, kv_heads, repeat),
             "attend_back",
@@ -940,19 +946,19 @@
         return swap(rows_at(total.reshape(model, shard, -1)))
 
     def in_grad_phase():
-        own, _, got = project_and_send(
+        own, far, got = project_and_send(
             back_flat, w_attn, [0] * cores, half, near_rows, "normed_in_grad"
         )
-        return own, got, [exchanged(total) for total in first_sums]
-
-    in_part, in_got, first_got = phase(always, in_grad_phase)
+        hidden_out = rows_call(
+            "sum", down_parts[0], middle, after(down_got, *far), None, None, False, "hidden_out_sum"
+        )[0]
+        return own, got, [exchanged(total) for total in first_sums], hidden_out
+
+    in_part, in_got, first_got, hidden_out = phase(always, in_grad_phase)
     in_got, last_sum = lax.optimization_barrier((in_got, mlp_sums[-1]))
 
     def last_phase():
         last_got = exchanged(last_sum)
-        hidden_out = rows_call(
-            "sum", down_parts[0], middle, down_got, None, None, False, "hidden_out_sum"
-        )[0]
         grad_in = rows_call(
             "back", in_part, hidden_in, in_got, gain_in, middle_grad, False, "grad_in"
         )[0]
@@ -964,10 +970,10 @@
         owned = owned_call(
             me, first_got + [last_got], layout, [w_gate, w_up], mlp_gain, shapes, "hidden_owned"
         )
-        return hidden_out, grad_in, owned[:3], owned[3][:, 0]
+        return grad_in, owned[:3], owned[3][:, 0]
 
     got = phase(always, last_phase)
-    hidden_out, grad_in, (grad_gate, grad_up, grad_down), mlp_part = got
+    grad_in, (grad_gate, grad_up, grad_down), mlp_part = got
     attn_sum = after(attn_sum, grad_in)
     weight_rows = attn_sum[:near_rows].reshape(model, shard, wide)
     gain_row = attn_sum[near_rows:]

time: 570 us -> 563 us (0.988)
  Pallas kernels: 230 us -> 223 us
    pallas_call x4 -> x3, Pallas kernels: 24.1 us -> 20.8 us  [rows_product(): pl.pallas_call(functools.partial(rows_product_kernel, len(pieces), gain i...]
  transfers between devices with their start and end apart: 81 -> 81, of which waited for: 38 -> 39; matrix products, arithmetic and copies ran while one was open for 6% -> 5% of each run, Pallas kernels for 41% -> 40%
where the time goes in v3:
time: 563 us; the launch traced here: 555 us
  Pallas kernels  223 us (40%)
  waiting for transfers between devices  196 us (35%)
  starting transfers between devices  68.2 us (12%)
  local copies, waits for them, and re-layouts  27.8 us (5%)
  other arithmetic  18.7 us (3%)
  between operations  17.2 us (3%)
    ppermute x75, waiting for transfers between devices, trade(): lax.ppermute(block, axis, [(i, i ^ step) for i in range(lax.axis_size(axi...  195 us
    ppermute x75, starting transfers between devices, trade(): lax.ppermute(block, axis, [(i, i ^ step) for i in range(lax.axis_size(axi...  67.9 us
    pallas_call x7, Pallas kernels, project(): pl.pallas_call(functools.partial(project_kernel, len(lefts), bool(first))...  56.6 us
    pallas_call x4, Pallas kernels, hidden_call(): pl.pallas_call(functools.partial(hidden_kernel, first, cores, len(x_piece...  48.4 us
    pallas_call x3, Pallas kernels, weight_grad(): pl.pallas_call(functools.partial(weight_grad_kernel, [len(group) for grou...  44.6 us
    pallas_call x2, Pallas kernels, attention_call(): pl.pallas_call(kernel, grid=(halves[0].shape[0],), in_specs=[pl.BlockSpec...  27.5 us
    pallas_call x3, Pallas kernels, rows_product(): pl.pallas_call(functools.partial(rows_product_kernel, len(pieces), gain i...  20.8 us
    pallas_call x4, Pallas kernels, rows_call(): pl.pallas_call(functools.partial(rows_kernel, kind, len(got)), grid=(2,),...  18.4 us
  transfers between devices with their start and end apart: 81, of which 39 were waited for; matrix products, arithmetic and copies ran while one was open for 5% of the time, Pallas kernels for 40%

profile of v3, /device:TPU:0, one launch (start us, length us, event | category | flops | bytes accessed | tf_op | source)
XLA Modules:
  0.0 555.0 jit_solution(11069328400840922053)
XLA Ops:
  12.8 3.0 collective-permute-start.53
  17.5 4.6 collective-permute-done.53
  22.1 5.4 collective-permute-done.54
  36.4 10.2 %collective-permute-done.56 = bf16[128,2048]{1,0:T(8,128)(2,1)S(1)} collective-permute-done((bf16[128,2048]{1,0:T(8,128)(2,1)S(1)}, bf16[128,2048]{1,0:T(8,128)(2,1)S(1)}, u32[]{:S(2)}, u32[]{:S(2)}) %collective-permute-start.56) | collective-permute-done | bytes 524320 | tf_op jit(solution)/shard_map/ppermute | solution.py:586
  46.6 9.0 %collective-permute-done.57 = bf16[128,2048]{1,0:T(8,128)(2,1)S(1)} collective-permute-done((bf16[128,2048]{1,0:T(8,128)(2,1)S(1)}, bf16[128,2048]{1,0:T(8,128)(2,1)S(1)}, u32[]{:S(2)}, u32[]{:S(2)}) %collective-permute-start.57) | collective-permute-done | bytes 524320 | tf_op jit(solution)/shard_map/ppermute | solution.py:586
  62.5 3.7 fusion.2
  68.8 4.7 collective-permute-done.60.refs_1_
  73.5 13.7 %collective-permute-done.61.refs_2_ = bf16[128,2304]{1,0:T(8,128)(2,1)S(1)} collective-permute-done((bf16[128,2304]{1,0:T(8,128)(2,1)S(1)}, bf16[128,2304]{1,0:T(8,128)(2,1)S(1)}, u32[]{:S(2)}, u32[]{:S(2)}) %collective-permute-start.61) | collective-permute-done | bytes 589856 | tf_op jit(solution)/shard_map/ppermute | solution.py:586
  88.8 6.5 %collective-permute-done.63 = bf16[128,2048]{1,0:T(8,128)(2,1)S(1)} collective-permute-done((bf16[128,2048]{1,0:T(8,128)(2,1)S(1)}, bf16[128,2048]{1,0:T(8,128)(2,1)S(1)}, u32[]{:S(2)}, u32[]{:S(2)}) %collective-permute-start.63) | collective-permute-done | bytes 524320 | tf_op jit(solution)/shard_map/ppermute | solution.py:586
  105.3 19.0 %conditional.10 = (bf16[4,528,768]{2,1,0:T(8,128)(2,1)}, bf16[1024,2048]{1,0:T(8,128)(2,1)}, f32[4,256,512]{2,1,0:T(8,128)S(1)}, f32[4,256,512]{2,1,0:T(8,128)}) conditional(s32[]{:T(128)} %convert_element_type.143, () %tuple.115, (bf16[4,528,768]{2,1,0:T(8,128)(2,1)}, f32[16,128]{1,0:T(8,128)S(1)}, bf16[128,2048]{1,0:T(8,128)(2,1)S(1)}, ...), branch_computations={%region_0.1_spmd, %region_1.2_spmd} | conditional | flops 2097152 | bytes 25690280 | solution.py:582
  106.5 6.8 %query_key_value.1 = (bf16[1024,2048]{1,0:T(8,128)(2,1)}, f32[1024,512]{1,0:T(8,128)S(1)}) custom-call(bf16[128,2048]{1,0:T(8,128)(2,1)S(1)} %get-tuple-element.251.refs_0_, bf16[128,2048]{1,0:T(8,128)(2,1)S(1)} %get-tuple-element.252.refs_1_, bf16[128,2048]{1,0:T(8,128)(2,1)} %copy-done.27, bf16[128,2048]{1,0:T(8,128)(2,1)} %get-tuple-element.254.refs_3_, ...), custom_call_target="tpu_custom_call" | custom-call | flops 1048576 | bytes 65536 | tf_op jit(solution)/shard_map/cond/branch_1_fun/query_key_value/pallas_call | solution.py:348
  113.3 6.6 %query_key_value_other.1 = f32[1024,512]{1,0:T(8,128)} custom-call(bf16[1024,2048]{1,0:T(8,128)(2,1)} %get-tuple-element.860.refs_0_, bf16[4,528,768]{2,1,0:T(8,128)(2,1)} %collective-permute-done.refs_1_), custom_call_target="tpu_custom_call" | custom-call | flops 1048576 | bytes 65536 | tf_op jit(solution)/shard_map/cond/branch_1_fun/query_key_value_other/pallas_call | solution.py:348
  119.9 4.5 collective-permute-done.1
  125.7 17.5 %conditional.11 = (bf16[1024,2048]{1,0:T(8,128)(2,1)}, bf16[1024,256]{1,0:T(8,128)(2,1)}, bf16[1024,256]{1,0:T(8,128)(2,1)}, bf16[4,256,256]{2,1,0:T(8,128)(2,1)...) conditional(s32[]{:T(128)} %convert_element_type.143, () %tuple.114, ...), branch_computations={%region_2.3_spmd, %region_3.4_spmd} | conditional | flops 1048576 | bytes 24199384 | solution.py:582
  128.0 11.5 %attend.1 = (bf16[4,256,256]{2,1,0:T(8,128)(2,1)}, bf16[4,256,256]{2,1,0:T(8,128)(2,1)}) custom-call(s32[1]{0:T(128)} %bitcast.3.core_ref, f32[4,256,512]{2,1,0:T(8,128)S(1)} %get-tuple-element.264.refs_0_, f32[4,256,512]{2,1,0:T(8,128)} %get-tuple-element.265.refs_1_, f32[4,512,128]{2,1,0:T(8,128)} %get-tuple-element.266.refs_2_, ...), custom_call_target="tpu_custom_call" | custom-call | flops 1048576 | bytes 65536 | tf_op jit(solution)/shard_map/cond/branch_1_fun/attend/pallas_call | solution.py:179
  143.2 82.4 %conditional.12 = (f32[256,2048]{1,0:T(8,128)}, bf16[128,2048]{1,0:T(8,128)(2,1)}, bf16[128,2048]{1,0:T(8,128)(2,1)}, bf16[128,2048]{1,0:T(8,128)(2,1)}, bf16[12...) conditional(s32[]{:T(128)} %convert_element_type.143, ...), branch_computations={%region_4.5_spmd, %region_5.6_spmd} | conditional | flops 5242880 | bytes 54067836 | solution.py:582
  143.2 4.6 attention_out_far.1
  149.9 5.2 attention_out.1
  155.2 6.8 %collective-permute-done.19 = bf16[128,2048]{1,0:T(8,128)(2,1)S(1)} collective-permute-done((bf16[128,2048]{1,0:T(8,128)(2,1)}, bf16[128,2048]{1,0:T(8,128)(2,1)S(1)}, u32[]{:S(2)}, u32[]{:S(2)}) %collective-permute-start.19) | collective-permute-done | bytes 524320 | tf_op jit(solution)/shard_map/cond/branch_1_fun/ppermute | solution.py:586
  169.1 8.5 %collective-permute-done.21.refs_2_ = bf16[128,2048]{1,0:T(8,128)(2,1)S(1)} collective-permute-done((bf16[128,2048]{1,0:T(8,128)(2,1)}, bf16[128,2048]{1,0:T(8,128)(2,1)S(1)}, u32[]{:S(2)}, u32[]{:S(2)}) %collective-permute-start.21) | collective-permute-done | bytes 524320 | tf_op jit(solution)/shard_map/cond/branch_1_fun/ppermute | solution.py:586
  178.8 9.0 %collective-permute-done.22.refs_3_ = bf16[128,2048]{1,0:T(8,128)(2,1)S(1)} collective-permute-done((bf16[128,2048]{1,0:T(8,128)(2,1)S(1)}, bf16[128,2048]{1,0:T(8,128)(2,1)S(1)}, u32[]{:S(2)}, u32[]{:S(2)}) %collective-permute-start.22) | collective-permute-done | bytes 524320 | tf_op jit(solution)/shard_map/cond/branch_1_fun/ppermute | solution.py:586
  187.8 2.7 middle.1
  194.5 11.1 %collective-permute-done.25 = bf16[128,2048]{1,0:T(8,128)(2,1)} collective-permute-done((bf16[128,2048]{1,0:T(8,128)(2,1)}, bf16[128,2048]{1,0:T(8,128)(2,1)}, u32[]{:S(2)}, u32[]{:S(2)}) %collective-permute-start.25) | collective-permute-done | bytes 524320 | tf_op jit(solution)/shard_map/cond/branch_1_fun/ppermute | solution.py:586
  207.7 9.1 %collective-permute-done.26 = bf16[128,2048]{1,0:T(8,128)(2,1)} collective-permute-done((bf16[128,2048]{1,0:T(8,128)(2,1)}, bf16[128,2048]{1,0:T(8,128)(2,1)}, u32[]{:S(2)}, u32[]{:S(2)}) %collective-permute-start.26) | collective-permute-done | bytes 524320 | tf_op jit(solution)/shard_map/cond/branch_1_fun/ppermute | solution.py:586
  217.7 7.9 %collective-permute-done.29 = bf16[128,2048]{1,0:T(8,128)(2,1)} collective-permute-done((bf16[128,2048]{1,0:T(8,128)(2,1)}, bf16[128,2048]{1,0:T(8,128)(2,1)}, u32[]{:S(2)}, u32[]{:S(2)}) %collective-permute-start.29) | collective-permute-done | bytes 524320 | tf_op jit(solution)/shard_map/cond/branch_1_fun/ppermute | solution.py:586
  225.6 58.7 %conditional.13 = (bf16[4,512,1536]{2,1,0:T(8,128)(2,1)}, bf16[1024,2048]{1,0:T(8,128)(2,1)}, bf16[1024,2048]{1,0:T(8,128)(2,1)}, bf16[1024,2048]{1,0:T(8,128)(2...) conditional(s32[]{:T(128)} %convert_element_type.143, ...), branch_computations={%region_6.7_spmd, %region_7.8_spmd} | conditional | flops 3145728 | bytes 84083016 | solution.py:582
  226.1 16.8 %hidden_units_a.1 = (bf16[1024,2048]{1,0:T(8,128)(2,1)}, bf16[1024,2048]{1,0:T(8,128)(2,1)}, bf16[1024,1024]{1,0:T(8,128)(2,1)}, bf16[1024,512]{1,0:T(8,128)(2,1)}) custom-call(bf16[128,2048]{1,0:T(8,128)(2,1)} %get-tuple-element.298.refs_0_, bf16[128,2048]{1,0:T(8,128)(2,1)} %get-tuple-element.299.refs_1_, bf16[128,2048]{1,0:T(8,128)(2,1)} %get-tuple-element.300.refs_2_, ...), custom_call_target="tpu_custom_call" | custom-call | flops 1048576 | bytes 65536 | tf_op jit(solution)/shard_map/cond/branch_1_fun/hidden_units_a/pallas_call | solution.py:561
  243.6 13.7 %hidden_units_a_other.1 = (bf16[1024,1024]{1,0:T(8,128)(2,1)}, bf16[1024,512]{1,0:T(8,128)(2,1)}) custom-call(bf16[1024,2048]{1,0:T(8,128)(2,1)} %get-tuple-element.906.refs_0_, bf16[1024,2048]{1,0:T(8,128)(2,1)} %get-tuple-element.908.refs_1_.refs_2_, bf16[4,512,1536]{2,1,0:T(8,128)(2,1)} %collective-permute-done.6.refs_2_.refs_3_.refs_4_, ...), custom_call_target="tpu_custom_call" | custom-call | flops 1048576 | bytes 65536 | tf_op jit(solution)/shard_map/cond/branch_1_fun/hidden_units_a_other/pallas_call | solution.py:561
  257.8 5.4 collective-permute-done.10.refs_7_
  265.0 19.4 %hidden_weights_a.1 = bf16[4,512,1536]{2,1,0:T(8,128)(2,1)} custom-call(bf16[1024,2048]{1,0:T(8,128)(2,1)} %get-tuple-element.906.refs_0_, bf16[1024,2048]{1,0:T(8,128)(2,1)} %collective-permute-done.7.refs_1_, bf16[1024,2048]{1,0:T(8,128)(2,1)} %get-tuple-element.908.refs_1_.refs_2_, bf16[1024,2048]{1,0:T(8,128)(2,1)} %collective-permute-done.8.refs_3_, ...), custom_call_target="tpu_custom_call" | custom-call | flops 1048576 | bytes 65536 | tf_op jit(solution)/shard_map/cond/branch_1_fun/hidden_weights_a/pallas_call | solution.py:392
  284.4 74.8 %conditional.14 = (f32[256,2048]{1,0:T(8,128)}, bf16[128,2048]{1,0:T(8,128)(2,1)}, bf16[128,2048]{1,0:T(8,128)(2,1)}, bf16[128,2048]{1,0:T(8,128)(2,1)}, bf16[12...) conditional(s32[]{:T(128)} %convert_element_type.143, ...), branch_computations={%region_8.9_spmd, %region_9.10_spmd} | conditional | flops 7340032 | bytes 68485760 | solution.py:582
  285.1 9.0 %hidden_units_b.2 = (bf16[1024,512]{1,0:T(8,128)(2,1)}, bf16[1024,256]{1,0:T(8,128)(2,1)}) custom-call(bf16[1024,2048]{1,0:T(8,128)(2,1)} %get-tuple-element.322.refs_0_, bf16[1024,2048]{1,0:T(8,128)(2,1)} %get-tuple-element.323.refs_1_.refs_2_, bf16[4,512,768]{2,1,0:T(8,128)(2,1)} %get-tuple-element.324.refs_2_.refs_3_.refs_4_.refs_6_, ...), custom_call_target="tpu_custom_call" | custom-call | flops 1048576 | bytes 65536 | tf_op jit(solution)/shard_map/cond/branch_1_fun/hidden_units_b/pallas_call | solution.py:561
  294.1 8.9 %hidden_units_b.3 = (bf16[1024,512]{1,0:T(8,128)(2,1)}, bf16[1024,256]{1,0:T(8,128)(2,1)S(1)}) custom-call(bf16[1024,2048]{1,0:T(8,128)(2,1)} %get-tuple-element.322.refs_0_, bf16[1024,2048]{1,0:T(8,128)(2,1)} %get-tuple-element.323.refs_1_.refs_2_, bf16[4,512,768]{2,1,0:T(8,128)(2,1)} %collective-permute-done.31.refs_2_.refs_3_.refs_4_.refs_7_, ...), custom_call_target="tpu_custom_call" | custom-call | flops 1048576 | bytes 65536 | tf_op jit(solution)/shard_map/cond/branch_1_fun/hidden_units_b/pallas_call | solution.py:561
  302.9 9.7 %normed_mid_grad_far.1 = (bf16[128,2048]{1,0:T(8,128)(2,1)}, bf16[128,2048]{1,0:T(8,128)(2,1)}) custom-call(bf16[1024,1024]{1,0:T(8,128)(2,1)} %get-tuple-element.320.refs_0_, bf16[1024,1024]{1,0:T(8,128)(2,1)} %get-tuple-element.321.refs_1_, bf16[1024,512]{1,0:T(8,128)(2,1)} %get-tuple-element.342.refs_2_.refs_4_, ...), custom_call_target="tpu_custom_call" | custom-call | flops 1048576 | bytes 65536 | tf_op jit(solution)/shard_map/cond/branch_1_fun/normed_mid_grad_far/pallas_call | solution.py:228
  315.6 14.7 %normed_mid_grad.1 = (f32[256,2048]{1,0:T(8,128)}, bf16[128,2048]{1,0:T(8,128)(2,1)}, bf16[128,2048]{1,0:T(8,128)(2,1)}, bf16[128,2048]{1,0:T(8,128)(2,1)}, bf16[128,2048]{1,0:T(8,128)(2,1)}) custom-call(bf16[1024,1024]{1,0:T(8,128)(2,1)} %get-tuple-element.320.refs_0_, bf16[1024,1024]{1,0:T(8,128)(2,1)} %get-tuple-element.321.refs_1_, ...), custom_call_target="tpu_custom_call" | custom-call | flops 1048576 | bytes 65536 | tf_op jit(solution)/shard_map/cond/branch_1_fun/normed_mid_grad/pallas_call | solution.py:228
  337.3 2.3 copy.159
  339.6 12.6 %hidden_weights_b.1 = bf16[4,512,768]{2,1,0:T(8,128)(2,1)} custom-call(bf16[1024,2048]{1,0:T(8,128)(2,1)} %get-tuple-element.322.refs_0_, bf16[1024,2048]{1,0:T(8,128)(2,1)} %get-tuple-element.338.refs_1_, bf16[1024,2048]{1,0:T(8,128)(2,1)} %get-tuple-element.323.refs_1_.refs_2_, bf16[1024,2048]{1,0:T(8,128)(2,1)} %get-tuple-element.339.refs_3_, ...), custom_call_target="tpu_custom_call" | custom-call | flops 1048576 | bytes 65536 | tf_op jit(solution)/shard_map/cond/branch_1_fun/hidden_weights_b/pallas_call | solution.py:392
  352.2 4.8 collective-permute-done.34
  357.0 2.0 collective-permute-done.37
  359.3 42.9 %conditional.15 = (f32[256,2048]{1,0:T(8,128)}, bf16[128,2048]{1,0:T(8,128)(2,1)}, bf16[128,2048]{1,0:T(8,128)(2,1)}, bf16[128,2048]{1,0:T(8,128)(2,1)}, bf16[12...) conditional(s32[]{:T(128)} %convert_element_type.143, ...), branch_computations={%region_10.11_spmd, %region_11.12_spmd} | conditional | flops 2097152 | bytes 37880180 | solution.py:582
  359.3 6.3 %middle_grad.1 = (f32[256,2048]{1,0:T(8,128)}, bf16[128,2048]{1,0:T(8,128)(2,1)}, bf16[128,2048]{1,0:T(8,128)(2,1)}) custom-call(f32[256,2048]{1,0:T(8,128)} %get-tuple-element.348.refs_0_, f32[256,2048]{1,0:T(8,128)} %get-tuple-element.349.refs_1_, bf16[128,2048]{1,0:T(8,128)(2,1)} %get-tuple-element.350.refs_2_, ...), custom_call_target="tpu_custom_call" | custom-call | flops 1048576 | bytes 65536 | tf_op jit(solution)/shard_map/cond/branch_1_fun/middle_grad/pallas_call | solution.py:311
  369.7 10.7 %hidden_out.1 = (f32[256,2048]{1,0:T(8,128)}, bf16[256,2048]{1,0:T(8,128)(2,1)}, bf16[256,2048]{1,0:T(8,128)(2,1)}, bf16[256,2048]{1,0:T(8,128)(2,1)}) custom-call(bf16[1024,512]{1,0:T(8,128)(2,1)} %get-tuple-element.359.refs_0_, bf16[1024,512]{1,0:T(8,128)(2,1)} %get-tuple-element.360.refs_1_, bf16[1024,256]{1,0:T(8,128)(2,1)} %get-tuple-element.361.refs_2_, ...), custom_call_target="tpu_custom_call" | custom-call | flops 1048576 | bytes 65536 | tf_op jit(solution)/shard_map/cond/branch_1_fun/hidden_out/pallas_call | solution.py:228
  383.7 8.4 %collective-permute-done.12 = bf16[128,2048]{1,0:T(8,128)(2,1)} collective-permute-done((bf16[128,2048]{1,0:T(8,128)(2,1)}, bf16[128,2048]{1,0:T(8,128)(2,1)}, u32[]{:S(2)}, u32[]{:S(2)}) %collective-permute-start.12) | collective-permute-done | bytes 524320 | tf_op jit(solution)/shard_map/cond/branch_1_fun/ppermute | solution.py:586
  393.3 8.8 %collective-permute-done.15 = bf16[128,2048]{1,0:T(8,128)(2,1)} collective-permute-done((bf16[128,2048]{1,0:T(8,128)(2,1)}, bf16[128,2048]{1,0:T(8,128)(2,1)}, u32[]{:S(2)}, u32[]{:S(2)}) %collective-permute-start.15) | collective-permute-done | bytes 524320 | tf_op jit(solution)/shard_map/cond/branch_1_fun/ppermute | solution.py:586
  405.7 32.1 %conditional.16 = (bf16[1024,2048]{1,0:T(8,128)(2,1)}, bf16[1024,2048]{1,0:T(8,128)(2,1)}, bf16[4,256,512]{2,1,0:T(8,128)(2,1)}, bf16[4,256,512]{2,1,0:T(8,128)(2,1)}, f32[8,128]{1,0:T(8,128)S(1)}) conditional(s32[]{:T(128)} %convert_element_type.143, () %tuple.106, (bf16[128,2048]{1,0:T(8,128)(2,1)}, bf16[128,2048]{1,0:T(8,128)(2,1)}, ...), branch_computations={%region_12.13_spmd, %region_13.14_spmd} | conditional | flops 2097152 | bytes 21119124 | solution.py:582
  405.7 7.5 %attended_grad.1 = (bf16[1024,2048]{1,0:T(8,128)(2,1)}, bf16[1024,256]{1,0:T(8,128)(2,1)}, bf16[1024,256]{1,0:T(8,128)(2,1)}) custom-call(bf16[128,2048]{1,0:T(8,128)(2,1)} %get-tuple-element.373.refs_0_, bf16[128,2048]{1,0:T(8,128)(2,1)} %get-tuple-element.374.refs_1_, bf16[128,2048]{1,0:T(8,128)(2,1)} %get-tuple-element.375.refs_2_, ...), custom_call_target="tpu_custom_call" | custom-call | flops 1048576 | bytes 65536 | tf_op jit(solution)/shard_map/cond/branch_1_fun/attended_grad/pallas_call | solution.py:348
  414.0 6.7 %collective-permute-done.18.refs_3_ = bf16[4,256,256]{2,1,0:T(8,128)(2,1)S(1)} collective-permute-done((bf16[4,256,256]{2,1,0:T(8,128)(2,1)}, bf16[4,256,256]{2,1,0:T(8,128)(2,1)S(1)}, u32[]{:S(2)}, u32[]{:S(2)}) %collective-permute-start.18) | collective-permute-done | bytes 524320 | tf_op jit(solution)/shard_map/cond/branch_1_fun/ppermute | solution.py:586
  421.8 16.0 %attend_back.1 = (bf16[4,256,512]{2,1,0:T(8,128)(2,1)}, bf16[4,256,512]{2,1,0:T(8,128)(2,1)}, f32[8,128]{1,0:T(8,128)S(1)}) custom-call(s32[1]{0:T(128)} %bitcast.8.core_ref, f32[4,256,512]{2,1,0:T(8,128)} %get-tuple-element.385.refs_0_, f32[4,256,512]{2,1,0:T(8,128)} %get-tuple-element.386.refs_1_, bf16[4,256,256]{2,1,0:T(8,128)(2,1)S(1)} %bitcast.89, ...), custom_call_target="tpu_custom_call" | custom-call | flops 1048576 | bytes 65536 | tf_op jit(solution)/shard_map/cond/branch_1_fun/attend_back/pallas_call | solution.py:179
  437.7 13.9 %conditional.17 = (bf16[4,528,768]{2,1,0:T(8,128)(2,1)}, bf16[1024,512]{1,0:T(8,128)(2,1)}, bf16[1024,512]{1,0:T(8,128)(2,1)}) conditional(s32[]{:T(128)} %convert_element_type.143, () %tuple.105, (bf16[4,256,512]{2,1,0:T(8,128)(2,1)}, bf16[4,256,512]{2,1,0:T(8,128)(2,1)}, bf16[4,256,256]{2,1,0:T(8,128)(2,1)}, bf16[4,256,256]{2,1,0:T(8,128)(2,1)}, ...), branch_computations={%region_14.15_spmd, %region_15.16_spmd} | conditional | flops 1049600 | bytes 5341214 | solution.py:582
  439.0 12.6 %attention_weights.1 = bf16[4,528,768]{2,1,0:T(8,128)(2,1)} custom-call(bf16[1024,2048]{1,0:T(8,128)(2,1)} %get-tuple-element.397.refs_0_, bf16[1024,2048]{1,0:T(8,128)(2,1)} %get-tuple-element.398.refs_1_, bf16[1024,2048]{1,0:T(8,128)(2,1)} %get-tuple-element.399.refs_2_, bf16[1024,2048]{1,0:T(8,128)(2,1)} %get-tuple-element.400.refs_3_, ...), custom_call_target="tpu_custom_call" | custom-call | flops 1048576 | bytes 65536 | tf_op jit(solution)/shard_map/cond/branch_1_fun/attention_weights/pallas_call | solution.py:392
  453.6 59.1 %conditional.18 = (f32[256,2048]{1,0:T(8,128)}, bf16[128,2048]{1,0:T(8,128)(2,1)}, bf16[128,2048]{1,0:T(8,128)(2,1)}, bf16[128,2048]{1,0:T(8,128)(2,1)}, bf16[12...) conditional(s32[]{:T(128)} %convert_element_type.143, ...), branch_computations={%region_17.18_spmd, %region_18.19_spmd} | conditional | flops 5242898 | bytes 23790228 | solution.py:582
  453.6 4.9 normed_in_grad_far.1
  460.4 2.2 dynamic-slice_bitcast_fusion
  464.7 6.9 %normed_in_grad.1 = (f32[256,2048]{1,0:T(8,128)}, bf16[128,2048]{1,0:T(8,128)(2,1)}, bf16[128,2048]{1,0:T(8,128)(2,1)}, bf16[128,2048]{1,0:T(8,128)(2,1)}, bf16[128,2048]{1,0:T(8,128)(2,1)}) custom-call(bf16[1024,512]{1,0:T(8,128)(2,1)} %get-tuple-element.406.refs_0_, bf16[1024,512]{1,0:T(8,128)(2,1)} %get-tuple-element.407.refs_1_, ...), custom_call_target="tpu_custom_call" | custom-call | flops 1048576 | bytes 65536 | tf_op jit(solution)/shard_map/cond/branch_1_fun/normed_in_grad/pallas_call | solution.py:228
  471.6 1.9 collective-permute-done.41
  484.3 4.1 hidden_out_sum.1
  488.4 24.0 %collective-permute-done.49 = bf16[128,1536]{1,0:T(8,128)(2,1)} collective-permute-done((bf16[128,1536]{1,0:T(8,128)(2,1)S(1)}, bf16[128,1536]{1,0:T(8,128)(2,1)}, u32[]{:S(2)}, u32[]{:S(2)}) %collective-permute-start.49) | collective-permute-done | bytes 393248 | tf_op jit(solution)/shard_map/cond/branch_1_fun/ppermute | solution.py:586
  512.7 16.8 %conditional.19 = (f32[256,2048]{1,0:T(8,128)}, f32[128,3072]{1,0:T(8,128)}, f32[128,3072]{1,0:T(8,128)}, f32[3072,128]{1,0:T(8,128)}, f32[128]{0:T(128)S(1)}) conditional(s32[]{:T(128)} %convert_element_type.143, () %tuple.129, (f32[16,128]{1,0:T(8,128)S(1)}, f32[256,2048]{1,0:T(8,128)}, bf16[256,2048]{1,0:T(8,128)(2,1)}, ...), branch_computations={%region_20.21_spmd, %region_21.22_spmd} | conditional | flops 2097170 | bytes 14616272 | solution.py:582
  517.7 5.3 grad_in.1
  523.0 2.2 collective-permute-done.51.refs_6_
  525.3 4.1 hidden_owned.1
  535.2 4.2 collective-permute-done.72.refs_1_
  539.4 3.1 collective-permute-done.73.refs_2_
  544.1 2.5 psum.7
  (310 shorter events, 119.3 us)
Async XLA Ops:
  7.2 88.9 %all-gather.7.cloned.1.call-start = ((), (), s32[]{:S(2)}) async-start(), calls=%async_computation.6 | async-start | bytes 4055040 | tf_op jit(solution)/shard_map/all_gather | solution.py:717
  29.0 196.6 %all-gather.9.cloned.1.call-start = ((), (), s32[]{:S(2)}) async-start(), calls=%async_computation.7 | async-start | bytes 7864320 | tf_op jit(solution)/shard_map/all_gather | solution.py:717
  31.8 14.9 %collective-permute-start.56 = (bf16[128,2048]{1,0:T(8,128)(2,1)S(1)}, bf16[128,2048]{1,0:T(8,128)(2,1)S(1)}, u32[]{:S(2)}, u32[]{:S(2)}) collective-permute-start(bf16[128,2048]{1,0:T(8,128)(2,1)S(1)} %get-tuple-element.611), channel_id=1, source_target_pairs={{0,2},{2,0},{4,6},{6,4},{1,3},{3,1},{5,7},{7,5},{8,10},{10,8},{12,... | collective-permute-start | bytes 1572872 | tf_op jit(solution)/shard_map/ppermute | solution.py:586
  33.0 22.6 %collective-permute-start.58 = (bf16[128,2048]{1,0:T(8,128)(2,1)S(1)}, bf16[128,2048]{1,0:T(8,128)(2,1)S(1)}, u32[]{:S(2)}, u32[]{:S(2)}) collective-permute-start(bf16[128,2048]{1,0:T(8,128)(2,1)S(1)} %get-tuple-element.611), channel_id=1, source_target_pairs={{0,4},{2,6},{4,0},{6,2},{1,5},{3,7},{5,1},{7,3},{8,12},{10,14},{12... | collective-permute-start | bytes 1572872 | tf_op jit(solution)/shard_map/ppermute | solution.py:586
  33.8 21.8 %collective-permute-start.57 = (bf16[128,2048]{1,0:T(8,128)(2,1)S(1)}, bf16[128,2048]{1,0:T(8,128)(2,1)S(1)}, u32[]{:S(2)}, u32[]{:S(2)}) collective-permute-start(bf16[128,2048]{1,0:T(8,128)(2,1)S(1)} %get-tuple-element.612), channel_id=1, source_target_pairs={{0,2},{2,0},{4,6},{6,4},{1,3},{3,1},{5,7},{7,5},{8,10},{10,8},{12,... | collective-permute-start | bytes 1572872 | tf_op jit(solution)/shard_map/ppermute | solution.py:586
  35.3 21.4 %collective-permute-start.59 = (bf16[128,2048]{1,0:T(8,128)(2,1)S(1)}, bf16[128,2048]{1,0:T(8,128)(2,1)S(1)}, u32[]{:S(2)}, u32[]{:S(2)}) collective-permute-start(bf16[128,2048]{1,0:T(8,128)(2,1)S(1)} %get-tuple-element.612), channel_id=1, source_target_pairs={{0,4},{2,6},{4,0},{6,2},{1,5},{3,7},{5,1},{7,3},{8,12},{10,14},{12... | collective-permute-start | bytes 1572872 | tf_op jit(solution)/shard_map/ppermute | solution.py:586
  57.1 16.3 %collective-permute-start.60 = (bf16[128,2304]{1,0:T(8,128)(2,1)S(1)}, bf16[128,2304]{1,0:T(8,128)(2,1)S(1)}, u32[]{:S(2)}, u32[]{:S(2)}) collective-permute-start(bf16[128,2304]{1,0:T(8,128)(2,1)S(1)} %get-tuple-element.781), channel_id=1, source_target_pairs={{0,2},{2,0},{4,6},{6,4},{1,3},{3,1},{5,7},{7,5},{8,10},{10,8},{12,... | collective-permute-start | bytes 1769480 | tf_op jit(solution)/shard_map/ppermute | solution.py:586
  58.3 28.9 %collective-permute-start.61 = (bf16[128,2304]{1,0:T(8,128)(2,1)S(1)}, bf16[128,2304]{1,0:T(8,128)(2,1)S(1)}, u32[]{:S(2)}, u32[]{:S(2)}) collective-permute-start(bf16[128,2304]{1,0:T(8,128)(2,1)S(1)} %get-tuple-element.780), channel_id=1, source_target_pairs={{0,4},{2,6},{4,0},{6,2},{1,5},{3,7},{5,1},{7,3},{8,12},{10,14},{12... | collective-permute-start | bytes 1769480 | tf_op jit(solution)/shard_map/ppermute | solution.py:586
  58.9 28.4 %collective-permute-start.62 = (bf16[128,2304]{1,0:T(8,128)(2,1)S(1)}, bf16[128,2304]{1,0:T(8,128)(2,1)S(1)}, u32[]{:S(2)}, u32[]{:S(2)}) collective-permute-start(bf16[128,2304]{1,0:T(8,128)(2,1)S(1)} %get-tuple-element.779), channel_id=1, source_target_pairs={{0,6},{2,4},{4,2},{6,0},{1,7},{3,5},{5,3},{7,1},{8,14},{10,12},{12... | collective-permute-start | bytes 1769480 | tf_op jit(solution)/shard_map/ppermute | solution.py:586
  60.7 34.6 %collective-permute-start.63 = (bf16[128,2048]{1,0:T(8,128)(2,1)S(1)}, bf16[128,2048]{1,0:T(8,128)(2,1)S(1)}, u32[]{:S(2)}, u32[]{:S(2)}) collective-permute-start(bf16[128,2048]{1,0:T(8,128)(2,1)S(1)} %collective-permute-done.56), channel_id=1, source_target_pairs={{0,4},{2,6},{4,0},{6,2},{1,5},{3,7},{5,1},{7,3},{8,12},{10,14},{12... | collective-permute-start | bytes 1572872 | tf_op jit(solution)/shard_map/ppermute | solution.py:586
  61.4 34.7 %collective-permute-start.64 = (bf16[128,2048]{1,0:T(8,128)(2,1)S(1)}, bf16[128,2048]{1,0:T(8,128)(2,1)}, u32[]{:S(2)}, u32[]{:S(2)}) collective-permute-start(bf16[128,2048]{1,0:T(8,128)(2,1)S(1)} %collective-permute-done.59), channel_id=1, source_target_pairs={{0,2},{2,0},{4,6},{6,4},{1,3},{3,1},{5,7},{7,5},{8,10},{10,8},{12,... | collective-permute-start | bytes 1572872 | tf_op jit(solution)/shard_map/ppermute | solution.py:586
  96.1 188.3 %all-gather.11.cloned.1.call-start = ((), (), s32[]{:S(2)}) async-start(), calls=%async_computation.8 | async-start | bytes 3932160 | tf_op jit(solution)/shard_map/all_gather | solution.py:717
  96.8 355.0 %reduce-scatter.4.cloned.1.call-start = ((), (), s32[]{:S(2)}) async-start(), calls=%async_computation.3 | async-start | bytes 7864320 | tf_op jit(solution)/shard_map/reduce_scatter | solution.py:818
  100.1 24.3 %collective-permute-start.65 = (bf16[128,2048]{1,0:T(8,128)(2,1)}, bf16[128,2048]{1,0:T(8,128)(2,1)}, u32[]{:S(2)}, u32[]{:S(2)}) collective-permute-start(bf16[128,2048]{1,0:T(8,128)(2,1)} %get-tuple-element.644), channel_id=1, source_target_pairs={{0,2},{2,0},{4,6},{6,4},{1,3},{3,1},{5,7},{7,5},{8,10},{10,8},{12,... | collective-permute-start | bytes 1572872 | tf_op jit(solution)/shard_map/ppermute | solution.py:586
  100.8 23.6 %collective-permute-start.67 = (bf16[128,2048]{1,0:T(8,128)(2,1)}, bf16[128,2048]{1,0:T(8,128)(2,1)}, u32[]{:S(2)}, u32[]{:S(2)}) collective-permute-start(bf16[128,2048]{1,0:T(8,128)(2,1)} %get-tuple-element.644), channel_id=1, source_target_pairs={{0,4},{2,6},{4,0},{6,2},{1,5},{3,7},{5,1},{7,3},{8,12},{10,14},{12... | collective-permute-start | bytes 1572872 | tf_op jit(solution)/shard_map/ppermute | solution.py:586
  101.7 22.7 %collective-permute-start.66 = (bf16[128,2048]{1,0:T(8,128)(2,1)}, bf16[128,2048]{1,0:T(8,128)(2,1)}, u32[]{:S(2)}, u32[]{:S(2)}) collective-permute-start(bf16[128,2048]{1,0:T(8,128)(2,1)} %get-tuple-element.645), channel_id=1, source_target_pairs={{0,2},{2,0},{4,6},{6,4},{1,3},{3,1},{5,7},{7,5},{8,10},{10,8},{12,... | collective-permute-start | bytes 1572872 | tf_op jit(solution)/shard_map/ppermute | solution.py:586
  102.5 22.6 %collective-permute-start.68 = (bf16[128,2048]{1,0:T(8,128)(2,1)}, bf16[128,2048]{1,0:T(8,128)(2,1)}, u32[]{:S(2)}, u32[]{:S(2)}) collective-permute-start(bf16[128,2048]{1,0:T(8,128)(2,1)} %get-tuple-element.645), channel_id=1, source_target_pairs={{0,4},{2,6},{4,0},{6,2},{1,5},{3,7},{5,1},{7,3},{8,12},{10,14},{12... | collective-permute-start | bytes 1572872 | tf_op jit(solution)/shard_map/ppermute | solution.py:586
  125.7 17.5 %collective-permute-start.2 = (bf16[1024,2048]{1,0:T(8,128)(2,1)}, bf16[1024,2048]{1,0:T(8,128)(2,1)}, u32[]{:S(2)}, u32[]{:S(2)}) collective-permute-start(bf16[1024,2048]{1,0:T(8,128)(2,1)} %get-tuple-element.262), channel_id=1, source_target_pairs={{0,1},{1,0},{2,3},{3,2},{4,5},{5,4},{6,7},{7,6},{8,9},{9,8},{10,11... | collective-permute-start | bytes 12582920 | tf_op jit(solution)/shard_map/cond/branch_1_fun/ppermute | solution.py:586
  125.9 14.5 %collective-permute-start.3 = (bf16[128,2048]{1,0:T(8,128)(2,1)}, bf16[128,2048]{1,0:T(8,128)(2,1)}, u32[]{:S(2)}, u32[]{:S(2)}) collective-permute-start(bf16[128,2048]{1,0:T(8,128)(2,1)} %get-tuple-element.273), channel_id=1, source_target_pairs={{0,4},{2,6},{4,0},{6,2},{1,5},{3,7},{5,1},{7,3},{8,12},{10,14},{12... | collective-permute-start | bytes 1572872 | tf_op jit(solution)/shard_map/cond/branch_1_fun/ppermute | solution.py:586
  126.6 14.4 %collective-permute-start.4 = (bf16[128,2048]{1,0:T(8,128)(2,1)}, bf16[128,2048]{1,0:T(8,128)(2,1)}, u32[]{:S(2)}, u32[]{:S(2)}) collective-permute-start(bf16[128,2048]{1,0:T(8,128)(2,1)} %get-tuple-element.274), channel_id=1, source_target_pairs={{0,2},{2,0},{4,6},{6,4},{1,3},{3,1},{5,7},{7,5},{8,10},{10,8},{12,... | collective-permute-start | bytes 1572872 | tf_op jit(solution)/shard_map/cond/branch_1_fun/ppermute | solution.py:586
  147.8 14.2 %collective-permute-start.19 = (bf16[128,2048]{1,0:T(8,128)(2,1)}, bf16[128,2048]{1,0:T(8,128)(2,1)S(1)}, u32[]{:S(2)}, u32[]{:S(2)}) collective-permute-start(bf16[128,2048]{1,0:T(8,128)(2,1)} %get-tuple-element.287), channel_id=1, source_target_pairs={{0,2},{2,0},{4,6},{6,4},{1,3},{3,1},{5,7},{7,5},{8,10},{10,8},{12,... | collective-permute-start | bytes 1572872 | tf_op jit(solution)/shard_map/cond/branch_1_fun/ppermute | solution.py:586
  148.7 13.9 %collective-permute-start.20 = (bf16[128,2048]{1,0:T(8,128)(2,1)}, bf16[128,2048]{1,0:T(8,128)(2,1)S(1)}, u32[]{:S(2)}, u32[]{:S(2)}) collective-permute-start(bf16[128,2048]{1,0:T(8,128)(2,1)} %get-tuple-element.288), channel_id=1, source_target_pairs={{0,4},{2,6},{4,0},{6,2},{1,5},{3,7},{5,1},{7,3},{8,12},{10,14},{12... | collective-permute-start | bytes 1572872 | tf_op jit(solution)/shard_map/cond/branch_1_fun/ppermute | solution.py:586
  162.6 15.1 %collective-permute-start.21 = (bf16[128,2048]{1,0:T(8,128)(2,1)}, bf16[128,2048]{1,0:T(8,128)(2,1)S(1)}, u32[]{:S(2)}, u32[]{:S(2)}) collective-permute-start(bf16[128,2048]{1,0:T(8,128)(2,1)} %get-tuple-element.289), channel_id=1, source_target_pairs={{0,2},{2,0},{4,6},{6,4},{1,3},{3,1},{5,7},{7,5},{8,10},{10,8},{12,... | collective-permute-start | bytes 1572872 | tf_op jit(solution)/shard_map/cond/branch_1_fun/ppermute | solution.py:586
  163.7 15.1 %collective-permute-start.24 = (bf16[128,2048]{1,0:T(8,128)(2,1)}, bf16[128,2048]{1,0:T(8,128)(2,1)S(1)}, u32[]{:S(2)}, u32[]{:S(2)}) collective-permute-start(bf16[128,2048]{1,0:T(8,128)(2,1)} %get-tuple-element.292), channel_id=1, source_target_pairs={{0,4},{2,6},{4,0},{6,2},{1,5},{3,7},{5,1},{7,3},{8,12},{10,14},{12... | collective-permute-start | bytes 1572872 | tf_op jit(solution)/shard_map/cond/branch_1_fun/ppermute | solution.py:586
  166.1 21.7 %collective-permute-start.22 = (bf16[128,2048]{1,0:T(8,128)(2,1)S(1)}, bf16[128,2048]{1,0:T(8,128)(2,1)S(1)}, u32[]{:S(2)}, u32[]{:S(2)}) collective-permute-start(bf16[128,2048]{1,0:T(8,128)(2,1)S(1)} %add_convert_fusion.1), channel_id=1, source_target_pairs={{0,4},{2,6},{4,0},{6,2},{1,5},{3,7},{5,1},{7,3},{8,12},{10,14},{12... | collective-permute-start | bytes 1572872 | tf_op jit(solution)/shard_map/cond/branch_1_fun/ppermute | solution.py:586
  168.1 19.7 %collective-permute-start.23 = (bf16[128,2048]{1,0:T(8,128)(2,1)S(1)}, bf16[128,2048]{1,0:T(8,128)(2,1)S(1)}, u32[]{:S(2)}, u32[]{:S(2)}) collective-permute-start(bf16[128,2048]{1,0:T(8,128)(2,1)S(1)} %add_convert_fusion), channel_id=1, source_target_pairs={{0,2},{2,0},{4,6},{6,4},{1,3},{3,1},{5,7},{7,5},{8,10},{10,8},{12,... | collective-permute-start | bytes 1572872 | tf_op jit(solution)/shard_map/cond/branch_1_fun/ppermute | solution.py:586
  190.5 15.2 %collective-permute-start.25 = (bf16[128,2048]{1,0:T(8,128)(2,1)}, bf16[128,2048]{1,0:T(8,128)(2,1)}, u32[]{:S(2)}, u32[]{:S(2)}) collective-permute-start(bf16[128,2048]{1,0:T(8,128)(2,1)} %get-tuple-element.887), channel_id=1, source_target_pairs={{0,2},{2,0},{4,6},{6,4},{1,3},{3,1},{5,7},{7,5},{8,10},{10,8},{12,... | collective-permute-start | bytes 1572872 | tf_op jit(solution)/shard_map/cond/branch_1_fun/ppermute | solution.py:586
  191.3 15.5 %collective-permute-start.28 = (bf16[128,2048]{1,0:T(8,128)(2,1)}, bf16[128,2048]{1,0:T(8,128)(2,1)}, u32[]{:S(2)}, u32[]{:S(2)}) collective-permute-start(bf16[128,2048]{1,0:T(8,128)(2,1)} %get-tuple-element.888), channel_id=1, source_target_pairs={{0,4},{2,6},{4,0},{6,2},{1,5},{3,7},{5,1},{7,3},{8,12},{10,14},{12... | collective-permute-start | bytes 1572872 | tf_op jit(solution)/shard_map/cond/branch_1_fun/ppermute | solution.py:586
  192.6 24.3 %collective-permute-start.26 = (bf16[128,2048]{1,0:T(8,128)(2,1)}, bf16[128,2048]{1,0:T(8,128)(2,1)}, u32[]{:S(2)}, u32[]{:S(2)}) collective-permute-start(bf16[128,2048]{1,0:T(8,128)(2,1)} %get-tuple-element.888), channel_id=1, source_target_pairs={{0,2},{2,0},{4,6},{6,4},{1,3},{3,1},{5,7},{7,5},{8,10},{10,8},{12,... | collective-permute-start | bytes 1572872 | tf_op jit(solution)/shard_map/cond/branch_1_fun/ppermute | solution.py:586
  193.7 24.1 %collective-permute-start.27 = (bf16[128,2048]{1,0:T(8,128)(2,1)}, bf16[128,2048]{1,0:T(8,128)(2,1)}, u32[]{:S(2)}, u32[]{:S(2)}) collective-permute-start(bf16[128,2048]{1,0:T(8,128)(2,1)} %get-tuple-element.887), channel_id=1, source_target_pairs={{0,4},{2,6},{4,0},{6,2},{1,5},{3,7},{5,1},{7,3},{8,12},{10,14},{12... | collective-permute-start | bytes 1572872 | tf_op jit(solution)/shard_map/cond/branch_1_fun/ppermute | solution.py:586
  205.6 20.0 %collective-permute-start.29 = (bf16[128,2048]{1,0:T(8,128)(2,1)}, bf16[128,2048]{1,0:T(8,128)(2,1)}, u32[]{:S(2)}, u32[]{:S(2)}) collective-permute-start(bf16[128,2048]{1,0:T(8,128)(2,1)} %collective-permute-done.25), channel_id=1, source_target_pairs={{0,4},{2,6},{4,0},{6,2},{1,5},{3,7},{5,1},{7,3},{8,12},{10,14},{12... | collective-permute-start | bytes 1572872 | tf_op jit(solution)/shard_map/cond/branch_1_fun/ppermute | solution.py:586
  206.8 18.8 %collective-permute-start.30 = (bf16[128,2048]{1,0:T(8,128)(2,1)}, bf16[128,2048]{1,0:T(8,128)(2,1)}, u32[]{:S(2)}, u32[]{:S(2)}) collective-permute-start(bf16[128,2048]{1,0:T(8,128)(2,1)} %collective-permute-done.28), channel_id=1, source_target_pairs={{0,2},{2,0},{4,6},{6,4},{1,3},{3,1},{5,7},{7,5},{8,10},{10,8},{12,... | collective-permute-start | bytes 1572872 | tf_op jit(solution)/shard_map/cond/branch_1_fun/ppermute | solution.py:586
  226.0 17.6 %collective-permute-start.6 = (bf16[4,512,1536]{2,1,0:T(8,128)(2,1)}, bf16[4,512,1536]{2,1,0:T(8,128)(2,1)}, u32[]{:S(2)}, u32[]{:S(2)}) collective-permute-start(bf16[4,512,1536]{2,1,0:T(8,128)(2,1)} %get-tuple-element.297.refs_16_.refs_17_.refs_18_), channel_id=1, source_target_pairs={{0,1},{1,0},{2,3},{3,2},{4,5},{5,4},{6,7},{7,6},{8,9},{9,8},{10,11... | collective-permute-start | bytes 18874376 | tf_op jit(solution)/shard_map/cond/branch_1_fun/ppermute | solution.py:586
  243.0 14.9 %collective-permute-start.7 = (bf16[1024,2048]{1,0:T(8,128)(2,1)}, bf16[1024,2048]{1,0:T(8,128)(2,1)}, u32[]{:S(2)}, u32[]{:S(2)}) collective-permute-start(bf16[1024,2048]{1,0:T(8,128)(2,1)} %get-tuple-element.906.refs_0_), channel_id=1, source_target_pairs={{0,1},{1,0},{2,3},{3,2},{4,5},{5,4},{6,7},{7,6},{8,9},{9,8},{10,11... | collective-permute-start | bytes 12582920 | tf_op jit(solution)/shard_map/cond/branch_1_fun/ppermute | solution.py:586
  243.5 14.3 %collective-permute-start.8 = (bf16[1024,2048]{1,0:T(8,128)(2,1)}, bf16[1024,2048]{1,0:T(8,128)(2,1)}, u32[]{:S(2)}, u32[]{:S(2)}) collective-permute-start(bf16[1024,2048]{1,0:T(8,128)(2,1)} %get-tuple-element.908.refs_1_.refs_2_), channel_id=1, source_target_pairs={{0,1},{1,0},{2,3},{3,2},{4,5},{5,4},{6,7},{7,6},{8,9},{9,8},{10,11... | collective-permute-start | bytes 12582920 | tf_op jit(solution)/shard_map/cond/branch_1_fun/ppermute | solution.py:586
  284.4 228.3 %reduce-scatter.6.cloned.1.call-start = ((), (), s32[]{:S(2)}) async-start(), calls=%async_computation.4 | async-start | bytes 3932160 | tf_op jit(solution)/shard_map/reduce_scatter | solution.py:818
  312.6 17.7 %collective-permute-start.33 = (bf16[128,2048]{1,0:T(8,128)(2,1)}, bf16[128,2048]{1,0:T(8,128)(2,1)}, u32[]{:S(2)}, u32[]{:S(2)}) collective-permute-start(bf16[128,2048]{1,0:T(8,128)(2,1)} %get-tuple-element.333), channel_id=1, source_target_pairs={{0,4},{2,6},{4,0},{6,2},{1,5},{3,7},{5,1},{7,3},{8,12},{10,14},{12... | collective-permute-start | bytes 1572872 | tf_op jit(solution)/shard_map/cond/branch_1_fun/ppermute | solution.py:586
  313.9 18.8 %collective-permute-start.32 = (bf16[128,2048]{1,0:T(8,128)(2,1)}, bf16[128,2048]{1,0:T(8,128)(2,1)}, u32[]{:S(2)}, u32[]{:S(2)}) collective-permute-start(bf16[128,2048]{1,0:T(8,128)(2,1)} %get-tuple-element.332), channel_id=1, source_target_pairs={{0,2},{2,0},{4,6},{6,4},{1,3},{3,1},{5,7},{7,5},{8,10},{10,8},{12,... | collective-permute-start | bytes 1572872 | tf_op jit(solution)/shard_map/cond/branch_1_fun/ppermute | solution.py:586
  315.1 24.5 %collective-permute-start.38 = (bf16[1024,512]{1,0:T(8,128)(2,1)S(1)}, bf16[1024,512]{1,0:T(8,128)(2,1)}, u32[]{:S(2)}, u32[]{:S(2)}) collective-permute-start(bf16[1024,512]{1,0:T(8,128)(2,1)S(1)} %copy-done.13), channel_id=1, source_target_pairs={{0,1},{1,0},{2,3},{3,2},{4,5},{5,4},{6,7},{7,6},{8,9},{9,8},{10,11... | collective-permute-start | bytes 3145736 | tf_op jit(solution)/shard_map/cond/branch_1_fun/ppermute | solution.py:586
  315.1 21.0 %collective-permute-start.39 = (bf16[1024,256]{1,0:T(8,128)(2,1)S(1)}, bf16[1024,256]{1,0:T(8,128)(2,1)}, u32[]{:S(2)}, u32[]{:S(2)}) collective-permute-start(bf16[1024,256]{1,0:T(8,128)(2,1)S(1)} %get-tuple-element.935), channel_id=1, source_target_pairs={{0,1},{1,0},{2,3},{3,2},{4,5},{5,4},{6,7},{7,6},{8,9},{9,8},{10,11... | collective-permute-start | bytes 1572872 | tf_op jit(solution)/shard_map/cond/branch_1_fun/ppermute | solution.py:586
  331.7 20.4 %collective-permute-start.36 = (bf16[128,2048]{1,0:T(8,128)(2,1)S(1)}, bf16[128,2048]{1,0:T(8,128)(2,1)}, u32[]{:S(2)}, u32[]{:S(2)}) collective-permute-start(bf16[128,2048]{1,0:T(8,128)(2,1)S(1)} %add_convert_fusion.2), channel_id=1, source_target_pairs={{0,2},{2,0},{4,6},{6,4},{1,3},{3,1},{5,7},{7,5},{8,10},{10,8},{12,... | collective-permute-start | bytes 1572872 | tf_op jit(solution)/shard_map/cond/branch_1_fun/ppermute | solution.py:586
  334.0 18.2 %collective-permute-start.35 = (bf16[128,2048]{1,0:T(8,128)(2,1)S(1)}, bf16[128,2048]{1,0:T(8,128)(2,1)}, u32[]{:S(2)}, u32[]{:S(2)}) collective-permute-start(bf16[128,2048]{1,0:T(8,128)(2,1)S(1)} %add_convert_fusion.3), channel_id=1, source_target_pairs={{0,4},{2,6},{4,0},{6,2},{1,5},{3,7},{5,1},{7,3},{8,12},{10,14},{12... | collective-permute-start | bytes 1572872 | tf_op jit(solution)/shard_map/cond/branch_1_fun/ppermute | solution.py:586
  334.8 22.2 %collective-permute-start.34 = (bf16[128,2048]{1,0:T(8,128)(2,1)S(1)}, bf16[128,2048]{1,0:T(8,128)(2,1)}, u32[]{:S(2)}, u32[]{:S(2)}) collective-permute-start(bf16[128,2048]{1,0:T(8,128)(2,1)S(1)} %copy-done.38), channel_id=1, source_target_pairs={{0,2},{2,0},{4,6},{6,4},{1,3},{3,1},{5,7},{7,5},{8,10},{10,8},{12,... | collective-permute-start | bytes 1572872 | tf_op jit(solution)/shard_map/cond/branch_1_fun/ppermute | solution.py:586
  336.1 23.0 %collective-permute-start.37 = (bf16[128,2048]{1,0:T(8,128)(2,1)S(1)}, bf16[128,2048]{1,0:T(8,128)(2,1)}, u32[]{:S(2)}, u32[]{:S(2)}) collective-permute-start(bf16[128,2048]{1,0:T(8,128)(2,1)S(1)} %copy-done.37), channel_id=1, source_target_pairs={{0,4},{2,6},{4,0},{6,2},{1,5},{3,7},{5,1},{7,3},{8,12},{10,14},{12... | collective-permute-start | bytes 1572872 | tf_op jit(solution)/shard_map/cond/branch_1_fun/ppermute | solution.py:586
  359.2 170.3 %reduce-scatter.8.cloned.1.call-start = ((), (), s32[]{:S(2)}) async-start(), calls=%async_computation.5 | async-start | bytes 4055040 | tf_op jit(solution)/shard_map/reduce_scatter | solution.py:818
  365.7 15.2 %collective-permute-start.11 = (bf16[128,2048]{1,0:T(8,128)(2,1)}, bf16[128,2048]{1,0:T(8,128)(2,1)}, u32[]{:S(2)}, u32[]{:S(2)}) collective-permute-start(bf16[128,2048]{1,0:T(8,128)(2,1)} %get-tuple-element.951), channel_id=1, source_target_pairs={{0,2},{2,0},{4,6},{6,4},{1,3},{3,1},{5,7},{7,5},{8,10},{10,8},{12,... | collective-permute-start | bytes 1572872 | tf_op jit(solution)/shard_map/cond/branch_1_fun/ppermute | solution.py:586
  366.9 15.2 %collective-permute-start.14 = (bf16[128,2048]{1,0:T(8,128)(2,1)}, bf16[128,2048]{1,0:T(8,128)(2,1)}, u32[]{:S(2)}, u32[]{:S(2)}) collective-permute-start(bf16[128,2048]{1,0:T(8,128)(2,1)} %get-tuple-element.952), channel_id=1, source_target_pairs={{0,4},{2,6},{4,0},{6,2},{1,5},{3,7},{5,1},{7,3},{8,12},{10,14},{12... | collective-permute-start | bytes 1572872 | tf_op jit(solution)/shard_map/cond/branch_1_fun/ppermute | solution.py:586
  367.7 24.3 %collective-permute-start.12 = (bf16[128,2048]{1,0:T(8,128)(2,1)}, bf16[128,2048]{1,0:T(8,128)(2,1)}, u32[]{:S(2)}, u32[]{:S(2)}) collective-permute-start(bf16[128,2048]{1,0:T(8,128)(2,1)} %get-tuple-element.952), channel_id=1, source_target_pairs={{0,2},{2,0},{4,6},{6,4},{1,3},{3,1},{5,7},{7,5},{8,10},{10,8},{12,... | collective-permute-start | bytes 1572872 | tf_op jit(solution)/shard_map/cond/branch_1_fun/ppermute | solution.py:586
  368.6 24.8 %collective-permute-start.13 = (bf16[128,2048]{1,0:T(8,128)(2,1)}, bf16[128,2048]{1,0:T(8,128)(2,1)}, u32[]{:S(2)}, u32[]{:S(2)}) collective-permute-start(bf16[128,2048]{1,0:T(8,128)(2,1)} %get-tuple-element.951), channel_id=1, source_target_pairs={{0,4},{2,6},{4,0},{6,2},{1,5},{3,7},{5,1},{7,3},{8,12},{10,14},{12... | collective-permute-start | bytes 1572872 | tf_op jit(solution)/shard_map/cond/branch_1_fun/ppermute | solution.py:586
  382.1 20.1 %collective-permute-start.15 = (bf16[128,2048]{1,0:T(8,128)(2,1)}, bf16[128,2048]{1,0:T(8,128)(2,1)}, u32[]{:S(2)}, u32[]{:S(2)}) collective-permute-start(bf16[128,2048]{1,0:T(8,128)(2,1)} %collective-permute-done.11), channel_id=1, source_target_pairs={{0,4},{2,6},{4,0},{6,2},{1,5},{3,7},{5,1},{7,3},{8,12},{10,14},{12... | collective-permute-start | bytes 1572872 | tf_op jit(solution)/shard_map/cond/branch_1_fun/ppermute | solution.py:586
  382.9 19.2 %collective-permute-start.16 = (bf16[128,2048]{1,0:T(8,128)(2,1)}, bf16[128,2048]{1,0:T(8,128)(2,1)}, u32[]{:S(2)}, u32[]{:S(2)}) collective-permute-start(bf16[128,2048]{1,0:T(8,128)(2,1)} %collective-permute-done.14), channel_id=1, source_target_pairs={{0,2},{2,0},{4,6},{6,4},{1,3},{3,1},{5,7},{7,5},{8,10},{10,8},{12,... | collective-permute-start | bytes 1572872 | tf_op jit(solution)/shard_map/cond/branch_1_fun/ppermute | solution.py:586
  402.2 49.5 %collective-permute-start.69 = (bf16[256,2048]{1,0:T(8,128)(2,1)}, bf16[256,2048]{1,0:T(8,128)(2,1)}, u32[]{:S(2)}, u32[]{:S(2)}) collective-permute-start(bf16[256,2048]{1,0:T(8,128)(2,1)} %get-tuple-element.693), channel_id=1, source_target_pairs={{0,2},{2,0},{4,6},{6,4},{1,3},{3,1},{5,7},{7,5},{8,10},{10,8},{12,... | collective-permute-start | bytes 3145736 | tf_op jit(solution)/shard_map/ppermute | solution.py:586
  403.0 48.7 %collective-permute-start.70 = (bf16[256,2048]{1,0:T(8,128)(2,1)}, bf16[256,2048]{1,0:T(8,128)(2,1)}, u32[]{:S(2)}, u32[]{:S(2)}) collective-permute-start(bf16[256,2048]{1,0:T(8,128)(2,1)} %get-tuple-element.694), channel_id=1, source_target_pairs={{0,4},{2,6},{4,0},{6,2},{1,5},{3,7},{5,1},{7,3},{8,12},{10,14},{12... | collective-permute-start | bytes 3145736 | tf_op jit(solution)/shard_map/ppermute | solution.py:586
  403.8 48.0 %collective-permute-start.71 = (bf16[256,2048]{1,0:T(8,128)(2,1)}, bf16[256,2048]{1,0:T(8,128)(2,1)}, u32[]{:S(2)}, u32[]{:S(2)}) collective-permute-start(bf16[256,2048]{1,0:T(8,128)(2,1)} %get-tuple-element.695), channel_id=1, source_target_pairs={{0,6},{2,4},{4,2},{6,0},{1,7},{3,5},{5,3},{7,1},{8,14},{10,12},{12... | collective-permute-start | bytes 3145736 | tf_op jit(solution)/shard_map/ppermute | solution.py:586
  413.1 24.6 %collective-permute-start.17 = (bf16[1024,2048]{1,0:T(8,128)(2,1)}, bf16[1024,2048]{1,0:T(8,128)(2,1)}, u32[]{:S(2)}, u32[]{:S(2)}) collective-permute-start(bf16[1024,2048]{1,0:T(8,128)(2,1)} %get-tuple-element.968), channel_id=1, source_target_pairs={{0,1},{1,0},{2,3},{3,2},{4,5},{5,4},{6,7},{7,6},{8,9},{9,8},{10,11... | collective-permute-start | bytes 12582920 | tf_op jit(solution)/shard_map/cond/branch_1_fun/ppermute | solution.py:586
  458.5 15.1 %collective-permute-start.41 = (bf16[128,2048]{1,0:T(8,128)(2,1)}, bf16[128,2048]{1,0:T(8,128)(2,1)}, u32[]{:S(2)}, u32[]{:S(2)}) collective-permute-start(bf16[128,2048]{1,0:T(8,128)(2,1)} %get-tuple-element.413), channel_id=1, source_target_pairs={{0,2},{2,0},{4,6},{6,4},{1,3},{3,1},{5,7},{7,5},{8,10},{10,8},{12,... | collective-permute-start | bytes 1572872 | tf_op jit(solution)/shard_map/cond/branch_1_fun/ppermute | solution.py:586
  459.3 15.1 %collective-permute-start.42 = (bf16[128,2048]{1,0:T(8,128)(2,1)}, bf16[128,2048]{1,0:T(8,128)(2,1)}, u32[]{:S(2)}, u32[]{:S(2)}) collective-permute-start(bf16[128,2048]{1,0:T(8,128)(2,1)} %get-tuple-element.414), channel_id=1, source_target_pairs={{0,4},{2,6},{4,0},{6,2},{1,5},{3,7},{5,1},{7,3},{8,12},{10,14},{12... | collective-permute-start | bytes 1572872 | tf_op jit(solution)/shard_map/cond/branch_1_fun/ppermute | solution.py:586
  462.7 19.3 %collective-permute-start.47 = (bf16[128,1536]{1,0:T(8,128)(2,1)S(1)}, bf16[128,1536]{1,0:T(8,128)(2,1)}, u32[]{:S(2)}, u32[]{:S(2)}) collective-permute-start(bf16[128,1536]{1,0:T(8,128)(2,1)S(1)} %get-tuple-element.761), channel_id=1, source_target_pairs={{0,2},{2,0},{4,6},{6,4},{1,3},{3,1},{5,7},{7,5},{8,10},{10,8},{12,... | collective-permute-start | bytes 1179656 | tf_op jit(solution)/shard_map/cond/branch_1_fun/ppermute | solution.py:586
  463.5 19.4 %collective-permute-start.48 = (bf16[128,1536]{1,0:T(8,128)(2,1)S(1)}, bf16[128,1536]{1,0:T(8,128)(2,1)}, u32[]{:S(2)}, u32[]{:S(2)}) collective-permute-start(bf16[128,1536]{1,0:T(8,128)(2,1)S(1)} %get-tuple-element.760), channel_id=1, source_target_pairs={{0,4},{2,6},{4,0},{6,2},{1,5},{3,7},{5,1},{7,3},{8,12},{10,14},{12... | collective-permute-start | bytes 1179656 | tf_op jit(solution)/shard_map/cond/branch_1_fun/ppermute | solution.py:586
  474.5 37.9 %collective-permute-start.43 = (bf16[128,2048]{1,0:T(8,128)(2,1)}, bf16[128,2048]{1,0:T(8,128)(2,1)}, u32[]{:S(2)}, u32[]{:S(2)}) collective-permute-start(bf16[128,2048]{1,0:T(8,128)(2,1)} %get-tuple-element.415), channel_id=1, source_target_pairs={{0,2},{2,0},{4,6},{6,4},{1,3},{3,1},{5,7},{7,5},{8,10},{10,8},{12,... | collective-permute-start | bytes 1572872 | tf_op jit(solution)/shard_map/cond/branch_1_fun/ppermute | solution.py:586
  475.6 36.8 %collective-permute-start.46 = (bf16[128,2048]{1,0:T(8,128)(2,1)}, bf16[128,2048]{1,0:T(8,128)(2,1)}, u32[]{:S(2)}, u32[]{:S(2)}) collective-permute-start(bf16[128,2048]{1,0:T(8,128)(2,1)} %get-tuple-element.418), channel_id=1, source_target_pairs={{0,4},{2,6},{4,0},{6,2},{1,5},{3,7},{5,1},{7,3},{8,12},{10,14},{12... | collective-permute-start | bytes 1572872 | tf_op jit(solution)/shard_map/cond/branch_1_fun/ppermute | solution.py:586
  477.7 35.0 %collective-permute-start.44 = (bf16[128,2048]{1,0:T(8,128)(2,1)S(1)}, bf16[128,2048]{1,0:T(8,128)(2,1)}, u32[]{:S(2)}, u32[]{:S(2)}) collective-permute-start(bf16[128,2048]{1,0:T(8,128)(2,1)S(1)} %add_convert_fusion.5), channel_id=1, source_target_pairs={{0,4},{2,6},{4,0},{6,2},{1,5},{3,7},{5,1},{7,3},{8,12},{10,14},{12... | collective-permute-start | bytes 1572872 | tf_op jit(solution)/shard_map/cond/branch_1_fun/ppermute | solution.py:586
  482.0 30.7 %collective-permute-start.45 = (bf16[128,2048]{1,0:T(8,128)(2,1)S(1)}, bf16[128,2048]{1,0:T(8,128)(2,1)}, u32[]{:S(2)}, u32[]{:S(2)}) collective-permute-start(bf16[128,2048]{1,0:T(8,128)(2,1)S(1)} %add_convert_fusion.4), channel_id=1, source_target_pairs={{0,2},{2,0},{4,6},{6,4},{1,3},{3,1},{5,7},{7,5},{8,10},{10,8},{12,... | collective-permute-start | bytes 1572872 | tf_op jit(solution)/shard_map/cond/branch_1_fun/ppermute | solution.py:586
  482.9 29.5 %collective-permute-start.49 = (bf16[128,1536]{1,0:T(8,128)(2,1)S(1)}, bf16[128,1536]{1,0:T(8,128)(2,1)}, u32[]{:S(2)}, u32[]{:S(2)}) collective-permute-start(bf16[128,1536]{1,0:T(8,128)(2,1)S(1)} %get-tuple-element.759), channel_id=1, source_target_pairs={{0,6},{2,4},{4,2},{6,0},{1,7},{3,5},{5,3},{7,1},{8,14},{10,12},{12... | collective-permute-start | bytes 1179656 | tf_op jit(solution)/shard_map/cond/branch_1_fun/ppermute | solution.py:586
  (60 other events, 699.3 us)
Sparse Core Ops, SparseCore 0:
  29.1 65.4 all-gather.6
  96.8 114.2 all-gather.8
  212.6 61.7 all-gather.10
  284.5 111.4 reduce-scatter.3
  398.1 60.7 reduce-scatter.5
  461.1 61.8 reduce-scatter.7

commit v4 on v3

--- a/solution.py
+++ b/solution.py
@@ -196,16 +196,12 @@
     return pl.BlockSpec(shape, lambda i: zeros, pipeline_mode=pl.Buffered(1))
 
 
-def project_kernel(count, few, *refs):
+def project_kernel(count, *refs):
     lefts, rights, outs = refs[:count], refs[count : 2 * count], refs[2 * count :]
 
-    def product(left, right):
-        return dot_right_t(right[0], left[...]) if few else dot_right_t(left[...], right[0])
-
-    total = product(lefts[0], rights[0])
+    total = dot_right_t(lefts[0][...], rights[0][0])
     for left, right in zip(lefts[1:], rights[1:]):
-        total = total + product(left, right)
-    total = total.T if few else total
+        total = total + dot_right_t(left[...], right[0])
     first = 0
     for out in outs:
         out[...] = total[first : first + out.shape[0]].astype(out.dtype)
@@ -226,7 +222,7 @@
 
     return list(
         pl.pallas_call(
-            functools.partial(project_kernel, len(lefts), bool(first)),
+            functools.partial(project_kernel, len(lefts)),
             grid=(parts,),
             in_specs=[left_spec(left) for left in lefts]
             + [right_spec(left, place) for left, place in zip(lefts, places)],
@@ -242,14 +238,14 @@
     )
 
 
-def project_and_send(lefts, rights, places, rows, step, name):
+def project_and_send(lefts, rights, places, rows, step, name, near_too=True):
     if lax.axis_size("model") == 1:
         return project(lefts, rights, places, 0, [rows], step, name)[0], [], []
     half = rows // 2
     far = project(lefts, rights, places, 3 * rows, [half] * 2, step, name + "_far")
     got = [trade(far[0], "model", 1), trade(far[1], "model", 2)]
     own, *near = project(lefts, rights, places, 0, [rows] + [half] * 4, step, name)
-    return own, got, send_near(near, got)
+    return own, got, send_near(near, got) if near_too else near
 
 
 def put_rows(whole, pieces, change):
@@ -488,18 +484,37 @@
     )(me.reshape(1), *operands)
 
 
-def hidden_kernel(first, cores, x_count, g_count, tiles, *refs):
+def join_kernel(*refs):
+    put_rows(refs[-1], refs[:-1], lambda rows: rows)
+
+
+def join(pieces, name):
+    rows, width = sum(piece.shape[0] for piece in pieces), pieces[0].shape[1]
+    return pl.pallas_call(
+        join_kernel,
+        grid=(1,),
+        in_specs=[resident(piece.shape) for piece in pieces],
+        out_specs=resident((rows, width)),
+        out_shape=jax.ShapeDtypeStruct((rows, width), pieces[0].dtype),
+        compiler_params=pltpu.CompilerParams(vmem_limit_bytes=32 << 20),
+        cost_estimate=BESIDE,
+        name=name,
+    )(*pieces)
+
+
+def hidden_kernel(first, cores, x_count, tiles, *refs):
     refs = list(refs)
 
     def pop(number):
         taken, refs[:number] = refs[:number], []
         return taken
 
-    x_pieces, g_pieces = (pop(x_count), pop(g_count)) if first else ([], [])
-    x_all, g_all = (None, None) if first else pop(2)
+    x_pieces = pop(x_count)
+    g_all = pop(1)[0]
+    x_all = x_pieces[0]
     weights = [pop(3) for _ in range(cores)]
     if first:
-        x_all, g_all = pop(2)
+        x_all = pop(1)[0]
     grads_out, acts_out = pop(cores), pop(cores)
     step = pl.program_id(0)
 
@@ -508,7 +523,6 @@
         @pl.when(step == 0)
         def _():
             put_rows(x_all, x_pieces, lambda rows: rows)
-            put_rows(g_all, g_pieces, lambda rows: rows)
 
     def one_core(j):
         w_gate, w_up, w_down = (ref[...].reshape(-1, ref.shape[2]) for ref in weights[j])
@@ -532,7 +546,7 @@
         pl.when((step >= j * tiles) & (step < (j + 1) * tiles))(functools.partial(one_core, j))
 
 
-def hidden_call(x_pieces, g_pieces, weights, name):
+def hidden_call(x_pieces, g_all, weights, name):
     cores, first = len(weights), len(x_pieces) > 1
     data, near, columns = weights[0].shape
     width = data * near
@@ -550,17 +564,17 @@
             for k in range(3)
         ]
 
-    operands = list(x_pieces) + list(g_pieces)
+    operands = list(x_pieces) + [g_all]
     in_specs = [resident(array.shape) for array in operands]
     for j, weight in enumerate(weights):
         in_specs += weight_specs(j)
         operands += [weight] * 3
-    shapes = [jax.ShapeDtypeStruct((rows, width), bf16)] * 2 if first else []
+    shapes = [jax.ShapeDtypeStruct((rows, width), bf16)] if first else []
     shapes += [jax.ShapeDtypeStruct((rows, 2 * units), bf16)] * cores
     shapes += [jax.ShapeDtypeStruct((rows, units), bf16)] * cores
     got = pl.pallas_call(
         functools.partial(
-            hidden_kernel, first, cores, len(x_pieces), len(g_pieces), tiles
+            hidden_kernel, first, cores, len(x_pieces), tiles
         ),
         grid=(cores * tiles,),
         in_specs=in_specs,
@@ -571,8 +585,8 @@
         name=name,
     )(*operands)
     got = list(got)
-    kept, got = (got[:2], got[2:]) if first else ([x_pieces[0], g_pieces[0]], got)
-    return kept, got[:cores], got[cores:]
+    whole, got = (got[0], got[1:]) if first else (x_pieces[0], got)
+    return whole, got[:cores], got[cores:]
 
 
 def phase(always, body):
@@ -806,11 +820,11 @@
             [((seq_len, cols), f32), ((seq_len, q_cols), bf16)],
         )
         attended, far = lax.optimization_barrier((list(attended), far))
-        att_pieces = [attended[0]] + [trade(attended[j], "tp", j) for j in range(1, cores)]
-        att_flat = [piece.reshape(-1, q_cols) for piece in att_pieces]
-        return with_cores(own_normed)[1:], att_flat, attended, far
-
-    normed_others, att_flat, attended, grad_far = phase(always, attention_phase)
+        got = [trade(attended[j], "tp", j) for j in range(1, cores)]
+        return with_cores(own_normed)[1:], got, attended, far
+
+    normed_others, got, attended, grad_far = phase(always, attention_phase)
+    att_flat = [piece.reshape(-1, q_cols) for piece in [attended[0]] + got]
     normed_in = [own_normed] + normed_others
     grad_blocks = grad_near + grad_far
 
@@ -821,11 +835,12 @@
         own, _, got = project_and_send(
             att_flat, w_attn, o_place, half, near_rows, "attention_out"
         )
+        own_grad = join(after(grad_blocks, own), "out_grad_rows")
         middle, *low = rows_call("norm", own, hidden_in, got, gain_mid, None, True, "middle")
         near = spread_near(low)
-        return middle, near + spread_far(near)
-
-    middle, mid_blocks = phase(always, out_phase)
+        return middle, near + spread_far(near), own_grad
+
+    middle, mid_blocks, own_grad = phase(always, out_phase)
 
     def for_own_core(rows):
         return [
@@ -838,19 +853,20 @@
 
     def first_phase():
         weights = with_cores(mlp_full[0])
-        rows, *by_core = hidden_call(mid_blocks, grad_blocks, weights[:1], "hidden_units_a")
-        kept = [with_cores(whole) for whole in rows]
+        whole, *by_core = hidden_call(mid_blocks, own_grad, weights[:1], "hidden_units_a")
+        normed_mid, grad_all = with_cores(whole), with_cores(own_grad)
         by_core = [by_core]
         for weight in weights[1:]:
-            got = hidden_call(*[[whole] for whole in rows], [weight], "hidden_units_a_other")
+            got = hidden_call([whole], own_grad, [weight], "hidden_units_a_other")
             by_core.append(got[1:])
         first_rows = [[got[k][0] for got in by_core] for k in range(2)]
+        kept = [normed_mid, grad_all]
         total = hidden_weights(kept, for_own_core(first_rows), "hidden_weights_a")
-        return weights[1:], kept, first_rows, total
-
-    other_weights, kept, first_rows, total = phase(always, first_phase)
+        return weights[1:], normed_mid, grad_all[1:], first_rows, total
+
+    other_weights, normed_mid, grad_others, first_rows, total = phase(always, first_phase)
+    kept = [normed_mid, [own_grad] + grad_others]
     w_mlp = [[mlp_full[0]] + other_weights]
-    wholes = [[kept[k][0]] for k in range(2)]
     mlp_sums = []
     if len(chunks) > 1:
         mlp_sums.append(data_sum(total))
@@ -861,7 +877,8 @@
         if len(chunks) > 1:
             weights.append(with_cores(mlp_full[1]))
             by_core = [
-                hidden_call(*wholes, [weight], "hidden_units_b")[1:] for weight in weights[1]
+                hidden_call([normed_mid[0]], own_grad, [weight], "hidden_units_b")[1:]
+                for weight in weights[1]
             ]
             rows.append([[got[k][0] for got in by_core] for k in range(2)])
         both_cores = [w for pair in weights for w in pair]
@@ -896,6 +913,8 @@
         return middle_grad, branch_blocks, down_parts
 
     middle_grad, branch_blocks, down_parts = phase(always, branch_phase)
+    tied = lax.optimization_barrier((branch_blocks, down_parts, mlp_sums[0]))
+    branch_blocks, down_parts, mlp_sums[0] = tied
     down_got = [trade(down_parts[k], "model", k) for k in range(1, model)]
 
     def attend_back_phase():
@@ -940,46 +959,46 @@
     attn_total, back_flat = phase(always, attention_weights_phase)
     attn_total, down_got = lax.optimization_barrier((attn_total, down_got))
     attn_sum = data_sum(attn_total)
-    back_flat, first_sums = lax.optimization_barrier((back_flat, mlp_sums[:-1]))
-
-    def exchanged(total):
-        return swap(rows_at(total.reshape(model, shard, -1)))
-
     def in_grad_phase():
-        own, far, got = project_and_send(
-            back_flat, w_attn, [0] * cores, half, near_rows, "normed_in_grad"
+        return project_and_send(
+            back_flat, w_attn, [0] * cores, half, near_rows, "normed_in_grad", False
         )
+
+    in_part, in_far, in_near = phase(always, in_grad_phase)
+    in_near, sums = lax.optimization_barrier((in_near, mlp_sums))
+
+    def last_phase():
+        in_got = send_near(in_near, in_far) if model > 1 else []
+        rows = jnp.concatenate([total.reshape(model, shard, -1) for total in sums], axis=2)
+        mlp_got = swap(rows_at(after(rows, *in_got)))
         hidden_out = rows_call(
-            "sum", down_parts[0], middle, after(down_got, *far), None, None, False, "hidden_out_sum"
+            "sum", down_parts[0], middle, after(down_got, *in_got), None, None, False, "hidden_out_sum"
         )[0]
-        return own, got, [exchanged(total) for total in first_sums], hidden_out
-
-    in_part, in_got, first_got, hidden_out = phase(always, in_grad_phase)
-    in_got, last_sum = lax.optimization_barrier((in_got, mlp_sums[-1]))
-
-    def last_phase():
-        last_got = exchanged(last_sum)
         grad_in = rows_call(
             "back", in_part, hidden_in, in_got, gain_in, middle_grad, False, "grad_in"
         )[0]
-        layout = [
-            [(kind, first, ff, size, kind == 2) for kind in range(3)]
-            for first, size in zip(starts, chunks)
-        ]
-        shapes = [w_gate.shape, w_up.shape, w_down.shape]
-        owned = owned_call(
-            me, first_got + [last_got], layout, [w_gate, w_up], mlp_gain, shapes, "hidden_owned"
-        )
-        return grad_in, owned[:3], owned[3][:, 0]
-
-    got = phase(always, last_phase)
-    grad_in, (grad_gate, grad_up, grad_down), mlp_part = got
+        return hidden_out, grad_in, mlp_got
+
+    hidden_out, grad_in, mlp_got = phase(always, last_phase)
     attn_sum = after(attn_sum, grad_in)
     weight_rows = attn_sum[:near_rows].reshape(model, shard, wide)
     gain_row = attn_sum[near_rows:]
     gain_row = jnp.broadcast_to(gain_row, (model,) + gain_row.shape)
     attn_rows = jnp.concatenate([weight_rows, gain_row], axis=1)
     attn_got = swap(rows_at(attn_rows))
+    layout = [
+        [
+            (kind, first, ff, size, kind == 2)
+            for first, size in zip(starts, chunks)
+            for kind in range(3)
+        ]
+    ]
+    shapes = [w_gate.shape, w_up.shape, w_down.shape]
+    mlp_got = after(mlp_got, attn_rows)
+    owned = owned_call(
+        me, [mlp_got], layout, [w_gate, w_up], mlp_gain, shapes, "hidden_owned"
+    )
+    grad_gate, grad_up, grad_down, mlp_part = owned[:4]
     layout = [
         [
             (0, 0, q_cols, q_cols, False),
@@ -993,7 +1012,7 @@
     owned = owned_call(me, [attn_got], layout, weights, attn_gain, shapes, "attention_owned")
     grad_query, grad_key, grad_value, grad_output, attn_part, gain_sums = owned
     gain_sums = gain_sums[:ride_rows].reshape(-1)[: 2 * head_size]
-    sums = lax.psum(jnp.concatenate([attn_part[:, 0], mlp_part, gain_sums]), "tp")
+    sums = lax.psum(jnp.concatenate([attn_part[:, 0], mlp_part[:, 0], gain_sums]), "tp")
     where = lax.axis_index("data") * model + lax.axis_index("model")
     first = 2 * shard + where * part
     return (

time: 563 us -> 558 us (level)
  waiting for transfers between devices: 196 us -> 190 us
    ppermute x75 -> x72, waiting for transfers between devices: 195 us -> 190 us  [trade(): lax.ppermute(block, axis, [(i, i ^ step) for i in range(lax.axis_size(axi...]
    ppermute x75 -> x72, starting transfers between devices: 67.9 us -> 64.1 us  [trade(): lax.ppermute(block, axis, [(i, i ^ step) for i in range(lax.axis_size(axi...]
    pallas_call x7 -> x8, Pallas kernels: 56.6 us -> 60.2 us  [the longest x7 56 us: project(): pl.pallas_call(functools.partial(project_kernel, len(lefts)), grid=(parts...]
  transfers between devices with their start and end apart: 81 -> 78, of which waited for: 39 -> 40; matrix products, arithmetic and copies ran while one was open for 5% -> 6% of each run, Pallas kernels for 40% -> 41%
where the time goes in v4:
time: 558 us; the launch traced here: 550 us
  Pallas kernels  227 us (41%)
  waiting for transfers between devices  190 us (34%)
  starting transfers between devices  64.4 us (12%)
  local copies, waits for them, and re-layouts  24.6 us (4%)
  other arithmetic  22.7 us (4%)
  between operations  17.2 us (3%)
    ppermute x72, waiting for transfers between devices, trade(): lax.ppermute(block, axis, [(i, i ^ step) for i in range(lax.axis_size(axi...  190 us
    ppermute x72, starting transfers between devices, trade(): lax.ppermute(block, axis, [(i, i ^ step) for i in range(lax.axis_size(axi...  64.1 us
    pallas_call x7, Pallas kernels, project(): pl.pallas_call(functools.partial(project_kernel, len(lefts)), grid=(parts...  56 us
    pallas_call x4, Pallas kernels, hidden_call(): pl.pallas_call(functools.partial(hidden_kernel, first, cores, len(x_piece...  47.1 us
    pallas_call x3, Pallas kernels, weight_grad(): pl.pallas_call(functools.partial(weight_grad_kernel, [len(group) for grou...  44.6 us
    pallas_call x2, Pallas kernels, attention_call(): pl.pallas_call(kernel, grid=(halves[0].shape[0],), in_specs=[pl.BlockSpec...  27.8 us
    pallas_call x3, Pallas kernels, rows_product(): pl.pallas_call(functools.partial(rows_product_kernel, len(pieces), gain i...  21.7 us
    pallas_call x4, Pallas kernels, rows_call(): pl.pallas_call(functools.partial(rows_kernel, kind, len(got)), grid=(2,),...  18 us
  transfers between devices with their start and end apart: 78, of which 40 were waited for; matrix products, arithmetic and copies ran while one was open for 6% of the time, Pallas kernels for 41%

profile of v4, /device:TPU:0, one launch (start us, length us, event | category | flops | bytes accessed | tf_op | source)
XLA Modules:
  0.0 550.1 jit_solution(15709596289887856760)
XLA Ops:
  12.8 3.0 collective-permute-start.50
  17.5 4.6 collective-permute-done.50
  22.1 5.4 collective-permute-done.51
  31.1 2.4 fusion.36
  40.0 8.3 %collective-permute-done.53 = bf16[128,2048]{1,0:T(8,128)(2,1)S(1)} collective-permute-done((bf16[128,2048]{1,0:T(8,128)(2,1)S(1)}, bf16[128,2048]{1,0:T(8,128)(2,1)S(1)}, u32[]{:S(2)}, u32[]{:S(2)}) %collective-permute-start.53) | collective-permute-done | bytes 524320 | tf_op jit(solution)/shard_map/ppermute | solution.py:600
  48.4 8.9 %collective-permute-done.54 = bf16[128,2048]{1,0:T(8,128)(2,1)S(1)} collective-permute-done((bf16[128,2048]{1,0:T(8,128)(2,1)S(1)}, bf16[128,2048]{1,0:T(8,128)(2,1)S(1)}, u32[]{:S(2)}, u32[]{:S(2)}) %collective-permute-start.54) | collective-permute-done | bytes 524320 | tf_op jit(solution)/shard_map/ppermute | solution.py:600
  64.2 3.7 fusion.2
  70.6 4.5 collective-permute-done.57.refs_1_
  75.1 13.9 %collective-permute-done.58.refs_2_ = bf16[128,2304]{1,0:T(8,128)(2,1)S(1)} collective-permute-done((bf16[128,2304]{1,0:T(8,128)(2,1)S(1)}, bf16[128,2304]{1,0:T(8,128)(2,1)S(1)}, u32[]{:S(2)}, u32[]{:S(2)}) %collective-permute-start.58) | collective-permute-done | bytes 589856 | tf_op jit(solution)/shard_map/ppermute | solution.py:600
  90.6 6.5 %collective-permute-done.60 = bf16[128,2048]{1,0:T(8,128)(2,1)S(1)} collective-permute-done((bf16[128,2048]{1,0:T(8,128)(2,1)S(1)}, bf16[128,2048]{1,0:T(8,128)(2,1)S(1)}, u32[]{:S(2)}, u32[]{:S(2)}) %collective-permute-start.60) | collective-permute-done | bytes 524320 | tf_op jit(solution)/shard_map/ppermute | solution.py:600
  107.1 19.2 %conditional.10 = (bf16[4,528,768]{2,1,0:T(8,128)(2,1)}, bf16[1024,2048]{1,0:T(8,128)(2,1)}, f32[4,256,512]{2,1,0:T(8,128)}, f32[4,256,512]{2,1,0:T(8,128)}) conditional(s32[]{:T(128)} %convert_element_type.143, () %tuple.123, (bf16[4,528,768]{2,1,0:T(8,128)(2,1)}, f32[16,128]{1,0:T(8,128)S(1)}, bf16[128,2048]{1,0:T(8,128)(2,1)S(1)}, ...), branch_computations={%region_0.1_spmd, %region_1.2_spmd} | conditional | flops 2097152 | bytes 21495920 | solution.py:596
  107.4 7.8 %query_key_value.1 = (bf16[1024,2048]{1,0:T(8,128)(2,1)}, f32[1024,512]{1,0:T(8,128)}) custom-call(bf16[128,2048]{1,0:T(8,128)(2,1)S(1)} %get-tuple-element.243.refs_0_, bf16[128,2048]{1,0:T(8,128)(2,1)} %get-tuple-element.244.refs_1_, bf16[128,2048]{1,0:T(8,128)(2,1)} %get-tuple-element.245.refs_2_, bf16[128,2048]{1,0:T(8,128)(2,1)} %get-tuple-element.246.refs_3_, ...), custom_call_target="tpu_custom_call" | custom-call | flops 1048576 | bytes 65536 | tf_op jit(solution)/shard_map/cond/branch_1_fun/query_key_value/pallas_call | solution.py:344
  115.2 6.5 %query_key_value_other.1 = f32[1024,512]{1,0:T(8,128)} custom-call(bf16[1024,2048]{1,0:T(8,128)(2,1)} %get-tuple-element.881.refs_0_, bf16[4,528,768]{2,1,0:T(8,128)(2,1)} %collective-permute-done.refs_1_), custom_call_target="tpu_custom_call" | custom-call | flops 1048576 | bytes 65536 | tf_op jit(solution)/shard_map/cond/branch_1_fun/query_key_value_other/pallas_call | solution.py:344
  122.2 4.1 collective-permute-done.1
  126.4 17.1 %conditional.11 = (bf16[1024,2048]{1,0:T(8,128)(2,1)}, bf16[4,256,256]{2,1,0:T(8,128)(2,1)}, bf16[4,256,256]{2,1,0:T(8,128)(2,1)}, bf16[128,2048]{1,0:T(8,128)(2...) conditional(s32[]{:T(128)} %convert_element_type.143, () %tuple.122, ...), branch_computations={%region_2.3_spmd, %region_3.4_spmd} | conditional | flops 1048576 | bytes 24199384 | solution.py:596
  128.2 11.7 %attend.1 = (bf16[4,256,256]{2,1,0:T(8,128)(2,1)}, bf16[4,256,256]{2,1,0:T(8,128)(2,1)}) custom-call(s32[1]{0:T(128)} %bitcast.3.core_ref, f32[4,256,512]{2,1,0:T(8,128)} %get-tuple-element.256.refs_0_, f32[4,256,512]{2,1,0:T(8,128)} %get-tuple-element.257.refs_1_, f32[4,512,128]{2,1,0:T(8,128)} %get-tuple-element.258.refs_2_, ...), custom_call_target="tpu_custom_call" | custom-call | flops 1048576 | bytes 65536 | tf_op jit(solution)/shard_map/cond/branch_1_fun/attend/pallas_call | solution.py:179
  143.5 82.1 %conditional.12 = (f32[256,2048]{1,0:T(8,128)}, bf16[128,2048]{1,0:T(8,128)(2,1)}, bf16[128,2048]{1,0:T(8,128)(2,1)}, bf16[128,2048]{1,0:T(8,128)(2,1)}, bf16[12...) conditional(s32[]{:T(128)} %convert_element_type.143, ...), branch_computations={%region_4.5_spmd, %region_5.6_spmd} | conditional | flops 6291456 | bytes 58327740 | solution.py:596
  143.5 4.4 attention_out_far.1
  150.1 5.1 attention_out.1
  155.2 6.9 %collective-permute-done.21 = bf16[128,2048]{1,0:T(8,128)(2,1)S(1)} collective-permute-done((bf16[128,2048]{1,0:T(8,128)(2,1)}, bf16[128,2048]{1,0:T(8,128)(2,1)S(1)}, u32[]{:S(2)}, u32[]{:S(2)}) %collective-permute-start.21) | collective-permute-done | bytes 524320 | tf_op jit(solution)/shard_map/cond/branch_1_fun/ppermute | solution.py:600
  169.0 8.4 %collective-permute-done.23.refs_2_ = bf16[128,2048]{1,0:T(8,128)(2,1)S(1)} collective-permute-done((bf16[128,2048]{1,0:T(8,128)(2,1)}, bf16[128,2048]{1,0:T(8,128)(2,1)S(1)}, u32[]{:S(2)}, u32[]{:S(2)}) %collective-permute-start.23) | collective-permute-done | bytes 524320 | tf_op jit(solution)/shard_map/cond/branch_1_fun/ppermute | solution.py:600
  178.9 9.0 %collective-permute-done.24.refs_3_ = bf16[128,2048]{1,0:T(8,128)(2,1)S(1)} collective-permute-done((bf16[128,2048]{1,0:T(8,128)(2,1)S(1)}, bf16[128,2048]{1,0:T(8,128)(2,1)S(1)}, u32[]{:S(2)}, u32[]{:S(2)}) %collective-permute-start.24) | collective-permute-done | bytes 524320 | tf_op jit(solution)/shard_map/cond/branch_1_fun/ppermute | solution.py:600
  187.9 2.7 middle.1
  194.7 11.1 %collective-permute-done.27 = bf16[128,2048]{1,0:T(8,128)(2,1)} collective-permute-done((bf16[128,2048]{1,0:T(8,128)(2,1)}, bf16[128,2048]{1,0:T(8,128)(2,1)}, u32[]{:S(2)}, u32[]{:S(2)}) %collective-permute-start.27) | collective-permute-done | bytes 524320 | tf_op jit(solution)/shard_map/cond/branch_1_fun/ppermute | solution.py:600
  208.0 4.1 out_grad_rows.1
  212.2 4.9 collective-permute-done.28
  217.6 7.9 %collective-permute-done.31 = bf16[128,2048]{1,0:T(8,128)(2,1)} collective-permute-done((bf16[128,2048]{1,0:T(8,128)(2,1)}, bf16[128,2048]{1,0:T(8,128)(2,1)}, u32[]{:S(2)}, u32[]{:S(2)}) %collective-permute-start.31) | collective-permute-done | bytes 524320 | tf_op jit(solution)/shard_map/cond/branch_1_fun/ppermute | solution.py:600
  225.6 57.1 %conditional.13 = (bf16[4,512,1536]{2,1,0:T(8,128)(2,1)}, bf16[1024,2048]{1,0:T(8,128)(2,1)}, bf16[1024,2048]{1,0:T(8,128)(2,1)}, bf16[1024,2048]{1,0:T(8,128)(2...) conditional(s32[]{:T(128)} %convert_element_type.143, ...), branch_computations={%region_6.7_spmd, %region_7.8_spmd} | conditional | flops 3145728 | bytes 84083008 | solution.py:596
  226.1 15.4 %hidden_units_a.1 = (bf16[1024,2048]{1,0:T(8,128)(2,1)}, bf16[1024,1024]{1,0:T(8,128)(2,1)}, bf16[1024,512]{1,0:T(8,128)(2,1)}) custom-call(bf16[128,2048]{1,0:T(8,128)(2,1)} %get-tuple-element.306.refs_0_, bf16[128,2048]{1,0:T(8,128)(2,1)} %get-tuple-element.307.refs_1_, bf16[128,2048]{1,0:T(8,128)(2,1)} %get-tuple-element.308.refs_2_, ...), custom_call_target="tpu_custom_call" | custom-call | flops 1048576 | bytes 65536 | tf_op jit(solution)/shard_map/cond/branch_1_fun/hidden_units_a/pallas_call | solution.py:575
  242.0 13.7 %hidden_units_a_other.1 = (bf16[1024,1024]{1,0:T(8,128)(2,1)}, bf16[1024,512]{1,0:T(8,128)(2,1)}) custom-call(bf16[1024,2048]{1,0:T(8,128)(2,1)} %get-tuple-element.928.refs_0_, bf16[1024,2048]{1,0:T(8,128)(2,1)} %get-tuple-element.314.refs_8_.refs_1_.refs_2_, bf16[4,512,1536]{2,1,0:T(8,128)(2,1)} %collective-permute-done.6.refs_2_.refs_3_.refs_4_, ...), custom_call_target="tpu_custom_call" | custom-call | flops 1048576 | bytes 65536 | tf_op jit(solution)/shard_map/cond/branch_1_fun/hidden_units_a_other/pallas_call | solution.py:575
  256.3 5.4 collective-permute-done.10.refs_7_
  263.3 19.4 %hidden_weights_a.1 = bf16[4,512,1536]{2,1,0:T(8,128)(2,1)} custom-call(bf16[1024,2048]{1,0:T(8,128)(2,1)} %get-tuple-element.928.refs_0_, bf16[1024,2048]{1,0:T(8,128)(2,1)} %collective-permute-done.7.refs_1_, bf16[1024,2048]{1,0:T(8,128)(2,1)} %get-tuple-element.314.refs_8_.refs_1_.refs_2_, bf16[1024,2048]{1,0:T(8,128)(2,1)} %collective-permute-done.8.refs_3_, ...), custom_call_target="tpu_custom_call" | custom-call | flops 1048576 | bytes 65536 | tf_op jit(solution)/shard_map/cond/branch_1_fun/hidden_weights_a/pallas_call | solution.py:388
  282.8 74.4 %conditional.14 = (f32[256,2048]{1,0:T(8,128)}, bf16[128,2048]{1,0:T(8,128)(2,1)}, bf16[128,2048]{1,0:T(8,128)(2,1)}, bf16[128,2048]{1,0:T(8,128)(2,1)}, bf16[12...) conditional(s32[]{:T(128)} %convert_element_type.143, ...), branch_computations={%region_8.9_spmd, %region_9.10_spmd} | conditional | flops 7340032 | bytes 60097064 | solution.py:596
  283.4 9.0 %hidden_units_b.2 = (bf16[1024,512]{1,0:T(8,128)(2,1)}, bf16[1024,256]{1,0:T(8,128)(2,1)}) custom-call(bf16[1024,2048]{1,0:T(8,128)(2,1)} %get-tuple-element.322.refs_0_, bf16[1024,2048]{1,0:T(8,128)(2,1)} %get-tuple-element.323.refs_1_.refs_2_, bf16[4,512,768]{2,1,0:T(8,128)(2,1)} %get-tuple-element.324.refs_2_.refs_3_.refs_4_.refs_6_, ...), custom_call_target="tpu_custom_call" | custom-call | flops 1048576 | bytes 65536 | tf_op jit(solution)/shard_map/cond/branch_1_fun/hidden_units_b/pallas_call | solution.py:575
  292.4 9.0 %hidden_units_b.3 = (bf16[1024,512]{1,0:T(8,128)(2,1)}, bf16[1024,256]{1,0:T(8,128)(2,1)}) custom-call(bf16[1024,2048]{1,0:T(8,128)(2,1)} %get-tuple-element.322.refs_0_, bf16[1024,2048]{1,0:T(8,128)(2,1)} %get-tuple-element.323.refs_1_.refs_2_, bf16[4,512,768]{2,1,0:T(8,128)(2,1)} %collective-permute-done.33.refs_2_.refs_3_.refs_4_.refs_7_, ...), custom_call_target="tpu_custom_call" | custom-call | flops 1048576 | bytes 65536 | tf_op jit(solution)/shard_map/cond/branch_1_fun/hidden_units_b/pallas_call | solution.py:575
  301.4 9.1 %normed_mid_grad_far.1 = (bf16[128,2048]{1,0:T(8,128)(2,1)}, bf16[128,2048]{1,0:T(8,128)(2,1)}) custom-call(bf16[1024,1024]{1,0:T(8,128)(2,1)} %get-tuple-element.320.refs_0_, bf16[1024,1024]{1,0:T(8,128)(2,1)} %get-tuple-element.321.refs_1_, bf16[1024,512]{1,0:T(8,128)(2,1)} %get-tuple-element.342.refs_2_.refs_4_, ...), custom_call_target="tpu_custom_call" | custom-call | flops 1048576 | bytes 65536 | tf_op jit(solution)/shard_map/cond/branch_1_fun/normed_mid_grad_far/pallas_call | solution.py:224
  314.0 14.7 %normed_mid_grad.1 = (f32[256,2048]{1,0:T(8,128)}, bf16[128,2048]{1,0:T(8,128)(2,1)}, bf16[128,2048]{1,0:T(8,128)(2,1)}, bf16[128,2048]{1,0:T(8,128)(2,1)}, bf16[128,2048]{1,0:T(8,128)(2,1)}) custom-call(bf16[1024,1024]{1,0:T(8,128)(2,1)} %get-tuple-element.320.refs_0_, bf16[1024,1024]{1,0:T(8,128)(2,1)} %get-tuple-element.321.refs_1_, ...), custom_call_target="tpu_custom_call" | custom-call | flops 1048576 | bytes 65536 | tf_op jit(solution)/shard_map/cond/branch_1_fun/normed_mid_grad/pallas_call | solution.py:224
  338.0 12.5 %hidden_weights_b.1 = bf16[4,512,768]{2,1,0:T(8,128)(2,1)} custom-call(bf16[1024,2048]{1,0:T(8,128)(2,1)} %get-tuple-element.322.refs_0_, bf16[1024,2048]{1,0:T(8,128)(2,1)} %get-tuple-element.338.refs_1_, bf16[1024,2048]{1,0:T(8,128)(2,1)} %get-tuple-element.323.refs_1_.refs_2_, bf16[1024,2048]{1,0:T(8,128)(2,1)} %get-tuple-element.339.refs_3_, ...), custom_call_target="tpu_custom_call" | custom-call | flops 1048576 | bytes 65536 | tf_op jit(solution)/shard_map/cond/branch_1_fun/hidden_weights_b/pallas_call | solution.py:388
  350.5 4.9 collective-permute-done.36
  357.3 43.2 %conditional.15 = (f32[256,2048]{1,0:T(8,128)}, bf16[128,2048]{1,0:T(8,128)(2,1)}, bf16[128,2048]{1,0:T(8,128)(2,1)}, bf16[128,2048]{1,0:T(8,128)(2,1)}, bf16[12...) conditional(s32[]{:T(128)} %convert_element_type.143, ...), branch_computations={%region_10.11_spmd, %region_11.12_spmd} | conditional | flops 2097152 | bytes 37880180 | solution.py:596
  357.5 6.4 %middle_grad.1 = (f32[256,2048]{1,0:T(8,128)}, bf16[128,2048]{1,0:T(8,128)(2,1)}, bf16[128,2048]{1,0:T(8,128)(2,1)}) custom-call(f32[256,2048]{1,0:T(8,128)} %get-tuple-element.348.refs_0_, f32[256,2048]{1,0:T(8,128)} %get-tuple-element.349.refs_1_, bf16[128,2048]{1,0:T(8,128)(2,1)} %get-tuple-element.350.refs_2_, ...), custom_call_target="tpu_custom_call" | custom-call | flops 1048576 | bytes 65536 | tf_op jit(solution)/shard_map/cond/branch_1_fun/middle_grad/pallas_call | solution.py:307
  368.0 10.8 %hidden_out.1 = (f32[256,2048]{1,0:T(8,128)}, bf16[256,2048]{1,0:T(8,128)(2,1)}, bf16[256,2048]{1,0:T(8,128)(2,1)}, bf16[256,2048]{1,0:T(8,128)(2,1)}) custom-call(bf16[1024,512]{1,0:T(8,128)(2,1)} %get-tuple-element.359.refs_0_, bf16[1024,512]{1,0:T(8,128)(2,1)} %get-tuple-element.360.refs_1_, bf16[1024,256]{1,0:T(8,128)(2,1)} %get-tuple-element.361.refs_2_, ...), custom_call_target="tpu_custom_call" | custom-call | flops 1048576 | bytes 65536 | tf_op jit(solution)/shard_map/cond/branch_1_fun/hidden_out/pallas_call | solution.py:224
  381.5 8.9 %collective-permute-done.12 = bf16[128,2048]{1,0:T(8,128)(2,1)} collective-permute-done((bf16[128,2048]{1,0:T(8,128)(2,1)}, bf16[128,2048]{1,0:T(8,128)(2,1)}, u32[]{:S(2)}, u32[]{:S(2)}) %collective-permute-start.12) | collective-permute-done | bytes 524320 | tf_op jit(solution)/shard_map/cond/branch_1_fun/ppermute | solution.py:600
  391.8 8.7 %collective-permute-done.15 = bf16[128,2048]{1,0:T(8,128)(2,1)} collective-permute-done((bf16[128,2048]{1,0:T(8,128)(2,1)}, bf16[128,2048]{1,0:T(8,128)(2,1)}, u32[]{:S(2)}, u32[]{:S(2)}) %collective-permute-start.15) | collective-permute-done | bytes 524320 | tf_op jit(solution)/shard_map/cond/branch_1_fun/ppermute | solution.py:600
  401.4 2.5 collective-permute-start.68
  404.0 32.1 %conditional.16 = (bf16[1024,2048]{1,0:T(8,128)(2,1)}, bf16[1024,2048]{1,0:T(8,128)(2,1)}, bf16[4,256,512]{2,1,0:T(8,128)(2,1)}, bf16[4,256,512]{2,1,0:T(8,128)(2,1)}, f32[8,128]{1,0:T(8,128)S(1)}) conditional(s32[]{:T(128)} %convert_element_type.143, () %tuple.114, (bf16[128,2048]{1,0:T(8,128)(2,1)}, bf16[128,2048]{1,0:T(8,128)(2,1)}, ...), branch_computations={%region_13.14_spmd, %region_14.15_spmd} | conditional | flops 2097152 | bytes 21119124 | solution.py:596
  404.0 7.4 %attended_grad.1 = (bf16[1024,2048]{1,0:T(8,128)(2,1)}, bf16[1024,256]{1,0:T(8,128)(2,1)}, bf16[1024,256]{1,0:T(8,128)(2,1)}) custom-call(bf16[128,2048]{1,0:T(8,128)(2,1)} %get-tuple-element.373.refs_0_, bf16[128,2048]{1,0:T(8,128)(2,1)} %get-tuple-element.374.refs_1_, bf16[128,2048]{1,0:T(8,128)(2,1)} %get-tuple-element.375.refs_2_, ...), custom_call_target="tpu_custom_call" | custom-call | flops 1048576 | bytes 65536 | tf_op jit(solution)/shard_map/cond/branch_1_fun/attended_grad/pallas_call | solution.py:344
  412.2 6.7 %collective-permute-done.18.refs_3_ = bf16[4,256,256]{2,1,0:T(8,128)(2,1)S(1)} collective-permute-done((bf16[4,256,256]{2,1,0:T(8,128)(2,1)}, bf16[4,256,256]{2,1,0:T(8,128)(2,1)S(1)}, u32[]{:S(2)}, u32[]{:S(2)}) %collective-permute-start.18) | collective-permute-done | bytes 524320 | tf_op jit(solution)/shard_map/cond/branch_1_fun/ppermute | solution.py:600
  420.0 16.1 %attend_back.1 = (bf16[4,256,512]{2,1,0:T(8,128)(2,1)}, bf16[4,256,512]{2,1,0:T(8,128)(2,1)}, f32[8,128]{1,0:T(8,128)S(1)}) custom-call(s32[1]{0:T(128)} %bitcast.8.core_ref, f32[4,256,512]{2,1,0:T(8,128)} %get-tuple-element.385.refs_0_, f32[4,256,512]{2,1,0:T(8,128)} %get-tuple-element.386.refs_1_, bf16[4,256,256]{2,1,0:T(8,128)(2,1)S(1)} %bitcast.80, ...), custom_call_target="tpu_custom_call" | custom-call | flops 1048576 | bytes 65536 | tf_op jit(solution)/shard_map/cond/branch_1_fun/attend_back/pallas_call | solution.py:179
  436.1 13.8 %conditional.17 = (bf16[4,528,768]{2,1,0:T(8,128)(2,1)}, bf16[1024,512]{1,0:T(8,128)(2,1)}, bf16[1024,512]{1,0:T(8,128)(2,1)}) conditional(s32[]{:T(128)} %convert_element_type.143, () %tuple.113, (bf16[4,256,512]{2,1,0:T(8,128)(2,1)}, bf16[4,256,512]{2,1,0:T(8,128)(2,1)}, bf16[4,256,256]{2,1,0:T(8,128)(2,1)}, bf16[4,256,256]{2,1,0:T(8,128)(2,1)}, ...), branch_computations={%region_15.16_spmd, %region_16.17_spmd} | conditional | flops 1049600 | bytes 5341214 | solution.py:596
  437.2 12.7 %attention_weights.1 = bf16[4,528,768]{2,1,0:T(8,128)(2,1)} custom-call(bf16[1024,2048]{1,0:T(8,128)(2,1)} %get-tuple-element.397.refs_0_, bf16[1024,2048]{1,0:T(8,128)(2,1)} %get-tuple-element.398.refs_1_, bf16[1024,2048]{1,0:T(8,128)(2,1)} %get-tuple-element.399.refs_2_, bf16[1024,2048]{1,0:T(8,128)(2,1)} %get-tuple-element.400.refs_3_, ...), custom_call_target="tpu_custom_call" | custom-call | flops 1048576 | bytes 65536 | tf_op jit(solution)/shard_map/cond/branch_1_fun/attention_weights/pallas_call | solution.py:388
  449.9 20.5 %conditional.18 = (f32[256,2048]{1,0:T(8,128)}, bf16[128,2048]{1,0:T(8,128)(2,1)}, bf16[128,2048]{1,0:T(8,128)(2,1)}, bf16[128,2048]{1,0:T(8,128)(2,1)}, bf16[12...) conditional(s32[]{:T(128)} %convert_element_type.143, () %tuple.112, ...), branch_computations={%region_17.18_spmd, %region_18.19_spmd} | conditional | flops 2097152 | bytes 17301668 | solution.py:596
  450.2 5.1 normed_in_grad_far.1
  456.9 6.9 %normed_in_grad.1 = (f32[256,2048]{1,0:T(8,128)}, bf16[128,2048]{1,0:T(8,128)(2,1)}, bf16[128,2048]{1,0:T(8,128)(2,1)}, bf16[128,2048]{1,0:T(8,128)(2,1)S(1)}, bf16[128,2048]{1,0:T(8,128)(2,1)}) custom-call(bf16[1024,512]{1,0:T(8,128)(2,1)} %get-tuple-element.406.refs_0_, bf16[1024,512]{1,0:T(8,128)(2,1)} %get-tuple-element.407.refs_1_, ...), custom_call_target="tpu_custom_call" | custom-call | flops 1048576 | bytes 65536 | tf_op jit(solution)/shard_map/cond/branch_1_fun/normed_in_grad/pallas_call | solution.py:224
  463.7 5.8 %collective-permute-done.19 = bf16[128,2048]{1,0:T(8,128)(2,1)} collective-permute-done((bf16[128,2048]{1,0:T(8,128)(2,1)}, bf16[128,2048]{1,0:T(8,128)(2,1)}, u32[]{:S(2)}, u32[]{:S(2)}) %collective-permute-start.19) | collective-permute-done | bytes 524320 | tf_op jit(solution)/shard_map/cond/branch_1_fun/ppermute | solution.py:600
  470.5 52.6 %conditional.19 = (bf16[256,2048]{1,0:T(8,128)(2,1)}, f32[256,2048]{1,0:T(8,128)}, bf16[128,2304]{1,0:T(8,128)(2,1)}, bf16[128,2304]{1,0:T(8,128)(2,1)}, bf16[12...) conditional(s32[]{:T(128)} %convert_element_type.143, () %tuple.111, (bf16[128,2048]{1,0:T(8,128)(2,1)}, ...), branch_computations={%region_20.21_spmd, %region_21.22_spmd} | conditional | flops 8912914 | bytes 32375352 | solution.py:596
  480.4 5.1 collective-permute-done.43.refs_2_
  486.4 8.9 %collective-permute-done.44.refs_3_ = bf16[128,2048]{1,0:T(8,128)(2,1)S(1)} collective-permute-done((bf16[128,2048]{1,0:T(8,128)(2,1)}, bf16[128,2048]{1,0:T(8,128)(2,1)S(1)}, u32[]{:S(2)}, u32[]{:S(2)}) %collective-permute-start.44) | collective-permute-done | bytes 524320 | tf_op jit(solution)/shard_map/cond/branch_1_fun/ppermute | solution.py:600
  499.8 4.3 hidden_out_sum.1
  504.1 4.7 grad_in.1
  508.7 3.9 collective-permute-done.47
  512.7 10.4 %collective-permute-done.48 = bf16[128,2304]{1,0:T(8,128)(2,1)} collective-permute-done((bf16[128,2304]{1,0:T(8,128)(2,1)S(1)}, bf16[128,2304]{1,0:T(8,128)(2,1)}, u32[]{:S(2)}, u32[]{:S(2)}) %collective-permute-start.48) | collective-permute-done | bytes 589856 | tf_op jit(solution)/shard_map/cond/branch_1_fun/ppermute | solution.py:600
  529.5 4.6 hidden_owned.1
  539.2 2.5 psum.7
  (299 shorter events, 120.0 us)
Async XLA Ops:
  7.2 90.7 %all-gather.7.cloned.1.call-start = ((), (), s32[]{:S(2)}) async-start(), calls=%async_computation.6 | async-start | bytes 4055040 | tf_op jit(solution)/shard_map/all_gather | solution.py:731
  29.4 196.2 %all-gather.9.cloned.1.call-start = ((), (), s32[]{:S(2)}) async-start(), calls=%async_computation.7 | async-start | bytes 7864320 | tf_op jit(solution)/shard_map/all_gather | solution.py:731
  33.4 14.9 %collective-permute-start.53 = (bf16[128,2048]{1,0:T(8,128)(2,1)S(1)}, bf16[128,2048]{1,0:T(8,128)(2,1)S(1)}, u32[]{:S(2)}, u32[]{:S(2)}) collective-permute-start(bf16[128,2048]{1,0:T(8,128)(2,1)S(1)} %get-tuple-element.619), channel_id=1, source_target_pairs={{0,2},{2,0},{4,6},{6,4},{1,3},{3,1},{5,7},{7,5},{8,10},{10,8},{12,... | collective-permute-start | bytes 1572872 | tf_op jit(solution)/shard_map/ppermute | solution.py:600
  34.7 22.6 %collective-permute-start.55 = (bf16[128,2048]{1,0:T(8,128)(2,1)S(1)}, bf16[128,2048]{1,0:T(8,128)(2,1)S(1)}, u32[]{:S(2)}, u32[]{:S(2)}) collective-permute-start(bf16[128,2048]{1,0:T(8,128)(2,1)S(1)} %get-tuple-element.619), channel_id=1, source_target_pairs={{0,4},{2,6},{4,0},{6,2},{1,5},{3,7},{5,1},{7,3},{8,12},{10,14},{12... | collective-permute-start | bytes 1572872 | tf_op jit(solution)/shard_map/ppermute | solution.py:600
  35.6 21.7 %collective-permute-start.54 = (bf16[128,2048]{1,0:T(8,128)(2,1)S(1)}, bf16[128,2048]{1,0:T(8,128)(2,1)S(1)}, u32[]{:S(2)}, u32[]{:S(2)}) collective-permute-start(bf16[128,2048]{1,0:T(8,128)(2,1)S(1)} %get-tuple-element.620), channel_id=1, source_target_pairs={{0,2},{2,0},{4,6},{6,4},{1,3},{3,1},{5,7},{7,5},{8,10},{10,8},{12,... | collective-permute-start | bytes 1572872 | tf_op jit(solution)/shard_map/ppermute | solution.py:600
  37.0 21.4 %collective-permute-start.56 = (bf16[128,2048]{1,0:T(8,128)(2,1)S(1)}, bf16[128,2048]{1,0:T(8,128)(2,1)S(1)}, u32[]{:S(2)}, u32[]{:S(2)}) collective-permute-start(bf16[128,2048]{1,0:T(8,128)(2,1)S(1)} %get-tuple-element.620), channel_id=1, source_target_pairs={{0,4},{2,6},{4,0},{6,2},{1,5},{3,7},{5,1},{7,3},{8,12},{10,14},{12... | collective-permute-start | bytes 1572872 | tf_op jit(solution)/shard_map/ppermute | solution.py:600
  58.8 16.3 %collective-permute-start.57 = (bf16[128,2304]{1,0:T(8,128)(2,1)S(1)}, bf16[128,2304]{1,0:T(8,128)(2,1)S(1)}, u32[]{:S(2)}, u32[]{:S(2)}) collective-permute-start(bf16[128,2304]{1,0:T(8,128)(2,1)S(1)} %get-tuple-element.802), channel_id=1, source_target_pairs={{0,2},{2,0},{4,6},{6,4},{1,3},{3,1},{5,7},{7,5},{8,10},{10,8},{12,... | collective-permute-start | bytes 1769480 | tf_op jit(solution)/shard_map/ppermute | solution.py:600
  60.1 28.9 %collective-permute-start.58 = (bf16[128,2304]{1,0:T(8,128)(2,1)S(1)}, bf16[128,2304]{1,0:T(8,128)(2,1)S(1)}, u32[]{:S(2)}, u32[]{:S(2)}) collective-permute-start(bf16[128,2304]{1,0:T(8,128)(2,1)S(1)} %get-tuple-element.801), channel_id=1, source_target_pairs={{0,4},{2,6},{4,0},{6,2},{1,5},{3,7},{5,1},{7,3},{8,12},{10,14},{12... | collective-permute-start | bytes 1769480 | tf_op jit(solution)/shard_map/ppermute | solution.py:600
  60.6 28.4 %collective-permute-start.59 = (bf16[128,2304]{1,0:T(8,128)(2,1)S(1)}, bf16[128,2304]{1,0:T(8,128)(2,1)S(1)}, u32[]{:S(2)}, u32[]{:S(2)}) collective-permute-start(bf16[128,2304]{1,0:T(8,128)(2,1)S(1)} %get-tuple-element.800), channel_id=1, source_target_pairs={{0,6},{2,4},{4,2},{6,0},{1,7},{3,5},{5,3},{7,1},{8,14},{10,12},{12... | collective-permute-start | bytes 1769480 | tf_op jit(solution)/shard_map/ppermute | solution.py:600
  62.4 34.7 %collective-permute-start.60 = (bf16[128,2048]{1,0:T(8,128)(2,1)S(1)}, bf16[128,2048]{1,0:T(8,128)(2,1)S(1)}, u32[]{:S(2)}, u32[]{:S(2)}) collective-permute-start(bf16[128,2048]{1,0:T(8,128)(2,1)S(1)} %collective-permute-done.53), channel_id=1, source_target_pairs={{0,4},{2,6},{4,0},{6,2},{1,5},{3,7},{5,1},{7,3},{8,12},{10,14},{12... | collective-permute-start | bytes 1572872 | tf_op jit(solution)/shard_map/ppermute | solution.py:600
  63.0 34.9 %collective-permute-start.61 = (bf16[128,2048]{1,0:T(8,128)(2,1)S(1)}, bf16[128,2048]{1,0:T(8,128)(2,1)}, u32[]{:S(2)}, u32[]{:S(2)}) collective-permute-start(bf16[128,2048]{1,0:T(8,128)(2,1)S(1)} %collective-permute-done.56), channel_id=1, source_target_pairs={{0,2},{2,0},{4,6},{6,4},{1,3},{3,1},{5,7},{7,5},{8,10},{10,8},{12,... | collective-permute-start | bytes 1572872 | tf_op jit(solution)/shard_map/ppermute | solution.py:600
  97.9 184.9 %all-gather.11.cloned.1.call-start = ((), (), s32[]{:S(2)}) async-start(), calls=%async_computation.8 | async-start | bytes 3932160 | tf_op jit(solution)/shard_map/all_gather | solution.py:731
  98.6 301.8 %reduce-scatter.4.cloned.1.call-start = ((), (), s32[]{:S(2)}) async-start(), calls=%async_computation.3 | async-start | bytes 7864320 | tf_op jit(solution)/shard_map/reduce_scatter | solution.py:832
  101.9 24.5 %collective-permute-start.62 = (bf16[128,2048]{1,0:T(8,128)(2,1)S(1)}, bf16[128,2048]{1,0:T(8,128)(2,1)}, u32[]{:S(2)}, u32[]{:S(2)}) collective-permute-start(bf16[128,2048]{1,0:T(8,128)(2,1)S(1)} %copy-done.16), channel_id=1, source_target_pairs={{0,2},{2,0},{4,6},{6,4},{1,3},{3,1},{5,7},{7,5},{8,10},{10,8},{12,... | collective-permute-start | bytes 1572872 | tf_op jit(solution)/shard_map/ppermute | solution.py:600
  102.5 23.9 %collective-permute-start.64 = (bf16[128,2048]{1,0:T(8,128)(2,1)S(1)}, bf16[128,2048]{1,0:T(8,128)(2,1)}, u32[]{:S(2)}, u32[]{:S(2)}) collective-permute-start(bf16[128,2048]{1,0:T(8,128)(2,1)S(1)} %copy-done.16), channel_id=1, source_target_pairs={{0,4},{2,6},{4,0},{6,2},{1,5},{3,7},{5,1},{7,3},{8,12},{10,14},{12... | collective-permute-start | bytes 1572872 | tf_op jit(solution)/shard_map/ppermute | solution.py:600
  102.7 23.6 %collective-permute-start.63 = (bf16[128,2048]{1,0:T(8,128)(2,1)S(1)}, bf16[128,2048]{1,0:T(8,128)(2,1)}, u32[]{:S(2)}, u32[]{:S(2)}) collective-permute-start(bf16[128,2048]{1,0:T(8,128)(2,1)S(1)} %copy-done.14), channel_id=1, source_target_pairs={{0,2},{2,0},{4,6},{6,4},{1,3},{3,1},{5,7},{7,5},{8,10},{10,8},{12,... | collective-permute-start | bytes 1572872 | tf_op jit(solution)/shard_map/ppermute | solution.py:600
  104.3 22.1 %collective-permute-start.65 = (bf16[128,2048]{1,0:T(8,128)(2,1)S(1)}, bf16[128,2048]{1,0:T(8,128)(2,1)}, u32[]{:S(2)}, u32[]{:S(2)}) collective-permute-start(bf16[128,2048]{1,0:T(8,128)(2,1)S(1)} %copy-done.14), channel_id=1, source_target_pairs={{0,4},{2,6},{4,0},{6,2},{1,5},{3,7},{5,1},{7,3},{8,12},{10,14},{12... | collective-permute-start | bytes 1572872 | tf_op jit(solution)/shard_map/ppermute | solution.py:600
  126.4 17.1 %collective-permute-start.2 = (bf16[1024,2048]{1,0:T(8,128)(2,1)}, bf16[1024,2048]{1,0:T(8,128)(2,1)}, u32[]{:S(2)}, u32[]{:S(2)}) collective-permute-start(bf16[1024,2048]{1,0:T(8,128)(2,1)} %get-tuple-element.254), channel_id=1, source_target_pairs={{0,1},{1,0},{2,3},{3,2},{4,5},{5,4},{6,7},{7,6},{8,9},{9,8},{10,11... | collective-permute-start | bytes 12582920 | tf_op jit(solution)/shard_map/cond/branch_1_fun/ppermute | solution.py:600
  126.8 14.3 %collective-permute-start.3 = (bf16[128,2048]{1,0:T(8,128)(2,1)}, bf16[128,2048]{1,0:T(8,128)(2,1)}, u32[]{:S(2)}, u32[]{:S(2)}) collective-permute-start(bf16[128,2048]{1,0:T(8,128)(2,1)} %get-tuple-element.265), channel_id=1, source_target_pairs={{0,4},{2,6},{4,0},{6,2},{1,5},{3,7},{5,1},{7,3},{8,12},{10,14},{12... | collective-permute-start | bytes 1572872 | tf_op jit(solution)/shard_map/cond/branch_1_fun/ppermute | solution.py:600
  127.3 14.0 %collective-permute-start.4 = (bf16[128,2048]{1,0:T(8,128)(2,1)}, bf16[128,2048]{1,0:T(8,128)(2,1)}, u32[]{:S(2)}, u32[]{:S(2)}) collective-permute-start(bf16[128,2048]{1,0:T(8,128)(2,1)} %get-tuple-element.266), channel_id=1, source_target_pairs={{0,2},{2,0},{4,6},{6,4},{1,3},{3,1},{5,7},{7,5},{8,10},{10,8},{12,... | collective-permute-start | bytes 1572872 | tf_op jit(solution)/shard_map/cond/branch_1_fun/ppermute | solution.py:600
  147.9 14.2 %collective-permute-start.21 = (bf16[128,2048]{1,0:T(8,128)(2,1)}, bf16[128,2048]{1,0:T(8,128)(2,1)S(1)}, u32[]{:S(2)}, u32[]{:S(2)}) collective-permute-start(bf16[128,2048]{1,0:T(8,128)(2,1)} %get-tuple-element.279), channel_id=1, source_target_pairs={{0,2},{2,0},{4,6},{6,4},{1,3},{3,1},{5,7},{7,5},{8,10},{10,8},{12,... | collective-permute-start | bytes 1572872 | tf_op jit(solution)/shard_map/cond/branch_1_fun/ppermute | solution.py:600
  148.5 13.9 %collective-permute-start.22 = (bf16[128,2048]{1,0:T(8,128)(2,1)}, bf16[128,2048]{1,0:T(8,128)(2,1)S(1)}, u32[]{:S(2)}, u32[]{:S(2)}) collective-permute-start(bf16[128,2048]{1,0:T(8,128)(2,1)} %get-tuple-element.280), channel_id=1, source_target_pairs={{0,4},{2,6},{4,0},{6,2},{1,5},{3,7},{5,1},{7,3},{8,12},{10,14},{12... | collective-permute-start | bytes 1572872 | tf_op jit(solution)/shard_map/cond/branch_1_fun/ppermute | solution.py:600
  162.4 15.1 %collective-permute-start.23 = (bf16[128,2048]{1,0:T(8,128)(2,1)}, bf16[128,2048]{1,0:T(8,128)(2,1)S(1)}, u32[]{:S(2)}, u32[]{:S(2)}) collective-permute-start(bf16[128,2048]{1,0:T(8,128)(2,1)} %get-tuple-element.281), channel_id=1, source_target_pairs={{0,2},{2,0},{4,6},{6,4},{1,3},{3,1},{5,7},{7,5},{8,10},{10,8},{12,... | collective-permute-start | bytes 1572872 | tf_op jit(solution)/shard_map/cond/branch_1_fun/ppermute | solution.py:600
  163.8 15.1 %collective-permute-start.26 = (bf16[128,2048]{1,0:T(8,128)(2,1)}, bf16[128,2048]{1,0:T(8,128)(2,1)S(1)}, u32[]{:S(2)}, u32[]{:S(2)}) collective-permute-start(bf16[128,2048]{1,0:T(8,128)(2,1)} %get-tuple-element.284), channel_id=1, source_target_pairs={{0,4},{2,6},{4,0},{6,2},{1,5},{3,7},{5,1},{7,3},{8,12},{10,14},{12... | collective-permute-start | bytes 1572872 | tf_op jit(solution)/shard_map/cond/branch_1_fun/ppermute | solution.py:600
  166.6 21.3 %collective-permute-start.24 = (bf16[128,2048]{1,0:T(8,128)(2,1)S(1)}, bf16[128,2048]{1,0:T(8,128)(2,1)S(1)}, u32[]{:S(2)}, u32[]{:S(2)}) collective-permute-start(bf16[128,2048]{1,0:T(8,128)(2,1)S(1)} %add_convert_fusion.1), channel_id=1, source_target_pairs={{0,4},{2,6},{4,0},{6,2},{1,5},{3,7},{5,1},{7,3},{8,12},{10,14},{12... | collective-permute-start | bytes 1572872 | tf_op jit(solution)/shard_map/cond/branch_1_fun/ppermute | solution.py:600
  168.4 19.6 %collective-permute-start.25 = (bf16[128,2048]{1,0:T(8,128)(2,1)S(1)}, bf16[128,2048]{1,0:T(8,128)(2,1)S(1)}, u32[]{:S(2)}, u32[]{:S(2)}) collective-permute-start(bf16[128,2048]{1,0:T(8,128)(2,1)S(1)} %add_convert_fusion), channel_id=1, source_target_pairs={{0,2},{2,0},{4,6},{6,4},{1,3},{3,1},{5,7},{7,5},{8,10},{10,8},{12,... | collective-permute-start | bytes 1572872 | tf_op jit(solution)/shard_map/cond/branch_1_fun/ppermute | solution.py:600
  190.6 15.2 %collective-permute-start.27 = (bf16[128,2048]{1,0:T(8,128)(2,1)}, bf16[128,2048]{1,0:T(8,128)(2,1)}, u32[]{:S(2)}, u32[]{:S(2)}) collective-permute-start(bf16[128,2048]{1,0:T(8,128)(2,1)} %get-tuple-element.909), channel_id=1, source_target_pairs={{0,2},{2,0},{4,6},{6,4},{1,3},{3,1},{5,7},{7,5},{8,10},{10,8},{12,... | collective-permute-start | bytes 1572872 | tf_op jit(solution)/shard_map/cond/branch_1_fun/ppermute | solution.py:600
  191.2 16.2 %collective-permute-start.30 = (bf16[128,2048]{1,0:T(8,128)(2,1)}, bf16[128,2048]{1,0:T(8,128)(2,1)}, u32[]{:S(2)}, u32[]{:S(2)}) collective-permute-start(bf16[128,2048]{1,0:T(8,128)(2,1)} %get-tuple-element.910), channel_id=1, source_target_pairs={{0,4},{2,6},{4,0},{6,2},{1,5},{3,7},{5,1},{7,3},{8,12},{10,14},{12... | collective-permute-start | bytes 1572872 | tf_op jit(solution)/shard_map/cond/branch_1_fun/ppermute | solution.py:600
  192.9 24.2 %collective-permute-start.28 = (bf16[128,2048]{1,0:T(8,128)(2,1)}, bf16[128,2048]{1,0:T(8,128)(2,1)}, u32[]{:S(2)}, u32[]{:S(2)}) collective-permute-start(bf16[128,2048]{1,0:T(8,128)(2,1)} %get-tuple-element.910), channel_id=1, source_target_pairs={{0,2},{2,0},{4,6},{6,4},{1,3},{3,1},{5,7},{7,5},{8,10},{10,8},{12,... | collective-permute-start | bytes 1572872 | tf_op jit(solution)/shard_map/cond/branch_1_fun/ppermute | solution.py:600
  194.3 23.4 %collective-permute-start.29 = (bf16[128,2048]{1,0:T(8,128)(2,1)}, bf16[128,2048]{1,0:T(8,128)(2,1)}, u32[]{:S(2)}, u32[]{:S(2)}) collective-permute-start(bf16[128,2048]{1,0:T(8,128)(2,1)} %get-tuple-element.909), channel_id=1, source_target_pairs={{0,4},{2,6},{4,0},{6,2},{1,5},{3,7},{5,1},{7,3},{8,12},{10,14},{12... | collective-permute-start | bytes 1572872 | tf_op jit(solution)/shard_map/cond/branch_1_fun/ppermute | solution.py:600
  205.8 19.8 %collective-permute-start.31 = (bf16[128,2048]{1,0:T(8,128)(2,1)}, bf16[128,2048]{1,0:T(8,128)(2,1)}, u32[]{:S(2)}, u32[]{:S(2)}) collective-permute-start(bf16[128,2048]{1,0:T(8,128)(2,1)} %collective-permute-done.27), channel_id=1, source_target_pairs={{0,4},{2,6},{4,0},{6,2},{1,5},{3,7},{5,1},{7,3},{8,12},{10,14},{12... | collective-permute-start | bytes 1572872 | tf_op jit(solution)/shard_map/cond/branch_1_fun/ppermute | solution.py:600
  207.4 18.2 %collective-permute-start.32 = (bf16[128,2048]{1,0:T(8,128)(2,1)}, bf16[128,2048]{1,0:T(8,128)(2,1)}, u32[]{:S(2)}, u32[]{:S(2)}) collective-permute-start(bf16[128,2048]{1,0:T(8,128)(2,1)} %collective-permute-done.30), channel_id=1, source_target_pairs={{0,2},{2,0},{4,6},{6,4},{1,3},{3,1},{5,7},{7,5},{8,10},{10,8},{12,... | collective-permute-start | bytes 1572872 | tf_op jit(solution)/shard_map/cond/branch_1_fun/ppermute | solution.py:600
  226.0 16.0 %collective-permute-start.6 = (bf16[4,512,1536]{2,1,0:T(8,128)(2,1)}, bf16[4,512,1536]{2,1,0:T(8,128)(2,1)}, u32[]{:S(2)}, u32[]{:S(2)}) collective-permute-start(bf16[4,512,1536]{2,1,0:T(8,128)(2,1)} %get-tuple-element.305.refs_9_.refs_10_.refs_11_), channel_id=1, source_target_pairs={{0,1},{1,0},{2,3},{3,2},{4,5},{5,4},{6,7},{7,6},{8,9},{9,8},{10,11... | collective-permute-start | bytes 18874376 | tf_op jit(solution)/shard_map/cond/branch_1_fun/ppermute | solution.py:600
  241.5 14.8 %collective-permute-start.7 = (bf16[1024,2048]{1,0:T(8,128)(2,1)}, bf16[1024,2048]{1,0:T(8,128)(2,1)}, u32[]{:S(2)}, u32[]{:S(2)}) collective-permute-start(bf16[1024,2048]{1,0:T(8,128)(2,1)} %get-tuple-element.928.refs_0_), channel_id=1, source_target_pairs={{0,1},{1,0},{2,3},{3,2},{4,5},{5,4},{6,7},{7,6},{8,9},{9,8},{10,11... | collective-permute-start | bytes 12582920 | tf_op jit(solution)/shard_map/cond/branch_1_fun/ppermute | solution.py:600
  241.9 14.3 %collective-permute-start.8 = (bf16[1024,2048]{1,0:T(8,128)(2,1)}, bf16[1024,2048]{1,0:T(8,128)(2,1)}, u32[]{:S(2)}, u32[]{:S(2)}) collective-permute-start(bf16[1024,2048]{1,0:T(8,128)(2,1)} %get-tuple-element.314.refs_8_.refs_1_.refs_2_), channel_id=1, source_target_pairs={{0,1},{1,0},{2,3},{3,2},{4,5},{5,4},{6,7},{7,6},{8,9},{9,8},{10,11... | collective-permute-start | bytes 12582920 | tf_op jit(solution)/shard_map/cond/branch_1_fun/ppermute | solution.py:600
  282.7 187.8 %reduce-scatter.6.cloned.1.call-start = ((), (), s32[]{:S(2)}) async-start(), calls=%async_computation.4 | async-start | bytes 3932160 | tf_op jit(solution)/shard_map/reduce_scatter | solution.py:832
  310.5 18.3 %collective-permute-start.35 = (bf16[128,2048]{1,0:T(8,128)(2,1)}, bf16[128,2048]{1,0:T(8,128)(2,1)}, u32[]{:S(2)}, u32[]{:S(2)}) collective-permute-start(bf16[128,2048]{1,0:T(8,128)(2,1)} %get-tuple-element.333), channel_id=1, source_target_pairs={{0,4},{2,6},{4,0},{6,2},{1,5},{3,7},{5,1},{7,3},{8,12},{10,14},{12... | collective-permute-start | bytes 1572872 | tf_op jit(solution)/shard_map/cond/branch_1_fun/ppermute | solution.py:600
  312.1 18.8 %collective-permute-start.34 = (bf16[128,2048]{1,0:T(8,128)(2,1)}, bf16[128,2048]{1,0:T(8,128)(2,1)}, u32[]{:S(2)}, u32[]{:S(2)}) collective-permute-start(bf16[128,2048]{1,0:T(8,128)(2,1)} %get-tuple-element.332), channel_id=1, source_target_pairs={{0,2},{2,0},{4,6},{6,4},{1,3},{3,1},{5,7},{7,5},{8,10},{10,8},{12,... | collective-permute-start | bytes 1572872 | tf_op jit(solution)/shard_map/cond/branch_1_fun/ppermute | solution.py:600
  313.5 24.5 %collective-permute-start.40 = (bf16[1024,512]{1,0:T(8,128)(2,1)}, bf16[1024,512]{1,0:T(8,128)(2,1)}, u32[]{:S(2)}, u32[]{:S(2)}) collective-permute-start(bf16[1024,512]{1,0:T(8,128)(2,1)} %get-tuple-element.326.refs_3_), channel_id=1, source_target_pairs={{0,1},{1,0},{2,3},{3,2},{4,5},{5,4},{6,7},{7,6},{8,9},{9,8},{10,11... | collective-permute-start | bytes 3145736 | tf_op jit(solution)/shard_map/cond/branch_1_fun/ppermute | solution.py:600
  313.5 20.6 %collective-permute-start.41 = (bf16[1024,256]{1,0:T(8,128)(2,1)}, bf16[1024,256]{1,0:T(8,128)(2,1)}, u32[]{:S(2)}, u32[]{:S(2)}) collective-permute-start(bf16[1024,256]{1,0:T(8,128)(2,1)} %get-tuple-element.956), channel_id=1, source_target_pairs={{0,1},{1,0},{2,3},{3,2},{4,5},{5,4},{6,7},{7,6},{8,9},{9,8},{10,11... | collective-permute-start | bytes 1572872 | tf_op jit(solution)/shard_map/cond/branch_1_fun/ppermute | solution.py:600
  330.2 20.3 %collective-permute-start.38 = (bf16[128,2048]{1,0:T(8,128)(2,1)S(1)}, bf16[128,2048]{1,0:T(8,128)(2,1)}, u32[]{:S(2)}, u32[]{:S(2)}) collective-permute-start(bf16[128,2048]{1,0:T(8,128)(2,1)S(1)} %add_convert_fusion.2), channel_id=1, source_target_pairs={{0,2},{2,0},{4,6},{6,4},{1,3},{3,1},{5,7},{7,5},{8,10},{10,8},{12,... | collective-permute-start | bytes 1572872 | tf_op jit(solution)/shard_map/cond/branch_1_fun/ppermute | solution.py:600
  332.2 18.3 %collective-permute-start.37 = (bf16[128,2048]{1,0:T(8,128)(2,1)S(1)}, bf16[128,2048]{1,0:T(8,128)(2,1)}, u32[]{:S(2)}, u32[]{:S(2)}) collective-permute-start(bf16[128,2048]{1,0:T(8,128)(2,1)S(1)} %add_convert_fusion.3), channel_id=1, source_target_pairs={{0,4},{2,6},{4,0},{6,2},{1,5},{3,7},{5,1},{7,3},{8,12},{10,14},{12... | collective-permute-start | bytes 1572872 | tf_op jit(solution)/shard_map/cond/branch_1_fun/ppermute | solution.py:600
  332.7 22.8 %collective-permute-start.36 = (bf16[128,2048]{1,0:T(8,128)(2,1)S(1)}, bf16[128,2048]{1,0:T(8,128)(2,1)}, u32[]{:S(2)}, u32[]{:S(2)}) collective-permute-start(bf16[128,2048]{1,0:T(8,128)(2,1)S(1)} %copy-done.35), channel_id=1, source_target_pairs={{0,2},{2,0},{4,6},{6,4},{1,3},{3,1},{5,7},{7,5},{8,10},{10,8},{12,... | collective-permute-start | bytes 1572872 | tf_op jit(solution)/shard_map/cond/branch_1_fun/ppermute | solution.py:600
  334.1 23.1 %collective-permute-start.39 = (bf16[128,2048]{1,0:T(8,128)(2,1)S(1)}, bf16[128,2048]{1,0:T(8,128)(2,1)}, u32[]{:S(2)}, u32[]{:S(2)}) collective-permute-start(bf16[128,2048]{1,0:T(8,128)(2,1)S(1)} %copy-done.34), channel_id=1, source_target_pairs={{0,4},{2,6},{4,0},{6,2},{1,5},{3,7},{5,1},{7,3},{8,12},{10,14},{12... | collective-permute-start | bytes 1572872 | tf_op jit(solution)/shard_map/cond/branch_1_fun/ppermute | solution.py:600
  357.2 165.8 %reduce-scatter.8.cloned.1.call-start = ((), (), s32[]{:S(2)}) async-start(), calls=%async_computation.5 | async-start | bytes 4055040 | tf_op jit(solution)/shard_map/reduce_scatter | solution.py:832
  363.9 15.2 %collective-permute-start.11 = (bf16[128,2048]{1,0:T(8,128)(2,1)}, bf16[128,2048]{1,0:T(8,128)(2,1)}, u32[]{:S(2)}, u32[]{:S(2)}) collective-permute-start(bf16[128,2048]{1,0:T(8,128)(2,1)} %get-tuple-element.972), channel_id=1, source_target_pairs={{0,2},{2,0},{4,6},{6,4},{1,3},{3,1},{5,7},{7,5},{8,10},{10,8},{12,... | collective-permute-start | bytes 1572872 | tf_op jit(solution)/shard_map/cond/branch_1_fun/ppermute | solution.py:600
  365.3 15.2 %collective-permute-start.14 = (bf16[128,2048]{1,0:T(8,128)(2,1)}, bf16[128,2048]{1,0:T(8,128)(2,1)}, u32[]{:S(2)}, u32[]{:S(2)}) collective-permute-start(bf16[128,2048]{1,0:T(8,128)(2,1)} %get-tuple-element.973), channel_id=1, source_target_pairs={{0,4},{2,6},{4,0},{6,2},{1,5},{3,7},{5,1},{7,3},{8,12},{10,14},{12... | collective-permute-start | bytes 1572872 | tf_op jit(solution)/shard_map/cond/branch_1_fun/ppermute | solution.py:600
  365.6 24.7 %collective-permute-start.12 = (bf16[128,2048]{1,0:T(8,128)(2,1)}, bf16[128,2048]{1,0:T(8,128)(2,1)}, u32[]{:S(2)}, u32[]{:S(2)}) collective-permute-start(bf16[128,2048]{1,0:T(8,128)(2,1)} %get-tuple-element.973), channel_id=1, source_target_pairs={{0,2},{2,0},{4,6},{6,4},{1,3},{3,1},{5,7},{7,5},{8,10},{10,8},{12,... | collective-permute-start | bytes 1572872 | tf_op jit(solution)/shard_map/cond/branch_1_fun/ppermute | solution.py:600
  366.3 25.5 %collective-permute-start.13 = (bf16[128,2048]{1,0:T(8,128)(2,1)}, bf16[128,2048]{1,0:T(8,128)(2,1)}, u32[]{:S(2)}, u32[]{:S(2)}) collective-permute-start(bf16[128,2048]{1,0:T(8,128)(2,1)} %get-tuple-element.972), channel_id=1, source_target_pairs={{0,4},{2,6},{4,0},{6,2},{1,5},{3,7},{5,1},{7,3},{8,12},{10,14},{12... | collective-permute-start | bytes 1572872 | tf_op jit(solution)/shard_map/cond/branch_1_fun/ppermute | solution.py:600
  380.5 19.9 %collective-permute-start.15 = (bf16[128,2048]{1,0:T(8,128)(2,1)}, bf16[128,2048]{1,0:T(8,128)(2,1)}, u32[]{:S(2)}, u32[]{:S(2)}) collective-permute-start(bf16[128,2048]{1,0:T(8,128)(2,1)} %collective-permute-done.11), channel_id=1, source_target_pairs={{0,4},{2,6},{4,0},{6,2},{1,5},{3,7},{5,1},{7,3},{8,12},{10,14},{12... | collective-permute-start | bytes 1572872 | tf_op jit(solution)/shard_map/cond/branch_1_fun/ppermute | solution.py:600
  380.8 19.6 %collective-permute-start.16 = (bf16[128,2048]{1,0:T(8,128)(2,1)}, bf16[128,2048]{1,0:T(8,128)(2,1)}, u32[]{:S(2)}, u32[]{:S(2)}) collective-permute-start(bf16[128,2048]{1,0:T(8,128)(2,1)} %collective-permute-done.14), channel_id=1, source_target_pairs={{0,2},{2,0},{4,6},{6,4},{1,3},{3,1},{5,7},{7,5},{8,10},{10,8},{12,... | collective-permute-start | bytes 1572872 | tf_op jit(solution)/shard_map/cond/branch_1_fun/ppermute | solution.py:600
  400.5 49.4 %collective-permute-start.66 = (bf16[256,2048]{1,0:T(8,128)(2,1)}, bf16[256,2048]{1,0:T(8,128)(2,1)}, u32[]{:S(2)}, u32[]{:S(2)}) collective-permute-start(bf16[256,2048]{1,0:T(8,128)(2,1)} %get-tuple-element.722), channel_id=1, source_target_pairs={{0,2},{2,0},{4,6},{6,4},{1,3},{3,1},{5,7},{7,5},{8,10},{10,8},{12,... | collective-permute-start | bytes 3145736 | tf_op jit(solution)/shard_map/ppermute | solution.py:600
  401.1 48.8 %collective-permute-start.67 = (bf16[256,2048]{1,0:T(8,128)(2,1)}, bf16[256,2048]{1,0:T(8,128)(2,1)}, u32[]{:S(2)}, u32[]{:S(2)}) collective-permute-start(bf16[256,2048]{1,0:T(8,128)(2,1)} %get-tuple-element.723), channel_id=1, source_target_pairs={{0,4},{2,6},{4,0},{6,2},{1,5},{3,7},{5,1},{7,3},{8,12},{10,14},{12... | collective-permute-start | bytes 3145736 | tf_op jit(solution)/shard_map/ppermute | solution.py:600
  401.4 48.4 %collective-permute-start.68 = (bf16[256,2048]{1,0:T(8,128)(2,1)}, bf16[256,2048]{1,0:T(8,128)(2,1)}, u32[]{:S(2)}, u32[]{:S(2)}) collective-permute-start(bf16[256,2048]{1,0:T(8,128)(2,1)} %get-tuple-element.724), channel_id=1, source_target_pairs={{0,6},{2,4},{4,2},{6,0},{1,7},{3,5},{5,3},{7,1},{8,14},{10,12},{12... | collective-permute-start | bytes 3145736 | tf_op jit(solution)/shard_map/ppermute | solution.py:600
  411.3 24.8 %collective-permute-start.17 = (bf16[1024,2048]{1,0:T(8,128)(2,1)}, bf16[1024,2048]{1,0:T(8,128)(2,1)}, u32[]{:S(2)}, u32[]{:S(2)}) collective-permute-start(bf16[1024,2048]{1,0:T(8,128)(2,1)} %get-tuple-element.989), channel_id=1, source_target_pairs={{0,1},{1,0},{2,3},{3,2},{4,5},{5,4},{6,7},{7,6},{8,9},{9,8},{10,11... | collective-permute-start | bytes 12582920 | tf_op jit(solution)/shard_map/cond/branch_1_fun/ppermute | solution.py:600
  455.3 14.3 %collective-permute-start.19 = (bf16[128,2048]{1,0:T(8,128)(2,1)}, bf16[128,2048]{1,0:T(8,128)(2,1)}, u32[]{:S(2)}, u32[]{:S(2)}) collective-permute-start(bf16[128,2048]{1,0:T(8,128)(2,1)} %get-tuple-element.411), channel_id=1, source_target_pairs={{0,2},{2,0},{4,6},{6,4},{1,3},{3,1},{5,7},{7,5},{8,10},{10,8},{12,... | collective-permute-start | bytes 1572872 | tf_op jit(solution)/shard_map/cond/branch_1_fun/ppermute | solution.py:600
  456.5 14.0 %collective-permute-start.20 = (bf16[128,2048]{1,0:T(8,128)(2,1)}, bf16[128,2048]{1,0:T(8,128)(2,1)}, u32[]{:S(2)}, u32[]{:S(2)}) collective-permute-start(bf16[128,2048]{1,0:T(8,128)(2,1)} %get-tuple-element.412), channel_id=1, source_target_pairs={{0,4},{2,6},{4,0},{6,2},{1,5},{3,7},{5,1},{7,3},{8,12},{10,14},{12... | collective-permute-start | bytes 1572872 | tf_op jit(solution)/shard_map/cond/branch_1_fun/ppermute | solution.py:600
  470.5 15.1 %collective-permute-start.43 = (bf16[128,2048]{1,0:T(8,128)(2,1)}, bf16[128,2048]{1,0:T(8,128)(2,1)S(1)}, u32[]{:S(2)}, u32[]{:S(2)}) collective-permute-start(bf16[128,2048]{1,0:T(8,128)(2,1)} %get-tuple-element.426), channel_id=1, source_target_pairs={{0,2},{2,0},{4,6},{6,4},{1,3},{3,1},{5,7},{7,5},{8,10},{10,8},{12,... | collective-permute-start | bytes 1572872 | tf_op jit(solution)/shard_map/cond/branch_1_fun/ppermute | solution.py:600
  471.3 15.1 %collective-permute-start.46 = (bf16[128,2048]{1,0:T(8,128)(2,1)}, bf16[128,2048]{1,0:T(8,128)(2,1)S(1)}, u32[]{:S(2)}, u32[]{:S(2)}) collective-permute-start(bf16[128,2048]{1,0:T(8,128)(2,1)} %get-tuple-element.429), channel_id=1, source_target_pairs={{0,4},{2,6},{4,0},{6,2},{1,5},{3,7},{5,1},{7,3},{8,12},{10,14},{12... | collective-permute-start | bytes 1572872 | tf_op jit(solution)/shard_map/cond/branch_1_fun/ppermute | solution.py:600
  474.3 21.0 %collective-permute-start.44 = (bf16[128,2048]{1,0:T(8,128)(2,1)}, bf16[128,2048]{1,0:T(8,128)(2,1)S(1)}, u32[]{:S(2)}, u32[]{:S(2)}) collective-permute-start(bf16[128,2048]{1,0:T(8,128)(2,1)} %add_convert_fusion.5), channel_id=1, source_target_pairs={{0,4},{2,6},{4,0},{6,2},{1,5},{3,7},{5,1},{7,3},{8,12},{10,14},{12... | collective-permute-start | bytes 1572872 | tf_op jit(solution)/shard_map/cond/branch_1_fun/ppermute | solution.py:600
  477.4 17.8 %collective-permute-start.45 = (bf16[128,2048]{1,0:T(8,128)(2,1)}, bf16[128,2048]{1,0:T(8,128)(2,1)}, u32[]{:S(2)}, u32[]{:S(2)}) collective-permute-start(bf16[128,2048]{1,0:T(8,128)(2,1)} %add_convert_fusion.4), channel_id=1, source_target_pairs={{0,2},{2,0},{4,6},{6,4},{1,3},{3,1},{5,7},{7,5},{8,10},{10,8},{12,... | collective-permute-start | bytes 1572872 | tf_op jit(solution)/shard_map/cond/branch_1_fun/ppermute | solution.py:600
  496.3 16.4 %collective-permute-start.47 = (bf16[128,2304]{1,0:T(8,128)(2,1)S(1)}, bf16[128,2304]{1,0:T(8,128)(2,1)}, u32[]{:S(2)}, u32[]{:S(2)}) collective-permute-start(bf16[128,2304]{1,0:T(8,128)(2,1)S(1)} %get-tuple-element.786), channel_id=1, source_target_pairs={{0,2},{2,0},{4,6},{6,4},{1,3},{3,1},{5,7},{7,5},{8,10},{10,8},{12,... | collective-permute-start | bytes 1769480 | tf_op jit(solution)/shard_map/cond/branch_1_fun/ppermute | solution.py:600
  497.5 25.6 %collective-permute-start.48 = (bf16[128,2304]{1,0:T(8,128)(2,1)S(1)}, bf16[128,2304]{1,0:T(8,128)(2,1)}, u32[]{:S(2)}, u32[]{:S(2)}) collective-permute-start(bf16[128,2304]{1,0:T(8,128)(2,1)S(1)} %get-tuple-element.785), channel_id=1, source_target_pairs={{0,4},{2,6},{4,0},{6,2},{1,5},{3,7},{5,1},{7,3},{8,12},{10,14},{12... | collective-permute-start | bytes 1769480 | tf_op jit(solution)/shard_map/cond/branch_1_fun/ppermute | solution.py:600
  497.9 25.2 %collective-permute-start.49 = (bf16[128,2304]{1,0:T(8,128)(2,1)S(1)}, bf16[128,2304]{1,0:T(8,128)(2,1)}, u32[]{:S(2)}, u32[]{:S(2)}) collective-permute-start(bf16[128,2304]{1,0:T(8,128)(2,1)S(1)} %get-tuple-element.784), channel_id=1, source_target_pairs={{0,6},{2,4},{4,2},{6,0},{1,7},{3,5},{5,3},{7,1},{8,14},{10,12},{12... | collective-permute-start | bytes 1769480 | tf_op jit(solution)/shard_map/cond/branch_1_fun/ppermute | solution.py:600
  (54 other events, 755.0 us)
Sparse Core Ops, SparseCore 0:
  29.5 65.4 all-gather.6
  98.0 114.7 all-gather.8
  214.3 61.7 all-gather.10
  282.8 112.0 reduce-scatter.3
  397.1 60.7 reduce-scatter.5
  460.1 61.8 reduce-scatter.7

commit v5 on v4

--- a/solution.py
+++ b/solution.py
@@ -319,7 +319,16 @@
 
 def rows_product_kernel(count, normed, number, *refs):
     pieces, refs = refs[:count], list(refs[count:])
-    gain = refs.pop(0)[...] if normed else None
+    gain = None
+    if normed:
+        source = refs.pop(0)
+        gain = source[...]
+        if len(source.shape) == 3:
+            size = pieces[0].shape[1] // (source.shape[0] * normed)
+            parts = [
+                gain[i, j : j + 1, :size] for i in range(source.shape[0]) for j in range(normed)
+            ]
+            gain = jnp.concatenate(parts, axis=1).astype(f32)
     weights, refs = refs[:number], refs[number:]
     whole = pieces[0]
     if count > 1 or normed:
@@ -340,11 +349,18 @@
     joined = len(pieces) > 1 or gain is not None
     shapes = [jax.ShapeDtypeStruct((rows, width), bf16)] if joined else []
     shapes += [jax.ShapeDtypeStruct((rows, block), dtype)] * len(weights)
-    gains = [] if gain is None else [gain.reshape(1, -1)]
+    gains, gain_specs, normed = [], [], int(gain is not None)
+    if isinstance(gain, tuple):
+        array, first, normed = gain
+        gains = [array]
+        gain_specs = [pl.BlockSpec((parts, 16, array.shape[2]), lambda i: (0, first // 16, 0))]
+    elif normed:
+        gains, gain_specs = [gain.reshape(1, -1)], [resident((1, gain.shape[0]))]
     got = pl.pallas_call(
-        functools.partial(rows_product_kernel, len(pieces), gain is not None, len(weights)),
+        functools.partial(rows_product_kernel, len(pieces), normed, len(weights)),
         grid=(1,),
-        in_specs=[resident(piece.shape) for piece in list(pieces) + gains]
+        in_specs=[resident(piece.shape) for piece in pieces]
+        + gain_specs
         + [
             pl.BlockSpec(
                 (parts, step, block), lambda i: (0, 0, place), pipeline_mode=pl.Buffered(1)
@@ -400,6 +416,102 @@
         cost_estimate=BESIDE,
         name=name,
     )(*[left for left, _ in pairs], *[right for _, right in pairs], *received, *below)
+
+
+def cut_kernel(size, parts, me_ref, *refs):
+    arrays, below, outs = refs[:parts], refs[parts], refs[parts + 1 :]
+    rows = outs[0].shape[0] - below.shape[0]
+    for k, out in enumerate(outs):
+        owner = me_ref[0] ^ k
+        first = 0
+        for array in arrays:
+            if array.shape[0] == rows:
+                wide = array.shape[1] // size
+                block = array[:, pl.ds(pl.multiple_of(owner * wide, 128), wide)]
+            else:
+                wide = array.shape[0] // size
+                block = array[pl.ds(pl.multiple_of(owner * wide, 128), wide)]
+                block = block.astype(f32).T.astype(bf16)
+            out[:rows, first : first + wide] = block
+            first += wide
+        out[rows:] = below[...]
+
+
+def cut_call(me, size, arrays, below, name):
+    rows = arrays[0].shape[0]
+    columns = sum(
+        array.shape[1 if array.shape[0] == rows else 0] // size for array in arrays
+    )
+    shape = jax.ShapeDtypeStruct((rows + below.shape[0], columns), bf16)
+    return list(
+        pl.pallas_call(
+            functools.partial(cut_kernel, size, len(arrays)),
+            grid=(1,),
+            in_specs=[pl.BlockSpec(memory_space=pltpu.SMEM)]
+            + [resident(array.shape) for array in list(arrays) + [below]],
+            out_specs=[resident(shape.shape)] * size,
+            out_shape=[shape] * size,
+            compiler_params=pltpu.CompilerParams(vmem_limit_bytes=32 << 20),
+            cost_estimate=BESIDE,
+            name=name,
+        )(me.reshape(1), *arrays, below)
+    )
+
+
+def rows_cut_kernel(size, rows, me_ref, source, *outs):
+    for k, out in enumerate(outs):
+        first = pl.multiple_of((me_ref[0] ^ k) * rows, rows)
+        out[:rows] = source[pl.ds(first, rows)]
+        out[rows:] = source[size * rows :]
+
+
+def rows_cut_call(me, size, source, rows, name):
+    deep = source.shape[0] - (size - 1) * rows
+    shape = jax.ShapeDtypeStruct((deep, source.shape[1]), bf16)
+    return list(
+        pl.pallas_call(
+            functools.partial(rows_cut_kernel, size, rows),
+            grid=(1,),
+            in_specs=[pl.BlockSpec(memory_space=pltpu.SMEM), resident(source.shape)],
+            out_specs=[resident(shape.shape)] * size,
+            out_shape=[shape] * size,
+            compiler_params=pltpu.CompilerParams(vmem_limit_bytes=32 << 20),
+            cost_estimate=BESIDE,
+            name=name,
+        )(me.reshape(1), source)
+    )
+
+
+def stack_kernel(size, below, me_ref, *refs):
+    pieces, out = refs[:size], refs[size]
+    rows = pieces[0].shape[0] - 16
+    under = jnp.zeros((16, out.shape[1]), f32)
+    place = lax.broadcasted_iota(jnp.int32, under.shape, 0)
+    for k, piece in enumerate(pieces):
+        owner = me_ref[0] ^ k
+        out[pl.ds(pl.multiple_of(owner * rows, rows), rows)] = piece[:rows]
+        more = piece[rows:].astype(f32)
+        for i in range(below):
+            under = jnp.where(place == owner * below + i, more[i : i + 1], under)
+    out[size * rows :] = under.astype(bf16)
+
+
+def stack_call(me, pieces, below, name):
+    size = len(pieces)
+    shape = jax.ShapeDtypeStruct(
+        (size * (pieces[0].shape[0] - 16) + 16, pieces[0].shape[1]), bf16
+    )
+    return pl.pallas_call(
+        functools.partial(stack_kernel, size, below),
+        grid=(1,),
+        in_specs=[pl.BlockSpec(memory_space=pltpu.SMEM)]
+        + [resident(piece.shape) for piece in pieces],
+        out_specs=resident(shape.shape),
+        out_shape=shape,
+        compiler_params=pltpu.CompilerParams(vmem_limit_bytes=32 << 20),
+        cost_estimate=BESIDE,
+        name=name,
+    )(me.reshape(1), *pieces)
 
 
 def near_kernel(size, widths, me_ref, *refs):
@@ -639,6 +751,10 @@
     return [piece_of(me)] + [trade(piece_of(me ^ k), "model", k) for k in others]
 
 
+def swap_pieces(pieces):
+    return [pieces[0]] + [trade(pieces[k], "model", k) for k in range(1, len(pieces))]
+
+
 def take(array, index, count):
     size = array.shape[1] // count
     return lax.dynamic_slice_in_dim(array, index * size, size, 1)
@@ -646,14 +762,6 @@
 
 def rows_at(array):
     return lambda i: lax.dynamic_index_in_dim(array, i, 0, keepdims=False)
-
-
-def in_order(pieces):
-    me = lax.axis_index("model")
-    size = len(pieces)
-    return jnp.stack(
-        [lax.select_n(me, *[pieces[j ^ i] for j in range(size)]) for i in range(size)]
-    )
 
 
 def after(value, *first):
@@ -694,7 +802,7 @@
     cols = q_cols + 2 * kv_cols
     wide = cols + q_cols
     ff = w_gate.shape[1] // model
-    always = (segments[0] * segments[0] + segments[0]) % 2 == 0
+    always = (segments[0] * segments[0] + segments[0]) & 1 == 0
 
     small = jnp.concatenate([attn_gain, mlp_gain, query_gain, key_gain])
     small_rows = -(-small.shape[0] // wide)
@@ -712,16 +820,8 @@
         ]
     )
     extra = jnp.pad(extra, ((0, -extra.shape[0] % 16), (0, 0)))
-    turned_output = w_output.T
-
-    def attn_piece(i):
-        parts = [
-            take(w_query, i, model),
-            take(key_weight, i, model),
-            take(value_weight, i, model),
-            take(turned_output, i, model),
-        ]
-        return jnp.concatenate([jnp.concatenate(parts, axis=1), extra])
+    me = lax.axis_index("model")
+    attn_arrays = [w_query, key_weight, value_weight, w_output]
 
     turned_down = w_down.T
     chunks = [ff - ff // 3, ff // 3] if ff % 768 == 0 else [ff]
@@ -730,9 +830,9 @@
     def over_data(pieces):
         return lax.all_gather(pieces, "data", axis=0, tiled=False)
 
-    attn_got = swap(attn_piece)
-    tied = lax.optimization_barrier((halves(hidden_in), halves(out_grad), attn_got))
-    grad_halves = tied[1]
+    attn_got = swap_pieces(cut_call(me, model, attn_arrays, extra, "attention_pieces"))
+    tied = lax.optimization_barrier((halves(hidden_in), halves(out_grad), always, attn_got))
+    grad_halves, always = tied[1:3]
     x_near = spread_near(tied[0])
     tied = lax.optimization_barrier((w_gate, w_up, turned_down, x_near))
     w_gate_sent, w_up_sent, turned_down, x_near = tied
@@ -759,38 +859,33 @@
     pos_all = 8.0 * places_of(small_rows + place_rows) + places_of(small_rows + 2 * place_rows)
     cosine, sine = tables(pos_all, head_size)
 
-    attn_near = in_order(attn_got)
-    gain_rows = attn_near[:, shard : shard + small_rows].reshape(-1, wide)
-    gain_rows = jnp.pad(gain_rows, ((0, -gain_rows.shape[0] % 16), (0, 0)))
-    near = jnp.concatenate([attn_near[:, :shard].reshape(-1, wide), gain_rows])
-    me = lax.axis_index("model")
+    near = stack_call(me, attn_got, small_rows, "attention_exchange")
     mlp_near = near_call(me, mlp_got, [3 * count for count in chunks], "hidden_exchange")
     attn_full = over_data(near)
-    tied = lax.optimization_barrier((attn_full, mlp_near, x_blocks, cosine, sine))
-    attn_full, mlp_near, x_blocks, cosine, sine = tied
+    seg_rows = jnp.pad(seg_all[:, None], ((0, 0), (0, 7), (0, 0)))
+    shared = [cosine, sine, seg_all[:, :, None], seg_rows]
+    tied = lax.optimization_barrier((attn_full, mlp_near, x_blocks, shared))
+    attn_full, mlp_near, x_blocks, shared = tied
     mlp_full = [over_data(piece) for piece in mlp_near]
 
-    gains = attn_full[:, model * shard : model * shard + model * small_rows]
-    gains = gains.reshape(data * model, -1).astype(f32)
-    part = query_gain.shape[0]
-    gain_in = gains[:, :shard].reshape(-1)
-    gain_mid = gains[:, shard : 2 * shard].reshape(-1)
-    gain_query = gains[:, 2 * shard : 2 * shard + part].reshape(-1)
-    gain_key = gains[:, 2 * shard + part : 2 * shard + 2 * part].reshape(-1)
     def with_cores(weight):
         return [weight] + [trade(weight, "tp", j) for j in range(1, cores)]
 
     near_rows = model * shard
+    part = query_gain.shape[0]
     grad_near = spread_near(after(grad_halves, *x_blocks, *mlp_near))
 
-    seg_rows = jnp.pad(seg_all[:, None], ((0, 0), (0, 7), (0, 0)))
-    seg_columns = seg_all[:, :, None]
-    head_gains = jnp.pad(jnp.stack([gain_query, gain_key]), ((0, 6), (0, 0)))
-    shared = [cosine, sine, seg_columns, seg_rows]
+    def gain_of(source, first, size):
+        rows = source[:, near_rows : near_rows + model * small_rows]
+        return rows.reshape(data * model, -1)[:, first : first + size].astype(f32).reshape(-1)
+
     o_place = [cols // q_cols] * cores
 
     def product_phase():
         w_attn = with_cores(attn_full)
+        gain_in = (attn_full, near_rows, model)
+        if shard % 128:
+            gain_in = gain_of(attn_full, 0, shard)
         normed_in, first_raw = rows_product(
             x_blocks, gain_in, w_attn[:1], cols, 0, near_rows, f32, "query_key_value"
         )
@@ -800,9 +895,14 @@
                 [normed_in], None, [w_attn[j]], cols, 0, near_rows, f32, "query_key_value_other"
             )[1][0]
             raw.append(trade(mine, "tp", j).reshape(model, half, cols))
-        return w_attn[1:], normed_in, raw
-
-    w_others, own_normed, raw = phase(always, product_phase)
+        source = after(attn_full, mine) if cores > 1 else attn_full
+        head_gains = [gain_of(source, 2 * shard + i * part, part) for i in range(2)]
+        head_gains = jnp.pad(jnp.stack(head_gains), ((0, 6), (0, 0)))
+        gains = gain_of(source, 0, shard), gain_of(source, shard, shard)
+        return w_attn[1:], normed_in, raw, head_gains, gains
+
+    w_others, own_normed, raw, head_gains, gains = phase(always, product_phase)
+    gain_in, gain_mid = gains
     w_attn = [attn_full] + w_others
     raw, grad_near = lax.optimization_barrier((raw, grad_near))
 
@@ -939,7 +1039,9 @@
                 ((seq_len, cols), bf16),
             ],
         )
-        return with_cores(branch), list(qkv_back), head_grads
+        sent = after(branch, *att_grads)
+        branches = [branch] + [trade(sent, "tp", j) for j in range(1, cores)]
+        return branches, list(qkv_back), head_grads
 
     branch, qkv_back, head_grads = phase(always, attend_back_phase)
 
@@ -981,11 +1083,8 @@
 
     hidden_out, grad_in, mlp_got = phase(always, last_phase)
     attn_sum = after(attn_sum, grad_in)
-    weight_rows = attn_sum[:near_rows].reshape(model, shard, wide)
-    gain_row = attn_sum[near_rows:]
-    gain_row = jnp.broadcast_to(gain_row, (model,) + gain_row.shape)
-    attn_rows = jnp.concatenate([weight_rows, gain_row], axis=1)
-    attn_got = swap(rows_at(attn_rows))
+    attn_pieces = rows_cut_call(me, model, attn_sum, shard, "attention_sums")
+    attn_got = swap_pieces(attn_pieces)
     layout = [
         [
             (kind, first, ff, size, kind == 2)
@@ -994,7 +1093,7 @@
         ]
     ]
     shapes = [w_gate.shape, w_up.shape, w_down.shape]
-    mlp_got = after(mlp_got, attn_rows)
+    mlp_got = after(mlp_got, attn_pieces[0])
     owned = owned_call(
         me, [mlp_got], layout, [w_gate, w_up], mlp_gain, shapes, "hidden_owned"
     )

time: 558 us -> 556 us (level)
    reduce_scatter x3, waiting for transfers between devices: 0.01 us -> 6.98 us  [data_sum(): return lax.psum_scatter(total, 'data', scatter_dimension=0, tiled=False)]
    ppermute x72, waiting for transfers between devices: 190 us -> 183 us  [trade(): lax.ppermute(block, axis, [(i, i ^ step) for i in range(lax.axis_size(axi...]
    pallas_call x3 -> x6, Pallas kernels: 21.7 us -> 24.2 us  [the longest x3 22.3 us: rows_product(): pl.pallas_call(functools.partial(rows_product_kernel, len(pieces), normed...]
  transfers between devices with their start and end apart: 78 -> 78, of which waited for: 40 -> 44; matrix products, arithmetic and copies ran while one was open for 6% -> 5% of each run, Pallas kernels for 41% -> 41%
where the time goes in v5:
time: 556 us; the launch traced here: 549 us
  Pallas kernels  230 us (41%)
  waiting for transfers between devices  191 us (34%)
  starting transfers between devices  66.3 us (12%)
  local copies, waits for them, and re-layouts  22.3 us (4%)
  other arithmetic  18.4 us (3%)
  between operations  16.9 us (3%)
    ppermute x72, waiting for transfers between devices, trade(): lax.ppermute(block, axis, [(i, i ^ step) for i in range(lax.axis_size(axi...  183 us
    ppermute x72, starting transfers between devices, trade(): lax.ppermute(block, axis, [(i, i ^ step) for i in range(lax.axis_size(axi...  66.1 us
    pallas_call x7, Pallas kernels, project(): pl.pallas_call(functools.partial(project_kernel, len(lefts)), grid=(parts...  56.1 us
    pallas_call x4, Pallas kernels, hidden_call(): pl.pallas_call(functools.partial(hidden_kernel, first, cores, len(x_piece...  47.1 us
    pallas_call x3, Pallas kernels, weight_grad(): pl.pallas_call(functools.partial(weight_grad_kernel, [len(group) for grou...  44.6 us
    pallas_call x2, Pallas kernels, attention_call(): pl.pallas_call(kernel, grid=(halves[0].shape[0],), in_specs=[pl.BlockSpec...  27.9 us
    pallas_call x3, Pallas kernels, rows_product(): pl.pallas_call(functools.partial(rows_product_kernel, len(pieces), normed...  22.3 us
    pallas_call x4, Pallas kernels, rows_call(): pl.pallas_call(functools.partial(rows_kernel, kind, len(got)), grid=(2,),...  18.2 us
  transfers between devices with their start and end apart: 78, of which 44 were waited for; matrix products, arithmetic and copies ran while one was open for 5% of the time, Pallas kernels for 41%

profile of v5, /device:TPU:0, one launch (start us, length us, event | category | flops | bytes accessed | tf_op | source)
XLA Modules:
  0.0 548.7 jit_solution(4069471246755515527)
XLA Ops:
  13.4 3.0 collective-permute-start.50
  17.9 4.7 collective-permute-done.50.refs_1_
  22.7 5.4 collective-permute-done.51.refs_2_
  34.7 2.5 fusion.33
  41.3 10.7 %collective-permute-done.53 = bf16[128,2048]{1,0:T(8,128)(2,1)S(1)} collective-permute-done((bf16[128,2048]{1,0:T(8,128)(2,1)S(1)}, bf16[128,2048]{1,0:T(8,128)(2,1)S(1)}, u32[]{:S(2)}, u32[]{:S(2)}) %collective-permute-start.53) | collective-permute-done | bytes 524320 | tf_op jit(solution)/shard_map/ppermute | solution.py:712
  52.0 8.9 %collective-permute-done.54 = bf16[128,2048]{1,0:T(8,128)(2,1)S(1)} collective-permute-done((bf16[128,2048]{1,0:T(8,128)(2,1)S(1)}, bf16[128,2048]{1,0:T(8,128)(2,1)S(1)}, u32[]{:S(2)}, u32[]{:S(2)}) %collective-permute-start.54) | collective-permute-done | bytes 524320 | tf_op jit(solution)/shard_map/ppermute | solution.py:712
  67.7 3.7 fusion.6
  73.4 5.4 collective-permute-done.57.refs_1_
  78.8 13.7 %collective-permute-done.58.refs_2_ = bf16[128,2304]{1,0:T(8,128)(2,1)S(1)} collective-permute-done((bf16[128,2304]{1,0:T(8,128)(2,1)S(1)}, bf16[128,2304]{1,0:T(8,128)(2,1)S(1)}, u32[]{:S(2)}, u32[]{:S(2)}) %collective-permute-start.58) | collective-permute-done | bytes 589856 | tf_op jit(solution)/shard_map/ppermute | solution.py:712
  94.1 6.5 %collective-permute-done.60 = bf16[128,2048]{1,0:T(8,128)(2,1)S(1)} collective-permute-done((bf16[128,2048]{1,0:T(8,128)(2,1)S(1)}, bf16[128,2048]{1,0:T(8,128)(2,1)S(1)}, u32[]{:S(2)}, u32[]{:S(2)}) %collective-permute-start.60) | collective-permute-done | bytes 524320 | tf_op jit(solution)/shard_map/ppermute | solution.py:712
  106.3 19.6 %conditional.10 = (bf16[4,528,768]{2,1,0:T(8,128)(2,1)}, bf16[1024,2048]{1,0:T(8,128)(2,1)}, f32[4,256,512]{2,1,0:T(8,128)}, f32[4,256,512]{2,1,0:T(8,128)}, f32...) conditional(s32[]{:T(128)} %convert_element_type.143, () %tuple.119, ...), branch_computations={%region_0.1_spmd, %region_1.2_spmd} | conditional | flops 2108416 | bytes 21625480 | solution.py:708
  106.6 8.1 %query_key_value.1 = (bf16[1024,2048]{1,0:T(8,128)(2,1)}, f32[1024,512]{1,0:T(8,128)}) custom-call(bf16[128,2048]{1,0:T(8,128)(2,1)S(1)} %get-tuple-element.241.refs_0_, bf16[128,2048]{1,0:T(8,128)(2,1)} %get-tuple-element.242.refs_1_, bf16[128,2048]{1,0:T(8,128)(2,1)} %get-tuple-element.243.refs_2_, bf16[128,2048]{1,0:T(8,128)(2,1)} %get-tuple-element.244.refs_3_, ...), custom_call_target="tpu_custom_call" | custom-call | flops 1048576 | bytes 65536 | tf_op jit(solution)/shard_map/cond/branch_1_fun/query_key_value/pallas_call | solution.py:359
  114.7 6.5 %query_key_value_other.1 = f32[1024,512]{1,0:T(8,128)} custom-call(bf16[1024,2048]{1,0:T(8,128)(2,1)} %get-tuple-element.884.refs_0_, bf16[4,528,768]{2,1,0:T(8,128)(2,1)} %collective-permute-done.48.refs_1_), custom_call_target="tpu_custom_call" | custom-call | flops 1048576 | bytes 65536 | tf_op jit(solution)/shard_map/cond/branch_1_fun/query_key_value_other/pallas_call | solution.py:359
  122.9 3.0 collective-permute-done.49
  125.9 17.0 %conditional.11 = (bf16[1024,2048]{1,0:T(8,128)(2,1)}, bf16[4,256,256]{2,1,0:T(8,128)(2,1)}, bf16[4,256,256]{2,1,0:T(8,128)(2,1)}, bf16[128,2048]{1,0:T(8,128)(2...) conditional(s32[]{:T(128)} %convert_element_type.143, () %tuple.126, ...), branch_computations={%region_2.3_spmd, %region_3.4_spmd} | conditional | flops 1048576 | bytes 24199384 | solution.py:708
  127.2 11.7 %attend.1 = (bf16[4,256,256]{2,1,0:T(8,128)(2,1)}, bf16[4,256,256]{2,1,0:T(8,128)(2,1)}) custom-call(s32[1]{0:T(128)} %bitcast.6.core_ref, f32[4,256,512]{2,1,0:T(8,128)} %get-tuple-element.254.refs_0_, f32[4,256,512]{2,1,0:T(8,128)} %get-tuple-element.255.refs_1_, f32[4,512,128]{2,1,0:T(8,128)} %get-tuple-element.256.refs_2_, ...), custom_call_target="tpu_custom_call" | custom-call | flops 1048576 | bytes 65536 | tf_op jit(solution)/shard_map/cond/branch_1_fun/attend/pallas_call | solution.py:179
  142.9 82.3 %conditional.12 = (f32[256,2048]{1,0:T(8,128)}, bf16[128,2048]{1,0:T(8,128)(2,1)}, bf16[128,2048]{1,0:T(8,128)(2,1)}, bf16[128,2048]{1,0:T(8,128)(2,1)}, bf16[12...) conditional(s32[]{:T(128)} %convert_element_type.143, ...), branch_computations={%region_4.5_spmd, %region_5.6_spmd} | conditional | flops 6291456 | bytes 58327740 | solution.py:708
  142.9 4.4 attention_out_far.1
  149.4 5.1 attention_out.1
  154.5 6.9 %collective-permute-done.19 = bf16[128,2048]{1,0:T(8,128)(2,1)S(1)} collective-permute-done((bf16[128,2048]{1,0:T(8,128)(2,1)}, bf16[128,2048]{1,0:T(8,128)(2,1)S(1)}, u32[]{:S(2)}, u32[]{:S(2)}) %collective-permute-start.19) | collective-permute-done | bytes 524320 | tf_op jit(solution)/shard_map/cond/branch_1_fun/ppermute | solution.py:712
  168.2 8.5 %collective-permute-done.21.refs_2_ = bf16[128,2048]{1,0:T(8,128)(2,1)S(1)} collective-permute-done((bf16[128,2048]{1,0:T(8,128)(2,1)}, bf16[128,2048]{1,0:T(8,128)(2,1)S(1)}, u32[]{:S(2)}, u32[]{:S(2)}) %collective-permute-start.21) | collective-permute-done | bytes 524320 | tf_op jit(solution)/shard_map/cond/branch_1_fun/ppermute | solution.py:712
  178.3 9.0 %collective-permute-done.22.refs_3_ = bf16[128,2048]{1,0:T(8,128)(2,1)S(1)} collective-permute-done((bf16[128,2048]{1,0:T(8,128)(2,1)S(1)}, bf16[128,2048]{1,0:T(8,128)(2,1)S(1)}, u32[]{:S(2)}, u32[]{:S(2)}) %collective-permute-start.22) | collective-permute-done | bytes 524320 | tf_op jit(solution)/shard_map/cond/branch_1_fun/ppermute | solution.py:712
  187.3 2.7 middle.1
  194.1 11.1 %collective-permute-done.25 = bf16[128,2048]{1,0:T(8,128)(2,1)} collective-permute-done((bf16[128,2048]{1,0:T(8,128)(2,1)}, bf16[128,2048]{1,0:T(8,128)(2,1)}, u32[]{:S(2)}, u32[]{:S(2)}) %collective-permute-start.25) | collective-permute-done | bytes 524320 | tf_op jit(solution)/shard_map/cond/branch_1_fun/ppermute | solution.py:712
  207.6 4.1 out_grad_rows.1
  211.7 4.8 collective-permute-done.26
  217.1 8.1 %collective-permute-done.29 = bf16[128,2048]{1,0:T(8,128)(2,1)} collective-permute-done((bf16[128,2048]{1,0:T(8,128)(2,1)}, bf16[128,2048]{1,0:T(8,128)(2,1)}, u32[]{:S(2)}, u32[]{:S(2)}) %collective-permute-start.29) | collective-permute-done | bytes 524320 | tf_op jit(solution)/shard_map/cond/branch_1_fun/ppermute | solution.py:712
  225.2 57.1 %conditional.13 = (bf16[4,512,1536]{2,1,0:T(8,128)(2,1)}, bf16[1024,2048]{1,0:T(8,128)(2,1)}, bf16[1024,2048]{1,0:T(8,128)(2,1)}, bf16[1024,2048]{1,0:T(8,128)(2...) conditional(s32[]{:T(128)} %convert_element_type.143, ...), branch_computations={%region_6.7_spmd, %region_7.8_spmd} | conditional | flops 3145728 | bytes 84083008 | solution.py:708
  225.7 15.4 %hidden_units_a.1 = (bf16[1024,2048]{1,0:T(8,128)(2,1)}, bf16[1024,1024]{1,0:T(8,128)(2,1)}, bf16[1024,512]{1,0:T(8,128)(2,1)}) custom-call(bf16[128,2048]{1,0:T(8,128)(2,1)} %get-tuple-element.304.refs_0_, bf16[128,2048]{1,0:T(8,128)(2,1)} %get-tuple-element.305.refs_1_, bf16[128,2048]{1,0:T(8,128)(2,1)} %get-tuple-element.306.refs_2_, ...), custom_call_target="tpu_custom_call" | custom-call | flops 1048576 | bytes 65536 | tf_op jit(solution)/shard_map/cond/branch_1_fun/hidden_units_a/pallas_call | solution.py:687
  241.6 13.7 %hidden_units_a_other.1 = (bf16[1024,1024]{1,0:T(8,128)(2,1)}, bf16[1024,512]{1,0:T(8,128)(2,1)}) custom-call(bf16[1024,2048]{1,0:T(8,128)(2,1)} %get-tuple-element.934.refs_0_, bf16[1024,2048]{1,0:T(8,128)(2,1)} %get-tuple-element.312.refs_8_.refs_1_.refs_2_, bf16[4,512,1536]{2,1,0:T(8,128)(2,1)} %collective-permute-done.4.refs_2_.refs_3_.refs_4_, ...), custom_call_target="tpu_custom_call" | custom-call | flops 1048576 | bytes 65536 | tf_op jit(solution)/shard_map/cond/branch_1_fun/hidden_units_a_other/pallas_call | solution.py:687
  255.8 5.4 collective-permute-done.8.refs_7_
  262.9 19.4 %hidden_weights_a.1 = bf16[4,512,1536]{2,1,0:T(8,128)(2,1)} custom-call(bf16[1024,2048]{1,0:T(8,128)(2,1)} %get-tuple-element.934.refs_0_, bf16[1024,2048]{1,0:T(8,128)(2,1)} %collective-permute-done.5.refs_1_, bf16[1024,2048]{1,0:T(8,128)(2,1)} %get-tuple-element.312.refs_8_.refs_1_.refs_2_, bf16[1024,2048]{1,0:T(8,128)(2,1)} %collective-permute-done.6.refs_3_, ...), custom_call_target="tpu_custom_call" | custom-call | flops 1048576 | bytes 65536 | tf_op jit(solution)/shard_map/cond/branch_1_fun/hidden_weights_a/pallas_call | solution.py:404
  282.4 74.6 %conditional.14 = (f32[256,2048]{1,0:T(8,128)}, bf16[128,2048]{1,0:T(8,128)(2,1)}, bf16[128,2048]{1,0:T(8,128)(2,1)}, bf16[128,2048]{1,0:T(8,128)(2,1)}, bf16[12...) conditional(s32[]{:T(128)} %convert_element_type.143, ...), branch_computations={%region_8.9_spmd, %region_9.10_spmd} | conditional | flops 7340032 | bytes 60097064 | solution.py:708
  283.0 9.0 %hidden_units_b.2 = (bf16[1024,512]{1,0:T(8,128)(2,1)}, bf16[1024,256]{1,0:T(8,128)(2,1)}) custom-call(bf16[1024,2048]{1,0:T(8,128)(2,1)} %get-tuple-element.320.refs_0_, bf16[1024,2048]{1,0:T(8,128)(2,1)} %get-tuple-element.321.refs_1_.refs_2_, bf16[4,512,768]{2,1,0:T(8,128)(2,1)} %get-tuple-element.322.refs_2_.refs_3_.refs_4_.refs_6_, ...), custom_call_target="tpu_custom_call" | custom-call | flops 1048576 | bytes 65536 | tf_op jit(solution)/shard_map/cond/branch_1_fun/hidden_units_b/pallas_call | solution.py:687
  292.0 9.0 %hidden_units_b.3 = (bf16[1024,512]{1,0:T(8,128)(2,1)}, bf16[1024,256]{1,0:T(8,128)(2,1)}) custom-call(bf16[1024,2048]{1,0:T(8,128)(2,1)} %get-tuple-element.320.refs_0_, bf16[1024,2048]{1,0:T(8,128)(2,1)} %get-tuple-element.321.refs_1_.refs_2_, bf16[4,512,768]{2,1,0:T(8,128)(2,1)} %collective-permute-done.31.refs_2_.refs_3_.refs_4_.refs_7_, ...), custom_call_target="tpu_custom_call" | custom-call | flops 1048576 | bytes 65536 | tf_op jit(solution)/shard_map/cond/branch_1_fun/hidden_units_b/pallas_call | solution.py:687
  301.0 9.1 %normed_mid_grad_far.1 = (bf16[128,2048]{1,0:T(8,128)(2,1)}, bf16[128,2048]{1,0:T(8,128)(2,1)}) custom-call(bf16[1024,1024]{1,0:T(8,128)(2,1)} %get-tuple-element.318.refs_0_, bf16[1024,1024]{1,0:T(8,128)(2,1)} %get-tuple-element.319.refs_1_, bf16[1024,512]{1,0:T(8,128)(2,1)} %get-tuple-element.340.refs_2_.refs_4_, ...), custom_call_target="tpu_custom_call" | custom-call | flops 1048576 | bytes 65536 | tf_op jit(solution)/shard_map/cond/branch_1_fun/normed_mid_grad_far/pallas_call | solution.py:224
  313.5 14.8 %normed_mid_grad.1 = (f32[256,2048]{1,0:T(8,128)}, bf16[128,2048]{1,0:T(8,128)(2,1)}, bf16[128,2048]{1,0:T(8,128)(2,1)}, bf16[128,2048]{1,0:T(8,128)(2,1)}, bf16[128,2048]{1,0:T(8,128)(2,1)}) custom-call(bf16[1024,1024]{1,0:T(8,128)(2,1)} %get-tuple-element.318.refs_0_, bf16[1024,1024]{1,0:T(8,128)(2,1)} %get-tuple-element.319.refs_1_, ...), custom_call_target="tpu_custom_call" | custom-call | flops 1048576 | bytes 65536 | tf_op jit(solution)/shard_map/cond/branch_1_fun/normed_mid_grad/pallas_call | solution.py:224
  337.6 12.5 %hidden_weights_b.1 = bf16[4,512,768]{2,1,0:T(8,128)(2,1)} custom-call(bf16[1024,2048]{1,0:T(8,128)(2,1)} %get-tuple-element.320.refs_0_, bf16[1024,2048]{1,0:T(8,128)(2,1)} %get-tuple-element.336.refs_1_, bf16[1024,2048]{1,0:T(8,128)(2,1)} %get-tuple-element.321.refs_1_.refs_2_, bf16[1024,2048]{1,0:T(8,128)(2,1)} %get-tuple-element.337.refs_3_, ...), custom_call_target="tpu_custom_call" | custom-call | flops 1048576 | bytes 65536 | tf_op jit(solution)/shard_map/cond/branch_1_fun/hidden_weights_b/pallas_call | solution.py:404
  350.1 4.9 collective-permute-done.34
  357.0 42.2 %conditional.15 = (f32[256,2048]{1,0:T(8,128)}, bf16[128,2048]{1,0:T(8,128)(2,1)}, bf16[128,2048]{1,0:T(8,128)(2,1)}, bf16[128,2048]{1,0:T(8,128)(2,1)}, bf16[12...) conditional(s32[]{:T(128)} %convert_element_type.143, ...), branch_computations={%region_10.11_spmd, %region_11.12_spmd} | conditional | flops 2097152 | bytes 37880180 | solution.py:708
  357.3 6.4 %middle_grad.1 = (f32[256,2048]{1,0:T(8,128)}, bf16[128,2048]{1,0:T(8,128)(2,1)}, bf16[128,2048]{1,0:T(8,128)(2,1)}) custom-call(f32[256,2048]{1,0:T(8,128)} %get-tuple-element.346.refs_0_, f32[256,2048]{1,0:T(8,128)} %get-tuple-element.347.refs_1_, bf16[128,2048]{1,0:T(8,128)(2,1)} %get-tuple-element.348.refs_2_, ...), custom_call_target="tpu_custom_call" | custom-call | flops 1048576 | bytes 65536 | tf_op jit(solution)/shard_map/cond/branch_1_fun/middle_grad/pallas_call | solution.py:307
  367.7 10.8 %hidden_out.1 = (f32[256,2048]{1,0:T(8,128)}, bf16[256,2048]{1,0:T(8,128)(2,1)}, bf16[256,2048]{1,0:T(8,128)(2,1)}, bf16[256,2048]{1,0:T(8,128)(2,1)}) custom-call(bf16[1024,512]{1,0:T(8,128)(2,1)} %get-tuple-element.357.refs_0_, bf16[1024,512]{1,0:T(8,128)(2,1)} %get-tuple-element.358.refs_1_, bf16[1024,256]{1,0:T(8,128)(2,1)} %get-tuple-element.359.refs_2_, ...), custom_call_target="tpu_custom_call" | custom-call | flops 1048576 | bytes 65536 | tf_op jit(solution)/shard_map/cond/branch_1_fun/hidden_out/pallas_call | solution.py:224
  382.1 8.2 %collective-permute-done.10 = bf16[128,2048]{1,0:T(8,128)(2,1)} collective-permute-done((bf16[128,2048]{1,0:T(8,128)(2,1)}, bf16[128,2048]{1,0:T(8,128)(2,1)}, u32[]{:S(2)}, u32[]{:S(2)}) %collective-permute-start.10) | collective-permute-done | bytes 524320 | tf_op jit(solution)/shard_map/cond/branch_1_fun/ppermute | solution.py:712
  390.3 8.8 %collective-permute-done.13 = bf16[128,2048]{1,0:T(8,128)(2,1)} collective-permute-done((bf16[128,2048]{1,0:T(8,128)(2,1)}, bf16[128,2048]{1,0:T(8,128)(2,1)}, u32[]{:S(2)}, u32[]{:S(2)}) %collective-permute-start.13) | collective-permute-done | bytes 524320 | tf_op jit(solution)/shard_map/cond/branch_1_fun/ppermute | solution.py:712
  402.7 27.5 %conditional.16 = (bf16[1024,2048]{1,0:T(8,128)(2,1)}, bf16[1024,2048]{1,0:T(8,128)(2,1)}, bf16[4,256,512]{2,1,0:T(8,128)(2,1)}, bf16[4,256,512]{2,1,0:T(8,128)(2,1)}, f32[8,128]{1,0:T(8,128)S(1)}) conditional(s32[]{:T(128)} %convert_element_type.143, () %tuple.117, (bf16[128,2048]{1,0:T(8,128)(2,1)}, bf16[128,2048]{1,0:T(8,128)(2,1)}, ...), branch_computations={%region_13.14_spmd, %region_14.15_spmd} | conditional | flops 2097152 | bytes 21119124 | solution.py:708
  402.7 7.7 %attended_grad.1 = (bf16[1024,2048]{1,0:T(8,128)(2,1)}, bf16[1024,256]{1,0:T(8,128)(2,1)}, bf16[1024,256]{1,0:T(8,128)(2,1)}) custom-call(bf16[128,2048]{1,0:T(8,128)(2,1)} %get-tuple-element.371.refs_0_, bf16[128,2048]{1,0:T(8,128)(2,1)} %get-tuple-element.372.refs_1_, bf16[128,2048]{1,0:T(8,128)(2,1)} %get-tuple-element.373.refs_2_, ...), custom_call_target="tpu_custom_call" | custom-call | flops 1048576 | bytes 65536 | tf_op jit(solution)/shard_map/cond/branch_1_fun/attended_grad/pallas_call | solution.py:359
  414.1 16.1 %attend_back.1 = (bf16[4,256,512]{2,1,0:T(8,128)(2,1)}, bf16[4,256,512]{2,1,0:T(8,128)(2,1)}, f32[8,128]{1,0:T(8,128)S(1)}) custom-call(s32[1]{0:T(128)} %bitcast.13.core_ref, f32[4,256,512]{2,1,0:T(8,128)} %get-tuple-element.386.refs_0_, f32[4,256,512]{2,1,0:T(8,128)} %get-tuple-element.387.refs_1_, bf16[4,256,256]{2,1,0:T(8,128)(2,1)S(1)} %bitcast.65, ...), custom_call_target="tpu_custom_call" | custom-call | flops 1048576 | bytes 65536 | tf_op jit(solution)/shard_map/cond/branch_1_fun/attend_back/pallas_call | solution.py:179
  430.2 13.8 %conditional.17 = (bf16[4,528,768]{2,1,0:T(8,128)(2,1)}, bf16[1024,512]{1,0:T(8,128)(2,1)}, bf16[1024,512]{1,0:T(8,128)(2,1)}) conditional(s32[]{:T(128)} %convert_element_type.143, () %tuple.116, (bf16[4,256,512]{2,1,0:T(8,128)(2,1)}, bf16[4,256,512]{2,1,0:T(8,128)(2,1)}, bf16[4,256,256]{2,1,0:T(8,128)(2,1)}, bf16[4,256,256]{2,1,0:T(8,128)(2,1)}, ...), branch_computations={%region_15.16_spmd, %region_16.17_spmd} | conditional | flops 1049600 | bytes 5341214 | solution.py:708
  431.3 12.7 %attention_weights.1 = bf16[4,528,768]{2,1,0:T(8,128)(2,1)} custom-call(bf16[1024,2048]{1,0:T(8,128)(2,1)} %get-tuple-element.396.refs_0_, bf16[1024,2048]{1,0:T(8,128)(2,1)} %get-tuple-element.397.refs_1_, bf16[1024,2048]{1,0:T(8,128)(2,1)} %get-tuple-element.398.refs_2_, bf16[1024,2048]{1,0:T(8,128)(2,1)} %get-tuple-element.399.refs_3_, ...), custom_call_target="tpu_custom_call" | custom-call | flops 1048576 | bytes 65536 | tf_op jit(solution)/shard_map/cond/branch_1_fun/attention_weights/pallas_call | solution.py:404
  445.8 19.0 %conditional.18 = (f32[256,2048]{1,0:T(8,128)}, bf16[128,2048]{1,0:T(8,128)(2,1)}, bf16[128,2048]{1,0:T(8,128)(2,1)}, bf16[128,2048]{1,0:T(8,128)(2,1)}, bf16[12...) conditional(s32[]{:T(128)} %convert_element_type.143, () %tuple.115, ...), branch_computations={%region_17.18_spmd, %region_18.19_spmd} | conditional | flops 2097152 | bytes 17301668 | solution.py:708
  446.1 5.1 normed_in_grad_far.1
  453.5 6.9 %normed_in_grad.1 = (f32[256,2048]{1,0:T(8,128)}, bf16[128,2048]{1,0:T(8,128)(2,1)}, bf16[128,2048]{1,0:T(8,128)(2,1)}, bf16[128,2048]{1,0:T(8,128)(2,1)}, bf16[128,2048]{1,0:T(8,128)(2,1)}) custom-call(bf16[1024,512]{1,0:T(8,128)(2,1)} %get-tuple-element.405.refs_0_, bf16[1024,512]{1,0:T(8,128)(2,1)} %get-tuple-element.406.refs_1_, ...), custom_call_target="tpu_custom_call" | custom-call | flops 1048576 | bytes 65536 | tf_op jit(solution)/shard_map/cond/branch_1_fun/normed_in_grad/pallas_call | solution.py:224
  460.4 3.2 collective-permute-done.17
  464.8 49.6 %conditional.19 = (bf16[256,2048]{1,0:T(8,128)(2,1)}, f32[256,2048]{1,0:T(8,128)}, bf16[128,2304]{1,0:T(8,128)(2,1)S(1)}, bf16[128,2304]{1,0:T(8,128)(2,1)}, bf1...) conditional(s32[]{:T(128)} %convert_element_type.143, () %tuple.114, (bf16[128,2048]{1,0:T(8,128)(2,1)}, ...), branch_computations={%region_20.21_spmd, %region_21.22_spmd} | conditional | flops 8912914 | bytes 32375352 | solution.py:708
  474.5 5.5 %collective-permute-done.41.refs_2_ = bf16[128,2048]{1,0:T(8,128)(2,1)S(1)} collective-permute-done((bf16[128,2048]{1,0:T(8,128)(2,1)}, bf16[128,2048]{1,0:T(8,128)(2,1)S(1)}, u32[]{:S(2)}, u32[]{:S(2)}) %collective-permute-start.41) | collective-permute-done | bytes 524320 | tf_op jit(solution)/shard_map/cond/branch_1_fun/ppermute | solution.py:712
  480.6 7.7 %collective-permute-done.42.refs_3_ = bf16[128,2048]{1,0:T(8,128)(2,1)} collective-permute-done((bf16[128,2048]{1,0:T(8,128)(2,1)S(1)}, bf16[128,2048]{1,0:T(8,128)(2,1)}, u32[]{:S(2)}, u32[]{:S(2)}) %collective-permute-start.42) | collective-permute-done | bytes 524320 | tf_op jit(solution)/shard_map/cond/branch_1_fun/ppermute | solution.py:712
  492.0 4.3 hidden_out_sum.1
  496.3 4.9 grad_in.1
  501.1 3.7 collective-permute-done.45
  504.9 8.5 %collective-permute-done.46 = bf16[128,2304]{1,0:T(8,128)(2,1)} collective-permute-done((bf16[128,2304]{1,0:T(8,128)(2,1)S(1)}, bf16[128,2304]{1,0:T(8,128)(2,1)}, u32[]{:S(2)}, u32[]{:S(2)}) %collective-permute-start.46) | collective-permute-done | bytes 589856 | tf_op jit(solution)/shard_map/cond/branch_1_fun/ppermute | solution.py:712
  514.4 7.0 %reduce-scatter.8.cloned.1.call-done = bf16[1,528,768]{2,1,0:T(8,128)(2,1)} async-done(((bf16[4,528,768]{2,1,0:T(8,128)(2,1)}), bf16[1,528,768]{2,1,0:T(8,128)(2,1)}) %reduce-scatter.8.cloned.1.call-update) | async-done | bytes 811024 | tf_op jit(solution)/shard_map/reduce_scatter | solution.py:932
  526.9 4.6 hidden_owned.1
  531.9 3.4 collective-permute-done.70.refs_2_
  537.8 2.5 psum.7
  (282 shorter events, 120.6 us)
Async XLA Ops:
  7.2 94.2 %all-gather.7.cloned.1.call-start = ((), (), s32[]{:S(2)}) async-start(), calls=%async_computation.6 | async-start | bytes 4055040 | tf_op jit(solution)/shard_map/all_gather | solution.py:831
  29.0 196.2 %all-gather.9.cloned.1.call-start = ((), (), s32[]{:S(2)}) async-start(), calls=%async_computation.7 | async-start | bytes 7864320 | tf_op jit(solution)/shard_map/all_gather | solution.py:831
  37.2 14.9 %collective-permute-start.53 = (bf16[128,2048]{1,0:T(8,128)(2,1)S(1)}, bf16[128,2048]{1,0:T(8,128)(2,1)S(1)}, u32[]{:S(2)}, u32[]{:S(2)}) collective-permute-start(bf16[128,2048]{1,0:T(8,128)(2,1)S(1)} %get-tuple-element.636), channel_id=1, source_target_pairs={{0,2},{2,0},{4,6},{6,4},{1,3},{3,1},{5,7},{7,5},{8,10},{10,8},{12,... | collective-permute-start | bytes 1572872 | tf_op jit(solution)/shard_map/ppermute | solution.py:712
  38.4 22.6 %collective-permute-start.55 = (bf16[128,2048]{1,0:T(8,128)(2,1)S(1)}, bf16[128,2048]{1,0:T(8,128)(2,1)S(1)}, u32[]{:S(2)}, u32[]{:S(2)}) collective-permute-start(bf16[128,2048]{1,0:T(8,128)(2,1)S(1)} %get-tuple-element.636), channel_id=1, source_target_pairs={{0,4},{2,6},{4,0},{6,2},{1,5},{3,7},{5,1},{7,3},{8,12},{10,14},{12... | collective-permute-start | bytes 1572872 | tf_op jit(solution)/shard_map/ppermute | solution.py:712
  39.2 21.8 %collective-permute-start.54 = (bf16[128,2048]{1,0:T(8,128)(2,1)S(1)}, bf16[128,2048]{1,0:T(8,128)(2,1)S(1)}, u32[]{:S(2)}, u32[]{:S(2)}) collective-permute-start(bf16[128,2048]{1,0:T(8,128)(2,1)S(1)} %get-tuple-element.637), channel_id=1, source_target_pairs={{0,2},{2,0},{4,6},{6,4},{1,3},{3,1},{5,7},{7,5},{8,10},{10,8},{12,... | collective-permute-start | bytes 1572872 | tf_op jit(solution)/shard_map/ppermute | solution.py:712
  40.7 21.4 %collective-permute-start.56 = (bf16[128,2048]{1,0:T(8,128)(2,1)S(1)}, bf16[128,2048]{1,0:T(8,128)(2,1)S(1)}, u32[]{:S(2)}, u32[]{:S(2)}) collective-permute-start(bf16[128,2048]{1,0:T(8,128)(2,1)S(1)} %get-tuple-element.637), channel_id=1, source_target_pairs={{0,4},{2,6},{4,0},{6,2},{1,5},{3,7},{5,1},{7,3},{8,12},{10,14},{12... | collective-permute-start | bytes 1572872 | tf_op jit(solution)/shard_map/ppermute | solution.py:712
  62.5 16.3 %collective-permute-start.57 = (bf16[128,2304]{1,0:T(8,128)(2,1)S(1)}, bf16[128,2304]{1,0:T(8,128)(2,1)S(1)}, u32[]{:S(2)}, u32[]{:S(2)}) collective-permute-start(bf16[128,2304]{1,0:T(8,128)(2,1)S(1)} %get-tuple-element.825), channel_id=1, source_target_pairs={{0,2},{2,0},{4,6},{6,4},{1,3},{3,1},{5,7},{7,5},{8,10},{10,8},{12,... | collective-permute-start | bytes 1769480 | tf_op jit(solution)/shard_map/ppermute | solution.py:712
  63.6 28.9 %collective-permute-start.58 = (bf16[128,2304]{1,0:T(8,128)(2,1)S(1)}, bf16[128,2304]{1,0:T(8,128)(2,1)S(1)}, u32[]{:S(2)}, u32[]{:S(2)}) collective-permute-start(bf16[128,2304]{1,0:T(8,128)(2,1)S(1)} %get-tuple-element.824), channel_id=1, source_target_pairs={{0,4},{2,6},{4,0},{6,2},{1,5},{3,7},{5,1},{7,3},{8,12},{10,14},{12... | collective-permute-start | bytes 1769480 | tf_op jit(solution)/shard_map/ppermute | solution.py:712
  64.1 28.4 %collective-permute-start.59 = (bf16[128,2304]{1,0:T(8,128)(2,1)S(1)}, bf16[128,2304]{1,0:T(8,128)(2,1)S(1)}, u32[]{:S(2)}, u32[]{:S(2)}) collective-permute-start(bf16[128,2304]{1,0:T(8,128)(2,1)S(1)} %get-tuple-element.823), channel_id=1, source_target_pairs={{0,6},{2,4},{4,2},{6,0},{1,7},{3,5},{5,3},{7,1},{8,14},{10,12},{12... | collective-permute-start | bytes 1769480 | tf_op jit(solution)/shard_map/ppermute | solution.py:712
  66.0 34.5 %collective-permute-start.60 = (bf16[128,2048]{1,0:T(8,128)(2,1)S(1)}, bf16[128,2048]{1,0:T(8,128)(2,1)S(1)}, u32[]{:S(2)}, u32[]{:S(2)}) collective-permute-start(bf16[128,2048]{1,0:T(8,128)(2,1)S(1)} %collective-permute-done.53), channel_id=1, source_target_pairs={{0,4},{2,6},{4,0},{6,2},{1,5},{3,7},{5,1},{7,3},{8,12},{10,14},{12... | collective-permute-start | bytes 1572872 | tf_op jit(solution)/shard_map/ppermute | solution.py:712
  66.7 34.7 %collective-permute-start.61 = (bf16[128,2048]{1,0:T(8,128)(2,1)S(1)}, bf16[128,2048]{1,0:T(8,128)(2,1)}, u32[]{:S(2)}, u32[]{:S(2)}) collective-permute-start(bf16[128,2048]{1,0:T(8,128)(2,1)S(1)} %collective-permute-done.56), channel_id=1, source_target_pairs={{0,2},{2,0},{4,6},{6,4},{1,3},{3,1},{5,7},{7,5},{8,10},{10,8},{12,... | collective-permute-start | bytes 1572872 | tf_op jit(solution)/shard_map/ppermute | solution.py:712
  101.4 181.0 %all-gather.11.cloned.1.call-start = ((), (), s32[]{:S(2)}) async-start(), calls=%async_computation.8 | async-start | bytes 3932160 | tf_op jit(solution)/shard_map/all_gather | solution.py:831
  102.1 297.1 %reduce-scatter.4.cloned.1.call-start = ((), (), s32[]{:S(2)}) async-start(), calls=%async_computation.3 | async-start | bytes 7864320 | tf_op jit(solution)/shard_map/reduce_scatter | solution.py:932
  102.2 23.7 %collective-permute-start.62 = (bf16[128,2048]{1,0:T(8,128)(2,1)S(1)}, bf16[128,2048]{1,0:T(8,128)(2,1)}, u32[]{:S(2)}, u32[]{:S(2)}) collective-permute-start(bf16[128,2048]{1,0:T(8,128)(2,1)S(1)} %copy-done.23), channel_id=1, source_target_pairs={{0,2},{2,0},{4,6},{6,4},{1,3},{3,1},{5,7},{7,5},{8,10},{10,8},{12,... | collective-permute-start | bytes 1572872 | tf_op jit(solution)/shard_map/ppermute | solution.py:712
  103.0 22.9 %collective-permute-start.63 = (bf16[128,2048]{1,0:T(8,128)(2,1)S(1)}, bf16[128,2048]{1,0:T(8,128)(2,1)}, u32[]{:S(2)}, u32[]{:S(2)}) collective-permute-start(bf16[128,2048]{1,0:T(8,128)(2,1)S(1)} %copy-done.21), channel_id=1, source_target_pairs={{0,2},{2,0},{4,6},{6,4},{1,3},{3,1},{5,7},{7,5},{8,10},{10,8},{12,... | collective-permute-start | bytes 1572872 | tf_op jit(solution)/shard_map/ppermute | solution.py:712
  104.3 21.6 %collective-permute-start.64 = (bf16[128,2048]{1,0:T(8,128)(2,1)S(1)}, bf16[128,2048]{1,0:T(8,128)(2,1)}, u32[]{:S(2)}, u32[]{:S(2)}) collective-permute-start(bf16[128,2048]{1,0:T(8,128)(2,1)S(1)} %copy-done.23), channel_id=1, source_target_pairs={{0,4},{2,6},{4,0},{6,2},{1,5},{3,7},{5,1},{7,3},{8,12},{10,14},{12... | collective-permute-start | bytes 1572872 | tf_op jit(solution)/shard_map/ppermute | solution.py:712
  104.6 21.4 %collective-permute-start.65 = (bf16[128,2048]{1,0:T(8,128)(2,1)S(1)}, bf16[128,2048]{1,0:T(8,128)(2,1)}, u32[]{:S(2)}, u32[]{:S(2)}) collective-permute-start(bf16[128,2048]{1,0:T(8,128)(2,1)S(1)} %copy-done.21), channel_id=1, source_target_pairs={{0,4},{2,6},{4,0},{6,2},{1,5},{3,7},{5,1},{7,3},{8,12},{10,14},{12... | collective-permute-start | bytes 1572872 | tf_op jit(solution)/shard_map/ppermute | solution.py:712
  125.9 17.0 %collective-permute-start = (bf16[1024,2048]{1,0:T(8,128)(2,1)}, bf16[1024,2048]{1,0:T(8,128)(2,1)}, u32[]{:S(2)}, u32[]{:S(2)}) collective-permute-start(bf16[1024,2048]{1,0:T(8,128)(2,1)} %get-tuple-element.252), channel_id=1, source_target_pairs={{0,1},{1,0},{2,3},{3,2},{4,5},{5,4},{6,7},{7,6},{8,9},{9,8},{10,11... | collective-permute-start | bytes 12582920 | tf_op jit(solution)/shard_map/cond/branch_1_fun/ppermute | solution.py:712
  126.3 14.3 %collective-permute-start.1 = (bf16[128,2048]{1,0:T(8,128)(2,1)}, bf16[128,2048]{1,0:T(8,128)(2,1)}, u32[]{:S(2)}, u32[]{:S(2)}) collective-permute-start(bf16[128,2048]{1,0:T(8,128)(2,1)} %get-tuple-element.263), channel_id=1, source_target_pairs={{0,4},{2,6},{4,0},{6,2},{1,5},{3,7},{5,1},{7,3},{8,12},{10,14},{12... | collective-permute-start | bytes 1572872 | tf_op jit(solution)/shard_map/cond/branch_1_fun/ppermute | solution.py:712
  126.3 14.3 %collective-permute-start.2 = (bf16[128,2048]{1,0:T(8,128)(2,1)}, bf16[128,2048]{1,0:T(8,128)(2,1)}, u32[]{:S(2)}, u32[]{:S(2)}) collective-permute-start(bf16[128,2048]{1,0:T(8,128)(2,1)} %get-tuple-element.264), channel_id=1, source_target_pairs={{0,2},{2,0},{4,6},{6,4},{1,3},{3,1},{5,7},{7,5},{8,10},{10,8},{12,... | collective-permute-start | bytes 1572872 | tf_op jit(solution)/shard_map/cond/branch_1_fun/ppermute | solution.py:712
  147.3 14.2 %collective-permute-start.19 = (bf16[128,2048]{1,0:T(8,128)(2,1)}, bf16[128,2048]{1,0:T(8,128)(2,1)S(1)}, u32[]{:S(2)}, u32[]{:S(2)}) collective-permute-start(bf16[128,2048]{1,0:T(8,128)(2,1)} %get-tuple-element.277), channel_id=1, source_target_pairs={{0,2},{2,0},{4,6},{6,4},{1,3},{3,1},{5,7},{7,5},{8,10},{10,8},{12,... | collective-permute-start | bytes 1572872 | tf_op jit(solution)/shard_map/cond/branch_1_fun/ppermute | solution.py:712
  147.7 13.9 %collective-permute-start.20 = (bf16[128,2048]{1,0:T(8,128)(2,1)}, bf16[128,2048]{1,0:T(8,128)(2,1)S(1)}, u32[]{:S(2)}, u32[]{:S(2)}) collective-permute-start(bf16[128,2048]{1,0:T(8,128)(2,1)} %get-tuple-element.278), channel_id=1, source_target_pairs={{0,4},{2,6},{4,0},{6,2},{1,5},{3,7},{5,1},{7,3},{8,12},{10,14},{12... | collective-permute-start | bytes 1572872 | tf_op jit(solution)/shard_map/cond/branch_1_fun/ppermute | solution.py:712
  161.6 15.1 %collective-permute-start.21 = (bf16[128,2048]{1,0:T(8,128)(2,1)}, bf16[128,2048]{1,0:T(8,128)(2,1)S(1)}, u32[]{:S(2)}, u32[]{:S(2)}) collective-permute-start(bf16[128,2048]{1,0:T(8,128)(2,1)} %get-tuple-element.279), channel_id=1, source_target_pairs={{0,2},{2,0},{4,6},{6,4},{1,3},{3,1},{5,7},{7,5},{8,10},{10,8},{12,... | collective-permute-start | bytes 1572872 | tf_op jit(solution)/shard_map/cond/branch_1_fun/ppermute | solution.py:712
  163.2 15.1 %collective-permute-start.24 = (bf16[128,2048]{1,0:T(8,128)(2,1)}, bf16[128,2048]{1,0:T(8,128)(2,1)S(1)}, u32[]{:S(2)}, u32[]{:S(2)}) collective-permute-start(bf16[128,2048]{1,0:T(8,128)(2,1)} %get-tuple-element.282), channel_id=1, source_target_pairs={{0,4},{2,6},{4,0},{6,2},{1,5},{3,7},{5,1},{7,3},{8,12},{10,14},{12... | collective-permute-start | bytes 1572872 | tf_op jit(solution)/shard_map/cond/branch_1_fun/ppermute | solution.py:712
  166.1 21.2 %collective-permute-start.22 = (bf16[128,2048]{1,0:T(8,128)(2,1)S(1)}, bf16[128,2048]{1,0:T(8,128)(2,1)S(1)}, u32[]{:S(2)}, u32[]{:S(2)}) collective-permute-start(bf16[128,2048]{1,0:T(8,128)(2,1)S(1)} %add_convert_fusion.1), channel_id=1, source_target_pairs={{0,4},{2,6},{4,0},{6,2},{1,5},{3,7},{5,1},{7,3},{8,12},{10,14},{12... | collective-permute-start | bytes 1572872 | tf_op jit(solution)/shard_map/cond/branch_1_fun/ppermute | solution.py:712
  167.8 19.6 %collective-permute-start.23 = (bf16[128,2048]{1,0:T(8,128)(2,1)S(1)}, bf16[128,2048]{1,0:T(8,128)(2,1)S(1)}, u32[]{:S(2)}, u32[]{:S(2)}) collective-permute-start(bf16[128,2048]{1,0:T(8,128)(2,1)S(1)} %add_convert_fusion), channel_id=1, source_target_pairs={{0,2},{2,0},{4,6},{6,4},{1,3},{3,1},{5,7},{7,5},{8,10},{10,8},{12,... | collective-permute-start | bytes 1572872 | tf_op jit(solution)/shard_map/cond/branch_1_fun/ppermute | solution.py:712
  190.0 15.2 %collective-permute-start.25 = (bf16[128,2048]{1,0:T(8,128)(2,1)}, bf16[128,2048]{1,0:T(8,128)(2,1)}, u32[]{:S(2)}, u32[]{:S(2)}) collective-permute-start(bf16[128,2048]{1,0:T(8,128)(2,1)} %get-tuple-element.915), channel_id=1, source_target_pairs={{0,2},{2,0},{4,6},{6,4},{1,3},{3,1},{5,7},{7,5},{8,10},{10,8},{12,... | collective-permute-start | bytes 1572872 | tf_op jit(solution)/shard_map/cond/branch_1_fun/ppermute | solution.py:712
  190.6 16.3 %collective-permute-start.28 = (bf16[128,2048]{1,0:T(8,128)(2,1)}, bf16[128,2048]{1,0:T(8,128)(2,1)}, u32[]{:S(2)}, u32[]{:S(2)}) collective-permute-start(bf16[128,2048]{1,0:T(8,128)(2,1)} %get-tuple-element.916), channel_id=1, source_target_pairs={{0,4},{2,6},{4,0},{6,2},{1,5},{3,7},{5,1},{7,3},{8,12},{10,14},{12... | collective-permute-start | bytes 1572872 | tf_op jit(solution)/shard_map/cond/branch_1_fun/ppermute | solution.py:712
  192.4 24.1 %collective-permute-start.26 = (bf16[128,2048]{1,0:T(8,128)(2,1)}, bf16[128,2048]{1,0:T(8,128)(2,1)}, u32[]{:S(2)}, u32[]{:S(2)}) collective-permute-start(bf16[128,2048]{1,0:T(8,128)(2,1)} %get-tuple-element.916), channel_id=1, source_target_pairs={{0,2},{2,0},{4,6},{6,4},{1,3},{3,1},{5,7},{7,5},{8,10},{10,8},{12,... | collective-permute-start | bytes 1572872 | tf_op jit(solution)/shard_map/cond/branch_1_fun/ppermute | solution.py:712
  193.8 23.3 %collective-permute-start.27 = (bf16[128,2048]{1,0:T(8,128)(2,1)}, bf16[128,2048]{1,0:T(8,128)(2,1)}, u32[]{:S(2)}, u32[]{:S(2)}) collective-permute-start(bf16[128,2048]{1,0:T(8,128)(2,1)} %get-tuple-element.915), channel_id=1, source_target_pairs={{0,4},{2,6},{4,0},{6,2},{1,5},{3,7},{5,1},{7,3},{8,12},{10,14},{12... | collective-permute-start | bytes 1572872 | tf_op jit(solution)/shard_map/cond/branch_1_fun/ppermute | solution.py:712
  205.2 20.0 %collective-permute-start.29 = (bf16[128,2048]{1,0:T(8,128)(2,1)}, bf16[128,2048]{1,0:T(8,128)(2,1)}, u32[]{:S(2)}, u32[]{:S(2)}) collective-permute-start(bf16[128,2048]{1,0:T(8,128)(2,1)} %collective-permute-done.25), channel_id=1, source_target_pairs={{0,4},{2,6},{4,0},{6,2},{1,5},{3,7},{5,1},{7,3},{8,12},{10,14},{12... | collective-permute-start | bytes 1572872 | tf_op jit(solution)/shard_map/cond/branch_1_fun/ppermute | solution.py:712
  207.0 18.2 %collective-permute-start.30 = (bf16[128,2048]{1,0:T(8,128)(2,1)}, bf16[128,2048]{1,0:T(8,128)(2,1)}, u32[]{:S(2)}, u32[]{:S(2)}) collective-permute-start(bf16[128,2048]{1,0:T(8,128)(2,1)} %collective-permute-done.28), channel_id=1, source_target_pairs={{0,2},{2,0},{4,6},{6,4},{1,3},{3,1},{5,7},{7,5},{8,10},{10,8},{12,... | collective-permute-start | bytes 1572872 | tf_op jit(solution)/shard_map/cond/branch_1_fun/ppermute | solution.py:712
  225.6 16.0 %collective-permute-start.4 = (bf16[4,512,1536]{2,1,0:T(8,128)(2,1)}, bf16[4,512,1536]{2,1,0:T(8,128)(2,1)}, u32[]{:S(2)}, u32[]{:S(2)}) collective-permute-start(bf16[4,512,1536]{2,1,0:T(8,128)(2,1)} %get-tuple-element.303.refs_9_.refs_10_.refs_11_), channel_id=1, source_target_pairs={{0,1},{1,0},{2,3},{3,2},{4,5},{5,4},{6,7},{7,6},{8,9},{9,8},{10,11... | collective-permute-start | bytes 18874376 | tf_op jit(solution)/shard_map/cond/branch_1_fun/ppermute | solution.py:712
  241.0 14.8 %collective-permute-start.5 = (bf16[1024,2048]{1,0:T(8,128)(2,1)}, bf16[1024,2048]{1,0:T(8,128)(2,1)}, u32[]{:S(2)}, u32[]{:S(2)}) collective-permute-start(bf16[1024,2048]{1,0:T(8,128)(2,1)} %get-tuple-element.934.refs_0_), channel_id=1, source_target_pairs={{0,1},{1,0},{2,3},{3,2},{4,5},{5,4},{6,7},{7,6},{8,9},{9,8},{10,11... | collective-permute-start | bytes 12582920 | tf_op jit(solution)/shard_map/cond/branch_1_fun/ppermute | solution.py:712
  241.5 14.3 %collective-permute-start.6 = (bf16[1024,2048]{1,0:T(8,128)(2,1)}, bf16[1024,2048]{1,0:T(8,128)(2,1)}, u32[]{:S(2)}, u32[]{:S(2)}) collective-permute-start(bf16[1024,2048]{1,0:T(8,128)(2,1)} %get-tuple-element.312.refs_8_.refs_1_.refs_2_), channel_id=1, source_target_pairs={{0,1},{1,0},{2,3},{3,2},{4,5},{5,4},{6,7},{7,6},{8,9},{9,8},{10,11... | collective-permute-start | bytes 12582920 | tf_op jit(solution)/shard_map/cond/branch_1_fun/ppermute | solution.py:712
  282.3 182.5 %reduce-scatter.6.cloned.1.call-start = ((), (), s32[]{:S(2)}) async-start(), calls=%async_computation.4 | async-start | bytes 3932160 | tf_op jit(solution)/shard_map/reduce_scatter | solution.py:932
  310.1 18.3 %collective-permute-start.33 = (bf16[128,2048]{1,0:T(8,128)(2,1)}, bf16[128,2048]{1,0:T(8,128)(2,1)}, u32[]{:S(2)}, u32[]{:S(2)}) collective-permute-start(bf16[128,2048]{1,0:T(8,128)(2,1)} %get-tuple-element.331), channel_id=1, source_target_pairs={{0,4},{2,6},{4,0},{6,2},{1,5},{3,7},{5,1},{7,3},{8,12},{10,14},{12... | collective-permute-start | bytes 1572872 | tf_op jit(solution)/shard_map/cond/branch_1_fun/ppermute | solution.py:712
  311.8 18.9 %collective-permute-start.32 = (bf16[128,2048]{1,0:T(8,128)(2,1)}, bf16[128,2048]{1,0:T(8,128)(2,1)}, u32[]{:S(2)}, u32[]{:S(2)}) collective-permute-start(bf16[128,2048]{1,0:T(8,128)(2,1)} %get-tuple-element.330), channel_id=1, source_target_pairs={{0,2},{2,0},{4,6},{6,4},{1,3},{3,1},{5,7},{7,5},{8,10},{10,8},{12,... | collective-permute-start | bytes 1572872 | tf_op jit(solution)/shard_map/cond/branch_1_fun/ppermute | solution.py:712
  313.0 24.6 %collective-permute-start.38 = (bf16[1024,512]{1,0:T(8,128)(2,1)}, bf16[1024,512]{1,0:T(8,128)(2,1)}, u32[]{:S(2)}, u32[]{:S(2)}) collective-permute-start(bf16[1024,512]{1,0:T(8,128)(2,1)} %get-tuple-element.324.refs_3_), channel_id=1, source_target_pairs={{0,1},{1,0},{2,3},{3,2},{4,5},{5,4},{6,7},{7,6},{8,9},{9,8},{10,11... | collective-permute-start | bytes 3145736 | tf_op jit(solution)/shard_map/cond/branch_1_fun/ppermute | solution.py:712
  313.0 20.6 %collective-permute-start.39 = (bf16[1024,256]{1,0:T(8,128)(2,1)}, bf16[1024,256]{1,0:T(8,128)(2,1)}, u32[]{:S(2)}, u32[]{:S(2)}) collective-permute-start(bf16[1024,256]{1,0:T(8,128)(2,1)} %get-tuple-element.962), channel_id=1, source_target_pairs={{0,1},{1,0},{2,3},{3,2},{4,5},{5,4},{6,7},{7,6},{8,9},{9,8},{10,11... | collective-permute-start | bytes 1572872 | tf_op jit(solution)/shard_map/cond/branch_1_fun/ppermute | solution.py:712
  329.8 20.3 %collective-permute-start.36 = (bf16[128,2048]{1,0:T(8,128)(2,1)S(1)}, bf16[128,2048]{1,0:T(8,128)(2,1)}, u32[]{:S(2)}, u32[]{:S(2)}) collective-permute-start(bf16[128,2048]{1,0:T(8,128)(2,1)S(1)} %add_convert_fusion.2), channel_id=1, source_target_pairs={{0,2},{2,0},{4,6},{6,4},{1,3},{3,1},{5,7},{7,5},{8,10},{10,8},{12,... | collective-permute-start | bytes 1572872 | tf_op jit(solution)/shard_map/cond/branch_1_fun/ppermute | solution.py:712
  332.0 18.1 %collective-permute-start.35 = (bf16[128,2048]{1,0:T(8,128)(2,1)S(1)}, bf16[128,2048]{1,0:T(8,128)(2,1)}, u32[]{:S(2)}, u32[]{:S(2)}) collective-permute-start(bf16[128,2048]{1,0:T(8,128)(2,1)S(1)} %add_convert_fusion.3), channel_id=1, source_target_pairs={{0,4},{2,6},{4,0},{6,2},{1,5},{3,7},{5,1},{7,3},{8,12},{10,14},{12... | collective-permute-start | bytes 1572872 | tf_op jit(solution)/shard_map/cond/branch_1_fun/ppermute | solution.py:712
  332.4 22.7 %collective-permute-start.34 = (bf16[128,2048]{1,0:T(8,128)(2,1)S(1)}, bf16[128,2048]{1,0:T(8,128)(2,1)}, u32[]{:S(2)}, u32[]{:S(2)}) collective-permute-start(bf16[128,2048]{1,0:T(8,128)(2,1)S(1)} %copy-done.37), channel_id=1, source_target_pairs={{0,2},{2,0},{4,6},{6,4},{1,3},{3,1},{5,7},{7,5},{8,10},{10,8},{12,... | collective-permute-start | bytes 1572872 | tf_op jit(solution)/shard_map/cond/branch_1_fun/ppermute | solution.py:712
  333.6 23.4 %collective-permute-start.37 = (bf16[128,2048]{1,0:T(8,128)(2,1)S(1)}, bf16[128,2048]{1,0:T(8,128)(2,1)}, u32[]{:S(2)}, u32[]{:S(2)}) collective-permute-start(bf16[128,2048]{1,0:T(8,128)(2,1)S(1)} %copy-done.36), channel_id=1, source_target_pairs={{0,4},{2,6},{4,0},{6,2},{1,5},{3,7},{5,1},{7,3},{8,12},{10,14},{12... | collective-permute-start | bytes 1572872 | tf_op jit(solution)/shard_map/cond/branch_1_fun/ppermute | solution.py:712
  357.0 164.4 %reduce-scatter.8.cloned.1.call-start = ((), (), s32[]{:S(2)}) async-start(), calls=%async_computation.5 | async-start | bytes 4055040 | tf_op jit(solution)/shard_map/reduce_scatter | solution.py:932
  363.6 15.2 %collective-permute-start.12 = (bf16[128,2048]{1,0:T(8,128)(2,1)}, bf16[128,2048]{1,0:T(8,128)(2,1)}, u32[]{:S(2)}, u32[]{:S(2)}) collective-permute-start(bf16[128,2048]{1,0:T(8,128)(2,1)} %get-tuple-element.979), channel_id=1, source_target_pairs={{0,4},{2,6},{4,0},{6,2},{1,5},{3,7},{5,1},{7,3},{8,12},{10,14},{12... | collective-permute-start | bytes 1572872 | tf_op jit(solution)/shard_map/cond/branch_1_fun/ppermute | solution.py:712
  363.9 15.2 %collective-permute-start.9 = (bf16[128,2048]{1,0:T(8,128)(2,1)}, bf16[128,2048]{1,0:T(8,128)(2,1)}, u32[]{:S(2)}, u32[]{:S(2)}) collective-permute-start(bf16[128,2048]{1,0:T(8,128)(2,1)} %get-tuple-element.978), channel_id=1, source_target_pairs={{0,2},{2,0},{4,6},{6,4},{1,3},{3,1},{5,7},{7,5},{8,10},{10,8},{12,... | collective-permute-start | bytes 1572872 | tf_op jit(solution)/shard_map/cond/branch_1_fun/ppermute | solution.py:712
  365.1 25.2 %collective-permute-start.10 = (bf16[128,2048]{1,0:T(8,128)(2,1)}, bf16[128,2048]{1,0:T(8,128)(2,1)}, u32[]{:S(2)}, u32[]{:S(2)}) collective-permute-start(bf16[128,2048]{1,0:T(8,128)(2,1)} %get-tuple-element.979), channel_id=1, source_target_pairs={{0,2},{2,0},{4,6},{6,4},{1,3},{3,1},{5,7},{7,5},{8,10},{10,8},{12,... | collective-permute-start | bytes 1572872 | tf_op jit(solution)/shard_map/cond/branch_1_fun/ppermute | solution.py:712
  365.9 24.4 %collective-permute-start.11 = (bf16[128,2048]{1,0:T(8,128)(2,1)}, bf16[128,2048]{1,0:T(8,128)(2,1)}, u32[]{:S(2)}, u32[]{:S(2)}) collective-permute-start(bf16[128,2048]{1,0:T(8,128)(2,1)} %get-tuple-element.978), channel_id=1, source_target_pairs={{0,4},{2,6},{4,0},{6,2},{1,5},{3,7},{5,1},{7,3},{8,12},{10,14},{12... | collective-permute-start | bytes 1572872 | tf_op jit(solution)/shard_map/cond/branch_1_fun/ppermute | solution.py:712
  379.1 20.0 %collective-permute-start.13 = (bf16[128,2048]{1,0:T(8,128)(2,1)}, bf16[128,2048]{1,0:T(8,128)(2,1)}, u32[]{:S(2)}, u32[]{:S(2)}) collective-permute-start(bf16[128,2048]{1,0:T(8,128)(2,1)} %collective-permute-done.9), channel_id=1, source_target_pairs={{0,4},{2,6},{4,0},{6,2},{1,5},{3,7},{5,1},{7,3},{8,12},{10,14},{12... | collective-permute-start | bytes 1572872 | tf_op jit(solution)/shard_map/cond/branch_1_fun/ppermute | solution.py:712
  380.9 18.3 %collective-permute-start.14 = (bf16[128,2048]{1,0:T(8,128)(2,1)}, bf16[128,2048]{1,0:T(8,128)(2,1)}, u32[]{:S(2)}, u32[]{:S(2)}) collective-permute-start(bf16[128,2048]{1,0:T(8,128)(2,1)} %collective-permute-done.12), channel_id=1, source_target_pairs={{0,2},{2,0},{4,6},{6,4},{1,3},{3,1},{5,7},{7,5},{8,10},{10,8},{12,... | collective-permute-start | bytes 1572872 | tf_op jit(solution)/shard_map/cond/branch_1_fun/ppermute | solution.py:712
  399.2 44.8 %collective-permute-start.66 = (bf16[256,2048]{1,0:T(8,128)(2,1)}, bf16[256,2048]{1,0:T(8,128)(2,1)}, u32[]{:S(2)}, u32[]{:S(2)}) collective-permute-start(bf16[256,2048]{1,0:T(8,128)(2,1)} %get-tuple-element.744), channel_id=1, source_target_pairs={{0,2},{2,0},{4,6},{6,4},{1,3},{3,1},{5,7},{7,5},{8,10},{10,8},{12,... | collective-permute-start | bytes 3145736 | tf_op jit(solution)/shard_map/ppermute | solution.py:712
  400.4 44.3 %collective-permute-start.67 = (bf16[256,2048]{1,0:T(8,128)(2,1)}, bf16[256,2048]{1,0:T(8,128)(2,1)}, u32[]{:S(2)}, u32[]{:S(2)}) collective-permute-start(bf16[256,2048]{1,0:T(8,128)(2,1)} %get-tuple-element.745), channel_id=1, source_target_pairs={{0,4},{2,6},{4,0},{6,2},{1,5},{3,7},{5,1},{7,3},{8,12},{10,14},{12... | collective-permute-start | bytes 3145736 | tf_op jit(solution)/shard_map/ppermute | solution.py:712
  402.0 43.8 %collective-permute-start.68 = (bf16[256,2048]{1,0:T(8,128)(2,1)}, bf16[256,2048]{1,0:T(8,128)(2,1)}, u32[]{:S(2)}, u32[]{:S(2)}) collective-permute-start(bf16[256,2048]{1,0:T(8,128)(2,1)} %get-tuple-element.746), channel_id=1, source_target_pairs={{0,6},{2,4},{4,2},{6,0},{1,7},{3,5},{5,3},{7,1},{8,14},{10,12},{12... | collective-permute-start | bytes 3145736 | tf_op jit(solution)/shard_map/ppermute | solution.py:712
  412.5 17.7 %collective-permute-start.16 = (bf16[1024,2048]{1,0:T(8,128)(2,1)}, bf16[1024,2048]{1,0:T(8,128)(2,1)}, u32[]{:S(2)}, u32[]{:S(2)}) collective-permute-start(bf16[1024,2048]{1,0:T(8,128)(2,1)} %get-tuple-element.384), channel_id=1, source_target_pairs={{0,1},{1,0},{2,3},{3,2},{4,5},{5,4},{6,7},{7,6},{8,9},{9,8},{10,11... | collective-permute-start | bytes 12582920 | tf_op jit(solution)/shard_map/cond/branch_1_fun/ppermute | solution.py:712
  430.2 13.7 %collective-permute-start.40 = (bf16[4,256,512]{2,1,0:T(8,128)(2,1)}, bf16[4,256,512]{2,1,0:T(8,128)(2,1)}, u32[]{:S(2)}, u32[]{:S(2)}) collective-permute-start(bf16[4,256,512]{2,1,0:T(8,128)(2,1)} %get-tuple-element.401), channel_id=1, source_target_pairs={{0,1},{1,0},{2,3},{3,2},{4,5},{5,4},{6,7},{7,6},{8,9},{9,8},{10,11... | collective-permute-start | bytes 3145736 | tf_op jit(solution)/shard_map/cond/branch_1_fun/ppermute | solution.py:712
  452.3 12.5 %collective-permute-start.18 = (bf16[128,2048]{1,0:T(8,128)(2,1)}, bf16[128,2048]{1,0:T(8,128)(2,1)}, u32[]{:S(2)}, u32[]{:S(2)}) collective-permute-start(bf16[128,2048]{1,0:T(8,128)(2,1)} %get-tuple-element.411), channel_id=1, source_target_pairs={{0,4},{2,6},{4,0},{6,2},{1,5},{3,7},{5,1},{7,3},{8,12},{10,14},{12... | collective-permute-start | bytes 1572872 | tf_op jit(solution)/shard_map/cond/branch_1_fun/ppermute | solution.py:712
  464.8 15.1 %collective-permute-start.41 = (bf16[128,2048]{1,0:T(8,128)(2,1)}, bf16[128,2048]{1,0:T(8,128)(2,1)S(1)}, u32[]{:S(2)}, u32[]{:S(2)}) collective-permute-start(bf16[128,2048]{1,0:T(8,128)(2,1)} %get-tuple-element.425), channel_id=1, source_target_pairs={{0,2},{2,0},{4,6},{6,4},{1,3},{3,1},{5,7},{7,5},{8,10},{10,8},{12,... | collective-permute-start | bytes 1572872 | tf_op jit(solution)/shard_map/cond/branch_1_fun/ppermute | solution.py:712
  465.5 15.1 %collective-permute-start.44 = (bf16[128,2048]{1,0:T(8,128)(2,1)}, bf16[128,2048]{1,0:T(8,128)(2,1)S(1)}, u32[]{:S(2)}, u32[]{:S(2)}) collective-permute-start(bf16[128,2048]{1,0:T(8,128)(2,1)} %get-tuple-element.428), channel_id=1, source_target_pairs={{0,4},{2,6},{4,0},{6,2},{1,5},{3,7},{5,1},{7,3},{8,12},{10,14},{12... | collective-permute-start | bytes 1572872 | tf_op jit(solution)/shard_map/cond/branch_1_fun/ppermute | solution.py:712
  468.6 19.7 %collective-permute-start.42 = (bf16[128,2048]{1,0:T(8,128)(2,1)S(1)}, bf16[128,2048]{1,0:T(8,128)(2,1)}, u32[]{:S(2)}, u32[]{:S(2)}) collective-permute-start(bf16[128,2048]{1,0:T(8,128)(2,1)S(1)} %add_convert_fusion.5), channel_id=1, source_target_pairs={{0,4},{2,6},{4,0},{6,2},{1,5},{3,7},{5,1},{7,3},{8,12},{10,14},{12... | collective-permute-start | bytes 1572872 | tf_op jit(solution)/shard_map/cond/branch_1_fun/ppermute | solution.py:712
  471.2 17.1 %collective-permute-start.43 = (bf16[128,2048]{1,0:T(8,128)(2,1)}, bf16[128,2048]{1,0:T(8,128)(2,1)}, u32[]{:S(2)}, u32[]{:S(2)}) collective-permute-start(bf16[128,2048]{1,0:T(8,128)(2,1)} %add_convert_fusion.4), channel_id=1, source_target_pairs={{0,2},{2,0},{4,6},{6,4},{1,3},{3,1},{5,7},{7,5},{8,10},{10,8},{12,... | collective-permute-start | bytes 1572872 | tf_op jit(solution)/shard_map/cond/branch_1_fun/ppermute | solution.py:712
  488.4 16.4 %collective-permute-start.45 = (bf16[128,2304]{1,0:T(8,128)(2,1)S(1)}, bf16[128,2304]{1,0:T(8,128)(2,1)}, u32[]{:S(2)}, u32[]{:S(2)}) collective-permute-start(bf16[128,2304]{1,0:T(8,128)(2,1)S(1)} %get-tuple-element.817), channel_id=1, source_target_pairs={{0,2},{2,0},{4,6},{6,4},{1,3},{3,1},{5,7},{7,5},{8,10},{10,8},{12,... | collective-permute-start | bytes 1769480 | tf_op jit(solution)/shard_map/cond/branch_1_fun/ppermute | solution.py:712
  490.1 23.3 %collective-permute-start.46 = (bf16[128,2304]{1,0:T(8,128)(2,1)S(1)}, bf16[128,2304]{1,0:T(8,128)(2,1)}, u32[]{:S(2)}, u32[]{:S(2)}) collective-permute-start(bf16[128,2304]{1,0:T(8,128)(2,1)S(1)} %get-tuple-element.816), channel_id=1, source_target_pairs={{0,4},{2,6},{4,0},{6,2},{1,5},{3,7},{5,1},{7,3},{8,12},{10,14},{12... | collective-permute-start | bytes 1769480 | tf_op jit(solution)/shard_map/cond/branch_1_fun/ppermute | solution.py:712
  491.8 22.6 %collective-permute-start.47 = (bf16[128,2304]{1,0:T(8,128)(2,1)S(1)}, bf16[128,2304]{1,0:T(8,128)(2,1)}, u32[]{:S(2)}, u32[]{:S(2)}) collective-permute-start(bf16[128,2304]{1,0:T(8,128)(2,1)S(1)} %get-tuple-element.815), channel_id=1, source_target_pairs={{0,6},{2,4},{4,2},{6,0},{1,7},{3,5},{5,3},{7,1},{8,14},{10,12},{12... | collective-permute-start | bytes 1769480 | tf_op jit(solution)/shard_map/cond/branch_1_fun/ppermute | solution.py:712
  (54 other events, 948.1 us)
Sparse Core Ops, SparseCore 0:
  29.1 65.4 all-gather.6
  101.5 114.8 all-gather.8
  218.0 61.7 all-gather.10
  282.4 111.9 reduce-scatter.3
  396.6 60.7 reduce-scatter.5
  459.6 61.7 reduce-scatter.7

commit v6 on v5

--- a/solution.py
+++ b/solution.py
@@ -831,9 +831,11 @@
         return lax.all_gather(pieces, "data", axis=0, tiled=False)
 
     attn_got = swap_pieces(cut_call(me, model, attn_arrays, extra, "attention_pieces"))
-    tied = lax.optimization_barrier((halves(hidden_in), halves(out_grad), always, attn_got))
-    grad_halves, always = tied[1:3]
-    x_near = spread_near(tied[0])
+    tied = lax.optimization_barrier(
+        (halves(hidden_in), halves(out_grad), turned_down, always, attn_got)
+    )
+    x_halves, grad_halves, turned_down, always, attn_got = tied
+    x_near = spread_near(x_halves)
     tied = lax.optimization_barrier((w_gate, w_up, turned_down, x_near))
     w_gate_sent, w_up_sent, turned_down, x_near = tied
     x_blocks = x_near + spread_far(x_near)

time: 556 us -> 550 us (0.989)
  transfers between devices with their start and end apart: 78 -> 78, of which waited for: 44 -> 44; matrix products, arithmetic and copies ran while one was open for 5% -> 5% of each run, Pallas kernels for 41% -> 42%
where the time goes in v6:
time: 550 us; the launch traced here: 542 us
  Pallas kernels  230 us (42%)
  waiting for transfers between devices  189 us (34%)
  starting transfers between devices  61.4 us (11%)
  local copies, waits for them, and re-layouts  22.7 us (4%)
  other arithmetic  19.1 us (3%)
  between operations  16.9 us (3%)
    ppermute x72, waiting for transfers between devices, trade(): lax.ppermute(block, axis, [(i, i ^ step) for i in range(lax.axis_size(axi...  183 us
    ppermute x72, starting transfers between devices, trade(): lax.ppermute(block, axis, [(i, i ^ step) for i in range(lax.axis_size(axi...  61.2 us
    pallas_call x7, Pallas kernels, project(): pl.pallas_call(functools.partial(project_kernel, len(lefts)), grid=(parts...  56 us
    pallas_call x4, Pallas kernels, hidden_call(): pl.pallas_call(functools.partial(hidden_kernel, first, cores, len(x_piece...  48.2 us
    pallas_call x3, Pallas kernels, weight_grad(): pl.pallas_call(functools.partial(weight_grad_kernel, [len(group) for grou...  44.8 us
    pallas_call x2, Pallas kernels, attention_call(): pl.pallas_call(kernel, grid=(halves[0].shape[0],), in_specs=[pl.BlockSpec...  27.8 us
    pallas_call x3, Pallas kernels, rows_product(): pl.pallas_call(functools.partial(rows_product_kernel, len(pieces), normed...  21.6 us
    pallas_call x4, Pallas kernels, rows_call(): pl.pallas_call(functools.partial(rows_kernel, kind, len(got)), grid=(2,),...  18 us
  transfers between devices with their start and end apart: 78, of which 44 were waited for; matrix products, arithmetic and copies ran while one was open for 5% of the time, Pallas kernels for 42%

profile of v6, /device:TPU:0, one launch (start us, length us, event | category | flops | bytes accessed | tf_op | source)
XLA Modules:
  0.0 542.5 jit_solution(3456278223607392645)
XLA Ops:
  13.4 3.0 collective-permute-start.50
  17.9 2.9 fusion.33
  33.3 10.9 %collective-permute-done.53 = bf16[128,2048]{1,0:T(8,128)(2,1)S(1)} collective-permute-done((bf16[128,2048]{1,0:T(8,128)(2,1)}, bf16[128,2048]{1,0:T(8,128)(2,1)S(1)}, u32[]{:S(2)}, u32[]{:S(2)}) %collective-permute-start.53) | collective-permute-done | bytes 524320 | tf_op jit(solution)/shard_map/ppermute | solution.py:712
  44.2 8.9 %collective-permute-done.54 = bf16[128,2048]{1,0:T(8,128)(2,1)S(1)} collective-permute-done((bf16[128,2048]{1,0:T(8,128)(2,1)}, bf16[128,2048]{1,0:T(8,128)(2,1)S(1)}, u32[]{:S(2)}, u32[]{:S(2)}) %collective-permute-start.54) | collective-permute-done | bytes 524320 | tf_op jit(solution)/shard_map/ppermute | solution.py:712
  59.5 3.7 fusion.6
  65.9 5.1 collective-permute-done.57.refs_1_
  71.0 13.2 %collective-permute-done.58.refs_2_ = bf16[128,2304]{1,0:T(8,128)(2,1)S(1)} collective-permute-done((bf16[128,2304]{1,0:T(8,128)(2,1)S(1)}, bf16[128,2304]{1,0:T(8,128)(2,1)S(1)}, u32[]{:S(2)}, u32[]{:S(2)}) %collective-permute-start.58) | collective-permute-done | bytes 589856 | tf_op jit(solution)/shard_map/ppermute | solution.py:712
  85.8 6.2 %collective-permute-done.60 = bf16[128,2048]{1,0:T(8,128)(2,1)S(1)} collective-permute-done((bf16[128,2048]{1,0:T(8,128)(2,1)S(1)}, bf16[128,2048]{1,0:T(8,128)(2,1)S(1)}, u32[]{:S(2)}, u32[]{:S(2)}) %collective-permute-start.60) | collective-permute-done | bytes 524320 | tf_op jit(solution)/shard_map/ppermute | solution.py:712
  99.5 19.2 %conditional.10 = (bf16[4,528,768]{2,1,0:T(8,128)(2,1)}, bf16[1024,2048]{1,0:T(8,128)(2,1)}, f32[4,256,512]{2,1,0:T(8,128)}, f32[4,256,512]{2,1,0:T(8,128)}, f32...) conditional(s32[]{:T(128)} %convert_element_type.143, () %tuple.119, ...), branch_computations={%region_0.1_spmd, %region_1.2_spmd} | conditional | flops 2108416 | bytes 21625480 | solution.py:708
  99.8 7.7 %query_key_value.1 = (bf16[1024,2048]{1,0:T(8,128)(2,1)}, f32[1024,512]{1,0:T(8,128)}) custom-call(bf16[128,2048]{1,0:T(8,128)(2,1)S(1)} %get-tuple-element.241.refs_0_, bf16[128,2048]{1,0:T(8,128)(2,1)} %get-tuple-element.242.refs_1_, bf16[128,2048]{1,0:T(8,128)(2,1)} %get-tuple-element.243.refs_2_, bf16[128,2048]{1,0:T(8,128)(2,1)} %get-tuple-element.244.refs_3_, ...), custom_call_target="tpu_custom_call" | custom-call | flops 1048576 | bytes 65536 | tf_op jit(solution)/shard_map/cond/branch_1_fun/query_key_value/pallas_call | solution.py:359
  107.5 6.5 %query_key_value_other.1 = f32[1024,512]{1,0:T(8,128)} custom-call(bf16[1024,2048]{1,0:T(8,128)(2,1)} %get-tuple-element.892.refs_0_, bf16[4,528,768]{2,1,0:T(8,128)(2,1)} %collective-permute-done.48.refs_1_), custom_call_target="tpu_custom_call" | custom-call | flops 1048576 | bytes 65536 | tf_op jit(solution)/shard_map/cond/branch_1_fun/query_key_value_other/pallas_call | solution.py:359
  115.7 3.0 collective-permute-done.49
  121.9 18.1 %conditional.11 = (bf16[1024,2048]{1,0:T(8,128)(2,1)}, bf16[4,256,256]{2,1,0:T(8,128)(2,1)}, bf16[4,256,256]{2,1,0:T(8,128)(2,1)}, bf16[128,2048]{1,0:T(8,128)(2...) conditional(s32[]{:T(128)} %convert_element_type.143, () %tuple.126, ...), branch_computations={%region_2.3_spmd, %region_3.4_spmd} | conditional | flops 1048576 | bytes 24199384 | solution.py:708
  125.2 11.7 %attend.1 = (bf16[4,256,256]{2,1,0:T(8,128)(2,1)}, bf16[4,256,256]{2,1,0:T(8,128)(2,1)}) custom-call(s32[1]{0:T(128)} %bitcast.6.core_ref, f32[4,256,512]{2,1,0:T(8,128)} %get-tuple-element.254.refs_0_, f32[4,256,512]{2,1,0:T(8,128)} %get-tuple-element.255.refs_1_, f32[4,512,128]{2,1,0:T(8,128)} %get-tuple-element.256.refs_2_, ...), custom_call_target="tpu_custom_call" | custom-call | flops 1048576 | bytes 65536 | tf_op jit(solution)/shard_map/cond/branch_1_fun/attend/pallas_call | solution.py:179
  140.0 82.9 %conditional.12 = (f32[256,2048]{1,0:T(8,128)}, bf16[128,2048]{1,0:T(8,128)(2,1)}, bf16[128,2048]{1,0:T(8,128)(2,1)}, bf16[128,2048]{1,0:T(8,128)(2,1)}, bf16[12...) conditional(s32[]{:T(128)} %convert_element_type.143, ...), branch_computations={%region_4.5_spmd, %region_5.6_spmd} | conditional | flops 6291456 | bytes 58327740 | solution.py:708
  140.0 4.4 attention_out_far.1
  146.4 5.1 attention_out.1
  151.5 7.1 %collective-permute-done.19 = bf16[128,2048]{1,0:T(8,128)(2,1)S(1)} collective-permute-done((bf16[128,2048]{1,0:T(8,128)(2,1)}, bf16[128,2048]{1,0:T(8,128)(2,1)S(1)}, u32[]{:S(2)}, u32[]{:S(2)}) %collective-permute-start.19) | collective-permute-done | bytes 524320 | tf_op jit(solution)/shard_map/cond/branch_1_fun/ppermute | solution.py:712
  166.4 8.4 %collective-permute-done.21.refs_2_ = bf16[128,2048]{1,0:T(8,128)(2,1)S(1)} collective-permute-done((bf16[128,2048]{1,0:T(8,128)(2,1)}, bf16[128,2048]{1,0:T(8,128)(2,1)S(1)}, u32[]{:S(2)}, u32[]{:S(2)}) %collective-permute-start.21) | collective-permute-done | bytes 524320 | tf_op jit(solution)/shard_map/cond/branch_1_fun/ppermute | solution.py:712
  175.4 9.0 %collective-permute-done.22.refs_3_ = bf16[128,2048]{1,0:T(8,128)(2,1)S(1)} collective-permute-done((bf16[128,2048]{1,0:T(8,128)(2,1)S(1)}, bf16[128,2048]{1,0:T(8,128)(2,1)S(1)}, u32[]{:S(2)}, u32[]{:S(2)}) %collective-permute-start.22) | collective-permute-done | bytes 524320 | tf_op jit(solution)/shard_map/cond/branch_1_fun/ppermute | solution.py:712
  184.5 2.7 middle.1
  191.2 11.1 %collective-permute-done.25 = bf16[128,2048]{1,0:T(8,128)(2,1)} collective-permute-done((bf16[128,2048]{1,0:T(8,128)(2,1)}, bf16[128,2048]{1,0:T(8,128)(2,1)}, u32[]{:S(2)}, u32[]{:S(2)}) %collective-permute-start.25) | collective-permute-done | bytes 524320 | tf_op jit(solution)/shard_map/cond/branch_1_fun/ppermute | solution.py:712
  204.4 4.1 out_grad_rows.1
  208.5 5.1 collective-permute-done.26
  215.0 7.9 %collective-permute-done.29 = bf16[128,2048]{1,0:T(8,128)(2,1)} collective-permute-done((bf16[128,2048]{1,0:T(8,128)(2,1)}, bf16[128,2048]{1,0:T(8,128)(2,1)}, u32[]{:S(2)}, u32[]{:S(2)}) %collective-permute-start.29) | collective-permute-done | bytes 524320 | tf_op jit(solution)/shard_map/cond/branch_1_fun/ppermute | solution.py:712
  222.9 57.0 %conditional.13 = (bf16[4,512,1536]{2,1,0:T(8,128)(2,1)}, bf16[1024,2048]{1,0:T(8,128)(2,1)}, bf16[1024,2048]{1,0:T(8,128)(2,1)}, bf16[1024,2048]{1,0:T(8,128)(2...) conditional(s32[]{:T(128)} %convert_element_type.143, ...), branch_computations={%region_6.7_spmd, %region_7.8_spmd} | conditional | flops 3145728 | bytes 84083008 | solution.py:708
  223.4 15.3 %hidden_units_a.1 = (bf16[1024,2048]{1,0:T(8,128)(2,1)}, bf16[1024,1024]{1,0:T(8,128)(2,1)}, bf16[1024,512]{1,0:T(8,128)(2,1)}) custom-call(bf16[128,2048]{1,0:T(8,128)(2,1)} %get-tuple-element.304.refs_0_, bf16[128,2048]{1,0:T(8,128)(2,1)} %get-tuple-element.305.refs_1_, bf16[128,2048]{1,0:T(8,128)(2,1)} %get-tuple-element.306.refs_2_, ...), custom_call_target="tpu_custom_call" | custom-call | flops 1048576 | bytes 65536 | tf_op jit(solution)/shard_map/cond/branch_1_fun/hidden_units_a/pallas_call | solution.py:687
  239.3 13.7 %hidden_units_a_other.1 = (bf16[1024,1024]{1,0:T(8,128)(2,1)}, bf16[1024,512]{1,0:T(8,128)(2,1)}) custom-call(bf16[1024,2048]{1,0:T(8,128)(2,1)} %get-tuple-element.942.refs_0_, bf16[1024,2048]{1,0:T(8,128)(2,1)} %get-tuple-element.312.refs_8_.refs_1_.refs_2_, bf16[4,512,1536]{2,1,0:T(8,128)(2,1)} %collective-permute-done.4.refs_2_.refs_3_.refs_4_, ...), custom_call_target="tpu_custom_call" | custom-call | flops 1048576 | bytes 65536 | tf_op jit(solution)/shard_map/cond/branch_1_fun/hidden_units_a_other/pallas_call | solution.py:687
  253.5 5.4 collective-permute-done.8.refs_7_
  260.6 19.4 %hidden_weights_a.1 = bf16[4,512,1536]{2,1,0:T(8,128)(2,1)} custom-call(bf16[1024,2048]{1,0:T(8,128)(2,1)} %get-tuple-element.942.refs_0_, bf16[1024,2048]{1,0:T(8,128)(2,1)} %collective-permute-done.5.refs_1_, bf16[1024,2048]{1,0:T(8,128)(2,1)} %get-tuple-element.312.refs_8_.refs_1_.refs_2_, bf16[1024,2048]{1,0:T(8,128)(2,1)} %collective-permute-done.6.refs_3_, ...), custom_call_target="tpu_custom_call" | custom-call | flops 1048576 | bytes 65536 | tf_op jit(solution)/shard_map/cond/branch_1_fun/hidden_weights_a/pallas_call | solution.py:404
  280.1 74.5 %conditional.14 = (f32[256,2048]{1,0:T(8,128)}, bf16[128,2048]{1,0:T(8,128)(2,1)}, bf16[128,2048]{1,0:T(8,128)(2,1)}, bf16[128,2048]{1,0:T(8,128)(2,1)}, bf16[12...) conditional(s32[]{:T(128)} %convert_element_type.143, ...), branch_computations={%region_8.9_spmd, %region_9.10_spmd} | conditional | flops 7340032 | bytes 60097064 | solution.py:708
  280.7 10.2 %hidden_units_b.2 = (bf16[1024,512]{1,0:T(8,128)(2,1)}, bf16[1024,256]{1,0:T(8,128)(2,1)}) custom-call(bf16[1024,2048]{1,0:T(8,128)(2,1)} %get-tuple-element.320.refs_0_, bf16[1024,2048]{1,0:T(8,128)(2,1)} %get-tuple-element.321.refs_1_.refs_2_, bf16[4,512,768]{2,1,0:T(8,128)(2,1)} %get-tuple-element.322.refs_2_.refs_3_.refs_4_.refs_6_, ...), custom_call_target="tpu_custom_call" | custom-call | flops 1048576 | bytes 65536 | tf_op jit(solution)/shard_map/cond/branch_1_fun/hidden_units_b/pallas_call | solution.py:687
  290.9 9.0 %hidden_units_b.3 = (bf16[1024,512]{1,0:T(8,128)(2,1)}, bf16[1024,256]{1,0:T(8,128)(2,1)}) custom-call(bf16[1024,2048]{1,0:T(8,128)(2,1)} %get-tuple-element.320.refs_0_, bf16[1024,2048]{1,0:T(8,128)(2,1)} %get-tuple-element.321.refs_1_.refs_2_, bf16[4,512,768]{2,1,0:T(8,128)(2,1)} %collective-permute-done.31.refs_2_.refs_3_.refs_4_.refs_7_, ...), custom_call_target="tpu_custom_call" | custom-call | flops 1048576 | bytes 65536 | tf_op jit(solution)/shard_map/cond/branch_1_fun/hidden_units_b/pallas_call | solution.py:687
  299.8 9.1 %normed_mid_grad_far.1 = (bf16[128,2048]{1,0:T(8,128)(2,1)}, bf16[128,2048]{1,0:T(8,128)(2,1)}) custom-call(bf16[1024,1024]{1,0:T(8,128)(2,1)} %get-tuple-element.318.refs_0_, bf16[1024,1024]{1,0:T(8,128)(2,1)} %get-tuple-element.319.refs_1_, bf16[1024,512]{1,0:T(8,128)(2,1)} %get-tuple-element.340.refs_2_.refs_4_, ...), custom_call_target="tpu_custom_call" | custom-call | flops 1048576 | bytes 65536 | tf_op jit(solution)/shard_map/cond/branch_1_fun/normed_mid_grad_far/pallas_call | solution.py:224
  309.6 14.8 %normed_mid_grad.1 = (f32[256,2048]{1,0:T(8,128)}, bf16[128,2048]{1,0:T(8,128)(2,1)}, bf16[128,2048]{1,0:T(8,128)(2,1)}, bf16[128,2048]{1,0:T(8,128)(2,1)}, bf16[128,2048]{1,0:T(8,128)(2,1)}) custom-call(bf16[1024,1024]{1,0:T(8,128)(2,1)} %get-tuple-element.318.refs_0_, bf16[1024,1024]{1,0:T(8,128)(2,1)} %get-tuple-element.319.refs_1_, ...), custom_call_target="tpu_custom_call" | custom-call | flops 1048576 | bytes 65536 | tf_op jit(solution)/shard_map/cond/branch_1_fun/normed_mid_grad/pallas_call | solution.py:224
  333.8 12.7 %hidden_weights_b.1 = bf16[4,512,768]{2,1,0:T(8,128)(2,1)} custom-call(bf16[1024,2048]{1,0:T(8,128)(2,1)} %get-tuple-element.320.refs_0_, bf16[1024,2048]{1,0:T(8,128)(2,1)} %get-tuple-element.336.refs_1_, bf16[1024,2048]{1,0:T(8,128)(2,1)} %get-tuple-element.321.refs_1_.refs_2_, bf16[1024,2048]{1,0:T(8,128)(2,1)} %get-tuple-element.337.refs_3_, ...), custom_call_target="tpu_custom_call" | custom-call | flops 1048576 | bytes 65536 | tf_op jit(solution)/shard_map/cond/branch_1_fun/hidden_weights_b/pallas_call | solution.py:404
  346.5 5.0 collective-permute-done.34
  351.4 3.1 collective-permute-done.37
  354.6 43.5 %conditional.15 = (f32[256,2048]{1,0:T(8,128)}, bf16[128,2048]{1,0:T(8,128)(2,1)}, bf16[128,2048]{1,0:T(8,128)(2,1)}, bf16[128,2048]{1,0:T(8,128)(2,1)}, bf16[12...) conditional(s32[]{:T(128)} %convert_element_type.143, ...), branch_computations={%region_10.11_spmd, %region_11.12_spmd} | conditional | flops 2097152 | bytes 37880180 | solution.py:708
  354.8 6.3 %middle_grad.1 = (f32[256,2048]{1,0:T(8,128)}, bf16[128,2048]{1,0:T(8,128)(2,1)}, bf16[128,2048]{1,0:T(8,128)(2,1)}) custom-call(f32[256,2048]{1,0:T(8,128)} %get-tuple-element.346.refs_0_, f32[256,2048]{1,0:T(8,128)} %get-tuple-element.347.refs_1_, bf16[128,2048]{1,0:T(8,128)(2,1)} %get-tuple-element.348.refs_2_, ...), custom_call_target="tpu_custom_call" | custom-call | flops 1048576 | bytes 65536 | tf_op jit(solution)/shard_map/cond/branch_1_fun/middle_grad/pallas_call | solution.py:307
  365.2 10.7 %hidden_out.1 = (f32[256,2048]{1,0:T(8,128)}, bf16[256,2048]{1,0:T(8,128)(2,1)}, bf16[256,2048]{1,0:T(8,128)(2,1)}, bf16[256,2048]{1,0:T(8,128)(2,1)}) custom-call(bf16[1024,512]{1,0:T(8,128)(2,1)} %get-tuple-element.357.refs_0_, bf16[1024,512]{1,0:T(8,128)(2,1)} %get-tuple-element.358.refs_1_, bf16[1024,256]{1,0:T(8,128)(2,1)} %get-tuple-element.359.refs_2_, ...), custom_call_target="tpu_custom_call" | custom-call | flops 1048576 | bytes 65536 | tf_op jit(solution)/shard_map/cond/branch_1_fun/hidden_out/pallas_call | solution.py:224
  378.7 10.6 %collective-permute-done.10 = bf16[128,2048]{1,0:T(8,128)(2,1)} collective-permute-done((bf16[128,2048]{1,0:T(8,128)(2,1)}, bf16[128,2048]{1,0:T(8,128)(2,1)}, u32[]{:S(2)}, u32[]{:S(2)}) %collective-permute-start.10) | collective-permute-done | bytes 524320 | tf_op jit(solution)/shard_map/cond/branch_1_fun/ppermute | solution.py:712
  389.3 7.7 %collective-permute-done.13 = bf16[128,2048]{1,0:T(8,128)(2,1)} collective-permute-done((bf16[128,2048]{1,0:T(8,128)(2,1)}, bf16[128,2048]{1,0:T(8,128)(2,1)}, u32[]{:S(2)}, u32[]{:S(2)}) %collective-permute-start.13) | collective-permute-done | bytes 524320 | tf_op jit(solution)/shard_map/cond/branch_1_fun/ppermute | solution.py:712
  401.6 27.2 %conditional.16 = (bf16[1024,2048]{1,0:T(8,128)(2,1)}, bf16[1024,2048]{1,0:T(8,128)(2,1)}, bf16[4,256,512]{2,1,0:T(8,128)(2,1)}, bf16[4,256,512]{2,1,0:T(8,128)(2,1)}, f32[8,128]{1,0:T(8,128)S(1)}) conditional(s32[]{:T(128)} %convert_element_type.143, () %tuple.117, (bf16[128,2048]{1,0:T(8,128)(2,1)}, bf16[128,2048]{1,0:T(8,128)(2,1)}, ...), branch_computations={%region_13.14_spmd, %region_14.15_spmd} | conditional | flops 2097152 | bytes 21119124 | solution.py:708
  401.6 7.4 %attended_grad.1 = (bf16[1024,2048]{1,0:T(8,128)(2,1)}, bf16[1024,256]{1,0:T(8,128)(2,1)}, bf16[1024,256]{1,0:T(8,128)(2,1)}) custom-call(bf16[128,2048]{1,0:T(8,128)(2,1)} %get-tuple-element.371.refs_0_, bf16[128,2048]{1,0:T(8,128)(2,1)} %get-tuple-element.372.refs_1_, bf16[128,2048]{1,0:T(8,128)(2,1)} %get-tuple-element.373.refs_2_, ...), custom_call_target="tpu_custom_call" | custom-call | flops 1048576 | bytes 65536 | tf_op jit(solution)/shard_map/cond/branch_1_fun/attended_grad/pallas_call | solution.py:359
  412.6 16.1 %attend_back.1 = (bf16[4,256,512]{2,1,0:T(8,128)(2,1)}, bf16[4,256,512]{2,1,0:T(8,128)(2,1)}, f32[8,128]{1,0:T(8,128)S(1)}) custom-call(s32[1]{0:T(128)} %bitcast.13.core_ref, f32[4,256,512]{2,1,0:T(8,128)} %get-tuple-element.386.refs_0_, f32[4,256,512]{2,1,0:T(8,128)} %get-tuple-element.387.refs_1_, bf16[4,256,256]{2,1,0:T(8,128)(2,1)S(1)} %bitcast.65, ...), custom_call_target="tpu_custom_call" | custom-call | flops 1048576 | bytes 65536 | tf_op jit(solution)/shard_map/cond/branch_1_fun/attend_back/pallas_call | solution.py:179
  428.8 13.8 %conditional.17 = (bf16[4,528,768]{2,1,0:T(8,128)(2,1)}, bf16[1024,512]{1,0:T(8,128)(2,1)}, bf16[1024,512]{1,0:T(8,128)(2,1)}) conditional(s32[]{:T(128)} %convert_element_type.143, () %tuple.116, (bf16[4,256,512]{2,1,0:T(8,128)(2,1)}, bf16[4,256,512]{2,1,0:T(8,128)(2,1)}, bf16[4,256,256]{2,1,0:T(8,128)(2,1)}, bf16[4,256,256]{2,1,0:T(8,128)(2,1)}, ...), branch_computations={%region_15.16_spmd, %region_16.17_spmd} | conditional | flops 1049600 | bytes 5341214 | solution.py:708
  429.9 12.7 %attention_weights.1 = bf16[4,528,768]{2,1,0:T(8,128)(2,1)} custom-call(bf16[1024,2048]{1,0:T(8,128)(2,1)} %get-tuple-element.396.refs_0_, bf16[1024,2048]{1,0:T(8,128)(2,1)} %get-tuple-element.397.refs_1_, bf16[1024,2048]{1,0:T(8,128)(2,1)} %get-tuple-element.398.refs_2_, bf16[1024,2048]{1,0:T(8,128)(2,1)} %get-tuple-element.399.refs_3_, ...), custom_call_target="tpu_custom_call" | custom-call | flops 1048576 | bytes 65536 | tf_op jit(solution)/shard_map/cond/branch_1_fun/attention_weights/pallas_call | solution.py:404
  444.3 18.2 %conditional.18 = (f32[256,2048]{1,0:T(8,128)}, bf16[128,2048]{1,0:T(8,128)(2,1)}, bf16[128,2048]{1,0:T(8,128)(2,1)}, bf16[128,2048]{1,0:T(8,128)(2,1)}, bf16[12...) conditional(s32[]{:T(128)} %convert_element_type.143, () %tuple.115, ...), branch_computations={%region_17.18_spmd, %region_18.19_spmd} | conditional | flops 2097152 | bytes 17301668 | solution.py:708
  444.6 5.1 normed_in_grad_far.1
  451.7 6.9 %normed_in_grad.1 = (f32[256,2048]{1,0:T(8,128)}, bf16[128,2048]{1,0:T(8,128)(2,1)}, bf16[128,2048]{1,0:T(8,128)(2,1)}, bf16[128,2048]{1,0:T(8,128)(2,1)}, bf16[128,2048]{1,0:T(8,128)(2,1)}) custom-call(bf16[1024,512]{1,0:T(8,128)(2,1)} %get-tuple-element.405.refs_0_, bf16[1024,512]{1,0:T(8,128)(2,1)} %get-tuple-element.406.refs_1_, ...), custom_call_target="tpu_custom_call" | custom-call | flops 1048576 | bytes 65536 | tf_op jit(solution)/shard_map/cond/branch_1_fun/normed_in_grad/pallas_call | solution.py:224
  458.6 3.6 collective-permute-done.17
  462.6 49.2 %conditional.19 = (bf16[256,2048]{1,0:T(8,128)(2,1)}, f32[256,2048]{1,0:T(8,128)}, bf16[128,2304]{1,0:T(8,128)(2,1)S(1)}, bf16[128,2304]{1,0:T(8,128)(2,1)}, bf1...) conditional(s32[]{:T(128)} %convert_element_type.143, () %tuple.114, (bf16[128,2048]{1,0:T(8,128)(2,1)}, ...), branch_computations={%region_20.21_spmd, %region_21.22_spmd} | conditional | flops 8912914 | bytes 32375352 | solution.py:708
  472.1 5.6 %collective-permute-done.41.refs_2_ = bf16[128,2048]{1,0:T(8,128)(2,1)S(1)} collective-permute-done((bf16[128,2048]{1,0:T(8,128)(2,1)}, bf16[128,2048]{1,0:T(8,128)(2,1)S(1)}, u32[]{:S(2)}, u32[]{:S(2)}) %collective-permute-start.41) | collective-permute-done | bytes 524320 | tf_op jit(solution)/shard_map/cond/branch_1_fun/ppermute | solution.py:712
  479.2 7.9 %collective-permute-done.42.refs_3_ = bf16[128,2048]{1,0:T(8,128)(2,1)} collective-permute-done((bf16[128,2048]{1,0:T(8,128)(2,1)S(1)}, bf16[128,2048]{1,0:T(8,128)(2,1)}, u32[]{:S(2)}, u32[]{:S(2)}) %collective-permute-start.42) | collective-permute-done | bytes 524320 | tf_op jit(solution)/shard_map/cond/branch_1_fun/ppermute | solution.py:712
  488.1 2.7 collective-permute-start.47
  490.8 4.2 hidden_out_sum.1
  495.0 4.8 grad_in.1
  499.9 3.8 collective-permute-done.45
  503.7 8.0 %collective-permute-done.46 = bf16[128,2304]{1,0:T(8,128)(2,1)} collective-permute-done((bf16[128,2304]{1,0:T(8,128)(2,1)S(1)}, bf16[128,2304]{1,0:T(8,128)(2,1)}, u32[]{:S(2)}, u32[]{:S(2)}) %collective-permute-start.46) | collective-permute-done | bytes 589856 | tf_op jit(solution)/shard_map/cond/branch_1_fun/ppermute | solution.py:712
  511.8 3.4 reduce-scatter.8.cloned.1.call-done
  520.6 4.6 hidden_owned.1
  525.6 3.4 collective-permute-done.70.refs_2_
  531.6 2.5 psum.7
  (277 shorter events, 120.4 us)
Async XLA Ops:
  7.2 87.4 %all-gather.7.cloned.1.call-start = ((), (), s32[]{:S(2)}) async-start(), calls=%async_computation.6 | async-start | bytes 4055040 | tf_op jit(solution)/shard_map/all_gather | solution.py:831
  13.4 13.0 %collective-permute-start.50 = (bf16[144,768]{1,0:T(8,128)(2,1)S(1)}, bf16[144,768]{1,0:T(8,128)(2,1)S(1)}, u32[]{:S(2)}, u32[]{:S(2)}) collective-permute-start(bf16[144,768]{1,0:T(8,128)(2,1)S(1)} %get-tuple-element.623), channel_id=1, source_target_pairs={{0,2},{2,0},{4,6},{6,4},{1,3},{3,1},{5,7},{7,5},{8,10},{10,8},{12,... | collective-permute-start | bytes 663560 | tf_op jit(solution)/shard_map/ppermute | solution.py:712
  29.0 193.9 %all-gather.9.cloned.1.call-start = ((), (), s32[]{:S(2)}) async-start(), calls=%async_computation.7 | async-start | bytes 7864320 | tf_op jit(solution)/shard_map/all_gather | solution.py:831
  29.1 15.1 %collective-permute-start.53 = (bf16[128,2048]{1,0:T(8,128)(2,1)}, bf16[128,2048]{1,0:T(8,128)(2,1)S(1)}, u32[]{:S(2)}, u32[]{:S(2)}) collective-permute-start(bf16[128,2048]{1,0:T(8,128)(2,1)} %get-tuple-element.646), channel_id=1, source_target_pairs={{0,2},{2,0},{4,6},{6,4},{1,3},{3,1},{5,7},{7,5},{8,10},{10,8},{12,... | collective-permute-start | bytes 1572872 | tf_op jit(solution)/shard_map/ppermute | solution.py:712
  30.4 22.8 %collective-permute-start.55 = (bf16[128,2048]{1,0:T(8,128)(2,1)}, bf16[128,2048]{1,0:T(8,128)(2,1)S(1)}, u32[]{:S(2)}, u32[]{:S(2)}) collective-permute-start(bf16[128,2048]{1,0:T(8,128)(2,1)} %get-tuple-element.646), channel_id=1, source_target_pairs={{0,4},{2,6},{4,0},{6,2},{1,5},{3,7},{5,1},{7,3},{8,12},{10,14},{12... | collective-permute-start | bytes 1572872 | tf_op jit(solution)/shard_map/ppermute | solution.py:712
  31.2 22.0 %collective-permute-start.54 = (bf16[128,2048]{1,0:T(8,128)(2,1)}, bf16[128,2048]{1,0:T(8,128)(2,1)S(1)}, u32[]{:S(2)}, u32[]{:S(2)}) collective-permute-start(bf16[128,2048]{1,0:T(8,128)(2,1)} %get-tuple-element.647), channel_id=1, source_target_pairs={{0,2},{2,0},{4,6},{6,4},{1,3},{3,1},{5,7},{7,5},{8,10},{10,8},{12,... | collective-permute-start | bytes 1572872 | tf_op jit(solution)/shard_map/ppermute | solution.py:712
  32.7 21.6 %collective-permute-start.56 = (bf16[128,2048]{1,0:T(8,128)(2,1)}, bf16[128,2048]{1,0:T(8,128)(2,1)S(1)}, u32[]{:S(2)}, u32[]{:S(2)}) collective-permute-start(bf16[128,2048]{1,0:T(8,128)(2,1)} %get-tuple-element.647), channel_id=1, source_target_pairs={{0,4},{2,6},{4,0},{6,2},{1,5},{3,7},{5,1},{7,3},{8,12},{10,14},{12... | collective-permute-start | bytes 1572872 | tf_op jit(solution)/shard_map/ppermute | solution.py:712
  54.7 16.3 %collective-permute-start.57 = (bf16[128,2304]{1,0:T(8,128)(2,1)S(1)}, bf16[128,2304]{1,0:T(8,128)(2,1)S(1)}, u32[]{:S(2)}, u32[]{:S(2)}) collective-permute-start(bf16[128,2304]{1,0:T(8,128)(2,1)S(1)} %get-tuple-element.835), channel_id=1, source_target_pairs={{0,2},{2,0},{4,6},{6,4},{1,3},{3,1},{5,7},{7,5},{8,10},{10,8},{12,... | collective-permute-start | bytes 1769480 | tf_op jit(solution)/shard_map/ppermute | solution.py:712
  55.3 28.9 %collective-permute-start.58 = (bf16[128,2304]{1,0:T(8,128)(2,1)S(1)}, bf16[128,2304]{1,0:T(8,128)(2,1)S(1)}, u32[]{:S(2)}, u32[]{:S(2)}) collective-permute-start(bf16[128,2304]{1,0:T(8,128)(2,1)S(1)} %get-tuple-element.834), channel_id=1, source_target_pairs={{0,4},{2,6},{4,0},{6,2},{1,5},{3,7},{5,1},{7,3},{8,12},{10,14},{12... | collective-permute-start | bytes 1769480 | tf_op jit(solution)/shard_map/ppermute | solution.py:712
  55.9 28.3 %collective-permute-start.59 = (bf16[128,2304]{1,0:T(8,128)(2,1)S(1)}, bf16[128,2304]{1,0:T(8,128)(2,1)S(1)}, u32[]{:S(2)}, u32[]{:S(2)}) collective-permute-start(bf16[128,2304]{1,0:T(8,128)(2,1)S(1)} %get-tuple-element.833), channel_id=1, source_target_pairs={{0,6},{2,4},{4,2},{6,0},{1,7},{3,5},{5,3},{7,1},{8,14},{10,12},{12... | collective-permute-start | bytes 1769480 | tf_op jit(solution)/shard_map/ppermute | solution.py:712
  58.3 33.8 %collective-permute-start.60 = (bf16[128,2048]{1,0:T(8,128)(2,1)S(1)}, bf16[128,2048]{1,0:T(8,128)(2,1)S(1)}, u32[]{:S(2)}, u32[]{:S(2)}) collective-permute-start(bf16[128,2048]{1,0:T(8,128)(2,1)S(1)} %collective-permute-done.53), channel_id=1, source_target_pairs={{0,4},{2,6},{4,0},{6,2},{1,5},{3,7},{5,1},{7,3},{8,12},{10,14},{12... | collective-permute-start | bytes 1572872 | tf_op jit(solution)/shard_map/ppermute | solution.py:712
  59.0 33.9 %collective-permute-start.61 = (bf16[128,2048]{1,0:T(8,128)(2,1)S(1)}, bf16[128,2048]{1,0:T(8,128)(2,1)}, u32[]{:S(2)}, u32[]{:S(2)}) collective-permute-start(bf16[128,2048]{1,0:T(8,128)(2,1)S(1)} %collective-permute-done.56), channel_id=1, source_target_pairs={{0,2},{2,0},{4,6},{6,4},{1,3},{3,1},{5,7},{7,5},{8,10},{10,8},{12,... | collective-permute-start | bytes 1572872 | tf_op jit(solution)/shard_map/ppermute | solution.py:712
  94.6 185.4 %all-gather.11.cloned.1.call-start = ((), (), s32[]{:S(2)}) async-start(), calls=%async_computation.8 | async-start | bytes 3932160 | tf_op jit(solution)/shard_map/all_gather | solution.py:831
  95.4 302.7 %reduce-scatter.4.cloned.1.call-start = ((), (), s32[]{:S(2)}) async-start(), calls=%async_computation.3 | async-start | bytes 7864320 | tf_op jit(solution)/shard_map/reduce_scatter | solution.py:934
  95.4 23.3 %collective-permute-start.62 = (bf16[128,2048]{1,0:T(8,128)(2,1)S(1)}, bf16[128,2048]{1,0:T(8,128)(2,1)}, u32[]{:S(2)}, u32[]{:S(2)}) collective-permute-start(bf16[128,2048]{1,0:T(8,128)(2,1)S(1)} %copy-done.22), channel_id=1, source_target_pairs={{0,2},{2,0},{4,6},{6,4},{1,3},{3,1},{5,7},{7,5},{8,10},{10,8},{12,... | collective-permute-start | bytes 1572872 | tf_op jit(solution)/shard_map/ppermute | solution.py:712
  97.0 23.5 %collective-permute-start.63 = (bf16[128,2048]{1,0:T(8,128)(2,1)S(1)}, bf16[128,2048]{1,0:T(8,128)(2,1)}, u32[]{:S(2)}, u32[]{:S(2)}) collective-permute-start(bf16[128,2048]{1,0:T(8,128)(2,1)S(1)} %copy-done.20), channel_id=1, source_target_pairs={{0,2},{2,0},{4,6},{6,4},{1,3},{3,1},{5,7},{7,5},{8,10},{10,8},{12,... | collective-permute-start | bytes 1572872 | tf_op jit(solution)/shard_map/ppermute | solution.py:712
  97.5 22.9 %collective-permute-start.64 = (bf16[128,2048]{1,0:T(8,128)(2,1)S(1)}, bf16[128,2048]{1,0:T(8,128)(2,1)}, u32[]{:S(2)}, u32[]{:S(2)}) collective-permute-start(bf16[128,2048]{1,0:T(8,128)(2,1)S(1)} %copy-done.22), channel_id=1, source_target_pairs={{0,4},{2,6},{4,0},{6,2},{1,5},{3,7},{5,1},{7,3},{8,12},{10,14},{12... | collective-permute-start | bytes 1572872 | tf_op jit(solution)/shard_map/ppermute | solution.py:712
  99.0 22.9 %collective-permute-start.65 = (bf16[128,2048]{1,0:T(8,128)(2,1)S(1)}, bf16[128,2048]{1,0:T(8,128)(2,1)}, u32[]{:S(2)}, u32[]{:S(2)}) collective-permute-start(bf16[128,2048]{1,0:T(8,128)(2,1)S(1)} %copy-done.20), channel_id=1, source_target_pairs={{0,4},{2,6},{4,0},{6,2},{1,5},{3,7},{5,1},{7,3},{8,12},{10,14},{12... | collective-permute-start | bytes 1572872 | tf_op jit(solution)/shard_map/ppermute | solution.py:712
  121.9 18.1 %collective-permute-start = (bf16[1024,2048]{1,0:T(8,128)(2,1)}, bf16[1024,2048]{1,0:T(8,128)(2,1)}, u32[]{:S(2)}, u32[]{:S(2)}) collective-permute-start(bf16[1024,2048]{1,0:T(8,128)(2,1)} %get-tuple-element.252), channel_id=1, source_target_pairs={{0,1},{1,0},{2,3},{3,2},{4,5},{5,4},{6,7},{7,6},{8,9},{9,8},{10,11... | collective-permute-start | bytes 12582920 | tf_op jit(solution)/shard_map/cond/branch_1_fun/ppermute | solution.py:712
  121.9 15.0 %collective-permute-start.1 = (bf16[128,2048]{1,0:T(8,128)(2,1)}, bf16[128,2048]{1,0:T(8,128)(2,1)}, u32[]{:S(2)}, u32[]{:S(2)}) collective-permute-start(bf16[128,2048]{1,0:T(8,128)(2,1)} %get-tuple-element.263), channel_id=1, source_target_pairs={{0,4},{2,6},{4,0},{6,2},{1,5},{3,7},{5,1},{7,3},{8,12},{10,14},{12... | collective-permute-start | bytes 1572872 | tf_op jit(solution)/shard_map/cond/branch_1_fun/ppermute | solution.py:712
  123.4 14.4 %collective-permute-start.2 = (bf16[128,2048]{1,0:T(8,128)(2,1)}, bf16[128,2048]{1,0:T(8,128)(2,1)}, u32[]{:S(2)}, u32[]{:S(2)}) collective-permute-start(bf16[128,2048]{1,0:T(8,128)(2,1)} %get-tuple-element.264), channel_id=1, source_target_pairs={{0,2},{2,0},{4,6},{6,4},{1,3},{3,1},{5,7},{7,5},{8,10},{10,8},{12,... | collective-permute-start | bytes 1572872 | tf_op jit(solution)/shard_map/cond/branch_1_fun/ppermute | solution.py:712
  144.4 14.2 %collective-permute-start.19 = (bf16[128,2048]{1,0:T(8,128)(2,1)}, bf16[128,2048]{1,0:T(8,128)(2,1)S(1)}, u32[]{:S(2)}, u32[]{:S(2)}) collective-permute-start(bf16[128,2048]{1,0:T(8,128)(2,1)} %get-tuple-element.277), channel_id=1, source_target_pairs={{0,2},{2,0},{4,6},{6,4},{1,3},{3,1},{5,7},{7,5},{8,10},{10,8},{12,... | collective-permute-start | bytes 1572872 | tf_op jit(solution)/shard_map/cond/branch_1_fun/ppermute | solution.py:712
  145.9 13.9 %collective-permute-start.20 = (bf16[128,2048]{1,0:T(8,128)(2,1)}, bf16[128,2048]{1,0:T(8,128)(2,1)S(1)}, u32[]{:S(2)}, u32[]{:S(2)}) collective-permute-start(bf16[128,2048]{1,0:T(8,128)(2,1)} %get-tuple-element.278), channel_id=1, source_target_pairs={{0,4},{2,6},{4,0},{6,2},{1,5},{3,7},{5,1},{7,3},{8,12},{10,14},{12... | collective-permute-start | bytes 1572872 | tf_op jit(solution)/shard_map/cond/branch_1_fun/ppermute | solution.py:712
  159.8 15.1 %collective-permute-start.21 = (bf16[128,2048]{1,0:T(8,128)(2,1)}, bf16[128,2048]{1,0:T(8,128)(2,1)S(1)}, u32[]{:S(2)}, u32[]{:S(2)}) collective-permute-start(bf16[128,2048]{1,0:T(8,128)(2,1)} %get-tuple-element.279), channel_id=1, source_target_pairs={{0,2},{2,0},{4,6},{6,4},{1,3},{3,1},{5,7},{7,5},{8,10},{10,8},{12,... | collective-permute-start | bytes 1572872 | tf_op jit(solution)/shard_map/cond/branch_1_fun/ppermute | solution.py:712
  160.3 15.1 %collective-permute-start.24 = (bf16[128,2048]{1,0:T(8,128)(2,1)}, bf16[128,2048]{1,0:T(8,128)(2,1)S(1)}, u32[]{:S(2)}, u32[]{:S(2)}) collective-permute-start(bf16[128,2048]{1,0:T(8,128)(2,1)} %get-tuple-element.282), channel_id=1, source_target_pairs={{0,4},{2,6},{4,0},{6,2},{1,5},{3,7},{5,1},{7,3},{8,12},{10,14},{12... | collective-permute-start | bytes 1572872 | tf_op jit(solution)/shard_map/cond/branch_1_fun/ppermute | solution.py:712
  162.1 22.4 %collective-permute-start.22 = (bf16[128,2048]{1,0:T(8,128)(2,1)S(1)}, bf16[128,2048]{1,0:T(8,128)(2,1)S(1)}, u32[]{:S(2)}, u32[]{:S(2)}) collective-permute-start(bf16[128,2048]{1,0:T(8,128)(2,1)S(1)} %add_convert_fusion.1), channel_id=1, source_target_pairs={{0,4},{2,6},{4,0},{6,2},{1,5},{3,7},{5,1},{7,3},{8,12},{10,14},{12... | collective-permute-start | bytes 1572872 | tf_op jit(solution)/shard_map/cond/branch_1_fun/ppermute | solution.py:712
  164.9 19.6 %collective-permute-start.23 = (bf16[128,2048]{1,0:T(8,128)(2,1)S(1)}, bf16[128,2048]{1,0:T(8,128)(2,1)S(1)}, u32[]{:S(2)}, u32[]{:S(2)}) collective-permute-start(bf16[128,2048]{1,0:T(8,128)(2,1)S(1)} %add_convert_fusion), channel_id=1, source_target_pairs={{0,2},{2,0},{4,6},{6,4},{1,3},{3,1},{5,7},{7,5},{8,10},{10,8},{12,... | collective-permute-start | bytes 1572872 | tf_op jit(solution)/shard_map/cond/branch_1_fun/ppermute | solution.py:712
  187.2 15.2 %collective-permute-start.25 = (bf16[128,2048]{1,0:T(8,128)(2,1)}, bf16[128,2048]{1,0:T(8,128)(2,1)}, u32[]{:S(2)}, u32[]{:S(2)}) collective-permute-start(bf16[128,2048]{1,0:T(8,128)(2,1)} %get-tuple-element.923), channel_id=1, source_target_pairs={{0,2},{2,0},{4,6},{6,4},{1,3},{3,1},{5,7},{7,5},{8,10},{10,8},{12,... | collective-permute-start | bytes 1572872 | tf_op jit(solution)/shard_map/cond/branch_1_fun/ppermute | solution.py:712
  188.6 15.2 %collective-permute-start.28 = (bf16[128,2048]{1,0:T(8,128)(2,1)}, bf16[128,2048]{1,0:T(8,128)(2,1)}, u32[]{:S(2)}, u32[]{:S(2)}) collective-permute-start(bf16[128,2048]{1,0:T(8,128)(2,1)} %get-tuple-element.924), channel_id=1, source_target_pairs={{0,4},{2,6},{4,0},{6,2},{1,5},{3,7},{5,1},{7,3},{8,12},{10,14},{12... | collective-permute-start | bytes 1572872 | tf_op jit(solution)/shard_map/cond/branch_1_fun/ppermute | solution.py:712
  189.2 24.4 %collective-permute-start.26 = (bf16[128,2048]{1,0:T(8,128)(2,1)}, bf16[128,2048]{1,0:T(8,128)(2,1)}, u32[]{:S(2)}, u32[]{:S(2)}) collective-permute-start(bf16[128,2048]{1,0:T(8,128)(2,1)} %get-tuple-element.924), channel_id=1, source_target_pairs={{0,2},{2,0},{4,6},{6,4},{1,3},{3,1},{5,7},{7,5},{8,10},{10,8},{12,... | collective-permute-start | bytes 1572872 | tf_op jit(solution)/shard_map/cond/branch_1_fun/ppermute | solution.py:712
  189.8 25.3 %collective-permute-start.27 = (bf16[128,2048]{1,0:T(8,128)(2,1)}, bf16[128,2048]{1,0:T(8,128)(2,1)}, u32[]{:S(2)}, u32[]{:S(2)}) collective-permute-start(bf16[128,2048]{1,0:T(8,128)(2,1)} %get-tuple-element.923), channel_id=1, source_target_pairs={{0,4},{2,6},{4,0},{6,2},{1,5},{3,7},{5,1},{7,3},{8,12},{10,14},{12... | collective-permute-start | bytes 1572872 | tf_op jit(solution)/shard_map/cond/branch_1_fun/ppermute | solution.py:712
  202.4 20.6 %collective-permute-start.29 = (bf16[128,2048]{1,0:T(8,128)(2,1)}, bf16[128,2048]{1,0:T(8,128)(2,1)}, u32[]{:S(2)}, u32[]{:S(2)}) collective-permute-start(bf16[128,2048]{1,0:T(8,128)(2,1)} %collective-permute-done.25), channel_id=1, source_target_pairs={{0,4},{2,6},{4,0},{6,2},{1,5},{3,7},{5,1},{7,3},{8,12},{10,14},{12... | collective-permute-start | bytes 1572872 | tf_op jit(solution)/shard_map/cond/branch_1_fun/ppermute | solution.py:712
  203.8 19.1 %collective-permute-start.30 = (bf16[128,2048]{1,0:T(8,128)(2,1)}, bf16[128,2048]{1,0:T(8,128)(2,1)}, u32[]{:S(2)}, u32[]{:S(2)}) collective-permute-start(bf16[128,2048]{1,0:T(8,128)(2,1)} %collective-permute-done.28), channel_id=1, source_target_pairs={{0,2},{2,0},{4,6},{6,4},{1,3},{3,1},{5,7},{7,5},{8,10},{10,8},{12,... | collective-permute-start | bytes 1572872 | tf_op jit(solution)/shard_map/cond/branch_1_fun/ppermute | solution.py:712
  223.3 15.9 %collective-permute-start.4 = (bf16[4,512,1536]{2,1,0:T(8,128)(2,1)}, bf16[4,512,1536]{2,1,0:T(8,128)(2,1)}, u32[]{:S(2)}, u32[]{:S(2)}) collective-permute-start(bf16[4,512,1536]{2,1,0:T(8,128)(2,1)} %get-tuple-element.303.refs_9_.refs_10_.refs_11_), channel_id=1, source_target_pairs={{0,1},{1,0},{2,3},{3,2},{4,5},{5,4},{6,7},{7,6},{8,9},{9,8},{10,11... | collective-permute-start | bytes 18874376 | tf_op jit(solution)/shard_map/cond/branch_1_fun/ppermute | solution.py:712
  238.7 14.8 %collective-permute-start.5 = (bf16[1024,2048]{1,0:T(8,128)(2,1)}, bf16[1024,2048]{1,0:T(8,128)(2,1)}, u32[]{:S(2)}, u32[]{:S(2)}) collective-permute-start(bf16[1024,2048]{1,0:T(8,128)(2,1)} %get-tuple-element.942.refs_0_), channel_id=1, source_target_pairs={{0,1},{1,0},{2,3},{3,2},{4,5},{5,4},{6,7},{7,6},{8,9},{9,8},{10,11... | collective-permute-start | bytes 12582920 | tf_op jit(solution)/shard_map/cond/branch_1_fun/ppermute | solution.py:712
  239.2 14.3 %collective-permute-start.6 = (bf16[1024,2048]{1,0:T(8,128)(2,1)}, bf16[1024,2048]{1,0:T(8,128)(2,1)}, u32[]{:S(2)}, u32[]{:S(2)}) collective-permute-start(bf16[1024,2048]{1,0:T(8,128)(2,1)} %get-tuple-element.312.refs_8_.refs_1_.refs_2_), channel_id=1, source_target_pairs={{0,1},{1,0},{2,3},{3,2},{4,5},{5,4},{6,7},{7,6},{8,9},{9,8},{10,11... | collective-permute-start | bytes 12582920 | tf_op jit(solution)/shard_map/cond/branch_1_fun/ppermute | solution.py:712
  280.0 182.6 %reduce-scatter.6.cloned.1.call-start = ((), (), s32[]{:S(2)}) async-start(), calls=%async_computation.4 | async-start | bytes 3932160 | tf_op jit(solution)/shard_map/reduce_scatter | solution.py:934
  308.9 15.5 %collective-permute-start.33 = (bf16[128,2048]{1,0:T(8,128)(2,1)}, bf16[128,2048]{1,0:T(8,128)(2,1)}, u32[]{:S(2)}, u32[]{:S(2)}) collective-permute-start(bf16[128,2048]{1,0:T(8,128)(2,1)} %get-tuple-element.331), channel_id=1, source_target_pairs={{0,4},{2,6},{4,0},{6,2},{1,5},{3,7},{5,1},{7,3},{8,12},{10,14},{12... | collective-permute-start | bytes 1572872 | tf_op jit(solution)/shard_map/cond/branch_1_fun/ppermute | solution.py:712
  308.9 19.0 %collective-permute-start.32 = (bf16[128,2048]{1,0:T(8,128)(2,1)}, bf16[128,2048]{1,0:T(8,128)(2,1)}, u32[]{:S(2)}, u32[]{:S(2)}) collective-permute-start(bf16[128,2048]{1,0:T(8,128)(2,1)} %get-tuple-element.330), channel_id=1, source_target_pairs={{0,2},{2,0},{4,6},{6,4},{1,3},{3,1},{5,7},{7,5},{8,10},{10,8},{12,... | collective-permute-start | bytes 1572872 | tf_op jit(solution)/shard_map/cond/branch_1_fun/ppermute | solution.py:712
  309.0 24.8 %collective-permute-start.38 = (bf16[1024,512]{1,0:T(8,128)(2,1)}, bf16[1024,512]{1,0:T(8,128)(2,1)}, u32[]{:S(2)}, u32[]{:S(2)}) collective-permute-start(bf16[1024,512]{1,0:T(8,128)(2,1)} %get-tuple-element.324.refs_3_), channel_id=1, source_target_pairs={{0,1},{1,0},{2,3},{3,2},{4,5},{5,4},{6,7},{7,6},{8,9},{9,8},{10,11... | collective-permute-start | bytes 3145736 | tf_op jit(solution)/shard_map/cond/branch_1_fun/ppermute | solution.py:712
  309.2 22.2 %collective-permute-start.39 = (bf16[1024,256]{1,0:T(8,128)(2,1)}, bf16[1024,256]{1,0:T(8,128)(2,1)}, u32[]{:S(2)}, u32[]{:S(2)}) collective-permute-start(bf16[1024,256]{1,0:T(8,128)(2,1)} %get-tuple-element.970), channel_id=1, source_target_pairs={{0,1},{1,0},{2,3},{3,2},{4,5},{5,4},{6,7},{7,6},{8,9},{9,8},{10,11... | collective-permute-start | bytes 1572872 | tf_op jit(solution)/shard_map/cond/branch_1_fun/ppermute | solution.py:712
  325.8 20.6 %collective-permute-start.36 = (bf16[128,2048]{1,0:T(8,128)(2,1)S(1)}, bf16[128,2048]{1,0:T(8,128)(2,1)}, u32[]{:S(2)}, u32[]{:S(2)}) collective-permute-start(bf16[128,2048]{1,0:T(8,128)(2,1)S(1)} %add_convert_fusion.2), channel_id=1, source_target_pairs={{0,2},{2,0},{4,6},{6,4},{1,3},{3,1},{5,7},{7,5},{8,10},{10,8},{12,... | collective-permute-start | bytes 1572872 | tf_op jit(solution)/shard_map/cond/branch_1_fun/ppermute | solution.py:712
  329.2 17.2 %collective-permute-start.35 = (bf16[128,2048]{1,0:T(8,128)(2,1)S(1)}, bf16[128,2048]{1,0:T(8,128)(2,1)}, u32[]{:S(2)}, u32[]{:S(2)}) collective-permute-start(bf16[128,2048]{1,0:T(8,128)(2,1)S(1)} %add_convert_fusion.3), channel_id=1, source_target_pairs={{0,4},{2,6},{4,0},{6,2},{1,5},{3,7},{5,1},{7,3},{8,12},{10,14},{12... | collective-permute-start | bytes 1572872 | tf_op jit(solution)/shard_map/cond/branch_1_fun/ppermute | solution.py:712
  331.3 20.1 %collective-permute-start.34 = (bf16[128,2048]{1,0:T(8,128)(2,1)S(1)}, bf16[128,2048]{1,0:T(8,128)(2,1)}, u32[]{:S(2)}, u32[]{:S(2)}) collective-permute-start(bf16[128,2048]{1,0:T(8,128)(2,1)S(1)} %copy-done.34), channel_id=1, source_target_pairs={{0,2},{2,0},{4,6},{6,4},{1,3},{3,1},{5,7},{7,5},{8,10},{10,8},{12,... | collective-permute-start | bytes 1572872 | tf_op jit(solution)/shard_map/cond/branch_1_fun/ppermute | solution.py:712
  331.4 23.2 %collective-permute-start.37 = (bf16[128,2048]{1,0:T(8,128)(2,1)S(1)}, bf16[128,2048]{1,0:T(8,128)(2,1)}, u32[]{:S(2)}, u32[]{:S(2)}) collective-permute-start(bf16[128,2048]{1,0:T(8,128)(2,1)S(1)} %copy-done.33), channel_id=1, source_target_pairs={{0,4},{2,6},{4,0},{6,2},{1,5},{3,7},{5,1},{7,3},{8,12},{10,14},{12... | collective-permute-start | bytes 1572872 | tf_op jit(solution)/shard_map/cond/branch_1_fun/ppermute | solution.py:712
  354.6 160.6 %reduce-scatter.8.cloned.1.call-start = ((), (), s32[]{:S(2)}) async-start(), calls=%async_computation.5 | async-start | bytes 4055040 | tf_op jit(solution)/shard_map/reduce_scatter | solution.py:934
  361.1 15.2 %collective-permute-start.12 = (bf16[128,2048]{1,0:T(8,128)(2,1)}, bf16[128,2048]{1,0:T(8,128)(2,1)}, u32[]{:S(2)}, u32[]{:S(2)}) collective-permute-start(bf16[128,2048]{1,0:T(8,128)(2,1)} %get-tuple-element.987), channel_id=1, source_target_pairs={{0,4},{2,6},{4,0},{6,2},{1,5},{3,7},{5,1},{7,3},{8,12},{10,14},{12... | collective-permute-start | bytes 1572872 | tf_op jit(solution)/shard_map/cond/branch_1_fun/ppermute | solution.py:712
  362.9 15.2 %collective-permute-start.9 = (bf16[128,2048]{1,0:T(8,128)(2,1)}, bf16[128,2048]{1,0:T(8,128)(2,1)}, u32[]{:S(2)}, u32[]{:S(2)}) collective-permute-start(bf16[128,2048]{1,0:T(8,128)(2,1)} %get-tuple-element.986), channel_id=1, source_target_pairs={{0,2},{2,0},{4,6},{6,4},{1,3},{3,1},{5,7},{7,5},{8,10},{10,8},{12,... | collective-permute-start | bytes 1572872 | tf_op jit(solution)/shard_map/cond/branch_1_fun/ppermute | solution.py:712
  363.2 26.1 %collective-permute-start.10 = (bf16[128,2048]{1,0:T(8,128)(2,1)}, bf16[128,2048]{1,0:T(8,128)(2,1)}, u32[]{:S(2)}, u32[]{:S(2)}) collective-permute-start(bf16[128,2048]{1,0:T(8,128)(2,1)} %get-tuple-element.987), channel_id=1, source_target_pairs={{0,2},{2,0},{4,6},{6,4},{1,3},{3,1},{5,7},{7,5},{8,10},{10,8},{12,... | collective-permute-start | bytes 1572872 | tf_op jit(solution)/shard_map/cond/branch_1_fun/ppermute | solution.py:712
  364.9 24.4 %collective-permute-start.11 = (bf16[128,2048]{1,0:T(8,128)(2,1)}, bf16[128,2048]{1,0:T(8,128)(2,1)}, u32[]{:S(2)}, u32[]{:S(2)}) collective-permute-start(bf16[128,2048]{1,0:T(8,128)(2,1)} %get-tuple-element.986), channel_id=1, source_target_pairs={{0,4},{2,6},{4,0},{6,2},{1,5},{3,7},{5,1},{7,3},{8,12},{10,14},{12... | collective-permute-start | bytes 1572872 | tf_op jit(solution)/shard_map/cond/branch_1_fun/ppermute | solution.py:712
  378.0 18.9 %collective-permute-start.13 = (bf16[128,2048]{1,0:T(8,128)(2,1)}, bf16[128,2048]{1,0:T(8,128)(2,1)}, u32[]{:S(2)}, u32[]{:S(2)}) collective-permute-start(bf16[128,2048]{1,0:T(8,128)(2,1)} %collective-permute-done.9), channel_id=1, source_target_pairs={{0,4},{2,6},{4,0},{6,2},{1,5},{3,7},{5,1},{7,3},{8,12},{10,14},{12... | collective-permute-start | bytes 1572872 | tf_op jit(solution)/shard_map/cond/branch_1_fun/ppermute | solution.py:712
  378.3 19.8 %collective-permute-start.14 = (bf16[128,2048]{1,0:T(8,128)(2,1)}, bf16[128,2048]{1,0:T(8,128)(2,1)}, u32[]{:S(2)}, u32[]{:S(2)}) collective-permute-start(bf16[128,2048]{1,0:T(8,128)(2,1)} %collective-permute-done.12), channel_id=1, source_target_pairs={{0,2},{2,0},{4,6},{6,4},{1,3},{3,1},{5,7},{7,5},{8,10},{10,8},{12,... | collective-permute-start | bytes 1572872 | tf_op jit(solution)/shard_map/cond/branch_1_fun/ppermute | solution.py:712
  398.1 44.5 %collective-permute-start.66 = (bf16[256,2048]{1,0:T(8,128)(2,1)}, bf16[256,2048]{1,0:T(8,128)(2,1)}, u32[]{:S(2)}, u32[]{:S(2)}) collective-permute-start(bf16[256,2048]{1,0:T(8,128)(2,1)} %get-tuple-element.754), channel_id=1, source_target_pairs={{0,2},{2,0},{4,6},{6,4},{1,3},{3,1},{5,7},{7,5},{8,10},{10,8},{12,... | collective-permute-start | bytes 3145736 | tf_op jit(solution)/shard_map/ppermute | solution.py:712
  398.7 45.6 %collective-permute-start.67 = (bf16[256,2048]{1,0:T(8,128)(2,1)}, bf16[256,2048]{1,0:T(8,128)(2,1)}, u32[]{:S(2)}, u32[]{:S(2)}) collective-permute-start(bf16[256,2048]{1,0:T(8,128)(2,1)} %get-tuple-element.755), channel_id=1, source_target_pairs={{0,4},{2,6},{4,0},{6,2},{1,5},{3,7},{5,1},{7,3},{8,12},{10,14},{12... | collective-permute-start | bytes 3145736 | tf_op jit(solution)/shard_map/ppermute | solution.py:712
  399.3 45.0 %collective-permute-start.68 = (bf16[256,2048]{1,0:T(8,128)(2,1)}, bf16[256,2048]{1,0:T(8,128)(2,1)}, u32[]{:S(2)}, u32[]{:S(2)}) collective-permute-start(bf16[256,2048]{1,0:T(8,128)(2,1)} %get-tuple-element.756), channel_id=1, source_target_pairs={{0,6},{2,4},{4,2},{6,0},{1,7},{3,5},{5,3},{7,1},{8,14},{10,12},{12... | collective-permute-start | bytes 3145736 | tf_op jit(solution)/shard_map/ppermute | solution.py:712
  411.1 17.7 %collective-permute-start.16 = (bf16[1024,2048]{1,0:T(8,128)(2,1)}, bf16[1024,2048]{1,0:T(8,128)(2,1)}, u32[]{:S(2)}, u32[]{:S(2)}) collective-permute-start(bf16[1024,2048]{1,0:T(8,128)(2,1)} %get-tuple-element.384), channel_id=1, source_target_pairs={{0,1},{1,0},{2,3},{3,2},{4,5},{5,4},{6,7},{7,6},{8,9},{9,8},{10,11... | collective-permute-start | bytes 12582920 | tf_op jit(solution)/shard_map/cond/branch_1_fun/ppermute | solution.py:712
  428.8 13.8 %collective-permute-start.40 = (bf16[4,256,512]{2,1,0:T(8,128)(2,1)}, bf16[4,256,512]{2,1,0:T(8,128)(2,1)}, u32[]{:S(2)}, u32[]{:S(2)}) collective-permute-start(bf16[4,256,512]{2,1,0:T(8,128)(2,1)} %get-tuple-element.401), channel_id=1, source_target_pairs={{0,1},{1,0},{2,3},{3,2},{4,5},{5,4},{6,7},{7,6},{8,9},{9,8},{10,11... | collective-permute-start | bytes 3145736 | tf_op jit(solution)/shard_map/cond/branch_1_fun/ppermute | solution.py:712
  462.6 15.1 %collective-permute-start.41 = (bf16[128,2048]{1,0:T(8,128)(2,1)}, bf16[128,2048]{1,0:T(8,128)(2,1)S(1)}, u32[]{:S(2)}, u32[]{:S(2)}) collective-permute-start(bf16[128,2048]{1,0:T(8,128)(2,1)} %get-tuple-element.425), channel_id=1, source_target_pairs={{0,2},{2,0},{4,6},{6,4},{1,3},{3,1},{5,7},{7,5},{8,10},{10,8},{12,... | collective-permute-start | bytes 1572872 | tf_op jit(solution)/shard_map/cond/branch_1_fun/ppermute | solution.py:712
  464.1 15.1 %collective-permute-start.44 = (bf16[128,2048]{1,0:T(8,128)(2,1)}, bf16[128,2048]{1,0:T(8,128)(2,1)S(1)}, u32[]{:S(2)}, u32[]{:S(2)}) collective-permute-start(bf16[128,2048]{1,0:T(8,128)(2,1)} %get-tuple-element.428), channel_id=1, source_target_pairs={{0,4},{2,6},{4,0},{6,2},{1,5},{3,7},{5,1},{7,3},{8,12},{10,14},{12... | collective-permute-start | bytes 1572872 | tf_op jit(solution)/shard_map/cond/branch_1_fun/ppermute | solution.py:712
  466.0 21.1 %collective-permute-start.42 = (bf16[128,2048]{1,0:T(8,128)(2,1)S(1)}, bf16[128,2048]{1,0:T(8,128)(2,1)}, u32[]{:S(2)}, u32[]{:S(2)}) collective-permute-start(bf16[128,2048]{1,0:T(8,128)(2,1)S(1)} %add_convert_fusion.5), channel_id=1, source_target_pairs={{0,4},{2,6},{4,0},{6,2},{1,5},{3,7},{5,1},{7,3},{8,12},{10,14},{12... | collective-permute-start | bytes 1572872 | tf_op jit(solution)/shard_map/cond/branch_1_fun/ppermute | solution.py:712
  469.7 17.5 %collective-permute-start.43 = (bf16[128,2048]{1,0:T(8,128)(2,1)}, bf16[128,2048]{1,0:T(8,128)(2,1)}, u32[]{:S(2)}, u32[]{:S(2)}) collective-permute-start(bf16[128,2048]{1,0:T(8,128)(2,1)} %add_convert_fusion.4), channel_id=1, source_target_pairs={{0,2},{2,0},{4,6},{6,4},{1,3},{3,1},{5,7},{7,5},{8,10},{10,8},{12,... | collective-permute-start | bytes 1572872 | tf_op jit(solution)/shard_map/cond/branch_1_fun/ppermute | solution.py:712
  487.3 16.4 %collective-permute-start.45 = (bf16[128,2304]{1,0:T(8,128)(2,1)S(1)}, bf16[128,2304]{1,0:T(8,128)(2,1)}, u32[]{:S(2)}, u32[]{:S(2)}) collective-permute-start(bf16[128,2304]{1,0:T(8,128)(2,1)S(1)} %get-tuple-element.827), channel_id=1, source_target_pairs={{0,2},{2,0},{4,6},{6,4},{1,3},{3,1},{5,7},{7,5},{8,10},{10,8},{12,... | collective-permute-start | bytes 1769480 | tf_op jit(solution)/shard_map/cond/branch_1_fun/ppermute | solution.py:712
  487.6 24.1 %collective-permute-start.46 = (bf16[128,2304]{1,0:T(8,128)(2,1)S(1)}, bf16[128,2304]{1,0:T(8,128)(2,1)}, u32[]{:S(2)}, u32[]{:S(2)}) collective-permute-start(bf16[128,2304]{1,0:T(8,128)(2,1)S(1)} %get-tuple-element.826), channel_id=1, source_target_pairs={{0,4},{2,6},{4,0},{6,2},{1,5},{3,7},{5,1},{7,3},{8,12},{10,14},{12... | collective-permute-start | bytes 1769480 | tf_op jit(solution)/shard_map/cond/branch_1_fun/ppermute | solution.py:712
  488.1 23.7 %collective-permute-start.47 = (bf16[128,2304]{1,0:T(8,128)(2,1)S(1)}, bf16[128,2304]{1,0:T(8,128)(2,1)}, u32[]{:S(2)}, u32[]{:S(2)}) collective-permute-start(bf16[128,2304]{1,0:T(8,128)(2,1)S(1)} %get-tuple-element.825), channel_id=1, source_target_pairs={{0,6},{2,4},{4,2},{6,0},{1,7},{3,5},{5,3},{7,1},{8,14},{10,12},{12... | collective-permute-start | bytes 1769480 | tf_op jit(solution)/shard_map/cond/branch_1_fun/ppermute | solution.py:712
  (51 other events, 850.5 us)
Sparse Core Ops, SparseCore 0:
  29.1 65.4 all-gather.6
  96.7 113.9 all-gather.8
  212.3 61.7 all-gather.10
  280.1 108.0 reduce-scatter.3
  390.4 60.7 reduce-scatter.5
  453.4 61.7 reduce-scatter.7
